TPU v7x, 32 devices: a whole 2x2x4 slice. The times are simulated.
32 devices in a mesh: seq: 16 (over z, y, x), head: 2 (over core).
Axes of the slice: x: 2, y: 2, z: 4, core: 2. Of those that a mesh axis runs over, the one named last changes fastest.
Arguments:
- queries: bfloat16 [8192, 8, 512], P('seq', 'head'), may hold values from -8 to 8
- token_keys: bfloat16 [8192, 8, 512], P('seq', 'head'), may hold values from -8 to 8
- token_values: bfloat16 [8192, 8, 512], P('seq', 'head'), may hold values from -8 to 8
- fast_weights: bfloat16 [512, 8, 3, 512], P(None, 'head'), may hold values from -0.25 to 0.25
- learn_rate: float32 [8], P('head'), may hold values from 1 to 10
- out_gain: float32 [8, 512], P('head'), may hold values from 0.5 to 1.5
- group_lengths: int32 [2], replicated, may hold values from 1 to 6144, 8192 in all
- slot_order: int32 [8192], P('seq'), may hold values from 0 to 8191, as said below
Outputs:
- balanced_out: bfloat16 [8192, 8, 512], P('seq', 'head')
Inputs may be any that keep to these rules, and one draw needn't show every extreme that they name: slot_order is a permutation of the positions; slot j, with r = j % 512, holds a position of the block [e * 512, (e + 1) * 512) with e = r // 32. `group_lengths`: the two lengths sum to 8192; each lies between 2048 and 6144.
All inputs are finite; a program needn't handle non-finite values.
Results may differ from a plain program's by a relative error of at most 0.0075.
Values may be sent and summed in bfloat16 or wider, within the bound.
No kernel may reach another device: no remote copies, remote signals or barrier semaphores. Data moves between devices by JAX's collectives and lax.ppermute only.
A program may use at most 192 MiB of HBM per device.

v0:
```python
import math

import jax
import jax.numpy as jnp
from jax import lax
from jax.sharding import PartitionSpec as P

WINDOW = 2048


eps = 1e-06


def shifted(value, axis, steps):
    count = lax.axis_size(axis)
    first, last = (max(0, -steps), min(count, count - steps))
    return lax.ppermute(value, axis, [(source, source + steps) for source in range(first, last)])


def window_attention(queries, token_keys, token_values):
    tok_rows, head_count, head_width = queries.shape
    device_pos = lax.axis_index("seq")
    shifts = (WINDOW + tok_rows - 1) // tok_rows
    own_rows = jnp.stack([token_keys, token_values])
    pieces = []
    for distance in range(shifts, 0, -1):
        pieces.append(shifted(own_rows, "seq", distance))
    pieces.append(own_rows)
    key_slab = jnp.concatenate(pieces, axis=1)
    block_rows = min(tok_rows, 512)
    key_span = WINDOW + block_rows
    score_scale = 1.0 / math.sqrt(head_width)

    def attend(block_index):
        first_row = block_index * block_rows
        scores = (
            jnp.einsum("qhd,khd->hqk", queries, key_slab[0], preferred_element_type=jnp.float32)
            * score_scale
        )
        query_pos = first_row + jnp.arange(block_rows, dtype=jnp.int32)[:, None]
        key_pos = first_row - WINDOW + jnp.arange(key_span, dtype=jnp.int32)[None, :]
        allowed = (
            (key_pos <= query_pos)
            & (key_pos > query_pos - WINDOW)
            & (device_pos * tok_rows + key_pos >= 0)
        )
        scores = jnp.where(allowed[None], scores, -jnp.inf)
        row_max = jnp.max(scores, axis=-1, keepdims=True)
        expo = jnp.exp(scores - row_max)
        prob_rows = (expo / jnp.sum(expo, axis=-1, keepdims=True)).astype(jnp.bfloat16)
        return jnp.einsum(
            "hqk,khd->qhd", prob_rows, key_slab[1], preferred_element_type=jnp.float32
        ).astype(jnp.bfloat16)

    blocks = lax.map(attend, jnp.arange(tok_rows // block_rows, dtype=jnp.int32))
    return blocks.reshape(tok_rows, head_count, head_width)


def swiglu_apply(inputs, weights):
    both_pre = jnp.einsum(
        "thd,fhcd->thcf", inputs, weights[:, :, 0:2, :], preferred_element_type=jnp.float32
    )
    hidden_act = (jax.nn.silu(both_pre[:, :, 0, :]) * both_pre[:, :, 1, :]).astype(jnp.bfloat16)
    return jnp.einsum(
        "thf,fhd->thd", hidden_act, weights[:, :, 2, :], preferred_element_type=jnp.float32
    ).astype(jnp.bfloat16)


def renormed(old_rows, summed, learn_rate, group_count):
    previous = old_rows.astype(jnp.float32)
    updated = previous + learn_rate[None, :, None, None] / group_count * summed
    old_norm = jnp.sqrt(jnp.sum(previous * previous, axis=-1, keepdims=True) + eps)
    new_norm = jnp.sqrt(jnp.sum(updated * updated, axis=-1, keepdims=True) + eps)
    return (updated * (old_norm / new_norm)).astype(jnp.bfloat16)


def fast_section(queries, token_keys, token_values, positions, fast_weights, learn_rate, first_len):
    member = positions < first_len
    group_count = first_len.astype(jnp.float32)
    both_pre = jnp.einsum(
        "thd,fhcd->thcf", token_keys, fast_weights[:, :, 0:2, :], preferred_element_type=jnp.float32
    )
    gate_pre = both_pre[:, :, 0, :]
    up_pre = both_pre[:, :, 1, :]
    sig_gate = jax.nn.sigmoid(gate_pre)
    activation = (jax.nn.silu(gate_pre) * up_pre).astype(jnp.bfloat16)
    masked_values = jnp.where(member[:, None, None], token_values, jnp.zeros_like(token_values))
    back_act = jnp.einsum(
        "thd,fhd->thf", masked_values, fast_weights[:, :, 2, :], preferred_element_type=jnp.float32
    )
    grad_up = (back_act * gate_pre * sig_gate).astype(jnp.bfloat16)
    grad_gate = (back_act * up_pre * sig_gate * (1.0 + gate_pre * (1.0 - sig_gate))).astype(
        jnp.bfloat16
    )
    term_gate = jnp.einsum(
        "thf,thd->fhd", grad_gate, token_keys, preferred_element_type=jnp.float32
    )
    term_up = jnp.einsum("thf,thd->fhd", grad_up, token_keys, preferred_element_type=jnp.float32)
    term_down = jnp.einsum(
        "thf,thd->fhd", activation, masked_values, preferred_element_type=jnp.float32
    )
    summed = lax.psum(jnp.stack([term_gate, term_up, term_down], axis=2), "seq")
    new_weights = renormed(fast_weights, summed, learn_rate, group_count)
    first_out = swiglu_apply(queries, fast_weights)
    second_out = swiglu_apply(queries, new_weights)
    return jnp.where(member[:, None, None], first_out, second_out)


def token_norm(attention, fast_out, out_gain):
    summed_rows = attention.astype(jnp.float32) + fast_out.astype(jnp.float32)
    local_power = jnp.sum(summed_rows * summed_rows, axis=(1, 2))
    power = lax.psum(local_power, "head")
    total_width = summed_rows.shape[1] * summed_rows.shape[2] * lax.axis_size("head")
    row_scale = lax.rsqrt(power / total_width + eps)
    return (summed_rows * row_scale[:, None, None] * out_gain[None, :, :]).astype(jnp.bfloat16)


def gather_local(source, asked_rows):
    flat_rows = jnp.take(source, asked_rows.reshape(-1), axis=0)
    return flat_rows.reshape(asked_rows.shape + source.shape[1:])


def per_device(
    queries, token_keys, token_values, fast_weights, learn_rate, out_gain, group_lengths, slot_order
):
    tok_rows = queries.shape[0]
    seq_count = lax.axis_size("seq")
    seg_rows = tok_rows // seq_count
    first_len = group_lengths[0]
    attention = window_attention(queries, token_keys, token_values)
    source_dev = jnp.arange(tok_rows, dtype=jnp.int32) // seg_rows
    wanted = (slot_order - source_dev * tok_rows).reshape(seq_count, seg_rows)
    asked_rows = lax.all_to_all(wanted, "seq", split_axis=0, concat_axis=0, tiled=True)
    positions = lax.axis_index("seq") * tok_rows + jnp.arange(tok_rows, dtype=jnp.int32)
    fast_out = fast_section(
        queries, token_keys, token_values, positions, fast_weights, learn_rate, first_len
    )
    normed = token_norm(attention, fast_out, out_gain)
    mixed_here = lax.all_to_all(
        gather_local(normed, asked_rows), "seq", split_axis=0, concat_axis=0, tiled=True
    )
    return mixed_here.reshape(normed.shape)


def solution(mesh):
    return jax.shard_map(
        per_device,
        mesh=mesh,
        in_specs=(
            P("seq", "head", None),
            P("seq", "head", None),
            P("seq", "head", None),
            P(None, "head", None, None),
            P("head"),
            P("head", None),
            P(),
            P("seq"),
        ),
        out_specs=P("seq", "head", None),
        check_vma=False,
    )
```

profile of v0, /device:TPU:13, one launch (start us, length us, event | category | flops | bytes accessed | tf_op | source)
XLA Modules:
  0.0 815.6 jit_solution(17197666637886961048)
XLA Ops:
  6.5 5.6 slice.46
  12.1 4.4 copy.105
  16.6 3.0 copy.142
  19.6 6.2 fusion.26
  25.9 2.9 convolution_bitcast_fusion.1
  30.5 3.5 convolution_bitcast_fusion.2
  34.0 3.8 convolution_bitcast_fusion.3
  37.8 10.6 %pad_maximum_fusion = f32[512,4,3,512]{3,0,1,2:T(8,128)} fusion(f32[512,4,1,512]{3,0,1,2:T(8,128)} %convolution_bitcast_fusion.1, f32[512,4,1,512]{3,0,1,2:T(8,128)} %convolution_bitcast_fusion.2, f32[512,4,1,512]{3,0,1,2:T(8,128)} %convolution_bitcast_fusion.3), kind=kLoop, calls=%fused_computation.9 | loop fusion | flops 6291456 | bytes 25165824 | tf_op jit(solution)/shard_map/stack | solution.py:102
  48.5 2.4 copy_bitcast_fusion
  54.4 3.2 collective-permute-start
  57.6 4.1 collective-permute-start.1
  61.7 3.1 collective-permute-start.2
  67.5 8.8 %all-to-all-start = ((s32[16,1,32]{2,1,0:T(1,128)}), s32[16,1,32]{2,1,0:T(1,128)S(1)}, u32[]{:S(2)}, u32[]{:S(2)}) async-start(s32[16,1,32]{2,1,0:T(1,128)} %all_to_all.9), calls=%async_computation | async-start | bytes 16384 | tf_op jit(solution)/shard_map/all_to_all | solution.py:133
  78.4 8.7 %fusion.23 = f32[512,4,2,512]{0,3,2,1:T(8,128)} fusion(bf16[512,4,2,512]{3,1,2,0:T(4,128)(2,1)} %slice.46, bf16[512,4,512,1]{2,1,0,3:T(4,128)(2,1)S(1)} %bitcast.145), kind=kOutput, calls=%fused_computation.49 | convolution fusion | flops 2147483648 | bytes 14680064 | tf_op jit(solution)/shard_map/thd,fhcd->thcf/dot_general | solution.py:60
  87.1 506.3 %all-to-all-done = s32[16,1,32]{2,1,0:T(1,128)S(1)} async-done(((s32[16,1,32]{2,1,0:T(1,128)}), s32[16,1,32]{2,1,0:T(1,128)S(1)}, u32[]{:S(2)}, u32[]{:S(2)}) %all-to-all-start) | async-done | bytes 2080 | tf_op jit(solution)/shard_map/all_to_all | solution.py:133
  594.6 4.6 constant_dynamic-update-slice_fusion.4
  599.2 4.5 constant_dynamic-update-slice_fusion.3
  603.7 4.5 constant_dynamic-update-slice_fusion.2
  608.3 5.2 constant_dynamic-update-slice_fusion.1
  615.9 12.5 %fusion.3 = f32[4,2560,512]{2,1,0:T(8,128)} fusion(bf16[2,2560,4,512]{3,1,2,0:T(8,128)(2,1)} %constant_dynamic-update-slice_fusion, bf16[512,4,512]{2,1,0:T(4,128)(2,1)S(1)} %copy-done.1), kind=kOutput, calls=%fused_computation.13 | convolution fusion | flops 5368709120 | bytes 33554432 | tf_op jit(solution)/shard_map/while/body/eval_jaxpr/qhd,khd->hqk/dot_general | solution.py:37
  628.4 23.3 %fusion.67 = (f32[4,512]{1,0:T(4,128)S(1)}, f32[4,512,2560]{1,2,0:T(8,128)}) fusion(f32[4,2560,512]{2,1,0:T(8,128)} %fusion.3, pred[512,2560]{0,1:T(8,128)(4,1)S(1)} %fusion.9), kind=kOutput, calls=%fused_computation.111 | output fusion | flops 31459840 | bytes 43261952 | tf_op jit(solution)/shard_map/while/body/eval_jaxpr/sub | solution.py:49
  651.7 15.7 %fusion.41 = bf16[4,512,512]{2,1,0:T(8,128)(2,1)} fusion(f32[4,512,2560]{1,2,0:T(8,128)} %get-tuple-element.22, f32[4,512]{1,0:T(4,128)S(1)} %get-tuple-element.20, bf16[2,2560,4,512]{3,1,2,0:T(8,128)(2,1)} %constant_dynamic-update-slice_fusion), kind=kOutput, calls=%fused_computation.68 | convolution fusion | flops 5380243456 | bytes 33562624 | tf_op jit(solution)/shard_map/while/body/eval_jaxpr/hqk,khd->qhd/dot_general | solution.py:51
  667.4 43.8 %all-reduce.2.cloned.1.call-done = f32[512,4,3,512]{3,0,1,2:T(8,128)} async-done(((f32[512,4,3,512]{3,0,1,2:T(8,128)}), f32[512,4,3,512]{3,0,1,2:T(8,128)}) %all-reduce.2.cloned.1.call-update) | async-done | bytes 12582928 | tf_op jit(solution)/shard_map/psum | solution.py:102
  711.2 12.3 %fusion.2 = (f32[512,4,3]{0,1,2:T(4,128)S(1)}, f32[512,4,3]{0,1,2:T(4,128)S(1)}) fusion(bf16[512,4,3,512]{3,1,2,0:T(4,128)(2,1)} %param.11, f32[512,4,3,512]{3,0,1,2:T(8,128)} %all-reduce.2.cloned.1.call-done, f32[4]{0:T(128)S(1)} %broadcast_divide_fusion), kind=kLoop, calls=%fused_computation.8 | loop fusion | flops 22007808 | bytes 18923536 | tf_op jit(solution)/shard_map/reduce_sum | solution.py:72
  723.6 4.9 multiply_convert_fusion
  734.4 3.3 multiply_reduce_fusion.1
  737.7 3.1 psum.15
  740.7 3.0 multiply_convert_fusion.1
  743.7 3.3 copy.120
  747.0 4.2 gather_fusion
  752.0 53.3 %all_to_all.14 = bf16[16,32,4,512]{3,1,2,0:T(8,128)(2,1)S(1)} all-to-all(bf16[16,32,4,512]{3,1,2,0:T(8,128)(2,1)S(1)} %copy.122), channel_id=1, replica_groups=mesh['seq'=16,'head'=2] {'seq'}, dimensions={0} | all-to-all | bytes 4194304 | tf_op jit(solution)/shard_map/all_to_all | solution.py:139
  805.6 2.9 copy.124
  (69 shorter events, 20.3 us)
Async XLA Ops:
  6.5 704.7 %all-reduce.2.cloned.1.call-start = ((), (), s32[]{:S(2)}) async-start(), calls=%async_computation.2 | async-start | bytes 25165824 | tf_op jit(solution)/shard_map/psum | solution.py:102
  12.1 4.4 slice-start
  19.6 6.2 copy-start.13
  19.6 6.3 copy-start.9
  25.9 3.0 copy-start.7
  28.9 1.6 copy-start.6
  51.0 2.8 copy-start.2
  51.0 3.4 copy-start.4
  51.0 15.8 %copy-start.12 = (s32[512]{0:T(512)S(1)}, s32[512]{0:T(512)}, u32[]{:S(2)}) copy-start(s32[512]{0:T(512)} %param.15) | copy-start | bytes 6148
  51.0 27.4 %copy-start.1 = (bf16[512,4,512]{2,1,0:T(4,128)(2,1)S(1)}, bf16[512,4,512]{2,1,0:T(4,128)(2,1)}, u32[]{:S(2)}) copy-start(bf16[512,4,512]{2,1,0:T(4,128)(2,1)} %param.8) | copy-start | bytes 6291460
  54.4 540.2 %collective-permute-start = (bf16[2,512,4,512]{3,1,2,0:T(8,128)(2,1)}, bf16[2,512,4,512]{3,1,2,0:T(8,128)(2,1)}, u32[]{:S(2)}, u32[]{:S(2)}) collective-permute-start(bf16[2,512,4,512]{3,1,2,0:T(8,128)(2,1)} %pad_maximum_fusion.1), channel_id=1, source_target_pairs={{0,8},{2,10},{4,12},{6,14},{8,16},{10,18},{12,20},{14,22},{16,24},... | collective-permute-start | bytes 12582920 | tf_op jit(solution)/shard_map/ppermute | solution.py:17
  57.6 541.6 %collective-permute-start.1 = (bf16[2,512,4,512]{3,1,2,0:T(8,128)(2,1)}, bf16[2,512,4,512]{3,1,2,0:T(8,128)(2,1)}, u32[]{:S(2)}, u32[]{:S(2)}) collective-permute-start(bf16[2,512,4,512]{3,1,2,0:T(8,128)(2,1)} %pad_maximum_fusion.1), channel_id=1, source_target_pairs={{0,6},{2,8},{4,10},{6,12},{8,14},{10,16},{12,18},{14,20},{16,22},{... | collective-permute-start | bytes 12582920 | tf_op jit(solution)/shard_map/ppermute | solution.py:17
  61.7 542.0 %collective-permute-start.2 = (bf16[2,512,4,512]{3,1,2,0:T(8,128)(2,1)}, bf16[2,512,4,512]{3,1,2,0:T(8,128)(2,1)}, u32[]{:S(2)}, u32[]{:S(2)}) collective-permute-start(bf16[2,512,4,512]{3,1,2,0:T(8,128)(2,1)} %pad_maximum_fusion.1), channel_id=1, source_target_pairs={{0,4},{2,6},{4,8},{6,10},{8,12},{10,14},{12,16},{14,18},{16,20},{1... | collective-permute-start | bytes 12582920 | tf_op jit(solution)/shard_map/ppermute | solution.py:17
  64.9 543.4 %collective-permute-start.3 = (bf16[2,512,4,512]{3,1,2,0:T(8,128)(2,1)}, bf16[2,512,4,512]{3,1,2,0:T(8,128)(2,1)}, u32[]{:S(2)}, u32[]{:S(2)}) collective-permute-start(bf16[2,512,4,512]{3,1,2,0:T(8,128)(2,1)} %pad_maximum_fusion.1), channel_id=1, source_target_pairs={{0,2},{2,4},{4,6},{6,8},{8,10},{10,12},{12,14},{14,16},{16,18},{18... | collective-permute-start | bytes 12582920 | tf_op jit(solution)/shard_map/ppermute | solution.py:17
  67.5 525.9 %all-to-all-start = ((s32[16,1,32]{2,1,0:T(1,128)}), s32[16,1,32]{2,1,0:T(1,128)S(1)}, u32[]{:S(2)}, u32[]{:S(2)}) async-start(s32[16,1,32]{2,1,0:T(1,128)} %all_to_all.9), calls=%async_computation | async-start | bytes 16384 | tf_op jit(solution)/shard_map/all_to_all | solution.py:133
  78.4 8.7 %copy-start.14 = (f32[4]{0:T(128)S(1)}, f32[4]{0:T(128)}, u32[]{:S(2)}) copy-start(f32[4]{0:T(128)} %param.12) | copy-start | bytes 52
  608.3 5.2 copy-start.3
  608.3 5.2 copy-start.5
  711.2 12.3 %copy-start = (f32[512,4,3,512]{3,0,1,2:T(8,128)S(1)}, f32[512,4,3,512]{3,0,1,2:T(8,128)}, u32[]{:S(2)}) copy-start(f32[512,4,3,512]{3,0,1,2:T(8,128)} %all-reduce.2.cloned.1.call-done) | copy-start | bytes 37748740
  728.5 4.5 slice-start.1
  730.9 2.2 slice-start.2
  730.9 2.9 copy-start.8
  730.9 3.5 copy-start.10
  734.4 6.4 copy-start.11
Sparse Core Ops, SparseCore 0:
  48.6 662.5 all-reduce.1
where the time goes:
time: 829 us; the launch traced here: 816 us
  waiting for transfers between devices  550 us (66%)
  matrix products  62.5 us (8%)
  other arithmetic  61.9 us (7%)
  blocking collectives  56.4 us (7%)
  local copies, waits for them, and re-layouts  49.6 us (6%)
  starting transfers between devices  21.1 us (3%)
  between operations  14 us (2%)
    all_to_all x1, waiting for transfers between devices, per_device(): lax.all_to_all(wanted, 'seq', split_axis=0, concat_axis=0, tiled=True)  506 us
    all_to_all x1, blocking collectives, per_device(): lax.all_to_all(gather_local(normed, asked_rows), 'seq', split_axis=0, con...  53.3 us
    psum x1, waiting for transfers between devices, fast_section(): summed = lax.psum(jnp.stack([term_gate, term_up, term_down], axis=2), 'seq')  43.8 us
    unnamed x40, local copies, waits for them, and re-layouts  29 us
    sub x1, other arithmetic, attend(): expo = jnp.exp(scores - row_max)  23.3 us
  transfers between devices with their start and end apart: 6, of which 2 were waited for; matrix products, arithmetic and copies ran while one was open for 11% of the time, Pallas kernels for 0%

commit v1 on v0

v1 whole, which is shorter than its diff:
```python
import functools
import math

import jax
import jax.numpy as jnp
from jax import lax
from jax.experimental import pallas as pl
from jax.experimental.pallas import tpu as pltpu
from jax.sharding import PartitionSpec as P

WINDOW = 2048
NEG = -1e30
VMEM_BYTES = 58 * 1024 * 1024

eps = 1e-06

NT = (((1,), (1,)), ((), ()))
TN = (((0,), (0,)), ((), ()))
NN = (((1,), (0,)), ((), ()))


def dot(left, right, dims):
    return lax.dot_general(left, right, dims, preferred_element_type=jnp.float32)


def swap_pairs(count, distance):
    return [(index, index ^ distance) for index in range(count)]


def plane_pairs(count, steps):
    return [(index, index + steps) for index in range(count - steps)]


def spread_heads(value, member, count, order):
    group = value.shape[1]
    by_head = jnp.transpose(value, (1, 0, 2))
    pieces = [None] * group
    for distance in order:
        piece = lax.dynamic_index_in_dim(by_head, member ^ distance, 0, keepdims=False)
        if distance:
            piece = lax.ppermute(piece, "seq", swap_pairs(count, distance))
        pieces[distance] = piece
    return pieces


def grad_kernel(group, tok, info_ref, w_ref, *refs):
    k_any, v_any = refs[:group], refs[group : 2 * group]
    out_ref, kbuf, vbuf, acc, sems = refs[2 * group :]
    plane, member, first_len = info_ref[0], info_ref[1], info_ref[2]
    copies = []
    for d in range(group):
        pair = (
            pltpu.make_async_copy(k_any[d], kbuf.at[d], sems.at[0, d]),
            pltpu.make_async_copy(v_any[d], vbuf.at[d], sems.at[1, d]),
        )
        for copy in pair:
            copy.start()
        copies.append(pair)
    acc[...] = jnp.zeros_like(acc)
    hidden = w_ref.shape[1]
    part = min(256, hidden)
    for d in range(group):
        for copy in copies[d]:
            copy.wait()
        first_tok = (plane * group + (member ^ d)) * tok

        @pl.when(first_tok < first_len)
        def _():
            keys = kbuf[d]
            token = first_tok + lax.broadcasted_iota(jnp.int32, (tok, 1), 0)
            values = jnp.where(token < first_len, vbuf[d].astype(jnp.float32), 0.0)
            values = values.astype(jnp.bfloat16)
            for f in range(0, hidden, part):
                rows = pl.ds(f, part)
                gate = dot(keys, w_ref[0, rows, :], NT)
                up = dot(keys, w_ref[1, rows, :], NT)
                back = dot(values, w_ref[2, rows, :], NT)
                sig = jax.nn.sigmoid(gate)
                silu = gate * sig
                act = (silu * up).astype(jnp.bfloat16)
                grad_up = (back * silu).astype(jnp.bfloat16)
                grad_gate = (back * up * sig * (1.0 + gate * (1.0 - sig))).astype(jnp.bfloat16)
                acc[0, rows, :] += dot(grad_gate, keys, TN)
                acc[1, rows, :] += dot(grad_up, keys, TN)
                acc[2, rows, :] += dot(act, values, TN)

    out_ref[...] = acc[...].astype(out_ref.dtype)


def weight_sums(info, weights, keys, values):
    group = len(keys)
    tok, width = keys[0].shape
    rows, hidden, _ = weights.shape
    flops = 2 * 6 * group * tok * hidden * width
    return pl.pallas_call(
        functools.partial(grad_kernel, group, tok),
        out_shape=jax.ShapeDtypeStruct(weights.shape, jnp.bfloat16),
        in_specs=[
            pl.BlockSpec(memory_space=pltpu.SMEM),
            pl.BlockSpec(memory_space=pltpu.VMEM),
        ]
        + [pl.BlockSpec(memory_space=pl.ANY)] * (2 * group),
        out_specs=pl.BlockSpec(memory_space=pltpu.VMEM),
        scratch_shapes=[
            pltpu.VMEM((group, tok, width), jnp.bfloat16),
            pltpu.VMEM((group, tok, width), jnp.bfloat16),
            pltpu.VMEM(weights.shape, jnp.float32),
            pltpu.SemaphoreType.DMA((2, group)),
        ],
        compiler_params=pltpu.CompilerParams(vmem_limit_bytes=VMEM_BYTES),
        cost_estimate=pl.CostEstimate(
            flops=flops,
            bytes_accessed=2 * (2 * group * tok * width + 2 * rows * hidden * width),
            transcendentals=group * tok * hidden,
        ),
        name="weight_sums",
    )(info, weights, *keys, *values)


def attend_kernel(group, tok, slots, block, info_ref, *refs):
    count = group * slots
    q_any, k_any, v_any = refs[:group], refs[group : group + count], refs[group + count : group + 2 * count]
    out_ref, qbuf, kbuf, vbuf, sems = refs[group + 2 * count :]
    plane, member = info_ref[0], info_ref[1]
    width = qbuf.shape[-1]
    copies = []
    for d in range(group):
        place = pl.ds(pl.multiple_of((member ^ d) * tok, tok), tok)
        copies.append(pltpu.make_async_copy(q_any[d], qbuf.at[place], sems.at[0, d]))
    for s in range(slots):
        for d in range(group):
            place = pl.ds(pl.multiple_of((s * group + (member ^ d)) * tok, tok), tok)
            at = s * group + d
            copies.append(pltpu.make_async_copy(k_any[at], kbuf.at[place], sems.at[1, at]))
            copies.append(pltpu.make_async_copy(v_any[at], vbuf.at[place], sems.at[2, at]))
    for copy in copies:
        copy.start()
    for copy in copies:
        copy.wait()
    behind = (slots - 1) * group * tok
    span = behind + block
    scale = math.log2(math.e) / math.sqrt(width)
    first_key = jnp.maximum(behind - plane * group * tok, 0)
    row = lax.broadcasted_iota(jnp.int32, (block, span), 0)
    col = lax.broadcasted_iota(jnp.int32, (block, span), 1)
    band = (col > row + (behind - WINDOW)) & (col <= row + behind)

    def one(step, carry):
        first_row = pl.multiple_of(step * block, block)
        rows = qbuf[pl.ds(first_row, block), :]
        keys = kbuf[pl.ds(first_row, span), :]
        values = vbuf[pl.ds(first_row, span), :]
        scores = dot(rows, keys, NT)
        scores = jnp.where(band & (col >= first_key - first_row), scores, NEG)
        top = jnp.max(scores, axis=1, keepdims=True)
        expo = jnp.exp2((scores - top) * scale)
        total = jnp.sum(expo, axis=1, keepdims=True)
        mixed = dot(expo.astype(jnp.bfloat16), values, NN) / total
        out_ref[pl.ds(first_row, block), :] = mixed.astype(out_ref.dtype)
        return carry

    lax.fori_loop(0, group * tok // block, one, 0)


def window_attention(info, queries, keys, values):
    group = len(queries)
    slots = len(keys) // group
    tok, width = queries[0].shape
    block = min(256, tok)
    span = (slots - 1) * group * tok + block
    total = group * tok
    return pl.pallas_call(
        functools.partial(attend_kernel, group, tok, slots, block),
        out_shape=jax.ShapeDtypeStruct((total, width), jnp.bfloat16),
        in_specs=[pl.BlockSpec(memory_space=pltpu.SMEM)]
        + [pl.BlockSpec(memory_space=pl.ANY)] * (group + 2 * len(keys)),
        out_specs=pl.BlockSpec(memory_space=pltpu.VMEM),
        scratch_shapes=[
            pltpu.VMEM((total, width), jnp.bfloat16),
            pltpu.VMEM((slots * total, width), jnp.bfloat16),
            pltpu.VMEM((slots * total, width), jnp.bfloat16),
            pltpu.SemaphoreType.DMA((3, slots * group)),
        ],
        compiler_params=pltpu.CompilerParams(vmem_limit_bytes=VMEM_BYTES),
        cost_estimate=pl.CostEstimate(
            flops=4 * total * span * width,
            bytes_accessed=2 * width * total * (2 + 2 * slots),
            transcendentals=total * span,
        ),
        name="window_attention",
    )(info, *queries, *keys, *values)


def finish_kernel(group, tok, count, info_ref, rate_ref, w_ref, sum_ref, att_ref, place_ref, *refs):
    q_refs = refs[:group]
    out_ref, new_w, rows_buf = refs[group:]
    plane, member, first_len = info_ref[0], info_ref[1], info_ref[2]
    step = rate_ref[0] / first_len.astype(jnp.float32)
    hidden = w_ref.shape[1]
    for c in range(w_ref.shape[0]):
        previous = w_ref[c].astype(jnp.float32)
        updated = previous + step * sum_ref[c].astype(jnp.float32)
        old_norm = jnp.sqrt(jnp.sum(previous * previous, axis=1, keepdims=True) + eps)
        new_norm = jnp.sqrt(jnp.sum(updated * updated, axis=1, keepdims=True) + eps)
        new_w[c] = (updated * (old_norm / new_norm)).astype(new_w.dtype)

    def apply(rows, weights):
        gate = dot(rows, weights[0], NT)
        up = dot(rows, weights[1], NT)
        act = (gate * jax.nn.sigmoid(gate) * up).astype(jnp.bfloat16)
        return dot(act, weights[2], NN)

    seg = tok // count
    for d in range(group):
        other = member ^ d
        first_tok = (plane * group + other) * tok
        place = pl.ds(pl.multiple_of(other * tok, tok), tok)

        @pl.when(first_tok < first_len)
        def _():
            rows_buf[...] = apply(q_refs[d][...], w_ref)

        @pl.when(first_tok + tok > first_len)
        def _():
            token = first_tok + lax.broadcasted_iota(jnp.int32, (tok, 1), 0)
            rows_buf[...] = jnp.where(token < first_len, rows_buf[...], apply(q_refs[d][...], new_w))

        rows = (rows_buf[...] + att_ref[place, :].astype(jnp.float32)).astype(jnp.bfloat16)
        wanted = place_ref[other]
        pick = (wanted == lax.broadcasted_iota(jnp.int32, (tok, tok), 1)).astype(jnp.bfloat16)
        sorted_rows = dot(pick, rows, NN).reshape(count, seg, rows.shape[-1])
        out_ref[:, other, :, :] = sorted_rows.astype(out_ref.dtype)


def finish_rows(info, rate, weights, sums, attention, places, queries, count):
    group = len(queries)
    tok, width = queries[0].shape
    hidden = weights.shape[1]
    seg = tok // count
    return pl.pallas_call(
        functools.partial(finish_kernel, group, tok, count),
        out_shape=jax.ShapeDtypeStruct((count, group, seg, width), jnp.bfloat16),
        in_specs=[pl.BlockSpec(memory_space=pltpu.SMEM)] * 2
        + [pl.BlockSpec(memory_space=pltpu.VMEM)] * (4 + group),
        out_specs=pl.BlockSpec(memory_space=pltpu.VMEM),
        scratch_shapes=[
            pltpu.VMEM(weights.shape, jnp.bfloat16),
            pltpu.VMEM((tok, width), jnp.float32),
        ],
        compiler_params=pltpu.CompilerParams(vmem_limit_bytes=VMEM_BYTES),
        cost_estimate=pl.CostEstimate(
            flops=2 * group * tok * width * (3 * hidden + tok),
            bytes_accessed=2 * (3 * group * tok * width + 2 * 3 * hidden * width),
            transcendentals=group * tok * hidden,
        ),
        name="finish_rows",
    )(info, rate, weights, sums, attention, places, *queries)


def total_over_planes(own, group, count):
    planes = count // group
    if planes > 8:
        groups = [[plane * group + m for plane in range(planes)] for m in range(group)]
        return lax.psum(own, "seq", axis_index_groups=groups)
    sums = [own[c] for c in range(own.shape[0])]
    for hop in range(1, planes):
        pairs = [((hop - 1) * group + m, hop * group + m) for m in range(group)]
        for c in range(len(sums)):
            came = lax.ppermute(sums[c], "seq", pairs)
            sums[c] = (sums[c].astype(jnp.float32) + came.astype(jnp.float32)).astype(own.dtype)
    return jnp.stack(sums)


def per_device(
    queries, token_keys, token_values, fast_weights, learn_rate, out_gain, group_lengths, slot_order
):
    tok, group, width = queries.shape
    count = lax.axis_size("seq")
    seg = tok // count
    planes = count // group
    behind = -(-WINDOW // (group * tok))
    position = lax.axis_index("seq")
    plane, member = position // group, position % group
    first_len = group_lengths[0]
    info = jnp.stack([plane, member, first_len]).astype(jnp.int32)

    order = list(range(group))
    keys = spread_heads(token_keys, member, count, order)
    values = spread_heads(token_values, member, count, order)
    rows = spread_heads(queries, member, count, order)
    all_keys, all_values = [], []
    for back in range(behind, 0, -1):
        pairs = plane_pairs(count, back * group)
        for d in range(group):
            all_keys.append(lax.ppermute(keys[d], "seq", pairs))
            all_values.append(lax.ppermute(values[d], "seq", pairs))
    all_keys, all_values = all_keys + keys, all_values + values

    weights = lax.dynamic_index_in_dim(fast_weights, member, 1, keepdims=False)
    weights = jnp.transpose(weights, (1, 0, 2))
    rate = lax.dynamic_slice_in_dim(learn_rate, member, 1)
    sums = total_over_planes(weight_sums(info, weights, keys, values), group, count)

    asked = lax.all_gather(slot_order, "seq").reshape(count, count, seg)
    asked = lax.dynamic_slice_in_dim(asked, plane * group, group, 1) % tok
    places = jnp.transpose(asked, (1, 0, 2)).reshape(group, tok, 1)

    attention = window_attention(info, rows, all_keys, all_values)
    leaving = finish_rows(info, rate, weights, sums, attention, places, rows, count)
    came = lax.all_to_all(leaving, "seq", split_axis=0, concat_axis=0, tiled=True)
    came = came.reshape(planes, group, group, seg, width).astype(jnp.float32)
    power = lax.psum(jnp.sum(came * came, axis=(1, 4)), "head")
    scale = lax.rsqrt(power / (group * lax.axis_size("head") * width) + eps)
    ordered = jnp.transpose(came * scale[:, None, :, :, None], (0, 2, 3, 1, 4))
    return (ordered.reshape(tok, group, width) * out_gain[None]).astype(jnp.bfloat16)


def solution(mesh):
    return jax.shard_map(
        per_device,
        mesh=mesh,
        in_specs=(
            P("seq", "head", None),
            P("seq", "head", None),
            P("seq", "head", None),
            P(None, "head", None, None),
            P("head"),
            P("head", None),
            P(),
            P("seq"),
        ),
        out_specs=P("seq", "head", None),
        check_vma=False,
    )
```

time: 829 us -> 350 us (0.42)
  waiting for transfers between devices: 550 us -> 51.8 us
  blocking collectives: 56.4 us -> 151 us
  matrix products: 62.5 us -> 0 us
  other arithmetic: 61.9 us -> 7.79 us
  Pallas kernels: 0 us -> 47.3 us
  starting transfers between devices: 21.1 us -> 36.8 us
  between operations: 14 us -> 1.01 us
    all_to_all x1 -> x0, waiting for transfers between devices: 506 us -> none  [per_device(): lax.all_to_all(wanted, 'seq', split_axis=0, concat_axis=0, tiled=True)]
    all_gather x0 -> x1, blocking collectives: none -> 67.3 us  [per_device(): asked = lax.all_gather(slot_order, 'seq').reshape(count, count, seg)]
    dot_general x11 -> x0, matrix products: 62.5 us -> none  [the longest x1 15.7 us: attend(): jnp.einsum('hqk,khd->qhd', prob_rows, key_slab[1], preferred_element_type...]
    ppermute x4 -> x26, waiting for transfers between devices: 0.01 us -> 51.8 us  [the longest x9 28 us: total_over_planes(): came = lax.ppermute(sums[c], 'seq', pairs)]
    pallas_call x0 -> x3, Pallas kernels: none -> 47.3 us  [the longest x1 21.5 us: window_attention(): pl.pallas_call(functools.partial(attend_kernel, group, tok, slots, block)...]
    psum x1 -> x0, waiting for transfers between devices: 43.8 us -> none  [fast_section(): summed = lax.psum(jnp.stack([term_gate, term_up, term_down], axis=2), 'seq')]
    ppermute x4 -> x26, starting transfers between devices: 12.3 us -> 36.8 us  [the longest x4 10 us: per_device(): all_values.append(lax.ppermute(values[d], 'seq', pairs))]
    sub x3 -> x0, other arithmetic: 23.3 us -> none  [the longest x1 23.3 us: attend(): expo = jnp.exp(scores - row_max)]
  transfers between devices with their start and end apart: 6 -> 26, of which waited for: 2 -> 7; matrix products, arithmetic and copies ran while one was open for 11% -> 9% of each run, Pallas kernels for 0% -> 10%
where the time goes in v1:
time: 350 us; the launch traced here: 344 us
  blocking collectives  151 us (43%)
  waiting for transfers between devices  51.8 us (15%)
  local copies, waits for them, and re-layouts  47.9 us (14%)
  Pallas kernels  47.3 us (14%)
  starting transfers between devices  36.8 us (11%)
  other arithmetic  7.79 us (2%)
    all_to_all x1, blocking collectives, per_device(): lax.all_to_all(leaving, 'seq', split_axis=0, concat_axis=0, tiled=True)  76.5 us
    all_gather x1, blocking collectives, per_device(): asked = lax.all_gather(slot_order, 'seq').reshape(count, count, seg)  67.3 us
    ppermute x9, waiting for transfers between devices, total_over_planes(): came = lax.ppermute(sums[c], 'seq', pairs)  28 us
    pallas_call x1, Pallas kernels, window_attention(): pl.pallas_call(functools.partial(attend_kernel, group, tok, slots, block)...  21.5 us
    another operation x2, local copies, waits for them, and re-layouts  21.4 us
    ppermute x9, waiting for transfers between devices, spread_heads(): piece = lax.ppermute(piece, 'seq', swap_pairs(count, distance))  17.3 us
    pallas_call x1, Pallas kernels, finish_rows(): pl.pallas_call(functools.partial(finish_kernel, group, tok, count), out_s...  14.3 us
    unnamed x46, local copies, waits for them, and re-layouts  11.7 us
  transfers between devices with their start and end apart: 26, of which 7 were waited for; matrix products, arithmetic and copies ran while one was open for 9% of the time, Pallas kernels for 10%

profile of v1, /device:TPU:13, one launch (start us, length us, event | category | flops | bytes accessed | tf_op | source)
XLA Modules:
  0.0 343.9 jit_solution(2170854035317290207)
XLA Ops:
  0.0 16.1 %constant_dynamic-slice_fusion = (bf16[512,1,512]{2,1,0:T(2,128)(2,1)S(1)}, bf16[512,1,512]{2,1,0:T(2,128)(2,1)}, bf16[512,1,512]{2,1,0:T(2,128)(2,1)}, bf16[512...) fusion(bf16[512,4,512]{2,1,0:T(4,128)(2,1)} %param.8, ...), kind=kLoop, calls=%fused_computation.40 | loop fusion | bytes 8388624 | tf_op jit(solution)/shard_map/dynamic-slice.11
  20.8 5.3 %constant_dynamic-slice_fusion.8 = (bf16[512,1,512]{2,1,0:T(2,128)(2,1)S(1)}, bf16[512,1,512]{2,1,0:T(2,128)(2,1)S(1)}, bf16[512,1,512]{2,1,0:T(2,128)(2,1)S(1)}, bf16[512,1,512]{2,1,0:T(2,128)(2,1)}) fusion(bf16[512,4,512]{2,1,0:T(4,128)(2,1)S(1)} %copy-done, s32[]{:T(128)S(6)} %select_n.49, s32[]{:T(128)S(6)} %select_n.48, s32[]{:T(128)S(6)} %select_n.47, ...), kind=kLoop, calls=%fused_computation.48 | loop fusion | bytes 4194320 | tf_op jit(solution)/shard_map/dynamic-slice.3
  32.4 2.2 copy.87
  37.6 6.0 %constant_dynamic-slice_fusion.12 = bf16[512,1,3,512]{3,1,2,0:T(2,128)(2,1)S(1)} fusion(bf16[512,4,3,512]{3,1,2,0:T(4,128)(2,1)} %param.11, s32[]{:T(128)S(6)} %select_n.46), kind=kLoop, calls=%fused_computation.52 | loop fusion | bytes 3145732 | tf_op jit(solution)/shard_map/jit(dynamic_index_in_dim)/dynamic_slice | solution.py:299
  43.6 1.6 copy.84
  47.4 4.4 %collective-permute-done.refs_1_.refs_9_ = bf16[512,512]{1,0:T(8,128)(2,1)} collective-permute-done((bf16[512,512]{1,0:T(8,128)(2,1)}, bf16[512,512]{1,0:T(8,128)(2,1)}, u32[]{:S(2)}, u32[]{:S(2)}) %collective-permute-start) | collective-permute-done | bytes 524320 | tf_op jit(solution)/shard_map/ppermute | solution.py:41
  52.9 11.7 %collective-permute-done.1.refs_2_.refs_10_ = bf16[512,512]{1,0:T(8,128)(2,1)} collective-permute-done((bf16[512,512]{1,0:T(8,128)(2,1)}, bf16[512,512]{1,0:T(8,128)(2,1)}, u32[]{:S(2)}, u32[]{:S(2)}) %collective-permute-start.1) | collective-permute-done | bytes 524320 | tf_op jit(solution)/shard_map/ppermute | solution.py:41
  64.6 3.2 collective-permute-start.22
  67.8 3.2 collective-permute-start.18
  71.1 11.5 %weight_sums.1 = bf16[3,512,512]{2,1,0:T(8,128)(2,1)} custom-call(s32[3]{0:T(128)} %pad_add_fusion.info_ref, bf16[3,512,512]{2,1,0:T(8,128)(2,1)} %bitcast.76, bf16[512,512]{1,0:T(8,128)(2,1)} %bitcast.73.refs_0_.refs_8_, bf16[512,512]{1,0:T(8,128)(2,1)} %collective-permute-done.refs_1_.refs_9_, bf16[512,512]{1,0:T(8,128)(2,1)} %collective-permute-done.1.refs_2_.refs_10_, ...), custom_call_target="tpu_custom_call" | custom-call | flops 6442450944 | bytes 7340032 | tf_op jit(solution)/shard_map/weight_sums/pallas_call | solution.py:95
  82.5 1.5 slice_bitcast_fusion.2
  84.1 2.1 collective-permute-start.23
  91.3 2.8 collective-permute-start.24
  94.1 6.6 %collective-permute-done.23.refs_13_ = bf16[512,512]{1,0:T(8,128)(2,1)S(1)} collective-permute-done((bf16[512,512]{1,0:T(8,128)(2,1)S(1)}, bf16[512,512]{1,0:T(8,128)(2,1)S(1)}, u32[]{:S(2)}, u32[]{:S(2)}) %collective-permute-start.23) | collective-permute-done | bytes 524320 | tf_op jit(solution)/shard_map/ppermute | solution.py:296
  100.7 1.9 collective-permute-start.25
  102.6 9.4 %collective-permute-done.12 = bf16[512,512]{1,0:T(8,128)(2,1)} collective-permute-done((bf16[512,512]{1,0:T(8,128)(2,1)S(1)}, bf16[512,512]{1,0:T(8,128)(2,1)}, u32[]{:S(2)}, u32[]{:S(2)}) %collective-permute-start.12) | collective-permute-done | bytes 524320 | tf_op jit(solution)/shard_map/ppermute | solution.py:269
  112.0 1.9 collective-permute-start.19
  114.0 9.3 %collective-permute-done.6 = bf16[512,512]{1,0:T(8,128)(2,1)} collective-permute-done((bf16[512,512]{1,0:T(8,128)(2,1)S(1)}, bf16[512,512]{1,0:T(8,128)(2,1)}, u32[]{:S(2)}, u32[]{:S(2)}) %collective-permute-start.6) | collective-permute-done | bytes 524320 | tf_op jit(solution)/shard_map/ppermute | solution.py:269
  123.3 1.9 collective-permute-start.20
  125.2 9.2 %collective-permute-done.9 = bf16[512,512]{1,0:T(8,128)(2,1)S(1)} collective-permute-done((bf16[512,512]{1,0:T(8,128)(2,1)S(1)}, bf16[512,512]{1,0:T(8,128)(2,1)S(1)}, u32[]{:S(2)}, u32[]{:S(2)}) %collective-permute-start.9) | collective-permute-done | bytes 524320 | tf_op jit(solution)/shard_map/ppermute | solution.py:269
  134.4 1.9 collective-permute-start.21
  137.3 67.3 %all-gather.1 = s32[16,1,512]{2,1,0:T(1,128)S(1)} all-gather(s32[1,1,512]{2,1,0:T(1,128)S(1)} %bitcast.84), channel_id=2, replica_groups=mesh['seq'=16,'head'=2] {'seq'}, dimensions={0}, use_global_device_ids=true | all-gather | bytes 34816 | tf_op jit(solution)/shard_map/all_gather | solution.py:304
  204.8 2.1 reshape.48.place_ref
  207.6 1.6 add_convert_fusion.8
  210.5 1.3 collective-permute-start.10
  213.2 21.5 %window_attention.1.att_ref = bf16[2048,512]{1,0:T(8,128)(2,1)} custom-call(s32[3]{0:T(128)} %pad_add_fusion.info_ref, bf16[512,512]{1,0:T(8,128)(2,1)} %bitcast.81, bf16[512,512]{1,0:T(8,128)(2,1)} %copy-done.10, bf16[512,512]{1,0:T(8,128)(2,1)} %copy-done.11, bf16[512,512]{1,0:T(8,128)(2,1)} %copy-done.12, bf16[512,512]{1,0:T(8,128)(2,1)} %copy-done.14, ...), custom_call_target="tpu_custom_call" | custom-call | flops 9663676416 | bytes 12582912 | tf_op jit(solution)/shard_map/window_attention/pallas_call | solution.py:172
  237.8 1.4 pad_maximum_fusion.sum_ref
  239.1 14.3 %finish_rows.1 = bf16[16,4,32,512]{3,2,1,0:T(8,128)(2,1)} custom-call(s32[3]{0:T(128)} %pad_add_fusion.info_ref, f32[1]{0:T(128)} %dynamic_slice.23.rate_ref, bf16[3,512,512]{2,1,0:T(8,128)(2,1)} %bitcast.77, bf16[3,512,512]{2,1,0:T(8,128)(2,1)} %pad_maximum_fusion.sum_ref, bf16[2048,512]{1,0:T(8,128)(2,1)} %window_attention.1.att_ref, ...), custom_call_target="tpu_custom_call" | custom-call | flops 4294967296 | bytes 9437184 | tf_op jit(solution)/shard_map/finish_rows/pallas_call | solution.py:240
  253.5 76.5 %all_to_all.5 = bf16[16,4,32,512]{3,2,1,0:T(8,128)(2,1)S(1)} all-to-all(bf16[16,4,32,512]{3,2,1,0:T(8,128)(2,1)} %finish_rows.1), channel_id=1, replica_groups=mesh['seq'=16,'head'=2] {'seq'}, dimensions={0} | all-to-all | bytes 4194304 | tf_op jit(solution)/shard_map/all_to_all | solution.py:310
  330.4 7.6 %psum.7 = f32[4,4,32]{2,1,0:T(4,128)S(1)} all-reduce(f32[4,4,32]{2,1,0:T(4,128)S(1)} %bitcast_reduce_fusion), channel_id=1, replica_groups=mesh['seq'=16,'head'=2] {'head'}, use_global_device_ids=true, to_apply=%region_2.3 | all-reduce | flops 512 | bytes 4096 | tf_op jit(solution)/shard_map/psum | solution.py:312
  338.4 2.8 copy.58
  341.2 2.3 fusion
  (98 shorter events, 30.5 us)
Async XLA Ops:
  16.3 14.1 %collective-permute-start.3 = (bf16[512,512]{1,0:T(8,128)(2,1)S(1)}, bf16[512,512]{1,0:T(8,128)(2,1)S(1)}, u32[]{:S(2)}, u32[]{:S(2)}) collective-permute-start(bf16[512,512]{1,0:T(8,128)(2,1)S(1)} %bitcast.83), channel_id=1, source_target_pairs={{0,2},{2,0},{4,6},{6,4},{8,10},{10,8},{12,14},{14,12},{16,18},{18,... | collective-permute-start | bytes 1572872 | tf_op jit(solution)/shard_map/ppermute | solution.py:41
  18.5 27.5 %collective-permute-start.4 = (bf16[512,512]{1,0:T(8,128)(2,1)}, bf16[512,512]{1,0:T(8,128)(2,1)}, u32[]{:S(2)}, u32[]{:S(2)}) collective-permute-start(bf16[512,512]{1,0:T(8,128)(2,1)} %bitcast.67), channel_id=1, source_target_pairs={{0,4},{2,6},{4,0},{6,2},{8,12},{10,14},{12,8},{14,10},{16,20},{18,... | collective-permute-start | bytes 1572872 | tf_op jit(solution)/shard_map/ppermute | solution.py:41
  19.6 27.5 %collective-permute-start.5 = (bf16[512,512]{1,0:T(8,128)(2,1)}, bf16[512,512]{1,0:T(8,128)(2,1)}, u32[]{:S(2)}, u32[]{:S(2)}) collective-permute-start(bf16[512,512]{1,0:T(8,128)(2,1)} %bitcast.66), channel_id=1, source_target_pairs={{0,6},{2,4},{4,2},{6,0},{8,14},{10,12},{12,10},{14,8},{16,22},{18,... | collective-permute-start | bytes 1572872 | tf_op jit(solution)/shard_map/ppermute | solution.py:41
  27.0 24.7 %collective-permute-start = (bf16[512,512]{1,0:T(8,128)(2,1)}, bf16[512,512]{1,0:T(8,128)(2,1)}, u32[]{:S(2)}, u32[]{:S(2)}) collective-permute-start(bf16[512,512]{1,0:T(8,128)(2,1)} %bitcast.72), channel_id=1, source_target_pairs={{0,2},{2,0},{4,6},{6,4},{8,10},{10,8},{12,14},{14,12},{16,18},{18,... | collective-permute-start | bytes 1572872 | tf_op jit(solution)/shard_map/ppermute | solution.py:41
  29.2 35.4 %collective-permute-start.1 = (bf16[512,512]{1,0:T(8,128)(2,1)}, bf16[512,512]{1,0:T(8,128)(2,1)}, u32[]{:S(2)}, u32[]{:S(2)}) collective-permute-start(bf16[512,512]{1,0:T(8,128)(2,1)} %bitcast.71), channel_id=1, source_target_pairs={{0,4},{2,6},{4,0},{6,2},{8,12},{10,14},{12,8},{14,10},{16,20},{18,... | collective-permute-start | bytes 1572872 | tf_op jit(solution)/shard_map/ppermute | solution.py:41
  31.2 36.6 %collective-permute-start.2 = (bf16[512,512]{1,0:T(8,128)(2,1)}, bf16[512,512]{1,0:T(8,128)(2,1)}, u32[]{:S(2)}, u32[]{:S(2)}) collective-permute-start(bf16[512,512]{1,0:T(8,128)(2,1)} %bitcast.70), channel_id=1, source_target_pairs={{0,6},{2,4},{4,2},{6,0},{8,14},{10,12},{12,10},{14,8},{16,22},{18,... | collective-permute-start | bytes 1572872 | tf_op jit(solution)/shard_map/ppermute | solution.py:41
  45.9 38.2 %collective-permute-start.15 = (bf16[512,512]{1,0:T(8,128)(2,1)}, bf16[512,512]{1,0:T(8,128)(2,1)S(1)}, u32[]{:S(2)}, u32[]{:S(2)}) collective-permute-start(bf16[512,512]{1,0:T(8,128)(2,1)} %bitcast.64), channel_id=1, source_target_pairs={{0,2},{2,0},{4,6},{6,4},{8,10},{10,8},{12,14},{14,12},{16,18},{18,... | collective-permute-start | bytes 1572872 | tf_op jit(solution)/shard_map/ppermute | solution.py:41
  47.1 40.2 %collective-permute-start.16 = (bf16[512,512]{1,0:T(8,128)(2,1)}, bf16[512,512]{1,0:T(8,128)(2,1)S(1)}, u32[]{:S(2)}, u32[]{:S(2)}) collective-permute-start(bf16[512,512]{1,0:T(8,128)(2,1)} %bitcast.63), channel_id=1, source_target_pairs={{0,4},{2,6},{4,0},{6,2},{8,12},{10,14},{12,8},{14,10},{16,20},{18,... | collective-permute-start | bytes 1572872 | tf_op jit(solution)/shard_map/ppermute | solution.py:41
  51.7 36.9 %collective-permute-start.17 = (bf16[512,512]{1,0:T(8,128)(2,1)}, bf16[512,512]{1,0:T(8,128)(2,1)S(1)}, u32[]{:S(2)}, u32[]{:S(2)}) collective-permute-start(bf16[512,512]{1,0:T(8,128)(2,1)} %bitcast.62), channel_id=1, source_target_pairs={{0,6},{2,4},{4,2},{6,0},{8,14},{10,12},{12,10},{14,8},{16,22},{18,... | collective-permute-start | bytes 1572872 | tf_op jit(solution)/shard_map/ppermute | solution.py:41
  64.6 25.3 %collective-permute-start.22 = (bf16[512,512]{1,0:T(8,128)(2,1)S(1)}, bf16[512,512]{1,0:T(8,128)(2,1)S(1)}, u32[]{:S(2)}, u32[]{:S(2)}) collective-permute-start(bf16[512,512]{1,0:T(8,128)(2,1)S(1)} %bitcast.78), channel_id=1, source_target_pairs={{0,8},{2,10},{4,12},{6,14},{8,16},{10,18},{12,20},{14,22},{16,24},... | collective-permute-start | bytes 1572872 | tf_op jit(solution)/shard_map/ppermute | solution.py:296
  67.8 23.4 %collective-permute-start.18 = (bf16[512,512]{1,0:T(8,128)(2,1)}, bf16[512,512]{1,0:T(8,128)(2,1)S(1)}, u32[]{:S(2)}, u32[]{:S(2)}) collective-permute-start(bf16[512,512]{1,0:T(8,128)(2,1)} %bitcast.73.refs_0_.refs_8_), channel_id=1, source_target_pairs={{0,8},{2,10},{4,12},{6,14},{8,16},{10,18},{12,20},{14,22},{16,24},... | collective-permute-start | bytes 1572872 | tf_op jit(solution)/shard_map/ppermute | solution.py:295
  82.5 54.7 %copy-start.6 = (s32[512]{0:T(512)S(1)}, s32[512]{0:T(512)}, u32[]{:S(2)}) copy-start(s32[512]{0:T(512)} %param.15) | copy-start | bytes 6148
  84.1 122.8 %copy-start.16 = (f32[4]{0:T(128)S(1)}, f32[4]{0:T(128)}, u32[]{:S(2)}) copy-start(f32[4]{0:T(128)} %param.12) | copy-start | bytes 52
  84.1 123.5 %copy-start.1 = (bf16[3,512,512]{2,1,0:T(8,128)(2,1)S(1)}, bf16[3,512,512]{2,1,0:T(8,128)(2,1)}, u32[]{:S(2)}) copy-start(bf16[3,512,512]{2,1,0:T(8,128)(2,1)} %weight_sums.1) | copy-start | bytes 4718596
  84.1 50.3 %copy-start.10 = (bf16[512,512]{1,0:T(8,128)(2,1)}, bf16[512,512]{1,0:T(8,128)(2,1)S(1)}, u32[]{:S(2)}) copy-start(bf16[512,512]{1,0:T(8,128)(2,1)S(1)} %collective-permute-done.15.refs_1_) | copy-start | bytes 1572868
  84.1 16.6 %collective-permute-start.23 = (bf16[512,512]{1,0:T(8,128)(2,1)S(1)}, bf16[512,512]{1,0:T(8,128)(2,1)S(1)}, u32[]{:S(2)}, u32[]{:S(2)}) collective-permute-start(bf16[512,512]{1,0:T(8,128)(2,1)S(1)} %copy-done.9), channel_id=1, source_target_pairs={{0,8},{2,10},{4,12},{6,14},{8,16},{10,18},{12,20},{14,22},{16,24},... | collective-permute-start | bytes 1572872 | tf_op jit(solution)/shard_map/ppermute | solution.py:296
  87.3 47.1 %copy-start.11 = (bf16[512,512]{1,0:T(8,128)(2,1)}, bf16[512,512]{1,0:T(8,128)(2,1)S(1)}, u32[]{:S(2)}) copy-start(bf16[512,512]{1,0:T(8,128)(2,1)S(1)} %collective-permute-done.16.refs_2_) | copy-start | bytes 1572868
  87.3 24.7 %collective-permute-start.12 = (bf16[512,512]{1,0:T(8,128)(2,1)S(1)}, bf16[512,512]{1,0:T(8,128)(2,1)}, u32[]{:S(2)}, u32[]{:S(2)}) collective-permute-start(bf16[512,512]{1,0:T(8,128)(2,1)S(1)} %get-tuple-element.21), channel_id=1, source_target_pairs={{0,8},{2,10},{4,12},{6,14},{1,9},{3,11},{5,13},{7,15}} | collective-permute-start | bytes 1572872 | tf_op jit(solution)/shard_map/ppermute | solution.py:269
  88.6 45.8 %copy-start.12 = (bf16[512,512]{1,0:T(8,128)(2,1)}, bf16[512,512]{1,0:T(8,128)(2,1)S(1)}, u32[]{:S(2)}) copy-start(bf16[512,512]{1,0:T(8,128)(2,1)S(1)} %collective-permute-done.17.refs_3_) | copy-start | bytes 1572868
  88.6 34.6 %collective-permute-start.6 = (bf16[512,512]{1,0:T(8,128)(2,1)S(1)}, bf16[512,512]{1,0:T(8,128)(2,1)}, u32[]{:S(2)}, u32[]{:S(2)}) collective-permute-start(bf16[512,512]{1,0:T(8,128)(2,1)S(1)} %get-tuple-element.20), channel_id=1, source_target_pairs={{0,8},{2,10},{4,12},{6,14},{1,9},{3,11},{5,13},{7,15}} | collective-permute-start | bytes 1572872 | tf_op jit(solution)/shard_map/ppermute | solution.py:269
  89.9 44.5 %collective-permute-start.9 = (bf16[512,512]{1,0:T(8,128)(2,1)S(1)}, bf16[512,512]{1,0:T(8,128)(2,1)S(1)}, u32[]{:S(2)}, u32[]{:S(2)}) collective-permute-start(bf16[512,512]{1,0:T(8,128)(2,1)S(1)} %get-tuple-element.22), channel_id=1, source_target_pairs={{0,8},{2,10},{4,12},{6,14},{1,9},{3,11},{5,13},{7,15}} | collective-permute-start | bytes 1572872 | tf_op jit(solution)/shard_map/ppermute | solution.py:269
  91.3 117.9 %collective-permute-start.24 = (bf16[512,512]{1,0:T(8,128)(2,1)}, bf16[512,512]{1,0:T(8,128)(2,1)}, u32[]{:S(2)}, u32[]{:S(2)}) collective-permute-start(bf16[512,512]{1,0:T(8,128)(2,1)} %collective-permute-done.4.refs_6_.refs_18_), channel_id=1, source_target_pairs={{0,8},{2,10},{4,12},{6,14},{8,16},{10,18},{12,20},{14,22},{16,24},... | collective-permute-start | bytes 1572872 | tf_op jit(solution)/shard_map/ppermute | solution.py:296
  100.7 109.8 %collective-permute-start.25 = (bf16[512,512]{1,0:T(8,128)(2,1)}, bf16[512,512]{1,0:T(8,128)(2,1)}, u32[]{:S(2)}, u32[]{:S(2)}) collective-permute-start(bf16[512,512]{1,0:T(8,128)(2,1)} %collective-permute-done.5.refs_7_.refs_19_), channel_id=1, source_target_pairs={{0,8},{2,10},{4,12},{6,14},{8,16},{10,18},{12,20},{14,22},{16,24},... | collective-permute-start | bytes 1572872 | tf_op jit(solution)/shard_map/ppermute | solution.py:296
  112.0 99.8 %collective-permute-start.19 = (bf16[512,512]{1,0:T(8,128)(2,1)}, bf16[512,512]{1,0:T(8,128)(2,1)}, u32[]{:S(2)}, u32[]{:S(2)}) collective-permute-start(bf16[512,512]{1,0:T(8,128)(2,1)} %collective-permute-done.refs_1_.refs_9_), channel_id=1, source_target_pairs={{0,8},{2,10},{4,12},{6,14},{8,16},{10,18},{12,20},{14,22},{16,24},... | collective-permute-start | bytes 1572872 | tf_op jit(solution)/shard_map/ppermute | solution.py:295
  123.3 89.9 %collective-permute-start.20 = (bf16[512,512]{1,0:T(8,128)(2,1)}, bf16[512,512]{1,0:T(8,128)(2,1)}, u32[]{:S(2)}, u32[]{:S(2)}) collective-permute-start(bf16[512,512]{1,0:T(8,128)(2,1)} %collective-permute-done.1.refs_2_.refs_10_), channel_id=1, source_target_pairs={{0,8},{2,10},{4,12},{6,14},{8,16},{10,18},{12,20},{14,22},{16,24},... | collective-permute-start | bytes 1572872 | tf_op jit(solution)/shard_map/ppermute | solution.py:295
  134.4 78.8 %collective-permute-start.21 = (bf16[512,512]{1,0:T(8,128)(2,1)}, bf16[512,512]{1,0:T(8,128)(2,1)}, u32[]{:S(2)}, u32[]{:S(2)}) collective-permute-start(bf16[512,512]{1,0:T(8,128)(2,1)} %collective-permute-done.2.refs_3_.refs_11_), channel_id=1, source_target_pairs={{0,8},{2,10},{4,12},{6,14},{8,16},{10,18},{12,20},{14,22},{16,24},... | collective-permute-start | bytes 1572872 | tf_op jit(solution)/shard_map/ppermute | solution.py:295
  209.2 25.5 %collective-permute-start.7 = (bf16[512,512]{1,0:T(8,128)(2,1)S(1)}, bf16[512,512]{1,0:T(8,128)(2,1)S(1)}, u32[]{:S(2)}, u32[]{:S(2)}) collective-permute-start(bf16[512,512]{1,0:T(8,128)(2,1)S(1)} %get-tuple-element.17), channel_id=1, source_target_pairs={{8,16},{10,18},{12,20},{14,22},{9,17},{11,19},{13,21},{15,23}} | collective-permute-start | bytes 1572872 | tf_op jit(solution)/shard_map/ppermute | solution.py:269
  210.5 25.0 %collective-permute-start.10 = (bf16[512,512]{1,0:T(8,128)(2,1)S(1)}, bf16[512,512]{1,0:T(8,128)(2,1)S(1)}, u32[]{:S(2)}, u32[]{:S(2)}) collective-permute-start(bf16[512,512]{1,0:T(8,128)(2,1)S(1)} %get-tuple-element.19), channel_id=1, source_target_pairs={{8,16},{10,18},{12,20},{14,22},{9,17},{11,19},{13,21},{15,23}} | collective-permute-start | bytes 1572872 | tf_op jit(solution)/shard_map/ppermute | solution.py:269
  211.9 24.6 %collective-permute-start.13 = (bf16[512,512]{1,0:T(8,128)(2,1)S(1)}, bf16[512,512]{1,0:T(8,128)(2,1)S(1)}, u32[]{:S(2)}, u32[]{:S(2)}) collective-permute-start(bf16[512,512]{1,0:T(8,128)(2,1)S(1)} %get-tuple-element.18), channel_id=1, source_target_pairs={{8,16},{10,18},{12,20},{14,22},{9,17},{11,19},{13,21},{15,23}} | collective-permute-start | bytes 1572872 | tf_op jit(solution)/shard_map/ppermute | solution.py:269
  234.9 2.4 collective-permute-start.8
  235.7 1.7 collective-permute-start.11
  236.6 1.0 collective-permute-start.14
  (11 other events, 165.1 us)

commit v2 on v1

v2 whole, which is shorter than its diff:
```python
import functools
import math

import jax
import jax.numpy as jnp
from jax import lax
from jax.experimental import pallas as pl
from jax.experimental.pallas import tpu as pltpu
from jax.sharding import PartitionSpec as P

WINDOW = 2048
NEG = -1e30
MIB = 1024 * 1024

eps = 1e-06

NT = (((1,), (1,)), ((), ()))
TN = (((0,), (0,)), ((), ()))
NN = (((1,), (0,)), ((), ()))

ANY = pl.BlockSpec(memory_space=pl.ANY)
SMEM = pl.BlockSpec(memory_space=pltpu.SMEM)
VMEM = pl.BlockSpec(memory_space=pltpu.VMEM)


def dot(left, right, dims):
    return lax.dot_general(left, right, dims, preferred_element_type=jnp.float32)


def params(mib):
    return pltpu.CompilerParams(vmem_limit_bytes=mib * MIB)


def swap_pairs(count, distance):
    return [(index, index ^ distance) for index in range(count)]


def plane_pairs(count, steps):
    return [(index, index + steps) for index in range(count - steps)]


def split_kernel(total, group, info_ref, *refs):
    x_refs = refs[:total]
    outs = refs[len(refs) - group - 2 : len(refs) - 2]
    buf, sems = refs[-2:]
    member = info_ref[1]
    for t, x_ref in enumerate(x_refs):
        buf[:, t] = jnp.swapaxes(x_ref[...], 0, 1)
    copies = [
        pltpu.make_async_copy(buf.at[member ^ d], outs[d], sems.at[d]) for d in range(group)
    ]
    for copy in copies:
        copy.start()
    for copy in copies:
        copy.wait()


def split_heads(info, arrays, after=()):
    tok, group, width = arrays[0].shape
    total = len(arrays)
    return pl.pallas_call(
        functools.partial(split_kernel, total, group),
        out_shape=[jax.ShapeDtypeStruct((total, tok, width), jnp.bfloat16)] * group,
        in_specs=[SMEM] + [VMEM] * total + [ANY] * len(after),
        out_specs=[ANY] * group,
        scratch_shapes=[
            pltpu.VMEM((group, total, tok, width), jnp.bfloat16),
            pltpu.SemaphoreType.DMA((group,)),
        ],
        compiler_params=params(20),
        cost_estimate=pl.CostEstimate(
            flops=0, bytes_accessed=4 * total * group * tok * width, transcendentals=0
        ),
        name="split_heads",
    )(info, *arrays, *after)


def trade(pieces, count):
    return [
        lax.ppermute(piece, "seq", swap_pairs(count, d)) if d else piece
        for d, piece in enumerate(pieces)
    ]


def grad_kernel(group, tok, info_ref, w_ref, *refs):
    kv_any = refs[:group]
    own, sent, kvbuf, acc, sems, out_sems = (
        refs[group],
        refs[group + 1 : group + 4],
        *refs[group + 4 :],
    )
    plane, member, first_len = info_ref[0], info_ref[1], info_ref[2]
    copies = [pltpu.make_async_copy(kv_any[d], kvbuf.at[d], sems.at[d]) for d in range(group)]
    for copy in copies:
        copy.start()
    acc[...] = jnp.zeros_like(acc)
    hidden = w_ref.shape[1]
    part = min(256, hidden)
    for d in range(group):
        copies[d].wait()
    def piece(d, carry):
        first_tok = (plane * group + (member ^ d)) * tok

        @pl.when(first_tok < first_len)
        def _():
            keys = kvbuf[d, 0]
            token = first_tok + lax.broadcasted_iota(jnp.int32, (tok, 1), 0)
            values = jnp.where(token < first_len, kvbuf[d, 1].astype(jnp.float32), 0.0)
            values = values.astype(jnp.bfloat16)
            for f in range(0, hidden, part):
                rows = pl.ds(f, part)
                gate = dot(keys, w_ref[0, rows, :], NT)
                up = dot(keys, w_ref[1, rows, :], NT)
                back = dot(values, w_ref[2, rows, :], NT)
                sig = jax.nn.sigmoid(gate)
                silu = gate * sig
                act = (silu * up).astype(jnp.bfloat16)
                grad_up = (back * silu).astype(jnp.bfloat16)
                grad_gate = (back * up * sig * (1.0 + gate * (1.0 - sig))).astype(jnp.bfloat16)
                acc[0, rows, :] += dot(grad_gate, keys, TN)
                acc[1, rows, :] += dot(grad_up, keys, TN)
                acc[2, rows, :] += dot(act, values, TN)

        return carry

    lax.fori_loop(0, group, piece, 0)
    keep = pltpu.make_async_copy(acc, own, out_sems.at[0])
    keep.start()
    for c in range(3):
        sent[c][...] = acc[c].astype(sent[c].dtype)
    keep.wait()


def weight_sums(info, weights, pairs):
    group = len(pairs)
    _, tok, width = pairs[0].shape
    rows, hidden, _ = weights.shape
    return pl.pallas_call(
        functools.partial(grad_kernel, group, tok),
        out_shape=[jax.ShapeDtypeStruct(weights.shape, jnp.float32)]
        + [jax.ShapeDtypeStruct((hidden, width), jnp.bfloat16)] * rows,
        in_specs=[SMEM, VMEM] + [ANY] * group,
        out_specs=[ANY] + [VMEM] * rows,
        scratch_shapes=[
            pltpu.VMEM((group, 2, tok, width), jnp.bfloat16),
            pltpu.VMEM(weights.shape, jnp.float32),
            pltpu.SemaphoreType.DMA((group,)),
            pltpu.SemaphoreType.DMA((1,)),
        ],
        compiler_params=params(28),
        cost_estimate=pl.CostEstimate(
            flops=2 * 6 * group * tok * hidden * width,
            bytes_accessed=2 * (2 * group * tok * width + 2 * rows * hidden * width),
            transcendentals=group * tok * hidden,
        ),
        name="weight_sums",
    )(info, weights, *pairs)


def lanes_sum(expo):
    total = expo[:, :128]
    for lane in range(128, expo.shape[1], 128):
        total = total + expo[:, lane : lane + 128]
    return total


def soft_steps(parts, scale, fresh, acc, top, norm):
    scores = [
        dot(rows, keys, NT) if mask is None else jnp.where(mask, dot(rows, keys, NT), NEG)
        for _, rows, keys, _, mask in parts
    ]
    done = []
    for (where, _, _, _, _), score in zip(parts, scores):
        peak = jnp.max(score, axis=1, keepdims=True)
        if fresh:
            decay = None
        else:
            before = top[where, :1]
            peak = jnp.maximum(peak, before)
            decay = jnp.exp2((before - peak) * scale)
        expo = jnp.exp2((score - peak) * scale)
        done.append((peak, decay, lanes_sum(expo), expo.astype(jnp.bfloat16)))
    for (where, _, _, values, _), (peak, decay, total, expo) in zip(parts, done):
        mixed = dot(expo, values, NN)
        wide = (peak.shape[0], 128)
        top[where, :] = jnp.broadcast_to(peak, wide)
        if fresh:
            norm[where, :] = total
            acc[where, :] = mixed
        else:
            norm[where, :] = norm[where, :] * decay + total
            acc[where, :] = acc[where, :] * decay + mixed


def score_scale(width):
    return math.log2(math.e) / math.sqrt(width)


def triangle(rows, cols, first_row, first_col, lower):
    row = first_row + lax.broadcasted_iota(jnp.int32, (rows, cols), 0)
    col = first_col + lax.broadcasted_iota(jnp.int32, (rows, cols), 1)
    return col <= row if lower else col > row


def own_kernel(group, tok, part, info_ref, *refs):
    q_any, kv_any = refs[:group], refs[group : 2 * group]
    acc_ref, top_ref, norm_ref, qbuf, kvbuf, sems = refs[2 * group :]
    member = info_ref[1]
    copies = []
    for d in range(group):
        copies.append(pltpu.make_async_copy(q_any[d], qbuf.at[pl.ds(d, 1)], sems.at[0, d]))
        copies.append(pltpu.make_async_copy(kv_any[d], kvbuf.at[d], sems.at[1, d]))
    for copy in copies:
        copy.start()
    for copy in copies:
        copy.wait()
    scale = score_scale(qbuf.shape[-1])

    def piece(d, carry):
        at = member ^ d
        acc, top, norm = acc_ref.at[d], top_ref.at[d], norm_ref.at[d]
        parts = []
        for r in range(0, tok, part):
            where, keys = pl.ds(r, part), pl.ds(0, r + part)
            mask = triangle(part, r + part, r, 0, True)
            parts.append((where, qbuf[d, where], kvbuf[d, 0, keys], kvbuf[d, 1, keys], mask))
        soft_steps(parts, scale, True, acc, top, norm)

        def earlier(other, carry):
            e = member ^ other
            parts = []
            for r in range(0, tok, part):
                where = pl.ds(r, part)
                parts.append((where, qbuf[d, where], kvbuf[e, 0], kvbuf[e, 1], None))
            soft_steps(parts, scale, False, acc, top, norm)
            return carry

        lax.fori_loop(0, at, earlier, 0)
        return carry

    lax.fori_loop(0, group, piece, 0)


def own_attention(info, queries, pairs):
    group = len(queries)
    _, tok, width = pairs[0].shape
    part = min(256, tok)
    return pl.pallas_call(
        functools.partial(own_kernel, group, tok, part),
        out_shape=[
            jax.ShapeDtypeStruct((group, tok, width), jnp.float32),
            jax.ShapeDtypeStruct((group, tok, 128), jnp.float32),
            jax.ShapeDtypeStruct((group, tok, 128), jnp.float32),
        ],
        in_specs=[SMEM] + [ANY] * (2 * group),
        out_specs=[VMEM] * 3,
        scratch_shapes=[
            pltpu.VMEM((group, tok, width), jnp.bfloat16),
            pltpu.VMEM((group, 2, tok, width), jnp.bfloat16),
            pltpu.SemaphoreType.DMA((2, group)),
        ],
        compiler_params=params(28),
        cost_estimate=pl.CostEstimate(
            flops=2 * group * group * tok * tok * width,
            bytes_accessed=width * group * tok * 10,
            transcendentals=group * group * tok * tok // 2,
        ),
        name="own_attention",
    )(info, *queries, *pairs)


def fast_kernel(group, tok, hops, info_ref, rate_ref, w_ref, own_ref, *refs):
    came, q_any = refs[: 3 * hops], refs[3 * hops : 3 * hops + group]
    out_ref, new_w, qbuf, sems = refs[3 * hops + group :]
    plane, member, first_len = info_ref[0], info_ref[1], info_ref[2]
    copies = [
        pltpu.make_async_copy(q_any[d], qbuf.at[pl.ds(d, 1)], sems.at[d]) for d in range(group)
    ]
    for copy in copies:
        copy.start()
    step = rate_ref[0] / first_len.astype(jnp.float32)
    for c in range(3):
        previous = w_ref[c].astype(jnp.float32)
        summed = own_ref[c]
        for hop in range(hops):
            summed = summed + came[3 * hop + c][...].astype(jnp.float32)
        updated = previous + step * summed
        old_norm = jnp.sqrt(jnp.sum(previous * previous, axis=1, keepdims=True) + eps)
        new_norm = jnp.sqrt(jnp.sum(updated * updated, axis=1, keepdims=True) + eps)
        new_w[c] = (updated * (old_norm / new_norm)).astype(new_w.dtype)
    for copy in copies:
        copy.wait()

    def apply(rows, weights):
        gate = dot(rows, weights[0], NT)
        up = dot(rows, weights[1], NT)
        act = (gate * jax.nn.sigmoid(gate) * up).astype(jnp.bfloat16)
        return dot(act, weights[2], NN).astype(jnp.bfloat16)

    def piece(d, carry):
        first_tok = (plane * group + (member ^ d)) * tok

        @pl.when(first_tok < first_len)
        def _():
            out_ref[d] = apply(qbuf[d], w_ref)

        @pl.when(first_tok + tok > first_len)
        def _():
            token = first_tok + lax.broadcasted_iota(jnp.int32, (tok, 1), 0)
            second = apply(qbuf[d], new_w).astype(jnp.float32)
            first = out_ref[d].astype(jnp.float32)
            out_ref[d] = jnp.where(token < first_len, first, second).astype(jnp.bfloat16)

        return carry

    lax.fori_loop(0, group, piece, 0)


def fast_rows(info, rate, weights, own, came, queries):
    group = len(queries)
    _, tok, width = queries[0].shape
    hidden = weights.shape[1]
    hops = len(came) // 3
    return pl.pallas_call(
        functools.partial(fast_kernel, group, tok, hops),
        out_shape=jax.ShapeDtypeStruct((group, tok, width), jnp.bfloat16),
        in_specs=[SMEM] * 2 + [VMEM] * (2 + 3 * hops) + [ANY] * group,
        out_specs=VMEM,
        scratch_shapes=[
            pltpu.VMEM(weights.shape, jnp.bfloat16),
            pltpu.VMEM((group, tok, width), jnp.bfloat16),
            pltpu.SemaphoreType.DMA((group,)),
        ],
        compiler_params=params(28),
        cost_estimate=pl.CostEstimate(
            flops=2 * 3 * group * tok * width * hidden,
            bytes_accessed=2 * (2 * group * tok * width + 6 * hidden * width),
            transcendentals=group * tok * hidden,
        ),
        name="fast_rows",
    )(info, rate, weights, own, *came, *queries)


def cross_kernel(group, tok, count, behind, part, info_ref, *refs):
    pieces = behind * group
    q_any, refs = refs[:group], refs[group:]
    kv_any, refs = refs[:pieces], refs[pieces:]
    acc_any, top_ref, norm_ref, fast_ref, place_ref, out_ref = refs[:6]
    qbuf, kvbuf, acc_ref, sems, kv_sems = refs[6:]
    plane, member = info_ref[0], info_ref[1]
    kv_copies = [
        pltpu.make_async_copy(kv_any[at], kvbuf.at[at], kv_sems.at[at]) for at in range(pieces)
    ]
    copies = []
    for d in range(group):
        copies.append(pltpu.make_async_copy(q_any[d], qbuf.at[pl.ds(d, 1)], sems.at[0, d]))
        copies.append(pltpu.make_async_copy(acc_any.at[d], acc_ref.at[d], sems.at[1, d]))
    for copy in kv_copies + copies:
        copy.start()
    for copy in kv_copies + copies:
        copy.wait()
    scale = score_scale(qbuf.shape[-1])
    seg = tok // count
    valid = jnp.maximum(behind - plane, 0) * group

    def at_piece(order):
        return order // group * group + (member ^ (order % group))

    def piece(d, carry):
        at = member ^ d
        acc, top, norm = acc_ref.at[d], top_ref.at[d], norm_ref.at[d]

        @pl.when(at >= valid)
        def _():
            parts = []
            for r in range(0, tok, part):
                where, keys = pl.ds(r, part), pl.ds(r, tok - r)
                mask = triangle(part, tok - r, r, r, False)
                parts.append((where, qbuf[d, where], kvbuf[d, 0, keys], kvbuf[d, 1, keys], mask))
            soft_steps(parts, scale, False, acc, top, norm)

        def later(other, carry):
            e = at_piece(other)
            parts = []
            for r in range(0, tok, part):
                where = pl.ds(r, part)
                parts.append((where, qbuf[d, where], kvbuf[e, 0], kvbuf[e, 1], None))
            soft_steps(parts, scale, False, acc, top, norm)
            return carry

        lax.fori_loop(jnp.maximum(at + 1, valid), pieces, later, 0)
        total = jnp.sum(norm[...], axis=1, keepdims=True)
        mixed = (acc[...] / total).astype(jnp.bfloat16)
        rows = (mixed.astype(jnp.float32) + fast_ref[d].astype(jnp.float32)).astype(jnp.bfloat16)
        pick = place_ref[at] == lax.broadcasted_iota(jnp.int32, (tok, tok), 1)
        sorted_rows = dot(pick.astype(jnp.bfloat16), rows, NN)
        out_ref[:, at] = sorted_rows.reshape(count, seg, rows.shape[-1]).astype(out_ref.dtype)
        return carry

    lax.fori_loop(0, group, piece, 0)


def cross_rows(info, queries, earlier, state, fast, places, count):
    group = len(queries)
    _, tok, width = queries[0].shape
    behind = len(earlier) // group
    part = min(256, tok)
    return pl.pallas_call(
        functools.partial(cross_kernel, group, tok, count, behind, part),
        out_shape=jax.ShapeDtypeStruct((count, group, tok // count, width), jnp.bfloat16),
        in_specs=[SMEM] + [ANY] * (group + len(earlier) + 1) + [VMEM] * 4,
        out_specs=VMEM,
        scratch_shapes=[
            pltpu.VMEM((group, tok, width), jnp.bfloat16),
            pltpu.VMEM((len(earlier), 2, tok, width), jnp.bfloat16),
            pltpu.VMEM((group, tok, width), jnp.float32),
            pltpu.SemaphoreType.DMA((2, group)),
            pltpu.SemaphoreType.DMA((len(earlier),)),
        ],
        compiler_params=params(36),
        cost_estimate=pl.CostEstimate(
            flops=2 * group * group * tok * tok * width,
            bytes_accessed=width * group * tok * 16,
            transcendentals=group * group * tok * tok // 2,
        ),
        name="cross_rows",
    )(info, *queries, *earlier, *state, fast, places)


def norm_kernel(came_ref, scale_ref, gain_ref, out_ref):
    group = out_ref.shape[1]
    for h in range(group):
        pass
    scaled = came_ref[0].astype(jnp.float32) * scale_ref[...] * gain_ref[...]
    out_ref[...] = jnp.swapaxes(scaled.astype(out_ref.dtype), 0, 1)


def norm_rows(came, scale, gain):
    planes, group, rows, width = came.shape
    return pl.pallas_call(
        norm_kernel,
        grid=(planes,),
        out_shape=jax.ShapeDtypeStruct((planes * rows, group, width), jnp.bfloat16),
        in_specs=[
            pl.BlockSpec((1, group, rows, width), lambda z: (z, 0, 0, 0)),
            pl.BlockSpec((1, rows, 1), lambda z: (z, 0, 0)),
            pl.BlockSpec((group, 1, width), lambda z: (0, 0, 0)),
        ],
        out_specs=pl.BlockSpec((rows, group, width), lambda z: (z, 0, 0)),
        compiler_params=params(20),
        name="norm_rows",
    )(came, scale, gain)


def forward_sums(own, sent, group, count):
    planes = count // group
    if planes > 8:
        groups = [[plane * group + m for plane in range(planes)] for m in range(group)]
        whole = lax.psum(own.astype(jnp.bfloat16), "seq", axis_index_groups=groups)
        return whole.astype(jnp.float32), []
    came = []
    for hop in range(1, planes):
        pairs = [((hop - 1) * group + m, hop * group + m) for m in range(group)]
        if hop > 1:
            sent = [
                (own[c] + came[-3 + c].astype(jnp.float32)).astype(jnp.bfloat16) for c in range(3)
            ]
        came.extend([lax.ppermute(sent[c], "seq", pairs) for c in range(3)])
    return own, came


def asked_places(slot_order, plane, member, group, count):
    tok = slot_order.shape[0]
    seg, planes = tok // count, count // group
    wanted = slot_order.reshape(planes, group, seg) % tok
    if planes > 8:
        asked = lax.all_gather(wanted.reshape(tok), "seq").reshape(count, count, seg)
        asked = lax.dynamic_slice_in_dim(asked, plane * group, group, 1)
        return jnp.transpose(asked, (1, 0, 2)).reshape(group, tok, 1)
    column = jnp.zeros_like(wanted)
    for step in range(planes):
        target = (plane + step) % planes
        part = lax.dynamic_index_in_dim(wanted, target, 0, keepdims=True)
        if step:
            pairs = [(index, (index + step * group) % count) for index in range(count)]
            part = lax.ppermute(part, "seq", pairs)
        source = (plane - step) % planes
        column = lax.dynamic_update_slice_in_dim(column, part, source, 0)
    whole = jnp.zeros((planes, group, group, seg), jnp.int32)
    for d in range(group):
        part = lax.ppermute(column, "seq", swap_pairs(count, d)) if d else column
        whole = lax.dynamic_update_slice_in_dim(whole, part[:, None], member ^ d, 1)
    return jnp.transpose(whole, (2, 0, 1, 3)).reshape(group, tok, 1)


def per_device(
    queries, token_keys, token_values, fast_weights, learn_rate, out_gain, group_lengths, slot_order
):
    tok, group, width = queries.shape
    count = lax.axis_size("seq")
    seg = tok // count
    planes = count // group
    behind = WINDOW // (group * tok)
    position = lax.axis_index("seq")
    plane, member = position // group, position % group
    info = jnp.stack([plane, member, group_lengths[0]]).astype(jnp.int32)

    mine = split_heads(info, [token_keys, token_values])
    pairs = trade(mine, count)
    earlier = []
    for back in range(behind, 0, -1):
        shift = plane_pairs(count, back * group)
        earlier.extend([lax.ppermute(pair, "seq", shift) for pair in pairs])
    asked = trade(split_heads(info, [queries], pairs[1:2]), count)

    weights = lax.dynamic_index_in_dim(fast_weights, member, 1, keepdims=False)
    weights = jnp.transpose(weights, (1, 0, 2))
    rate = lax.dynamic_slice_in_dim(learn_rate, member, 1)
    own, *sent = weight_sums(info, weights, pairs)
    own, came = forward_sums(own, sent, group, count)
    state = own_attention(info, asked, pairs)
    places = asked_places(slot_order, plane, member, group, count)
    fast = fast_rows(info, rate, weights, own, came, asked)
    leaving = cross_rows(info, asked, earlier, state, fast, places, count)

    came = lax.all_to_all(leaving, "seq", split_axis=0, concat_axis=0, tiled=True)
    came = came.reshape(planes, group, group * seg, width)
    wide = came.astype(jnp.float32)
    power = lax.psum(jnp.sum(wide * wide, axis=(1, 3)), "head")
    scale = lax.rsqrt(power / (group * lax.axis_size("head") * width) + eps)
    return norm_rows(came, scale[:, :, None], out_gain[:, None, :])


def solution(mesh):
    return jax.shard_map(
        per_device,
        mesh=mesh,
        in_specs=(
            P("seq", "head", None),
            P("seq", "head", None),
            P("seq", "head", None),
            P(None, "head", None, None),
            P("head"),
            P("head", None),
            P(),
            P("seq"),
        ),
        out_specs=P("seq", "head", None),
        check_vma=False,
    )
```

time: 350 us -> 372 us (1.063); the launches traced: 344 us -> 371 us
  waiting for transfers between devices: 51.8 us -> 208 us
  blocking collectives: 151 us -> 3.59 us
  starting transfers between devices: 36.8 us -> 71.6 us
  local copies, waits for them, and re-layouts: 47.9 us -> 24 us
  Pallas kernels: 47.3 us -> 57.5 us
    ppermute x26 -> x25, waiting for transfers between devices: 51.8 us -> 160 us  [the longest x4 45.2 us: per_device(): earlier.extend([lax.ppermute(pair, 'seq', shift) for pair in pairs])]
    all_to_all x1 -> x0, blocking collectives: 76.5 us -> none  [per_device(): lax.all_to_all(leaving, 'seq', split_axis=0, concat_axis=0, tiled=True)]
    all_gather x1 -> x0, blocking collectives: 67.3 us -> none  [per_device(): asked = lax.all_gather(slot_order, 'seq').reshape(count, count, seg)]
    all_to_all x0 -> x1, waiting for transfers between devices: none -> 48.1 us  [per_device(): lax.all_to_all(leaving, 'seq', split_axis=0, concat_axis=0, tiled=True)]
    all_to_all x0 -> x1, starting transfers between devices: none -> 34 us  [per_device(): lax.all_to_all(leaving, 'seq', split_axis=0, concat_axis=0, tiled=True)]
    another operation x2 -> x0, local copies, waits for them, and re-layouts: 21.4 us -> none
    pallas_call x3 -> x7, Pallas kernels: 47.3 us -> 57.5 us  [the longest x1 16.6 us: cross_rows(): pl.pallas_call(functools.partial(cross_kernel, group, tok, count, behind,...]
    psum x1, blocking collectives: 7.56 us -> 3.59 us  [per_device(): power = lax.psum(jnp.sum(wide * wide, axis=(1, 3)), 'head')]
  transfers between devices with their start and end apart: 26 -> 26, of which waited for: 7 -> 14; matrix products, arithmetic and copies ran while one was open for 9% -> 3% of each run, Pallas kernels for 10% -> 6%
where the time goes in v2:
time: 372 us; the launch traced here: 371 us
  waiting for transfers between devices  208 us (56%)
  starting transfers between devices  71.6 us (19%)
  Pallas kernels  57.5 us (15%)
  local copies, waits for them, and re-layouts  24 us (6%)
  other arithmetic  5.64 us (2%)
    all_to_all x1, waiting for transfers between devices, per_device(): lax.all_to_all(leaving, 'seq', split_axis=0, concat_axis=0, tiled=True)  48.1 us
    ppermute x4, waiting for transfers between devices, per_device(): earlier.extend([lax.ppermute(pair, 'seq', shift) for pair in pairs])  45.2 us
    ppermute x6, waiting for transfers between devices, trade(): lax.ppermute(piece, 'seq', swap_pairs(count, d))  37.7 us
    all_to_all x1, starting transfers between devices, per_device(): lax.all_to_all(leaving, 'seq', split_axis=0, concat_axis=0, tiled=True)  34 us
    ppermute x9, waiting for transfers between devices, forward_sums(): came.extend([lax.ppermute(sent[c], 'seq', pairs) for c in range(3)])  32.2 us
    ppermute x3, waiting for transfers between devices, asked_places(): part = lax.ppermute(part, 'seq', pairs)  25.6 us
    ppermute x3, waiting for transfers between devices, asked_places(): part = lax.ppermute(column, 'seq', swap_pairs(count, d)) if d else column  19.4 us
    pallas_call x1, Pallas kernels, cross_rows(): pl.pallas_call(functools.partial(cross_kernel, group, tok, count, behind,...  16.6 us
  transfers between devices with their start and end apart: 26, of which 14 were waited for; matrix products, arithmetic and copies ran while one was open for 3% of the time, Pallas kernels for 6%

profile of v2, /device:TPU:13, one launch (start us, length us, event | category | flops | bytes accessed | tf_op | source)
XLA Modules:
  0.0 371.2 jit_solution(11275266810701218718)
XLA Ops:
  3.9 3.5 split_heads.2
  10.2 6.0 %constant_dynamic-slice_fusion.3 = bf16[512,1,3,512]{3,1,2,0:T(2,128)(2,1)S(1)} fusion(bf16[512,4,3,512]{3,1,2,0:T(4,128)(2,1)} %param.11, s32[]{:T(128)S(6)} %select_n.87), kind=kLoop, calls=%fused_computation.25 | loop fusion | bytes 3145732 | tf_op jit(solution)/shard_map/jit(dynamic_index_in_dim)/dynamic_slice | solution.py:516
  16.6 15.2 %collective-permute-done.refs_1_.refs_5_ = bf16[2,512,512]{2,1,0:T(8,128)(2,1)} collective-permute-done((bf16[2,512,512]{2,1,0:T(8,128)(2,1)}, bf16[2,512,512]{2,1,0:T(8,128)(2,1)}, u32[]{:S(2)}, u32[]{:S(2)}) %collective-permute-start) | collective-permute-done | bytes 1048608 | tf_op jit(solution)/shard_map/ppermute | solution.py:80
  33.7 20.6 %collective-permute-done.8.refs_7_.refs_3_ = bf16[2,512,512]{2,1,0:T(8,128)(2,1)} collective-permute-done((bf16[2,512,512]{2,1,0:T(8,128)(2,1)}, bf16[2,512,512]{2,1,0:T(8,128)(2,1)}, u32[]{:S(2)}, u32[]{:S(2)}) %collective-permute-start.8) | collective-permute-done | bytes 1048608 | tf_op jit(solution)/shard_map/ppermute | solution.py:80
  54.3 10.8 %weight_sums.1 = (f32[3,512,512]{2,1,0:T(8,128)S(1)}, bf16[512,512]{1,0:T(8,128)(2,1)S(1)}, bf16[512,512]{1,0:T(8,128)(2,1)S(1)}, bf16[512,512]{1,0:T(8,128)(2,1)S(1)}) custom-call(s32[3]{0:T(128)S(1)} %pad_add_fusion.info_ref, bf16[3,512,512]{2,1,0:T(8,128)(2,1)S(1)} %bitcast.38, bf16[2,512,512]{2,1,0:T(8,128)(2,1)} %get-tuple-element.25.refs_4_.refs_0_, ...), custom_call_target="tpu_custom_call" | custom-call | flops 6442450944 | bytes 7340032 | tf_op jit(solution)/shard_map/weight_sums/pallas_call | solution.py:138
  69.0 9.7 %collective-permute-done.10.refs_0_ = bf16[512,512]{1,0:T(8,128)(2,1)S(1)} collective-permute-done((bf16[512,512]{1,0:T(8,128)(2,1)S(1)}, bf16[512,512]{1,0:T(8,128)(2,1)S(1)}, u32[]{:S(2)}, u32[]{:S(2)}) %collective-permute-start.10) | collective-permute-done | bytes 524320 | tf_op jit(solution)/shard_map/ppermute | solution.py:468
  78.7 11.2 %collective-permute-done.11.refs_1_ = bf16[512,512]{1,0:T(8,128)(2,1)S(1)} collective-permute-done((bf16[512,512]{1,0:T(8,128)(2,1)S(1)}, bf16[512,512]{1,0:T(8,128)(2,1)S(1)}, u32[]{:S(2)}, u32[]{:S(2)}) %collective-permute-start.11) | collective-permute-done | bytes 524320 | tf_op jit(solution)/shard_map/ppermute | solution.py:468
  90.0 11.2 %collective-permute-done.12.refs_2_ = bf16[512,512]{1,0:T(8,128)(2,1)S(1)} collective-permute-done((bf16[512,512]{1,0:T(8,128)(2,1)S(1)}, bf16[512,512]{1,0:T(8,128)(2,1)S(1)}, u32[]{:S(2)}, u32[]{:S(2)}) %collective-permute-start.12) | collective-permute-done | bytes 524320 | tf_op jit(solution)/shard_map/ppermute | solution.py:468
  102.8 2.1 collective-permute-start.13
  104.9 2.1 collective-permute-start.14
  107.0 2.1 collective-permute-start.15
  109.5 25.6 %collective-permute-done.19 = s32[1,4,32]{2,1,0:T(4,128)S(1)} collective-permute-done((s32[1,4,32]{2,1,0:T(4,128)S(1)}, s32[1,4,32]{2,1,0:T(4,128)S(1)}, u32[]{:S(2)}, u32[]{:S(2)}) %collective-permute-start.19) | collective-permute-done | bytes 544 | tf_op jit(solution)/shard_map/ppermute | solution.py:486
  137.9 2.9 collective-permute-start.1
  142.8 2.8 fusion.1
  147.7 13.7 %collective-permute-done.22 = s32[4,4,32]{2,1,0:T(4,128)S(1)} collective-permute-done((s32[4,4,32]{2,1,0:T(4,128)S(1)}, s32[4,4,32]{2,1,0:T(4,128)S(1)}, u32[]{:S(2)}, u32[]{:S(2)}) %collective-permute-start.22) | collective-permute-done | bytes 2080 | tf_op jit(solution)/shard_map/ppermute | solution.py:491
  161.4 1.9 collective-permute-start.23
  163.3 3.2 collective-permute-done.23
  167.4 2.5 collective-permute-done.24
  171.4 6.8 %collective-permute-start.4 = (bf16[2,512,512]{2,1,0:T(8,128)(2,1)}, bf16[2,512,512]{2,1,0:T(8,128)(2,1)}, u32[]{:S(2)}, u32[]{:S(2)}) collective-permute-start(bf16[2,512,512]{2,1,0:T(8,128)(2,1)} %get-tuple-element.25.refs_4_.refs_0_), channel_id=1, source_target_pairs={{0,8},{2,10},{4,12},{6,14},{8,16},{10,18},{12,20},{14,22},{16,24},... | collective-permute-start | bytes 3145736 | tf_op jit(solution)/shard_map/ppermute | solution.py:513
  179.1 1.9 collective-permute-start.5
  181.8 1.9 collective-permute-start.7
  184.5 2.1 collective-permute-start.9
  189.8 2.0 reshape.13.refs_12_
  196.1 13.0 %own_attention.1 = (f32[4,512,512]{2,1,0:T(8,128)S(1)}, f32[4,512,128]{2,1,0:T(8,128)S(1)}, f32[4,512,128]{2,1,0:T(8,128)S(1)}) custom-call(s32[3]{0:T(128)S(1)} %pad_add_fusion.info_ref, bf16[1,512,512]{2,1,0:T(8,128)(2,1)S(1)} %copy-done.11, bf16[1,512,512]{2,1,0:T(8,128)(2,1)S(1)} %copy-done.14, bf16[1,512,512]{2,1,0:T(8,128)(2,1)S(1)} %copy-done.16, ...), custom_call_target="tpu_custom_call" | custom-call | flops 4294967296 | bytes 10485760 | tf_op jit(solution)/shard_map/own_attention/pallas_call | solution.py:248
  209.2 9.8 %fast_rows.1.refs_11_ = bf16[4,512,512]{2,1,0:T(8,128)(2,1)S(1)} custom-call(s32[3]{0:T(128)S(1)} %pad_add_fusion.info_ref, f32[1]{0:T(128)} %dynamic_slice.20.rate_ref, bf16[3,512,512]{2,1,0:T(8,128)(2,1)S(1)} %bitcast.39, f32[3,512,512]{2,1,0:T(8,128)S(1)} %get-tuple-element.31.own_ref, bf16[512,512]{1,0:T(8,128)(2,1)S(1)} %copy-done.5, ...), custom_call_target="tpu_custom_call" | custom-call | flops 3221225472 | bytes 7340032 | tf_op jit(solution)/shard_map/fast_rows/pallas_call | solution.py:324
  219.3 22.5 %collective-permute-done.7.refs_6_ = bf16[2,512,512]{2,1,0:T(8,128)(2,1)} collective-permute-done((bf16[2,512,512]{2,1,0:T(8,128)(2,1)}, bf16[2,512,512]{2,1,0:T(8,128)(2,1)}, u32[]{:S(2)}, u32[]{:S(2)}) %collective-permute-start.7) | collective-permute-done | bytes 1048608 | tf_op jit(solution)/shard_map/ppermute | solution.py:513
  241.8 22.5 %collective-permute-done.9.refs_7_ = bf16[2,512,512]{2,1,0:T(8,128)(2,1)} collective-permute-done((bf16[2,512,512]{2,1,0:T(8,128)(2,1)}, bf16[2,512,512]{2,1,0:T(8,128)(2,1)}, u32[]{:S(2)}, u32[]{:S(2)}) %collective-permute-start.9) | collective-permute-done | bytes 1048608 | tf_op jit(solution)/shard_map/ppermute | solution.py:513
  264.2 16.6 %cross_rows.1 = bf16[16,4,32,512]{3,2,1,0:T(8,128)(2,1)S(1)} custom-call(s32[3]{0:T(128)S(1)} %pad_add_fusion.info_ref, bf16[1,512,512]{2,1,0:T(8,128)(2,1)S(1)} %copy-done.12, bf16[1,512,512]{2,1,0:T(8,128)(2,1)S(1)} %copy-done.14, bf16[1,512,512]{2,1,0:T(8,128)(2,1)S(1)} %copy-done.16, bf16[1,512,512]{2,1,0:T(8,128)(2,1)S(1)} %copy-done.18, ...), custom_call_target="tpu_custom_call" | custom-call | flops 4294967296 | bytes 16777216 | tf_op jit(solution)/shard_map/cross_rows/pallas_call | solution.py:408
  282.1 34.0 %all-to-all-start = ((bf16[16,4,32,512]{3,2,1,0:T(8,128)(2,1)}), bf16[16,4,32,512]{3,2,1,0:T(8,128)(2,1)S(1)}, u32[]{:S(2)}, u32[]{:S(2)}) async-start(bf16[16,4,32,512]{3,2,1,0:T(8,128)(2,1)} %copy-done), calls=%async_computation | async-start | bytes 4194304 | tf_op jit(solution)/shard_map/all_to_all | solution.py:526
  316.2 48.1 %all-to-all-done = bf16[16,4,32,512]{3,2,1,0:T(8,128)(2,1)S(1)} async-done(((bf16[16,4,32,512]{3,2,1,0:T(8,128)(2,1)}), bf16[16,4,32,512]{3,2,1,0:T(8,128)(2,1)S(1)}, u32[]{:S(2)}, u32[]{:S(2)}) %all-to-all-start) | async-done | bytes 2097184 | tf_op jit(solution)/shard_map/all_to_all | solution.py:526
  364.9 3.6 psum.7
  368.7 2.5 norm_rows.1
  (115 shorter events, 35.7 us)
Async XLA Ops:
  7.4 24.4 %collective-permute-start = (bf16[2,512,512]{2,1,0:T(8,128)(2,1)}, bf16[2,512,512]{2,1,0:T(8,128)(2,1)}, u32[]{:S(2)}, u32[]{:S(2)}) collective-permute-start(bf16[2,512,512]{2,1,0:T(8,128)(2,1)} %get-tuple-element.20), channel_id=1, source_target_pairs={{0,2},{2,0},{4,6},{6,4},{8,10},{10,8},{12,14},{14,12},{16,18},{18,... | collective-permute-start | bytes 3145736 | tf_op jit(solution)/shard_map/ppermute | solution.py:80
  8.7 25.0 %collective-permute-start.6 = (bf16[2,512,512]{2,1,0:T(8,128)(2,1)}, bf16[2,512,512]{2,1,0:T(8,128)(2,1)}, u32[]{:S(2)}, u32[]{:S(2)}) collective-permute-start(bf16[2,512,512]{2,1,0:T(8,128)(2,1)} %get-tuple-element.26), channel_id=1, source_target_pairs={{0,4},{2,6},{4,0},{6,2},{8,12},{10,14},{12,8},{14,10},{16,20},{18,... | collective-permute-start | bytes 3145736 | tf_op jit(solution)/shard_map/ppermute | solution.py:80
  8.9 45.4 %collective-permute-start.8 = (bf16[2,512,512]{2,1,0:T(8,128)(2,1)}, bf16[2,512,512]{2,1,0:T(8,128)(2,1)}, u32[]{:S(2)}, u32[]{:S(2)}) collective-permute-start(bf16[2,512,512]{2,1,0:T(8,128)(2,1)} %get-tuple-element.27), channel_id=1, source_target_pairs={{0,6},{2,4},{4,2},{6,0},{8,14},{10,12},{12,10},{14,8},{16,22},{18,... | collective-permute-start | bytes 3145736 | tf_op jit(solution)/shard_map/ppermute | solution.py:80
  16.6 48.5 %copy-start.1 = (bf16[512,1,3,512]{3,0,2,1:T(8,128)(2,1)}, bf16[512,1,3,512]{3,0,2,1:T(8,128)(2,1)S(1)}, u32[]{:S(2)}) copy-start(bf16[512,1,3,512]{3,0,2,1:T(8,128)(2,1)S(1)} %copy.28) | copy-start | bytes 4718596
  65.1 13.6 %collective-permute-start.10 = (bf16[512,512]{1,0:T(8,128)(2,1)S(1)}, bf16[512,512]{1,0:T(8,128)(2,1)S(1)}, u32[]{:S(2)}, u32[]{:S(2)}) collective-permute-start(bf16[512,512]{1,0:T(8,128)(2,1)S(1)} %get-tuple-element.32), channel_id=1, source_target_pairs={{0,8},{2,10},{4,12},{6,14},{1,9},{3,11},{5,13},{7,15}} | collective-permute-start | bytes 1572872 | tf_op jit(solution)/shard_map/ppermute | solution.py:468
  66.4 23.5 %collective-permute-start.11 = (bf16[512,512]{1,0:T(8,128)(2,1)S(1)}, bf16[512,512]{1,0:T(8,128)(2,1)S(1)}, u32[]{:S(2)}, u32[]{:S(2)}) collective-permute-start(bf16[512,512]{1,0:T(8,128)(2,1)S(1)} %get-tuple-element.33), channel_id=1, source_target_pairs={{0,8},{2,10},{4,12},{6,14},{1,9},{3,11},{5,13},{7,15}} | collective-permute-start | bytes 1572872 | tf_op jit(solution)/shard_map/ppermute | solution.py:468
  67.7 33.5 %collective-permute-start.12 = (bf16[512,512]{1,0:T(8,128)(2,1)S(1)}, bf16[512,512]{1,0:T(8,128)(2,1)S(1)}, u32[]{:S(2)}, u32[]{:S(2)}) collective-permute-start(bf16[512,512]{1,0:T(8,128)(2,1)S(1)} %get-tuple-element.34), channel_id=1, source_target_pairs={{0,8},{2,10},{4,12},{6,14},{1,9},{3,11},{5,13},{7,15}} | collective-permute-start | bytes 1572872 | tf_op jit(solution)/shard_map/ppermute | solution.py:468
  78.7 24.1 %copy-start.4 = (bf16[512,512]{1,0:T(8,128)(2,1)}, bf16[512,512]{1,0:T(8,128)(2,1)S(1)}, u32[]{:S(2)}) copy-start(bf16[512,512]{1,0:T(8,128)(2,1)S(1)} %collective-permute-done.10.refs_0_) | copy-start | bytes 1572868
  102.8 35.2 %collective-permute-start.13 = (bf16[512,512]{1,0:T(8,128)(2,1)}, bf16[512,512]{1,0:T(8,128)(2,1)}, u32[]{:S(2)}, u32[]{:S(2)}) collective-permute-start(bf16[512,512]{1,0:T(8,128)(2,1)} %get-tuple-element.40), channel_id=1, source_target_pairs={{8,16},{10,18},{12,20},{14,22},{9,17},{11,19},{13,21},{15,23}} | collective-permute-start | bytes 1572872 | tf_op jit(solution)/shard_map/ppermute | solution.py:468
  104.9 36.0 %collective-permute-start.14 = (bf16[512,512]{1,0:T(8,128)(2,1)}, bf16[512,512]{1,0:T(8,128)(2,1)}, u32[]{:S(2)}, u32[]{:S(2)}) collective-permute-start(bf16[512,512]{1,0:T(8,128)(2,1)} %get-tuple-element.39), channel_id=1, source_target_pairs={{8,16},{10,18},{12,20},{14,22},{9,17},{11,19},{13,21},{15,23}} | collective-permute-start | bytes 1572872 | tf_op jit(solution)/shard_map/ppermute | solution.py:468
  107.0 35.8 %collective-permute-start.15 = (bf16[512,512]{1,0:T(8,128)(2,1)}, bf16[512,512]{1,0:T(8,128)(2,1)}, u32[]{:S(2)}, u32[]{:S(2)}) collective-permute-start(bf16[512,512]{1,0:T(8,128)(2,1)} %get-tuple-element.38), channel_id=1, source_target_pairs={{8,16},{10,18},{12,20},{14,22},{9,17},{11,19},{13,21},{15,23}} | collective-permute-start | bytes 1572872 | tf_op jit(solution)/shard_map/ppermute | solution.py:468
  109.3 25.8 %collective-permute-start.19 = (s32[1,4,32]{2,1,0:T(4,128)S(1)}, s32[1,4,32]{2,1,0:T(4,128)S(1)}, u32[]{:S(2)}, u32[]{:S(2)}) collective-permute-start(s32[1,4,32]{2,1,0:T(4,128)S(1)} %get-tuple-element.43), channel_id=1, source_target_pairs={{0,8},{2,10},{4,12},{6,14},{8,16},{10,18},{12,20},{14,22},{16,24},... | collective-permute-start | bytes 1544 | tf_op jit(solution)/shard_map/ppermute | solution.py:486
  109.3 36.3 %collective-permute-start.20 = (s32[1,4,32]{2,1,0:T(4,128)S(1)}, s32[1,4,32]{2,1,0:T(4,128)S(1)}, u32[]{:S(2)}, u32[]{:S(2)}) collective-permute-start(s32[1,4,32]{2,1,0:T(4,128)S(1)} %get-tuple-element.42), channel_id=1, source_target_pairs={{0,16},{2,18},{4,20},{6,22},{8,24},{10,26},{12,28},{14,30},{16,0},... | collective-permute-start | bytes 1544 | tf_op jit(solution)/shard_map/ppermute | solution.py:486
  135.1 11.2 %collective-permute-start.21 = (s32[1,4,32]{2,1,0:T(4,128)S(1)}, s32[1,4,32]{2,1,0:T(4,128)S(1)}, u32[]{:S(2)}, u32[]{:S(2)}) collective-permute-start(s32[1,4,32]{2,1,0:T(4,128)S(1)} %get-tuple-element.41), channel_id=1, source_target_pairs={{0,24},{2,26},{4,28},{6,30},{8,0},{10,2},{12,4},{14,6},{16,8},{18,... | collective-permute-start | bytes 1544 | tf_op jit(solution)/shard_map/ppermute | solution.py:486
  137.9 32.7 %collective-permute-start.1 = (bf16[1,512,512]{2,1,0:T(8,128)(2,1)S(1)}, bf16[1,512,512]{2,1,0:T(8,128)(2,1)S(1)}, u32[]{:S(2)}, u32[]{:S(2)}) collective-permute-start(bf16[1,512,512]{2,1,0:T(8,128)(2,1)S(1)} %get-tuple-element.22), channel_id=1, source_target_pairs={{0,2},{2,0},{4,6},{6,4},{8,10},{10,8},{12,14},{14,12},{16,18},{18,... | collective-permute-start | bytes 1572872 | tf_op jit(solution)/shard_map/ppermute | solution.py:80
  140.9 37.4 %collective-permute-start.2 = (bf16[1,512,512]{2,1,0:T(8,128)(2,1)S(1)}, bf16[1,512,512]{2,1,0:T(8,128)(2,1)S(1)}, u32[]{:S(2)}, u32[]{:S(2)}) collective-permute-start(bf16[1,512,512]{2,1,0:T(8,128)(2,1)S(1)} %get-tuple-element.23), channel_id=1, source_target_pairs={{0,4},{2,6},{4,0},{6,2},{8,12},{10,14},{12,8},{14,10},{16,20},{18,... | collective-permute-start | bytes 1572872 | tf_op jit(solution)/shard_map/ppermute | solution.py:80
  142.8 46.2 %copy-start.28 = (f32[4]{0:T(128)S(1)}, f32[4]{0:T(128)}, u32[]{:S(2)}) copy-start(f32[4]{0:T(128)} %param.12) | copy-start | bytes 52
  142.8 38.2 %collective-permute-start.3 = (bf16[1,512,512]{2,1,0:T(8,128)(2,1)S(1)}, bf16[1,512,512]{2,1,0:T(8,128)(2,1)S(1)}, u32[]{:S(2)}, u32[]{:S(2)}) collective-permute-start(bf16[1,512,512]{2,1,0:T(8,128)(2,1)S(1)} %get-tuple-element.24), channel_id=1, source_target_pairs={{0,6},{2,4},{4,2},{6,0},{8,14},{10,12},{12,10},{14,8},{16,22},{18,... | collective-permute-start | bytes 1572872 | tf_op jit(solution)/shard_map/ppermute | solution.py:80
  145.6 38.1 %collective-permute-start.16 = (bf16[512,512]{1,0:T(8,128)(2,1)S(1)}, bf16[512,512]{1,0:T(8,128)(2,1)S(1)}, u32[]{:S(2)}, u32[]{:S(2)}) collective-permute-start(bf16[512,512]{1,0:T(8,128)(2,1)S(1)} %get-tuple-element.36), channel_id=1, source_target_pairs={{16,24},{18,26},{20,28},{22,30},{17,25},{19,27},{21,29},{23,31}} | collective-permute-start | bytes 1572872 | tf_op jit(solution)/shard_map/ppermute | solution.py:468
  146.3 15.1 %collective-permute-start.22 = (s32[4,4,32]{2,1,0:T(4,128)S(1)}, s32[4,4,32]{2,1,0:T(4,128)S(1)}, u32[]{:S(2)}, u32[]{:S(2)}) collective-permute-start(s32[4,4,32]{2,1,0:T(4,128)S(1)} %constant_dynamic-update-slice_fusion), channel_id=1, source_target_pairs={{0,2},{2,0},{4,6},{6,4},{8,10},{10,8},{12,14},{14,12},{16,18},{18,... | collective-permute-start | bytes 6152 | tf_op jit(solution)/shard_map/ppermute | solution.py:491
  161.4 5.1 %collective-permute-start.23 = (s32[4,4,32]{2,1,0:T(4,128)S(1)}, s32[4,4,32]{2,1,0:T(4,128)S(1)}, u32[]{:S(2)}, u32[]{:S(2)}) collective-permute-start(s32[4,4,32]{2,1,0:T(4,128)S(1)} %constant_dynamic-update-slice_fusion), channel_id=1, source_target_pairs={{0,4},{2,6},{4,0},{6,2},{8,12},{10,14},{12,8},{14,10},{16,20},{18,... | collective-permute-start | bytes 6152 | tf_op jit(solution)/shard_map/ppermute | solution.py:491
  166.5 3.4 collective-permute-start.24
  169.9 16.7 %collective-permute-start.17 = (bf16[512,512]{1,0:T(8,128)(2,1)S(1)}, bf16[512,512]{1,0:T(8,128)(2,1)S(1)}, u32[]{:S(2)}, u32[]{:S(2)}) collective-permute-start(bf16[512,512]{1,0:T(8,128)(2,1)S(1)} %get-tuple-element.37), channel_id=1, source_target_pairs={{16,24},{18,26},{20,28},{22,30},{17,25},{19,27},{21,29},{23,31}} | collective-permute-start | bytes 1572872 | tf_op jit(solution)/shard_map/ppermute | solution.py:468
  171.4 47.6 %collective-permute-start.4 = (bf16[2,512,512]{2,1,0:T(8,128)(2,1)}, bf16[2,512,512]{2,1,0:T(8,128)(2,1)}, u32[]{:S(2)}, u32[]{:S(2)}) collective-permute-start(bf16[2,512,512]{2,1,0:T(8,128)(2,1)} %get-tuple-element.25.refs_4_.refs_0_), channel_id=1, source_target_pairs={{0,8},{2,10},{4,12},{6,14},{8,16},{10,18},{12,20},{14,22},{16,24},... | collective-permute-start | bytes 3145736 | tf_op jit(solution)/shard_map/ppermute | solution.py:513
  179.1 40.2 %collective-permute-start.5 = (bf16[2,512,512]{2,1,0:T(8,128)(2,1)}, bf16[2,512,512]{2,1,0:T(8,128)(2,1)}, u32[]{:S(2)}, u32[]{:S(2)}) collective-permute-start(bf16[2,512,512]{2,1,0:T(8,128)(2,1)} %collective-permute-done.refs_1_.refs_5_), channel_id=1, source_target_pairs={{0,8},{2,10},{4,12},{6,14},{8,16},{10,18},{12,20},{14,22},{16,24},... | collective-permute-start | bytes 3145736 | tf_op jit(solution)/shard_map/ppermute | solution.py:513
  181.8 60.0 %collective-permute-start.7 = (bf16[2,512,512]{2,1,0:T(8,128)(2,1)}, bf16[2,512,512]{2,1,0:T(8,128)(2,1)}, u32[]{:S(2)}, u32[]{:S(2)}) collective-permute-start(bf16[2,512,512]{2,1,0:T(8,128)(2,1)} %collective-permute-done.6.refs_6_.refs_2_), channel_id=1, source_target_pairs={{0,8},{2,10},{4,12},{6,14},{8,16},{10,18},{12,20},{14,22},{16,24},... | collective-permute-start | bytes 3145736 | tf_op jit(solution)/shard_map/ppermute | solution.py:513
  184.5 79.7 %collective-permute-start.9 = (bf16[2,512,512]{2,1,0:T(8,128)(2,1)}, bf16[2,512,512]{2,1,0:T(8,128)(2,1)}, u32[]{:S(2)}, u32[]{:S(2)}) collective-permute-start(bf16[2,512,512]{2,1,0:T(8,128)(2,1)} %collective-permute-done.8.refs_7_.refs_3_), channel_id=1, source_target_pairs={{0,8},{2,10},{4,12},{6,14},{8,16},{10,18},{12,20},{14,22},{16,24},... | collective-permute-start | bytes 3145736 | tf_op jit(solution)/shard_map/ppermute | solution.py:513
  187.5 21.7 %collective-permute-start.18 = (bf16[512,512]{1,0:T(8,128)(2,1)}, bf16[512,512]{1,0:T(8,128)(2,1)}, u32[]{:S(2)}, u32[]{:S(2)}) collective-permute-start(bf16[512,512]{1,0:T(8,128)(2,1)} %get-tuple-element.35), channel_id=1, source_target_pairs={{16,24},{18,26},{20,28},{22,30},{17,25},{19,27},{21,29},{23,31}} | collective-permute-start | bytes 1572872 | tf_op jit(solution)/shard_map/ppermute | solution.py:468
  196.0 13.1 %copy-start.12 = (bf16[1,512,512]{2,1,0:T(8,128)(2,1)S(1)}, bf16[1,512,512]{2,1,0:T(8,128)(2,1)}, u32[]{:S(2)}) copy-start(bf16[1,512,512]{2,1,0:T(8,128)(2,1)} %copy-done.10) | copy-start | bytes 1572868
  209.1 55.1 %copy-start.3 = (s32[4,512,1]{2,1,0:T(8,128)S(1)}, s32[4,512,1]{2,1,0:T(8,128)}, u32[]{:S(2)}) copy-start(s32[4,512,1]{2,1,0:T(8,128)} %reshape.13.refs_12_) | copy-start | bytes 24580
  282.1 34.1 %copy-start.26 = (f32[4,512]{1,0:T(4,128)S(1)}, f32[4,512]{1,0:T(4,128)}, u32[]{:S(2)}) copy-start(f32[4,512]{1,0:T(4,128)} %param.13) | copy-start | bytes 24580
  282.1 82.2 %all-to-all-start = ((bf16[16,4,32,512]{3,2,1,0:T(8,128)(2,1)}), bf16[16,4,32,512]{3,2,1,0:T(8,128)(2,1)S(1)}, u32[]{:S(2)}, u32[]{:S(2)}) async-start(bf16[16,4,32,512]{3,2,1,0:T(8,128)(2,1)} %copy-done), calls=%async_computation | async-start | bytes 4194304 | tf_op jit(solution)/shard_map/all_to_all | solution.py:526
  (23 other events, 123.1 us)

commit v3 on v2

v3 whole, which is shorter than its diff:
```python
import functools
import math

import jax
import jax.numpy as jnp
from jax import lax
from jax.experimental import pallas as pl
from jax.experimental.pallas import tpu as pltpu
from jax.sharding import PartitionSpec as P

WINDOW = 2048
NEG = -1e30
MIB = 1024 * 1024

eps = 1e-06

NT = (((1,), (1,)), ((), ()))
TN = (((0,), (0,)), ((), ()))
NN = (((1,), (0,)), ((), ()))

ANY = pl.BlockSpec(memory_space=pl.ANY)
SMEM = pl.BlockSpec(memory_space=pltpu.SMEM)
VMEM = pl.BlockSpec(memory_space=pltpu.VMEM)


def dot(left, right, dims):
    return lax.dot_general(left, right, dims, preferred_element_type=jnp.float32)


def params(mib):
    return pltpu.CompilerParams(vmem_limit_bytes=mib * MIB)


def swap_pairs(count, distance):
    return [(index, index ^ distance) for index in range(count)]


def plane_pairs(count, steps):
    return [(index, index + steps) for index in range(count - steps)]


def split_kernel(total, group, info_ref, *refs):
    x_refs = refs[:total]
    outs = refs[len(refs) - group - 2 : len(refs) - 2]
    buf, sems = refs[-2:]
    member = info_ref[1]
    for t, x_ref in enumerate(x_refs):
        buf[:, t] = jnp.swapaxes(x_ref[...], 0, 1)
    copies = [
        pltpu.make_async_copy(buf.at[member ^ d], outs[d], sems.at[d]) for d in range(group)
    ]
    for copy in copies:
        copy.start()
    for copy in copies:
        copy.wait()


def split_heads(info, arrays, after=()):
    tok, group, width = arrays[0].shape
    total = len(arrays)
    return pl.pallas_call(
        functools.partial(split_kernel, total, group),
        out_shape=[jax.ShapeDtypeStruct((total, tok, width), jnp.bfloat16)] * group,
        in_specs=[SMEM] + [VMEM] * total + [ANY] * len(after),
        out_specs=[ANY] * group,
        scratch_shapes=[
            pltpu.VMEM((group, total, tok, width), jnp.bfloat16),
            pltpu.SemaphoreType.DMA((group,)),
        ],
        compiler_params=params(20),
        cost_estimate=pl.CostEstimate(
            flops=0, bytes_accessed=4 * total * group * tok * width, transcendentals=0
        ),
        name="split_heads",
    )(info, *arrays, *after)


def trade(pieces, count):
    return [
        lax.ppermute(piece, "seq", swap_pairs(count, d)) if d else piece
        for d, piece in enumerate(pieces)
    ]


def grad_kernel(group, tok, first, last, carried, info_ref, w_ref, *refs):
    pieces = last - first
    kv_any, refs = refs[:pieces], refs[pieces:]
    kvbuf, acc, sems, acc_sem = refs[-4:]
    plane, member, first_len = info_ref[0], info_ref[1], info_ref[2]
    copies = [pltpu.make_async_copy(kv_any[n], kvbuf.at[n], sems.at[n]) for n in range(pieces)]
    for copy in copies:
        copy.start()
    if carried:
        load = pltpu.make_async_copy(refs[0], acc, acc_sem.at[0])
        load.start()
        load.wait()
    else:
        acc[...] = jnp.zeros_like(acc)
    hidden = w_ref.shape[1]
    part = min(256, hidden)
    for copy in copies:
        copy.wait()

    def piece(n, carry):
        first_tok = (plane * group + (member ^ (first + n))) * tok

        @pl.when(first_tok < first_len)
        def _():
            keys = kvbuf[n, 0]
            token = first_tok + lax.broadcasted_iota(jnp.int32, (tok, 1), 0)
            values = jnp.where(token < first_len, kvbuf[n, 1].astype(jnp.float32), 0.0)
            values = values.astype(jnp.bfloat16)
            for f in range(0, hidden, part):
                rows = pl.ds(f, part)
                gate = dot(keys, w_ref[0, rows, :], NT)
                up = dot(keys, w_ref[1, rows, :], NT)
                back = dot(values, w_ref[2, rows, :], NT)
                sig = jax.nn.sigmoid(gate)
                silu = gate * sig
                act = (silu * up).astype(jnp.bfloat16)
                grad_up = (back * silu).astype(jnp.bfloat16)
                grad_gate = (back * up * sig * (1.0 + gate * (1.0 - sig))).astype(jnp.bfloat16)
                acc[0, rows, :] += dot(grad_gate, keys, TN)
                acc[1, rows, :] += dot(grad_up, keys, TN)
                acc[2, rows, :] += dot(act, values, TN)

        return carry

    lax.fori_loop(0, pieces, piece, 0)
    whole = last == group
    outs = refs[len(refs) - 4 - (4 if whole else 1) : len(refs) - 4]
    keep = pltpu.make_async_copy(acc, outs[0], acc_sem.at[1])
    keep.start()
    for c, sent in enumerate(outs[1:]):
        sent[...] = acc[c].astype(sent.dtype)
    keep.wait()


def weight_sums(info, weights, pairs, first, last, carried=(), after=()):
    group = len(pairs)
    _, tok, width = pairs[0].shape
    rows, hidden, _ = weights.shape
    pieces = last - first
    sent = rows if last == group else 0
    return pl.pallas_call(
        functools.partial(grad_kernel, group, tok, first, last, len(carried)),
        out_shape=[jax.ShapeDtypeStruct(weights.shape, jnp.float32)]
        + [jax.ShapeDtypeStruct((hidden, width), jnp.bfloat16)] * sent,
        in_specs=[SMEM, VMEM] + [ANY] * (pieces + len(carried) + len(after)),
        out_specs=[ANY] + [VMEM] * sent,
        scratch_shapes=[
            pltpu.VMEM((pieces, 2, tok, width), jnp.bfloat16),
            pltpu.VMEM(weights.shape, jnp.float32),
            pltpu.SemaphoreType.DMA((pieces,)),
            pltpu.SemaphoreType.DMA((2,)),
        ],
        compiler_params=params(28),
        cost_estimate=pl.CostEstimate(
            flops=2 * 6 * pieces * tok * hidden * width,
            bytes_accessed=2 * (2 * pieces * tok * width + 2 * rows * hidden * width),
            transcendentals=pieces * tok * hidden,
        ),
        name="weight_sums",
    )(info, weights, *pairs[first:last], *carried, *after)


def lanes_sum(expo):
    total = expo[:, :128]
    for lane in range(128, expo.shape[1], 128):
        total = total + expo[:, lane : lane + 128]
    return total


def soft_steps(parts, scale, fresh, acc, top, norm):
    scores = [
        dot(rows, keys, NT) if mask is None else jnp.where(mask, dot(rows, keys, NT), NEG)
        for _, rows, keys, _, mask in parts
    ]
    done = []
    for (where, _, _, _, _), score in zip(parts, scores):
        peak = jnp.max(score, axis=1, keepdims=True)
        if fresh:
            decay = None
        else:
            before = top[where, :1]
            peak = jnp.maximum(peak, before)
            decay = jnp.exp2((before - peak) * scale)
        expo = jnp.exp2((score - peak) * scale)
        done.append((peak, decay, lanes_sum(expo), expo.astype(jnp.bfloat16)))
    for (where, _, _, values, _), (peak, decay, total, expo) in zip(parts, done):
        mixed = dot(expo, values, NN)
        wide = (peak.shape[0], 128)
        top[where, :] = jnp.broadcast_to(peak, wide)
        if fresh:
            norm[where, :] = total
            acc[where, :] = mixed
        else:
            norm[where, :] = norm[where, :] * decay + total
            acc[where, :] = acc[where, :] * decay + mixed


def soft_close(scale, acc, top, norm, out_ref, level_ref):
    total = jnp.sum(norm[...], axis=1, keepdims=True)
    out_ref[...] = (acc[...] / jnp.maximum(total, 1e-30)).astype(out_ref.dtype)
    level = top[...] * scale + jnp.log2(jnp.maximum(total, 1e-30))
    level_ref[...] = jnp.transpose(level)[:8]


def as_column(rows):
    return jnp.transpose(jnp.concatenate([rows] * 16, axis=0))[:, :1]


def score_scale(width):
    return math.log2(math.e) / math.sqrt(width)


def triangle(rows, cols, first_row, first_col, lower):
    row = first_row + lax.broadcasted_iota(jnp.int32, (rows, cols), 0)
    col = first_col + lax.broadcasted_iota(jnp.int32, (rows, cols), 1)
    return col <= row if lower else col > row


def own_kernel(group, tok, part, info_ref, *refs):
    q_any, kv_any = refs[:group], refs[group : 2 * group]
    out_ref, level_ref, acc, top, norm, qbuf, kvbuf, sems = refs[-8:]
    member = info_ref[1]
    copies = []
    for d in range(group):
        copies.append(pltpu.make_async_copy(q_any[d], qbuf.at[pl.ds(d, 1)], sems.at[0, d]))
        copies.append(pltpu.make_async_copy(kv_any[d], kvbuf.at[d], sems.at[1, d]))
    for copy in copies:
        copy.start()
    for copy in copies:
        copy.wait()
    scale = score_scale(qbuf.shape[-1])

    def piece(d, carry):
        parts = []
        for r in range(0, tok, part):
            where, keys = pl.ds(r, part), pl.ds(0, r + part)
            mask = triangle(part, r + part, r, 0, True)
            parts.append((where, qbuf[d, where], kvbuf[d, 0, keys], kvbuf[d, 1, keys], mask))
        soft_steps(parts, scale, True, acc, top, norm)

        def earlier(other, carry):
            e = member ^ other
            parts = []
            for r in range(0, tok, part):
                where = pl.ds(r, part)
                parts.append((where, qbuf[d, where], kvbuf[e, 0], kvbuf[e, 1], None))
            soft_steps(parts, scale, False, acc, top, norm)
            return carry

        lax.fori_loop(0, member ^ d, earlier, 0)
        soft_close(scale, acc, top, norm, out_ref.at[d], level_ref.at[d])
        return carry

    lax.fori_loop(0, group, piece, 0)


def soft_shapes(group, tok, width):
    return [
        jax.ShapeDtypeStruct((group, tok, width), jnp.bfloat16),
        jax.ShapeDtypeStruct((group, 8, tok), jnp.float32),
    ]


def soft_scratch(tok, width):
    return [
        pltpu.VMEM((tok, width), jnp.float32),
        pltpu.VMEM((tok, 128), jnp.float32),
        pltpu.VMEM((tok, 128), jnp.float32),
    ]


def soft_cost(group, tok, width):
    return pl.CostEstimate(
        flops=2 * group * group * tok * tok * width,
        bytes_accessed=width * group * tok * 8,
        transcendentals=group * group * tok * tok // 2,
    )


def own_attention(info, queries, pairs, after=()):
    group = len(queries)
    _, tok, width = pairs[0].shape
    part = min(256, tok)
    return pl.pallas_call(
        functools.partial(own_kernel, group, tok, part),
        out_shape=soft_shapes(group, tok, width),
        in_specs=[SMEM] + [ANY] * (2 * group + len(after)),
        out_specs=[VMEM] * 2,
        scratch_shapes=soft_scratch(tok, width)
        + [
            pltpu.VMEM((group, tok, width), jnp.bfloat16),
            pltpu.VMEM((group, 2, tok, width), jnp.bfloat16),
            pltpu.SemaphoreType.DMA((2, group)),
        ],
        compiler_params=params(28),
        cost_estimate=soft_cost(group, tok, width),
        name="own_attention",
    )(info, *queries, *pairs, *after)


def pick_copy(flag, first, second, into, sem):
    if second is None:
        copy = pltpu.make_async_copy(first, into, sem)
        copy.start()
        return copy

    @pl.when(flag == 0)
    def _():
        pltpu.make_async_copy(first, into, sem).start()

    @pl.when(flag != 0)
    def _():
        pltpu.make_async_copy(second, into, sem).start()

    return pltpu.make_async_copy(first, into, sem)


def cross_kernel(group, tok, behind, part, lending, info_ref, *refs):
    pieces = behind * group
    q_any, refs = refs[:group], refs[group:]
    kv_any, refs = refs[:pieces], refs[pieces:]
    lent_q, lent_kv = [None] * group, [None] * pieces
    if lending:
        lent_q, lent_kv, refs = refs[:group], refs[group : 2 * group], refs[2 * group :]
    out_ref, level_ref, acc, top, norm, qbuf, kvbuf, sems, kv_sems = refs[-9:]
    plane, member, lends, planes = info_ref[0], info_ref[1], info_ref[3], info_ref[4]
    copies = [
        pick_copy(lends, kv_any[at], lent_kv[at], kvbuf.at[at], kv_sems.at[at])
        for at in range(pieces)
    ]
    for d in range(group):
        copies.append(pick_copy(lends, q_any[d], lent_q[d], qbuf.at[pl.ds(d, 1)], sems.at[d]))
    for copy in copies:
        copy.wait()
    scale = score_scale(qbuf.shape[-1])
    valid = jnp.maximum(behind - plane, 0) * group
    if lending:
        valid = jnp.where(lends == 0, valid, jnp.where(plane + 1 < planes, 0, pieces))

    def piece(d, carry):
        at = member ^ d

        @pl.when(at >= valid)
        def _():
            parts = []
            for r in range(0, tok, part):
                where, keys = pl.ds(r, part), pl.ds(r, tok - r)
                mask = triangle(part, tok - r, r, r, False)
                parts.append((where, qbuf[d, where], kvbuf[d, 0, keys], kvbuf[d, 1, keys], mask))
            soft_steps(parts, scale, True, acc, top, norm)

        @pl.when(at < valid)
        def _():
            acc[...] = jnp.zeros_like(acc)
            norm[...] = jnp.zeros_like(norm)
            top[...] = jnp.full_like(top, NEG)

        def later(other, carry):
            e = other // group * group + (member ^ (other % group))
            parts = []
            for r in range(0, tok, part):
                where = pl.ds(r, part)
                parts.append((where, qbuf[d, where], kvbuf[e, 0], kvbuf[e, 1], None))
            soft_steps(parts, scale, False, acc, top, norm)
            return carry

        lax.fori_loop(jnp.maximum(at + 1, valid), pieces, later, 0)
        soft_close(scale, acc, top, norm, out_ref.at[d], level_ref.at[d])
        return carry

    lax.fori_loop(0, group, piece, 0)


def cross_attention(info, queries, earlier, lent, after=()):
    group = len(queries)
    _, tok, width = queries[0].shape
    behind = len(earlier) // group
    part = min(256, tok)
    return pl.pallas_call(
        functools.partial(cross_kernel, group, tok, behind, part, len(lent)),
        out_shape=soft_shapes(group, tok, width),
        in_specs=[SMEM] + [ANY] * (group + len(earlier) + len(lent) + len(after)),
        out_specs=[VMEM] * 2,
        scratch_shapes=soft_scratch(tok, width)
        + [
            pltpu.VMEM((group, tok, width), jnp.bfloat16),
            pltpu.VMEM((len(earlier), 2, tok, width), jnp.bfloat16),
            pltpu.SemaphoreType.DMA((group,)),
            pltpu.SemaphoreType.DMA((len(earlier),)),
        ],
        compiler_params=params(28),
        cost_estimate=soft_cost(group, tok, width),
        name="cross_attention",
    )(info, *queries, *earlier, *lent, *after)


def finish_kernel(group, tok, count, hops, lending, info_ref, rate_ref, w_ref, place_ref, *refs):
    own_any, refs = refs[0], refs[1:]
    came, refs = refs[: 3 * hops], refs[3 * hops :]
    q_any, refs = refs[:group], refs[group:]
    own_rows, own_level, cross_any, cross_level = refs[:4]
    lent_any, lent_level = refs[4:6] if lending else (None, None)
    out_ref, new_w, sums, cbuf, qbuf, obuf, xbuf, lbuf, sems, q_sems = refs[-10:]
    plane, member, first_len, lends = info_ref[0], info_ref[1], info_ref[2], info_ref[3]
    own_copy = pltpu.make_async_copy(own_any, sums, sems.at[0])
    own_copy.start()

    def came_copy(hop, c):
        return pltpu.make_async_copy(came[3 * hop + c], cbuf.at[c], sems.at[1 + c])

    for hop in range(hops):

        @pl.when(plane == hop + 1)
        def _():
            for c in range(3):
                came_copy(hop, c).start()

    if hops:

        @pl.when((plane == 0) | (plane > hops))
        def _():
            cbuf[...] = jnp.zeros_like(cbuf)

    level_copies = [
        pltpu.make_async_copy(own_level, lbuf.at[0], sems.at[4]),
        pick_copy(lends, cross_level, lent_level, lbuf.at[1], sems.at[5]),
    ]
    level_copies[0].start()
    q_copies = [
        pltpu.make_async_copy(q_any[d], qbuf.at[pl.ds(d, 1)], q_sems.at[d]) for d in range(group)
    ]
    for copy in q_copies:
        copy.start()
    row_copies = [
        pltpu.make_async_copy(own_rows, obuf, sems.at[6]),
        pick_copy(lends, cross_any, lent_any, xbuf, sems.at[7]),
    ]
    row_copies[0].start()

    own_copy.wait()
    if hops:

        @pl.when((plane > 0) & (plane <= hops))
        def _():
            for c in range(3):
                came_copy(0, c).wait()

    step = rate_ref[0] / first_len.astype(jnp.float32)

    @pl.when((plane + 1) * group * tok > first_len)
    def _():
        for c in range(3):
            previous = w_ref[c].astype(jnp.float32)
            summed = sums[c]
            if hops:
                summed = summed + cbuf[c].astype(jnp.float32)
            updated = previous + step * summed
            old_norm = jnp.sqrt(jnp.sum(previous * previous, axis=1, keepdims=True) + eps)
            new_norm = jnp.sqrt(jnp.sum(updated * updated, axis=1, keepdims=True) + eps)
            new_w[c] = (updated * (old_norm / new_norm)).astype(new_w.dtype)

    for copy in q_copies + level_copies + row_copies:
        copy.wait()

    def apply(rows, weights):
        gate = dot(rows, weights[0], NT)
        up = dot(rows, weights[1], NT)
        act = (gate * jax.nn.sigmoid(gate) * up).astype(jnp.bfloat16)
        return dot(act, weights[2], NN)

    seg = tok // count

    def piece(d, carry):
        at = member ^ d
        first_tok = (plane * group + at) * tok
        own_log, cross_log = as_column(lbuf[0, d]), as_column(lbuf[1, d])
        cross_log = jnp.where(plane > 0, cross_log, NEG)
        own_part = 1.0 / (1.0 + jnp.exp2(cross_log - own_log))
        cross_part = 1.0 / (1.0 + jnp.exp2(own_log - cross_log))
        mixed = obuf[d].astype(jnp.float32) * own_part + xbuf[d].astype(jnp.float32) * cross_part
        mixed = mixed.astype(jnp.bfloat16).astype(jnp.float32)

        def leave(fast):
            rows = (mixed + fast).astype(jnp.bfloat16)
            pick = as_column(place_ref[at]).astype(jnp.int32)
            pick = pick == lax.broadcasted_iota(jnp.int32, (tok, tok), 1)
            sorted_rows = dot(pick.astype(jnp.bfloat16), rows, NN)
            out_ref[:, at] = sorted_rows.reshape(count, seg, rows.shape[-1]).astype(out_ref.dtype)

        @pl.when(first_tok + tok <= first_len)
        def _():
            leave(apply(qbuf[d], w_ref))

        @pl.when(first_tok >= first_len)
        def _():
            leave(apply(qbuf[d], new_w))

        @pl.when((first_tok < first_len) & (first_tok + tok > first_len))
        def _():
            token = first_tok + lax.broadcasted_iota(jnp.int32, (tok, 1), 0)
            leave(jnp.where(token < first_len, apply(qbuf[d], w_ref), apply(qbuf[d], new_w)))

        return carry

    lax.fori_loop(0, group, piece, 0)


def finish_rows(info, rate, weights, places, own, came, queries, own_part, cross_part, lent, count):
    group = len(queries)
    _, tok, width = queries[0].shape
    hidden = weights.shape[1]
    hops = len(came) // 3
    return pl.pallas_call(
        functools.partial(finish_kernel, group, tok, count, hops, len(lent)),
        out_shape=jax.ShapeDtypeStruct((count, group, tok // count, width), jnp.bfloat16),
        in_specs=[SMEM] * 2 + [VMEM] * 2 + [ANY] * (1 + 3 * hops + group + 4 + len(lent)),
        out_specs=VMEM,
        scratch_shapes=[
            pltpu.VMEM(weights.shape, jnp.bfloat16),
            pltpu.VMEM(weights.shape, jnp.float32),
            pltpu.VMEM(weights.shape, jnp.bfloat16),
            pltpu.VMEM((group, tok, width), jnp.bfloat16),
            pltpu.VMEM((group, tok, width), jnp.bfloat16),
            pltpu.VMEM((group, tok, width), jnp.bfloat16),
            pltpu.VMEM((2, group, 8, tok), jnp.float32),
            pltpu.SemaphoreType.DMA((8,)),
            pltpu.SemaphoreType.DMA((group,)),
        ],
        compiler_params=params(36),
        cost_estimate=pl.CostEstimate(
            flops=2 * group * tok * width * (3 * hidden + tok),
            bytes_accessed=2 * (4 * group * tok * width + 6 * hidden * width),
            transcendentals=group * tok * hidden,
        ),
        name="finish_rows",
    )(info, rate, weights, places, own, *came, *queries, *own_part, *cross_part, *lent)


def norm_kernel(came_ref, scale_ref, gain_ref, out_ref):
    scaled = came_ref[0].astype(jnp.float32) * scale_ref[...] * gain_ref[...]
    out_ref[...] = jnp.swapaxes(scaled.astype(out_ref.dtype), 0, 1)


def norm_rows(came, scale, gain):
    planes, group, rows, width = came.shape
    return pl.pallas_call(
        norm_kernel,
        grid=(planes,),
        out_shape=jax.ShapeDtypeStruct((planes * rows, group, width), jnp.bfloat16),
        in_specs=[
            pl.BlockSpec((1, group, rows, width), lambda z: (z, 0, 0, 0)),
            pl.BlockSpec((1, rows, 1), lambda z: (z, 0, 0)),
            pl.BlockSpec((group, 1, width), lambda z: (0, 0, 0)),
        ],
        out_specs=pl.BlockSpec((rows, group, width), lambda z: (z, 0, 0)),
        compiler_params=params(20),
        name="norm_rows",
    )(came, scale, gain)


def forward_sums(own, sent, group, count):
    planes = count // group
    if planes > 8:
        groups = [[plane * group + m for plane in range(planes)] for m in range(group)]
        whole = lax.psum(own.astype(jnp.bfloat16), "seq", axis_index_groups=groups)
        return whole.astype(jnp.float32), []
    came = []
    for hop in range(1, planes):
        pairs = [((hop - 1) * group + m, hop * group + m) for m in range(group)]
        if hop > 1:
            sent = [
                (own[c] + came[-3 + c].astype(jnp.float32)).astype(jnp.bfloat16) for c in range(3)
            ]
        came.extend([lax.ppermute(sent[c], "seq", pairs) for c in range(3)])
    return own, came


def as_places(asked, group, tok):
    places = jnp.transpose(asked, (1, 0, 2)).reshape(group, 1, tok).astype(jnp.float32)
    return jnp.broadcast_to(places, (group, 8, tok))


def asked_places(slot_order, plane, member, group, count):
    tok = slot_order.shape[0]
    seg, planes = tok // count, count // group
    wanted = slot_order.reshape(planes, group, seg) % tok
    if planes > 8:
        asked = lax.all_gather(wanted.reshape(tok), "seq").reshape(count, count, seg)
        asked = lax.dynamic_slice_in_dim(asked, plane * group, group, 1)
        return as_places(asked, group, tok)
    column = jnp.zeros_like(wanted)
    for step in range(planes):
        target = (plane + step) % planes
        part = lax.dynamic_index_in_dim(wanted, target, 0, keepdims=True)
        if step:
            pairs = [(index, (index + step * group) % count) for index in range(count)]
            part = lax.ppermute(part, "seq", pairs)
        source = (plane - step) % planes
        column = lax.dynamic_update_slice_in_dim(column, part, source, 0)
    whole = jnp.zeros((planes, group, group, seg), jnp.int32)
    for d in range(group):
        part = lax.ppermute(column, "seq", swap_pairs(count, d)) if d else column
        whole = lax.dynamic_update_slice_in_dim(whole, part[:, None], member ^ d, 1)
    return as_places(whole.reshape(count, group, seg), group, tok)


def per_device(
    queries, token_keys, token_values, fast_weights, learn_rate, out_gain, group_lengths, slot_order
):
    tok, group, width = queries.shape
    count = lax.axis_size("seq")
    seg = tok // count
    planes = count // group
    behind = WINDOW // (group * tok)
    sides = lax.axis_size("head")
    lending = behind == 1 and sides % 2 == 0
    position = lax.axis_index("seq")
    plane, member = position // group, position % group
    lends = lax.axis_index("head") % 2 if lending else jnp.int32(0)
    info = jnp.stack([plane, member, group_lengths[0], lends, jnp.int32(planes)])
    info = info.astype(jnp.int32)

    def across(value, steps, odd):
        pairs = plane_pairs(count, steps)
        if not lending:
            return lax.ppermute(value, "seq", pairs)
        both = [(a * sides + h, b * sides + h) for a, b in pairs for h in range(odd, sides, 2)]
        return lax.ppermute(value, ("seq", "head"), both)

    def back_across(value, odd):
        pairs = [(b, a) for a, b in plane_pairs(count, group)]
        both = [(a * sides + h, b * sides + h) for a, b in pairs for h in range(odd, sides, 2)]
        return lax.ppermute(value, ("seq", "head"), both)

    mine = split_heads(info, [token_keys, token_values])
    pairs = trade(mine, count)
    earlier = []
    for back in range(behind, 0, -1):
        earlier.extend([across(pair, back * group, 0) for pair in pairs])
    asked = trade(split_heads(info, [queries], pairs[1:2]), count)
    lent = [back_across(piece, 1) for piece in asked] + pairs if lending else []

    weights = lax.dynamic_index_in_dim(fast_weights, member, 1, keepdims=False)
    weights = jnp.transpose(weights, (1, 0, 2))
    rate = lax.dynamic_slice_in_dim(learn_rate, member, 1)
    half = group // 2
    carried = weight_sums(info, weights, pairs, 0, half) if half else []
    own, *sent = weight_sums(info, weights, pairs, half, group, carried, earlier[:half])
    own, came = forward_sums(own, sent, group, count)
    own_part = own_attention(info, asked, pairs, earlier[half:])
    cross_part = cross_attention(info, asked, earlier, lent, came[:3])
    lent_part = [across(value, group, 1) for value in cross_part] if lending else []
    places = asked_places(slot_order, plane, member, group, count)
    leaving = finish_rows(
        info, rate, weights, places, own, came, asked, own_part, cross_part, lent_part, count
    )

    came = lax.all_to_all(leaving, "seq", split_axis=0, concat_axis=0, tiled=True)
    came = came.reshape(planes, group, group * seg, width)
    wide = came.astype(jnp.float32)
    power = lax.psum(jnp.sum(wide * wide, axis=(1, 3)), "head")
    scale = lax.rsqrt(power / (group * lax.axis_size("head") * width) + eps)
    return norm_rows(came, scale[:, :, None], out_gain[:, None, :])


def solution(mesh):
    return jax.shard_map(
        per_device,
        mesh=mesh,
        in_specs=(
            P("seq", "head", None),
            P("seq", "head", None),
            P("seq", "head", None),
            P(None, "head", None, None),
            P("head"),
            P("head", None),
            P(),
            P("seq"),
        ),
        out_specs=P("seq", "head", None),
        check_vma=False,
    )
```

time: 372 us -> 310 us (0.83)
  waiting for transfers between devices: 208 us -> 166 us
  starting transfers between devices: 71.6 us -> 51.3 us
    ppermute x4 -> x10, waiting for transfers between devices: 45.2 us -> 0.03 us  [the longest x6 0.02 us: across(): return lax.ppermute(value, ('seq', 'head'), both)]
    all_to_all x1, starting transfers between devices: 34 us -> 4.89 us  [per_device(): lax.all_to_all(leaving, 'seq', split_axis=0, concat_axis=0, tiled=True)]
    ppermute x3, waiting for transfers between devices: 25.6 us -> 49 us  [asked_places(): part = lax.ppermute(part, 'seq', pairs)]
    ppermute x3, waiting for transfers between devices: 19.4 us -> 2.63 us  [asked_places(): part = lax.ppermute(column, 'seq', swap_pairs(count, d)) if d else column]
    all_to_all x1, waiting for transfers between devices: 48.1 us -> 36.5 us  [per_device(): lax.all_to_all(leaving, 'seq', split_axis=0, concat_axis=0, tiled=True)]
    ppermute x6, waiting for transfers between devices: 37.7 us -> 46.3 us  [trade(): lax.ppermute(piece, 'seq', swap_pairs(count, d))]
    ppermute x4 -> x10, starting transfers between devices: 12.8 us -> 18.9 us  [the longest x6 10.7 us: across(): return lax.ppermute(value, ('seq', 'head'), both)]
    pallas_call x3 -> x4, Pallas kernels: 37.2 us -> 39.5 us  [the longest x1 13.6 us: finish_rows(): pl.pallas_call(functools.partial(finish_kernel, group, tok, count, hops,...]
  transfers between devices with their start and end apart: 26 -> 32, of which waited for: 14 -> 11; matrix products, arithmetic and copies ran while one was open for 3% -> 4% of each run, Pallas kernels for 6% -> 9%
where the time goes in v3:
time: 310 us; the launch traced here: 309 us
  waiting for transfers between devices  166 us (54%)
  Pallas kernels  59.1 us (19%)
  starting transfers between devices  51.3 us (17%)
  local copies, waits for them, and re-layouts  24.1 us (8%)
  other arithmetic  4.98 us (2%)
    ppermute x3, waiting for transfers between devices, asked_places(): part = lax.ppermute(part, 'seq', pairs)  49 us
    ppermute x6, waiting for transfers between devices, trade(): lax.ppermute(piece, 'seq', swap_pairs(count, d))  46.3 us
    all_to_all x1, waiting for transfers between devices, per_device(): lax.all_to_all(leaving, 'seq', split_axis=0, concat_axis=0, tiled=True)  36.5 us
    ppermute x9, waiting for transfers between devices, forward_sums(): came.extend([lax.ppermute(sent[c], 'seq', pairs) for c in range(3)])  31.5 us
    unnamed x78, local copies, waits for them, and re-layouts  15.5 us
    pallas_call x1, Pallas kernels, finish_rows(): pl.pallas_call(functools.partial(finish_kernel, group, tok, count, hops,...  13.6 us
    pallas_call x1, Pallas kernels, cross_attention(): pl.pallas_call(functools.partial(cross_kernel, group, tok, behind, part,...  13.2 us
    pallas_call x1, Pallas kernels, own_attention(): pl.pallas_call(functools.partial(own_kernel, group, tok, part), out_shape...  12.9 us
  transfers between devices with their start and end apart: 32, of which 11 were waited for; matrix products, arithmetic and copies ran while one was open for 4% of the time, Pallas kernels for 9%

profile of v3, /device:TPU:13, one launch (start us, length us, event | category | flops | bytes accessed | tf_op | source)
XLA Modules:
  0.0 308.7 jit_solution(10200853705444400523)
XLA Ops:
  9.2 20.7 %collective-permute-done.8.refs_1_.refs_5_.refs_13_ = bf16[2,512,512]{2,1,0:T(8,128)(2,1)S(1)} collective-permute-done((bf16[2,512,512]{2,1,0:T(8,128)(2,1)S(1)}, bf16[2,512,512]{2,1,0:T(8,128)(2,1)S(1)}, u32[]{:S(2)}, u32[]{:S(2)}) %collective-permute-start.8) | collective-permute-done | bytes 1048608 | tf_op jit(solution)/shard_map/ppermute | solution.py:80
  31.5 2.3 split_heads.3
  35.3 17.0 %collective-permute-done.7.refs_1_.refs_7_.refs_15_ = bf16[2,512,512]{2,1,0:T(8,128)(2,1)S(1)} collective-permute-done((bf16[2,512,512]{2,1,0:T(8,128)(2,1)S(1)}, bf16[2,512,512]{2,1,0:T(8,128)(2,1)S(1)}, u32[]{:S(2)}, u32[]{:S(2)}) %collective-permute-start.7) | collective-permute-done | bytes 1048608 | tf_op jit(solution)/shard_map/ppermute | solution.py:80
  52.4 2.2 collective-permute-start.22
  55.5 2.1 collective-permute-start.25
  57.6 6.0 %constant_dynamic-slice_fusion.3 = bf16[512,1,3,512]{3,1,2,0:T(2,128)(2,1)S(1)} fusion(bf16[512,4,3,512]{3,1,2,0:T(4,128)(2,1)} %param.11, s32[]{:T(128)S(6)} %select_n.92), kind=kLoop, calls=%fused_computation.25 | loop fusion | bytes 3145732 | tf_op jit(solution)/shard_map/jit(dynamic_index_in_dim)/dynamic_slice | solution.py:647
  66.3 8.6 %collective-permute-done.22.refs_3_.refs_13_ = bf16[1,512,512]{2,1,0:T(8,128)(2,1)} collective-permute-done((bf16[1,512,512]{2,1,0:T(8,128)(2,1)}, bf16[1,512,512]{2,1,0:T(8,128)(2,1)}, u32[]{:S(2)}, u32[]{:S(2)}) %collective-permute-start.22) | collective-permute-done | bytes 524320 | tf_op jit(solution)/shard_map/ppermute | solution.py:80
  75.0 2.1 collective-permute-start.26
  77.9 1.9 collective-permute-start.27
  79.9 2.1 collective-permute-start.28
  82.0 6.3 %weight_sums.2.refs_2_ = f32[3,512,512]{2,1,0:T(8,128)S(1)} custom-call(s32[5]{0:T(128)S(1)} %stack.15.info_ref, bf16[3,512,512]{2,1,0:T(8,128)(2,1)S(1)} %bitcast.41, bf16[2,512,512]{2,1,0:T(8,128)(2,1)S(1)} %get-tuple-element.23.refs_0_.refs_4_.refs_12_, bf16[2,512,512]{2,1,0:T(8,128)(2,1)S(1)} %collective-permute-done.8.refs_1_.refs_5_.refs_13_), custom_call_target="tpu_custom_call" | custom-call | flops 3221225472 | bytes 5242880 | tf_op jit(solution)/shard_map/weight_sums/pallas_call | solution.py:145
  88.3 6.4 %weight_sums.3 = (f32[3,512,512]{2,1,0:T(8,128)S(1)}, bf16[512,512]{1,0:T(8,128)(2,1)S(1)}, bf16[512,512]{1,0:T(8,128)(2,1)S(1)}, bf16[512,512]{1,0:T(8,128)(2,1)S(1)}) custom-call(s32[5]{0:T(128)S(1)} %stack.15.info_ref, bf16[3,512,512]{2,1,0:T(8,128)(2,1)S(1)} %bitcast.42, bf16[2,512,512]{2,1,0:T(8,128)(2,1)S(1)} %copy-done.23, ...), custom_call_target="tpu_custom_call" | custom-call | flops 3221225472 | bytes 5242880 | tf_op jit(solution)/shard_map/weight_sums/pallas_call | solution.py:145
  98.7 9.0 %collective-permute-done.11.refs_16_.refs_1_ = bf16[512,512]{1,0:T(8,128)(2,1)S(1)} collective-permute-done((bf16[512,512]{1,0:T(8,128)(2,1)S(1)}, bf16[512,512]{1,0:T(8,128)(2,1)S(1)}, u32[]{:S(2)}, u32[]{:S(2)}) %collective-permute-start.11) | collective-permute-done | bytes 524320 | tf_op jit(solution)/shard_map/ppermute | solution.py:578
  107.8 11.2 %collective-permute-done.12.refs_17_.refs_2_ = bf16[512,512]{1,0:T(8,128)(2,1)S(1)} collective-permute-done((bf16[512,512]{1,0:T(8,128)(2,1)S(1)}, bf16[512,512]{1,0:T(8,128)(2,1)S(1)}, u32[]{:S(2)}, u32[]{:S(2)}) %collective-permute-start.12) | collective-permute-done | bytes 524320 | tf_op jit(solution)/shard_map/ppermute | solution.py:578
  119.0 11.2 %collective-permute-done.13.refs_18_.refs_3_ = bf16[512,512]{1,0:T(8,128)(2,1)S(1)} collective-permute-done((bf16[512,512]{1,0:T(8,128)(2,1)S(1)}, bf16[512,512]{1,0:T(8,128)(2,1)S(1)}, u32[]{:S(2)}, u32[]{:S(2)}) %collective-permute-start.13) | collective-permute-done | bytes 524320 | tf_op jit(solution)/shard_map/ppermute | solution.py:578
  130.3 13.2 %cross_attention.1 = (bf16[4,512,512]{2,1,0:T(8,128)(2,1)}, f32[4,8,512]{2,1,0:T(8,128)S(1)}) custom-call(s32[5]{0:T(128)S(1)} %stack.15.info_ref, bf16[1,512,512]{2,1,0:T(8,128)(2,1)S(1)} %copy-done.17, bf16[1,512,512]{2,1,0:T(8,128)(2,1)} %collective-permute-done.20.refs_1_.refs_11_, bf16[1,512,512]{2,1,0:T(8,128)(2,1)} %collective-permute-done.21.refs_2_.refs_12_, ...), custom_call_target="tpu_custom_call" | custom-call | flops 4294967296 | bytes 8388608 | tf_op jit(solution)/shard_map/cross_attention/pallas_call | solution.py:383
  143.5 1.9 collective-permute-start.29
  147.0 2.1 collective-permute-start.14
  149.1 2.1 collective-permute-start.15
  151.2 2.1 collective-permute-start.16
  153.5 49.0 %collective-permute-done = s32[1,4,32]{2,1,0:T(4,128)S(1)} collective-permute-done((s32[1,4,32]{2,1,0:T(4,128)S(1)}, s32[1,4,32]{2,1,0:T(4,128)S(1)}, u32[]{:S(2)}, u32[]{:S(2)}) %collective-permute-start) | collective-permute-done | bytes 544 | tf_op jit(solution)/shard_map/ppermute | solution.py:601
  202.6 3.1 %collective-permute-start.2 = (s32[1,4,32]{2,1,0:T(4,128)S(1)}, s32[1,4,32]{2,1,0:T(4,128)S(1)}, u32[]{:S(2)}, u32[]{:S(2)}) collective-permute-start(s32[1,4,32]{2,1,0:T(4,128)S(1)} %get-tuple-element.43), channel_id=1, source_target_pairs={{0,24},{2,26},{4,28},{6,30},{8,0},{10,2},{12,4},{14,6},{16,8},{18,... | collective-permute-start | bytes 1544 | tf_op jit(solution)/shard_map/ppermute | solution.py:601
  205.7 3.0 fusion.1
  210.8 2.1 collective-permute-start.3
  216.5 2.1 collective-permute-start.5
  220.3 5.0 %collective-permute-start.30 = (f32[4,8,512]{2,1,0:T(8,128)S(1)}, f32[4,8,512]{2,1,0:T(8,128)S(1)}, u32[]{:S(2)}, u32[]{:S(2)}) collective-permute-start(f32[4,8,512]{2,1,0:T(8,128)S(1)} %get-tuple-element.36.refs_17_), channel_id=1, source_target_pairs={{1,9},{3,11},{5,13},{7,15},{9,17},{11,19},{13,21},{15,23},{17,25},... | collective-permute-start | bytes 196616 | tf_op jit(solution)/shard_map/ppermute | solution.py:632
  233.6 12.9 %own_attention.1 = (bf16[4,512,512]{2,1,0:T(8,128)(2,1)S(1)}, f32[4,8,512]{2,1,0:T(8,128)S(1)}) custom-call(s32[5]{0:T(128)S(1)} %stack.15.info_ref, bf16[1,512,512]{2,1,0:T(8,128)(2,1)S(1)} %copy-done.18, bf16[1,512,512]{2,1,0:T(8,128)(2,1)} %collective-permute-done.20.refs_1_.refs_11_, bf16[1,512,512]{2,1,0:T(8,128)(2,1)} %collective-permute-done.21.refs_2_.refs_12_, ...), custom_call_target="tpu_custom_call" | custom-call | flops 4294967296 | bytes 8388608 | tf_op jit(solution)/shard_map/own_attention/pallas_call | solution.py:288
  246.7 13.6 %finish_rows.1 = bf16[16,4,32,512]{3,2,1,0:T(8,128)(2,1)S(1)} custom-call(s32[5]{0:T(128)S(1)} %stack.15.info_ref, f32[1]{0:T(128)} %dynamic_slice.20.rate_ref, bf16[3,512,512]{2,1,0:T(8,128)(2,1)S(1)} %bitcast.43, f32[4,8,512]{2,1,0:T(8,128)S(1)} %broadcast_in_dim.35.place_ref, f32[3,512,512]{2,1,0:T(8,128)} %copy-done, bf16[512,512]{1,0:T(8,128)(2,1)S(1)} %copy-done.5, ...), custom_call_target="tpu_custom_call" | custom-call | flops 4294967296 | bytes 11534336 | tf_op jit(solution)/shard_map/finish_rows/pallas_call | solution.py:517
  261.6 4.9 %all-to-all-start = ((bf16[16,4,32,512]{3,2,1,0:T(8,128)(2,1)}), bf16[16,4,32,512]{3,2,1,0:T(8,128)(2,1)S(1)}, u32[]{:S(2)}, u32[]{:S(2)}) async-start(bf16[16,4,32,512]{3,2,1,0:T(8,128)(2,1)} %copy-done.1), calls=%async_computation | async-start | bytes 4194304 | tf_op jit(solution)/shard_map/all_to_all | solution.py:662
  266.5 36.5 %all-to-all-done = bf16[16,4,32,512]{3,2,1,0:T(8,128)(2,1)S(1)} async-done(((bf16[16,4,32,512]{3,2,1,0:T(8,128)(2,1)}), bf16[16,4,32,512]{3,2,1,0:T(8,128)(2,1)S(1)}, u32[]{:S(2)}, u32[]{:S(2)}) %all-to-all-start) | async-done | bytes 2097184 | tf_op jit(solution)/shard_map/all_to_all | solution.py:662
  303.6 2.5 psum.7
  306.2 2.5 norm_rows.1
  (150 shorter events, 40.2 us)
Async XLA Ops:
  5.8 24.1 %collective-permute-start.8 = (bf16[2,512,512]{2,1,0:T(8,128)(2,1)S(1)}, bf16[2,512,512]{2,1,0:T(8,128)(2,1)S(1)}, u32[]{:S(2)}, u32[]{:S(2)}) collective-permute-start(bf16[2,512,512]{2,1,0:T(8,128)(2,1)S(1)} %get-tuple-element.24), channel_id=1, source_target_pairs={{0,2},{2,0},{4,6},{6,4},{8,10},{10,8},{12,14},{14,12},{16,18},{18,... | collective-permute-start | bytes 3145736 | tf_op jit(solution)/shard_map/ppermute | solution.py:80
  7.1 28.0 %collective-permute-start.6 = (bf16[2,512,512]{2,1,0:T(8,128)(2,1)S(1)}, bf16[2,512,512]{2,1,0:T(8,128)(2,1)S(1)}, u32[]{:S(2)}, u32[]{:S(2)}) collective-permute-start(bf16[2,512,512]{2,1,0:T(8,128)(2,1)S(1)} %get-tuple-element.21), channel_id=1, source_target_pairs={{0,4},{2,6},{4,0},{6,2},{8,12},{10,14},{12,8},{14,10},{16,20},{18,... | collective-permute-start | bytes 3145736 | tf_op jit(solution)/shard_map/ppermute | solution.py:80
  7.3 45.0 %collective-permute-start.7 = (bf16[2,512,512]{2,1,0:T(8,128)(2,1)S(1)}, bf16[2,512,512]{2,1,0:T(8,128)(2,1)S(1)}, u32[]{:S(2)}, u32[]{:S(2)}) collective-permute-start(bf16[2,512,512]{2,1,0:T(8,128)(2,1)S(1)} %get-tuple-element.22), channel_id=1, source_target_pairs={{0,6},{2,4},{4,2},{6,0},{8,14},{10,12},{12,10},{14,8},{16,22},{18,... | collective-permute-start | bytes 3145736 | tf_op jit(solution)/shard_map/ppermute | solution.py:80
  8.5 46.0 %collective-permute-start.9 = (bf16[2,512,512]{2,1,0:T(8,128)(2,1)S(1)}, bf16[2,512,512]{2,1,0:T(8,128)(2,1)S(1)}, u32[]{:S(2)}, u32[]{:S(2)}) collective-permute-start(bf16[2,512,512]{2,1,0:T(8,128)(2,1)S(1)} %get-tuple-element.23.refs_0_.refs_4_.refs_12_), channel_id=1, source_target_pairs={{0,8},{2,10},{4,12},{6,14},{8,16},{10,18},{12,20},{14,22},{16,24},... | collective-permute-start | bytes 3145736 | tf_op jit(solution)/shard_map/ppermute | solution.py:632
  29.9 50.0 %collective-permute-start.10 = (bf16[2,512,512]{2,1,0:T(8,128)(2,1)S(1)}, bf16[2,512,512]{2,1,0:T(8,128)(2,1)}, u32[]{:S(2)}, u32[]{:S(2)}) collective-permute-start(bf16[2,512,512]{2,1,0:T(8,128)(2,1)S(1)} %collective-permute-done.8.refs_1_.refs_5_.refs_13_), channel_id=1, source_target_pairs={{0,8},{2,10},{4,12},{6,14},{8,16},{10,18},{12,20},{14,22},{16,24},... | collective-permute-start | bytes 3145736 | tf_op jit(solution)/shard_map/ppermute | solution.py:632
  33.8 30.3 %collective-permute-start.20 = (bf16[1,512,512]{2,1,0:T(8,128)(2,1)}, bf16[1,512,512]{2,1,0:T(8,128)(2,1)}, u32[]{:S(2)}, u32[]{:S(2)}) collective-permute-start(bf16[1,512,512]{2,1,0:T(8,128)(2,1)} %get-tuple-element.30), channel_id=1, source_target_pairs={{0,2},{2,0},{4,6},{6,4},{8,10},{10,8},{12,14},{14,12},{16,18},{18,... | collective-permute-start | bytes 1572872 | tf_op jit(solution)/shard_map/ppermute | solution.py:80
  35.1 30.5 %collective-permute-start.21 = (bf16[1,512,512]{2,1,0:T(8,128)(2,1)}, bf16[1,512,512]{2,1,0:T(8,128)(2,1)}, u32[]{:S(2)}, u32[]{:S(2)}) collective-permute-start(bf16[1,512,512]{2,1,0:T(8,128)(2,1)} %get-tuple-element.31), channel_id=1, source_target_pairs={{0,4},{2,6},{4,0},{6,2},{8,12},{10,14},{12,8},{14,10},{16,20},{18,... | collective-permute-start | bytes 1572872 | tf_op jit(solution)/shard_map/ppermute | solution.py:80
  52.4 22.6 %collective-permute-start.22 = (bf16[1,512,512]{2,1,0:T(8,128)(2,1)}, bf16[1,512,512]{2,1,0:T(8,128)(2,1)}, u32[]{:S(2)}, u32[]{:S(2)}) collective-permute-start(bf16[1,512,512]{2,1,0:T(8,128)(2,1)} %get-tuple-element.32), channel_id=1, source_target_pairs={{0,6},{2,4},{4,2},{6,0},{8,14},{10,12},{12,10},{14,8},{16,22},{18,... | collective-permute-start | bytes 1572872 | tf_op jit(solution)/shard_map/ppermute | solution.py:80
  55.5 21.6 %collective-permute-start.25 = (bf16[1,512,512]{2,1,0:T(8,128)(2,1)S(1)}, bf16[1,512,512]{2,1,0:T(8,128)(2,1)S(1)}, u32[]{:S(2)}, u32[]{:S(2)}) collective-permute-start(bf16[1,512,512]{2,1,0:T(8,128)(2,1)S(1)} %get-tuple-element.29.refs_0_.refs_10_), channel_id=1, source_target_pairs={{9,1},{11,3},{13,5},{15,7},{17,9},{19,11},{21,13},{23,15},{25,17},... | collective-permute-start | bytes 1572872 | tf_op jit(solution)/shard_map/ppermute | solution.py:637
  64.8 33.9 %collective-permute-start.23 = (bf16[2,512,512]{2,1,0:T(8,128)(2,1)S(1)}, bf16[2,512,512]{2,1,0:T(8,128)(2,1)S(1)}, u32[]{:S(2)}, u32[]{:S(2)}) collective-permute-start(bf16[2,512,512]{2,1,0:T(8,128)(2,1)S(1)} %copy-done.23), channel_id=1, source_target_pairs={{0,8},{2,10},{4,12},{6,14},{8,16},{10,18},{12,20},{14,22},{16,24},... | collective-permute-start | bytes 3145736 | tf_op jit(solution)/shard_map/ppermute | solution.py:632
  65.6 33.1 %collective-permute-start.24 = (bf16[2,512,512]{2,1,0:T(8,128)(2,1)S(1)}, bf16[2,512,512]{2,1,0:T(8,128)(2,1)S(1)}, u32[]{:S(2)}, u32[]{:S(2)}) collective-permute-start(bf16[2,512,512]{2,1,0:T(8,128)(2,1)S(1)} %copy-done.26), channel_id=1, source_target_pairs={{0,8},{2,10},{4,12},{6,14},{8,16},{10,18},{12,20},{14,22},{16,24},... | collective-permute-start | bytes 3145736 | tf_op jit(solution)/shard_map/ppermute | solution.py:632
  75.0 19.8 %collective-permute-start.26 = (bf16[1,512,512]{2,1,0:T(8,128)(2,1)}, bf16[1,512,512]{2,1,0:T(8,128)(2,1)S(1)}, u32[]{:S(2)}, u32[]{:S(2)}) collective-permute-start(bf16[1,512,512]{2,1,0:T(8,128)(2,1)} %collective-permute-done.20.refs_1_.refs_11_), channel_id=1, source_target_pairs={{9,1},{11,3},{13,5},{15,7},{17,9},{19,11},{21,13},{23,15},{25,17},... | collective-permute-start | bytes 1572872 | tf_op jit(solution)/shard_map/ppermute | solution.py:637
  77.9 18.1 %collective-permute-start.27 = (bf16[1,512,512]{2,1,0:T(8,128)(2,1)}, bf16[1,512,512]{2,1,0:T(8,128)(2,1)S(1)}, u32[]{:S(2)}, u32[]{:S(2)}) collective-permute-start(bf16[1,512,512]{2,1,0:T(8,128)(2,1)} %collective-permute-done.21.refs_2_.refs_12_), channel_id=1, source_target_pairs={{9,1},{11,3},{13,5},{15,7},{17,9},{19,11},{21,13},{23,15},{25,17},... | collective-permute-start | bytes 1572872 | tf_op jit(solution)/shard_map/ppermute | solution.py:637
  79.9 17.5 %collective-permute-start.28 = (bf16[1,512,512]{2,1,0:T(8,128)(2,1)}, bf16[1,512,512]{2,1,0:T(8,128)(2,1)S(1)}, u32[]{:S(2)}, u32[]{:S(2)}) collective-permute-start(bf16[1,512,512]{2,1,0:T(8,128)(2,1)} %collective-permute-done.22.refs_3_.refs_13_), channel_id=1, source_target_pairs={{9,1},{11,3},{13,5},{15,7},{17,9},{19,11},{21,13},{23,15},{25,17},... | collective-permute-start | bytes 1572872 | tf_op jit(solution)/shard_map/ppermute | solution.py:637
  94.8 13.0 %collective-permute-start.11 = (bf16[512,512]{1,0:T(8,128)(2,1)S(1)}, bf16[512,512]{1,0:T(8,128)(2,1)S(1)}, u32[]{:S(2)}, u32[]{:S(2)}) collective-permute-start(bf16[512,512]{1,0:T(8,128)(2,1)S(1)} %get-tuple-element.26), channel_id=1, source_target_pairs={{0,8},{2,10},{4,12},{6,14},{1,9},{3,11},{5,13},{7,15}} | collective-permute-start | bytes 1572872 | tf_op jit(solution)/shard_map/ppermute | solution.py:578
  96.1 22.9 %collective-permute-start.12 = (bf16[512,512]{1,0:T(8,128)(2,1)S(1)}, bf16[512,512]{1,0:T(8,128)(2,1)S(1)}, u32[]{:S(2)}, u32[]{:S(2)}) collective-permute-start(bf16[512,512]{1,0:T(8,128)(2,1)S(1)} %get-tuple-element.27), channel_id=1, source_target_pairs={{0,8},{2,10},{4,12},{6,14},{1,9},{3,11},{5,13},{7,15}} | collective-permute-start | bytes 1572872 | tf_op jit(solution)/shard_map/ppermute | solution.py:578
  97.4 32.8 %collective-permute-start.13 = (bf16[512,512]{1,0:T(8,128)(2,1)S(1)}, bf16[512,512]{1,0:T(8,128)(2,1)S(1)}, u32[]{:S(2)}, u32[]{:S(2)}) collective-permute-start(bf16[512,512]{1,0:T(8,128)(2,1)S(1)} %get-tuple-element.28), channel_id=1, source_target_pairs={{0,8},{2,10},{4,12},{6,14},{1,9},{3,11},{5,13},{7,15}} | collective-permute-start | bytes 1572872 | tf_op jit(solution)/shard_map/ppermute | solution.py:578
  143.5 103.1 %collective-permute-start.29 = (bf16[4,512,512]{2,1,0:T(8,128)(2,1)}, bf16[4,512,512]{2,1,0:T(8,128)(2,1)}, u32[]{:S(2)}, u32[]{:S(2)}) collective-permute-start(bf16[4,512,512]{2,1,0:T(8,128)(2,1)} %get-tuple-element.35.refs_16_), channel_id=1, source_target_pairs={{1,9},{3,11},{5,13},{7,15},{9,17},{11,19},{13,21},{15,23},{17,25},... | collective-permute-start | bytes 6291464 | tf_op jit(solution)/shard_map/ppermute | solution.py:632
  147.0 55.5 %collective-permute-start.14 = (bf16[512,512]{1,0:T(8,128)(2,1)}, bf16[512,512]{1,0:T(8,128)(2,1)}, u32[]{:S(2)}, u32[]{:S(2)}) collective-permute-start(bf16[512,512]{1,0:T(8,128)(2,1)} %get-tuple-element.42), channel_id=1, source_target_pairs={{8,16},{10,18},{12,20},{14,22},{9,17},{11,19},{13,21},{15,23}} | collective-permute-start | bytes 1572872 | tf_op jit(solution)/shard_map/ppermute | solution.py:578
  149.1 56.6 %collective-permute-start.15 = (bf16[512,512]{1,0:T(8,128)(2,1)}, bf16[512,512]{1,0:T(8,128)(2,1)}, u32[]{:S(2)}, u32[]{:S(2)}) collective-permute-start(bf16[512,512]{1,0:T(8,128)(2,1)} %get-tuple-element.41), channel_id=1, source_target_pairs={{8,16},{10,18},{12,20},{14,22},{9,17},{11,19},{13,21},{15,23}} | collective-permute-start | bytes 1572872 | tf_op jit(solution)/shard_map/ppermute | solution.py:578
  151.2 54.5 %collective-permute-start.16 = (bf16[512,512]{1,0:T(8,128)(2,1)}, bf16[512,512]{1,0:T(8,128)(2,1)}, u32[]{:S(2)}, u32[]{:S(2)}) collective-permute-start(bf16[512,512]{1,0:T(8,128)(2,1)} %get-tuple-element.40), channel_id=1, source_target_pairs={{8,16},{10,18},{12,20},{14,22},{9,17},{11,19},{13,21},{15,23}} | collective-permute-start | bytes 1572872 | tf_op jit(solution)/shard_map/ppermute | solution.py:578
  153.4 49.1 %collective-permute-start = (s32[1,4,32]{2,1,0:T(4,128)S(1)}, s32[1,4,32]{2,1,0:T(4,128)S(1)}, u32[]{:S(2)}, u32[]{:S(2)}) collective-permute-start(s32[1,4,32]{2,1,0:T(4,128)S(1)} %get-tuple-element.45), channel_id=1, source_target_pairs={{0,8},{2,10},{4,12},{6,14},{8,16},{10,18},{12,20},{14,22},{16,24},... | collective-permute-start | bytes 1544 | tf_op jit(solution)/shard_map/ppermute | solution.py:601
  202.5 7.5 %collective-permute-start.1 = (s32[1,4,32]{2,1,0:T(4,128)S(1)}, s32[1,4,32]{2,1,0:T(4,128)S(1)}, u32[]{:S(2)}, u32[]{:S(2)}) collective-permute-start(s32[1,4,32]{2,1,0:T(4,128)S(1)} %get-tuple-element.44), channel_id=1, source_target_pairs={{0,16},{2,18},{4,20},{6,22},{8,24},{10,26},{12,28},{14,30},{16,0},... | collective-permute-start | bytes 1544 | tf_op jit(solution)/shard_map/ppermute | solution.py:601
  202.6 8.2 %collective-permute-start.2 = (s32[1,4,32]{2,1,0:T(4,128)S(1)}, s32[1,4,32]{2,1,0:T(4,128)S(1)}, u32[]{:S(2)}, u32[]{:S(2)}) collective-permute-start(s32[1,4,32]{2,1,0:T(4,128)S(1)} %get-tuple-element.43), channel_id=1, source_target_pairs={{0,24},{2,26},{4,28},{6,30},{8,0},{10,2},{12,4},{14,6},{16,8},{18,... | collective-permute-start | bytes 1544 | tf_op jit(solution)/shard_map/ppermute | solution.py:601
  208.6 37.9 %collective-permute-start.17 = (bf16[512,512]{1,0:T(8,128)(2,1)}, bf16[512,512]{1,0:T(8,128)(2,1)S(1)}, u32[]{:S(2)}, u32[]{:S(2)}) collective-permute-start(bf16[512,512]{1,0:T(8,128)(2,1)} %get-tuple-element.38), channel_id=1, source_target_pairs={{16,24},{18,26},{20,28},{22,30},{17,25},{19,27},{21,29},{23,31}} | collective-permute-start | bytes 1572872 | tf_op jit(solution)/shard_map/ppermute | solution.py:578
  209.3 37.3 %collective-permute-start.18 = (bf16[512,512]{1,0:T(8,128)(2,1)}, bf16[512,512]{1,0:T(8,128)(2,1)S(1)}, u32[]{:S(2)}, u32[]{:S(2)}) collective-permute-start(bf16[512,512]{1,0:T(8,128)(2,1)} %get-tuple-element.39), channel_id=1, source_target_pairs={{16,24},{18,26},{20,28},{22,30},{17,25},{19,27},{21,29},{23,31}} | collective-permute-start | bytes 1572872 | tf_op jit(solution)/shard_map/ppermute | solution.py:578
  210.0 36.6 %collective-permute-start.19 = (bf16[512,512]{1,0:T(8,128)(2,1)}, bf16[512,512]{1,0:T(8,128)(2,1)S(1)}, u32[]{:S(2)}, u32[]{:S(2)}) collective-permute-start(bf16[512,512]{1,0:T(8,128)(2,1)} %get-tuple-element.37), channel_id=1, source_target_pairs={{16,24},{18,26},{20,28},{22,30},{17,25},{19,27},{21,29},{23,31}} | collective-permute-start | bytes 1572872 | tf_op jit(solution)/shard_map/ppermute | solution.py:578
  210.8 3.2 %collective-permute-start.3 = (s32[4,4,32]{2,1,0:T(4,128)S(1)}, s32[4,4,32]{2,1,0:T(4,128)S(1)}, u32[]{:S(2)}, u32[]{:S(2)}) collective-permute-start(s32[4,4,32]{2,1,0:T(4,128)S(1)} %constant_dynamic-update-slice_fusion), channel_id=1, source_target_pairs={{0,2},{2,0},{4,6},{6,4},{8,10},{10,8},{12,14},{14,12},{16,18},{18,... | collective-permute-start | bytes 6152 | tf_op jit(solution)/shard_map/ppermute | solution.py:606
  214.0 2.6 collective-permute-start.4
  216.5 3.4 %collective-permute-start.5 = (s32[4,4,32]{2,1,0:T(4,128)S(1)}, s32[4,4,32]{2,1,0:T(4,128)S(1)}, u32[]{:S(2)}, u32[]{:S(2)}) collective-permute-start(s32[4,4,32]{2,1,0:T(4,128)S(1)} %constant_dynamic-update-slice_fusion), channel_id=1, source_target_pairs={{0,6},{2,4},{4,2},{6,0},{8,14},{10,12},{12,10},{14,8},{16,22},{18,... | collective-permute-start | bytes 6152 | tf_op jit(solution)/shard_map/ppermute | solution.py:606
  220.3 26.3 %collective-permute-start.30 = (f32[4,8,512]{2,1,0:T(8,128)S(1)}, f32[4,8,512]{2,1,0:T(8,128)S(1)}, u32[]{:S(2)}, u32[]{:S(2)}) collective-permute-start(f32[4,8,512]{2,1,0:T(8,128)S(1)} %get-tuple-element.36.refs_17_), channel_id=1, source_target_pairs={{1,9},{3,11},{5,13},{7,15},{9,17},{11,19},{13,21},{15,23},{17,25},... | collective-permute-start | bytes 196616 | tf_op jit(solution)/shard_map/ppermute | solution.py:632
  261.6 41.4 %all-to-all-start = ((bf16[16,4,32,512]{3,2,1,0:T(8,128)(2,1)}), bf16[16,4,32,512]{3,2,1,0:T(8,128)(2,1)S(1)}, u32[]{:S(2)}, u32[]{:S(2)}) async-start(bf16[16,4,32,512]{3,2,1,0:T(8,128)(2,1)} %copy-done.1), calls=%async_computation | async-start | bytes 4194304 | tf_op jit(solution)/shard_map/all_to_all | solution.py:662
  (39 other events, 838.7 us)

commit v4 on v3

--- a/solution.py
+++ b/solution.py
@@ -128,12 +128,17 @@
 
     lax.fori_loop(0, pieces, piece, 0)
     whole = last == group
-    outs = refs[len(refs) - 4 - (4 if whole else 1) : len(refs) - 4]
+    outs = refs[len(refs) - 4 - (5 if whole else 1) : len(refs) - 4]
     keep = pltpu.make_async_copy(acc, outs[0], acc_sem.at[1])
     keep.start()
-    for c, sent in enumerate(outs[1:]):
+    if whole:
+        onward = pltpu.make_async_copy(kvbuf, outs[1], acc_sem.at[0])
+        onward.start()
+    for c, sent in enumerate(outs[2:]):
         sent[...] = acc[c].astype(sent.dtype)
     keep.wait()
+    if whole:
+        onward.wait()
 
 
 def weight_sums(info, weights, pairs, first, last, carried=(), after=()):
@@ -141,13 +146,15 @@
     _, tok, width = pairs[0].shape
     rows, hidden, _ = weights.shape
     pieces = last - first
-    sent = rows if last == group else 0
+    whole = last == group
+    stacked = (pieces, 2, tok, width)
     return pl.pallas_call(
         functools.partial(grad_kernel, group, tok, first, last, len(carried)),
         out_shape=[jax.ShapeDtypeStruct(weights.shape, jnp.float32)]
-        + [jax.ShapeDtypeStruct((hidden, width), jnp.bfloat16)] * sent,
+        + [jax.ShapeDtypeStruct(stacked, jnp.bfloat16)] * whole
+        + [jax.ShapeDtypeStruct((hidden, width), jnp.bfloat16)] * (rows * whole),
         in_specs=[SMEM, VMEM] + [ANY] * (pieces + len(carried) + len(after)),
-        out_specs=[ANY] + [VMEM] * sent,
+        out_specs=[ANY] + [ANY] * whole + [VMEM] * (rows * whole),
         scratch_shapes=[
             pltpu.VMEM((pieces, 2, tok, width), jnp.bfloat16),
             pltpu.VMEM(weights.shape, jnp.float32),
@@ -319,10 +326,13 @@
     return pltpu.make_async_copy(first, into, sem)
 
 
-def cross_kernel(group, tok, behind, part, lending, info_ref, *refs):
+def cross_kernel(group, tok, behind, part, lending, whole, info_ref, *refs):
     pieces = behind * group
     q_any, refs = refs[:group], refs[group:]
-    kv_any, refs = refs[:pieces], refs[pieces:]
+    kv_any = []
+    for size in whole:
+        kv_any.extend(refs[0].at[n] if size > 1 else refs[0] for n in range(size))
+        refs = refs[1:]
     lent_q, lent_kv = [None] * group, [None] * pieces
     if lending:
         lent_q, lent_kv, refs = refs[:group], refs[group : 2 * group], refs[2 * group :]
@@ -378,19 +388,20 @@
 def cross_attention(info, queries, earlier, lent, after=()):
     group = len(queries)
     _, tok, width = queries[0].shape
-    behind = len(earlier) // group
+    whole = [array.shape[0] if array.ndim == 4 else 1 for array in earlier]
+    behind = sum(whole) // group
     part = min(256, tok)
     return pl.pallas_call(
-        functools.partial(cross_kernel, group, tok, behind, part, len(lent)),
+        functools.partial(cross_kernel, group, tok, behind, part, len(lent), whole),
         out_shape=soft_shapes(group, tok, width),
         in_specs=[SMEM] + [ANY] * (group + len(earlier) + len(lent) + len(after)),
         out_specs=[VMEM] * 2,
         scratch_shapes=soft_scratch(tok, width)
         + [
             pltpu.VMEM((group, tok, width), jnp.bfloat16),
-            pltpu.VMEM((len(earlier), 2, tok, width), jnp.bfloat16),
+            pltpu.VMEM((behind * group, 2, tok, width), jnp.bfloat16),
             pltpu.SemaphoreType.DMA((group,)),
-            pltpu.SemaphoreType.DMA((len(earlier),)),
+            pltpu.SemaphoreType.DMA((behind * group,)),
         ],
         compiler_params=params(28),
         cost_estimate=soft_cost(group, tok, width),
@@ -562,21 +573,42 @@
     )(came, scale, gain)
 
 
+def add_kernel(c, own_any, came_ref, out_ref, buf, sem):
+    copy = pltpu.make_async_copy(own_any.at[c], buf, sem.at[0])
+    copy.start()
+    copy.wait()
+    out_ref[...] = (buf[...] + came_ref[...].astype(jnp.float32)).astype(out_ref.dtype)
+
+
+def hop_add(own, came, c):
+    return pl.pallas_call(
+        functools.partial(add_kernel, c),
+        out_shape=jax.ShapeDtypeStruct(came.shape, came.dtype),
+        in_specs=[ANY, VMEM],
+        out_specs=VMEM,
+        scratch_shapes=[pltpu.VMEM(came.shape, jnp.float32), pltpu.SemaphoreType.DMA((1,))],
+        compiler_params=params(8),
+        cost_estimate=pl.CostEstimate(
+            flops=came.size, bytes_accessed=8 * came.size, transcendentals=0
+        ),
+        name="hop_add",
+    )(own, came)
+
+
 def forward_sums(own, sent, group, count):
     planes = count // group
     if planes > 8:
         groups = [[plane * group + m for plane in range(planes)] for m in range(group)]
         whole = lax.psum(own.astype(jnp.bfloat16), "seq", axis_index_groups=groups)
-        return whole.astype(jnp.float32), []
-    came = []
+        return whole.astype(jnp.float32), [], []
+    came, added = [], []
     for hop in range(1, planes):
         pairs = [((hop - 1) * group + m, hop * group + m) for m in range(group)]
         if hop > 1:
-            sent = [
-                (own[c] + came[-3 + c].astype(jnp.float32)).astype(jnp.bfloat16) for c in range(3)
-            ]
+            sent = [hop_add(own, came[-3 + c], c) for c in range(3)]
+            added.extend(sent)
         came.extend([lax.ppermute(sent[c], "seq", pairs) for c in range(3)])
-    return own, came
+    return own, came, added
 
 
 def as_places(asked, group, tok):
@@ -638,23 +670,29 @@
 
     mine = split_heads(info, [token_keys, token_values])
     pairs = trade(mine, count)
-    earlier = []
-    for back in range(behind, 0, -1):
-        earlier.extend([across(pair, back * group, 0) for pair in pairs])
-    asked = trade(split_heads(info, [queries], pairs[1:2]), count)
-    lent = [back_across(piece, 1) for piece in asked] + pairs if lending else []
-
     weights = lax.dynamic_index_in_dim(fast_weights, member, 1, keepdims=False)
     weights = jnp.transpose(weights, (1, 0, 2))
     rate = lax.dynamic_slice_in_dim(learn_rate, member, 1)
+    places = asked_places(slot_order, plane, member, group, count)
+
     half = group // 2
-    carried = weight_sums(info, weights, pairs, 0, half) if half else []
-    own, *sent = weight_sums(info, weights, pairs, half, group, carried, earlier[:half])
-    own, came = forward_sums(own, sent, group, count)
-    own_part = own_attention(info, asked, pairs, earlier[half:])
-    cross_part = cross_attention(info, asked, earlier, lent, came[:3])
+    carried, near = [], []
+    if half:
+        carried = weight_sums(info, weights, pairs, 0, half)
+        near = [[across(pair, back * group, 0) for pair in pairs[:half]] for back in range(behind, 0, -1)]
+    waits = [array for arrays in near for array in arrays] + [places]
+    own, onward, *sent = weight_sums(info, weights, pairs, half, group, carried, waits)
+    onward = onward if group - half > 1 else onward[0]
+    earlier = []
+    for n, back in enumerate(range(behind, 0, -1)):
+        earlier.extend((near[n] if half else []) + [across(onward, back * group, 0)])
+    asked = trade(split_heads(info, [queries], [own]), count)
+    lent = [back_across(piece, 1) for piece in asked] + pairs if lending else []
+
+    own, came, added = forward_sums(own, sent, group, count)
+    own_part = own_attention(info, asked, pairs, added[:1])
+    cross_part = cross_attention(info, asked, earlier, lent, list(own_part[:1]) + added[1:4])
     lent_part = [across(value, group, 1) for value in cross_part] if lending else []
-    places = asked_places(slot_order, plane, member, group, count)
     leaving = finish_rows(
         info, rate, weights, places, own, came, asked, own_part, cross_part, lent_part, count
     )

time: 310 us -> 295 us (0.952)
  waiting for transfers between devices: 166 us -> 138 us
  starting transfers between devices: 51.3 us -> 70.9 us
  local copies, waits for them, and re-layouts: 24.1 us -> 16.6 us
  other arithmetic: 4.98 us -> 0.52 us
  blocking collectives: 2.47 us -> 6.36 us
    ppermute x3, waiting for transfers between devices: 49 us -> 4.16 us  [asked_places(): part = lax.ppermute(part, 'seq', pairs)]
    ppermute x6, waiting for transfers between devices: 46.3 us -> 23.1 us  [trade(): lax.ppermute(piece, 'seq', swap_pairs(count, d))]
    ppermute x9, waiting for transfers between devices: 31.5 us -> 51.9 us  [forward_sums(): came.extend([lax.ppermute(sent[c], 'seq', pairs) for c in range(3)])]
    all_to_all x1, starting transfers between devices: 4.89 us -> 24.4 us  [per_device(): lax.all_to_all(leaving, 'seq', split_axis=0, concat_axis=0, tiled=True)]
    unnamed x78 -> x16, local copies, waits for them, and re-layouts: 15.5 us -> 4.52 us
    ppermute x3, waiting for transfers between devices: 2.63 us -> 12.6 us  [asked_places(): part = lax.ppermute(column, 'seq', swap_pairs(count, d)) if d else column]
    all_to_all x1, waiting for transfers between devices: 36.5 us -> 45.3 us  [per_device(): lax.all_to_all(leaving, 'seq', split_axis=0, concat_axis=0, tiled=True)]
    convert_element_type x2 -> x0, other arithmetic: 4.45 us -> none  [forward_sums(): (own[c] + came[-3 + c].astype(jnp.float32)).astype(jnp.bfloat16)]
  transfers between devices with their start and end apart: 32 -> 31, of which waited for: 11 -> 14; matrix products, arithmetic and copies ran while one was open for 4% -> 4% of each run, Pallas kernels for 9% -> 8%
where the time goes in v4:
time: 295 us; the launch traced here: 294 us
  waiting for transfers between devices  138 us (47%)
  starting transfers between devices  70.9 us (24%)
  Pallas kernels  61.2 us (21%)
  local copies, waits for them, and re-layouts  16.6 us (6%)
  blocking collectives  6.36 us (2%)
    ppermute x9, waiting for transfers between devices, forward_sums(): came.extend([lax.ppermute(sent[c], 'seq', pairs) for c in range(3)])  51.9 us
    all_to_all x1, waiting for transfers between devices, per_device(): lax.all_to_all(leaving, 'seq', split_axis=0, concat_axis=0, tiled=True)  45.3 us
    all_to_all x1, starting transfers between devices, per_device(): lax.all_to_all(leaving, 'seq', split_axis=0, concat_axis=0, tiled=True)  24.4 us
    ppermute x6, waiting for transfers between devices, trade(): lax.ppermute(piece, 'seq', swap_pairs(count, d))  23.1 us
    pallas_call x2, Pallas kernels, weight_sums(): pl.pallas_call(functools.partial(grad_kernel, group, tok, first, last, le...  15 us
    pallas_call x1, Pallas kernels, own_attention(): pl.pallas_call(functools.partial(own_kernel, group, tok, part), out_shape...  13.5 us
    pallas_call x1, Pallas kernels, cross_attention(): pl.pallas_call(functools.partial(cross_kernel, group, tok, behind, part,...  13.4 us
    ppermute x5, starting transfers between devices, across(): return lax.ppermute(value, ('seq', 'head'), both)  12.9 us
  transfers between devices with their start and end apart: 31, of which 14 were waited for; matrix products, arithmetic and copies ran while one was open for 4% of the time, Pallas kernels for 8%

profile of v4, /device:TPU:13, one launch (start us, length us, event | category | flops | bytes accessed | tf_op | source)
XLA Modules:
  0.0 293.8 jit_solution(2723361500521199276)
XLA Ops:
  3.9 3.1 %split_heads.2 = (bf16[2,512,512]{2,1,0:T(8,128)(2,1)S(1)}, bf16[2,512,512]{2,1,0:T(8,128)(2,1)S(1)}, bf16[2,512,512]{2,1,0:T(8,128)(2,1)}, bf16[2,512,512]{2,1,0:T(8,128)(2,1)}) custom-call(s32[5]{0:T(128)S(1)} %stack.15.info_ref, bf16[512,4,512]{2,1,0:T(4,128)(2,1)S(1)} %copy-done.2, bf16[512,4,512]{2,1,0:T(4,128)(2,1)S(1)} %copy-done.3), custom_call_target="tpu_custom_call" | custom-call | bytes 8388608 | tf_op jit(solution)/shard_map/split_heads/pallas_call | solution.py:61
  9.7 1.6 collective-permute-start.9
  11.4 19.8 %collective-permute-done.8.refs_1_.refs_5_.refs_12_ = bf16[2,512,512]{2,1,0:T(8,128)(2,1)} collective-permute-done((bf16[2,512,512]{2,1,0:T(8,128)(2,1)S(1)}, bf16[2,512,512]{2,1,0:T(8,128)(2,1)}, u32[]{:S(2)}, u32[]{:S(2)}) %collective-permute-start.8) | collective-permute-done | bytes 1048608 | tf_op jit(solution)/shard_map/ppermute | solution.py:80
  31.2 1.7 collective-permute-start.10
  35.8 2.3 collective-permute-start.1
  39.5 1.6 collective-permute-start.2
  43.6 10.3 %collective-permute-done.3 = s32[4,4,32]{2,1,0:T(4,128)S(1)} collective-permute-done((s32[4,4,32]{2,1,0:T(4,128)S(1)}, s32[4,4,32]{2,1,0:T(4,128)S(1)}, u32[]{:S(2)}, u32[]{:S(2)}) %collective-permute-start.3) | collective-permute-done | bytes 2080 | tf_op jit(solution)/shard_map/ppermute | solution.py:638
  54.1 2.3 collective-permute-done.4
  57.5 7.7 %constant_dynamic-slice_fusion.3 = bf16[512,1,3,512]{3,1,2,0:T(2,128)(2,1)} fusion(bf16[512,4,3,512]{3,1,2,0:T(4,128)(2,1)} %param.11, s32[]{:T(128)S(6)} %select_n.92), kind=kLoop, calls=%fused_computation.13 | loop fusion | bytes 3145732 | tf_op jit(solution)/shard_map/jit(dynamic_index_in_dim)/dynamic_slice | solution.py:673
  65.2 2.3 copy.28
  68.0 7.2 %weight_sums.2.refs_2_ = f32[3,512,512]{2,1,0:T(8,128)S(1)} custom-call(s32[5]{0:T(128)S(1)} %stack.15.info_ref, bf16[3,512,512]{2,1,0:T(8,128)(2,1)S(1)} %bitcast.20, bf16[2,512,512]{2,1,0:T(8,128)(2,1)S(1)} %get-tuple-element.24.refs_0_.refs_4_.refs_11_, bf16[2,512,512]{2,1,0:T(8,128)(2,1)} %collective-permute-done.8.refs_1_.refs_5_.refs_12_), custom_call_target="tpu_custom_call" | custom-call | flops 3221225472 | bytes 5242880 | tf_op jit(solution)/shard_map/weight_sums/pallas_call | solution.py:151
  75.3 7.8 %weight_sums.3 = (f32[3,512,512]{2,1,0:T(8,128)S(1)}, bf16[2,2,512,512]{3,2,1,0:T(8,128)(2,1)S(1)}, bf16[512,512]{1,0:T(8,128)(2,1)S(1)}, bf16[512,512]{1,0:T(8,128)(2,1)S(1)}, bf16[512,512]{1,0:T(8,128)(2,1)S(1)}) custom-call(s32[5]{0:T(128)S(1)} %stack.15.info_ref, bf16[3,512,512]{2,1,0:T(8,128)(2,1)S(1)} %bitcast.21, ...), custom_call_target="tpu_custom_call" | custom-call | flops 3221225472 | bytes 5242880 | tf_op jit(solution)/shard_map/weight_sums/pallas_call | solution.py:151
  89.4 4.5 %collective-permute-done.11.came_ref.refs_1_ = bf16[512,512]{1,0:T(8,128)(2,1)S(1)} collective-permute-done((bf16[512,512]{1,0:T(8,128)(2,1)S(1)}, bf16[512,512]{1,0:T(8,128)(2,1)S(1)}, u32[]{:S(2)}, u32[]{:S(2)}) %collective-permute-start.11) | collective-permute-done | bytes 524320 | tf_op jit(solution)/shard_map/ppermute | solution.py:610
  98.0 3.3 %collective-permute-done.22.refs_3_.refs_13_ = bf16[1,512,512]{2,1,0:T(8,128)(2,1)S(1)} collective-permute-done((bf16[1,512,512]{2,1,0:T(8,128)(2,1)S(1)}, bf16[1,512,512]{2,1,0:T(8,128)(2,1)S(1)}, u32[]{:S(2)}, u32[]{:S(2)}) %collective-permute-start.22) | collective-permute-done | bytes 524320 | tf_op jit(solution)/shard_map/ppermute | solution.py:80
  101.3 4.0 %collective-permute-start.24 = (bf16[1,512,512]{2,1,0:T(8,128)(2,1)S(1)}, bf16[1,512,512]{2,1,0:T(8,128)(2,1)S(1)}, u32[]{:S(2)}, u32[]{:S(2)}) collective-permute-start(bf16[1,512,512]{2,1,0:T(8,128)(2,1)S(1)} %get-tuple-element.30.refs_0_.refs_10_), channel_id=1, source_target_pairs={{9,1},{11,3},{13,5},{15,7},{17,9},{19,11},{21,13},{23,15},{25,17},... | collective-permute-start | bytes 1572872 | tf_op jit(solution)/shard_map/ppermute | solution.py:669
  105.3 4.4 %collective-permute-done.13.came_ref.refs_3_ = bf16[512,512]{1,0:T(8,128)(2,1)S(1)} collective-permute-done((bf16[512,512]{1,0:T(8,128)(2,1)S(1)}, bf16[512,512]{1,0:T(8,128)(2,1)S(1)}, u32[]{:S(2)}, u32[]{:S(2)}) %collective-permute-start.13) | collective-permute-done | bytes 524320 | tf_op jit(solution)/shard_map/ppermute | solution.py:610
  109.7 1.9 collective-permute-start.25
  111.6 9.3 %collective-permute-done.12.came_ref.refs_2_ = bf16[512,512]{1,0:T(8,128)(2,1)S(1)} collective-permute-done((bf16[512,512]{1,0:T(8,128)(2,1)S(1)}, bf16[512,512]{1,0:T(8,128)(2,1)S(1)}, u32[]{:S(2)}, u32[]{:S(2)}) %collective-permute-start.12) | collective-permute-done | bytes 524320 | tf_op jit(solution)/shard_map/ppermute | solution.py:610
  120.9 1.9 collective-permute-start.26
  122.8 1.9 collective-permute-start.27
  124.8 13.5 %own_attention.1 = (bf16[4,512,512]{2,1,0:T(8,128)(2,1)S(1)}, f32[4,8,512]{2,1,0:T(8,128)S(1)}) custom-call(s32[5]{0:T(128)S(1)} %stack.15.info_ref, bf16[1,512,512]{2,1,0:T(8,128)(2,1)S(1)} %get-tuple-element.30.refs_0_.refs_10_, bf16[1,512,512]{2,1,0:T(8,128)(2,1)S(1)} %collective-permute-done.20.refs_1_.refs_11_, ...), custom_call_target="tpu_custom_call" | custom-call | flops 4294967296 | bytes 8388608 | tf_op jit(solution)/shard_map/own_attention/pallas_call | solution.py:295
  138.9 13.4 %cross_attention.1 = (bf16[4,512,512]{2,1,0:T(8,128)(2,1)S(1)}, f32[4,8,512]{2,1,0:T(8,128)S(1)}) custom-call(s32[5]{0:T(128)S(1)} %stack.15.info_ref, bf16[1,512,512]{2,1,0:T(8,128)(2,1)S(1)} %get-tuple-element.30.refs_0_.refs_10_, bf16[1,512,512]{2,1,0:T(8,128)(2,1)S(1)} %collective-permute-done.20.refs_1_.refs_11_, ...), custom_call_target="tpu_custom_call" | custom-call | flops 4294967296 | bytes 8388608 | tf_op jit(solution)/shard_map/cross_attention/pallas_call | solution.py:394
  152.3 3.4 %collective-permute-start.28 = (bf16[4,512,512]{2,1,0:T(8,128)(2,1)S(1)}, bf16[4,512,512]{2,1,0:T(8,128)(2,1)S(1)}, u32[]{:S(2)}, u32[]{:S(2)}) collective-permute-start(bf16[4,512,512]{2,1,0:T(8,128)(2,1)S(1)} %get-tuple-element.37.refs_16_), channel_id=1, source_target_pairs={{1,9},{3,11},{5,13},{7,15},{9,17},{11,19},{13,21},{15,23},{17,25},... | collective-permute-start | bytes 6291464 | tf_op jit(solution)/shard_map/ppermute | solution.py:664
  155.7 1.9 collective-permute-start.16
  159.0 25.3 %collective-permute-done.16.came_ref.refs_6_ = bf16[512,512]{1,0:T(8,128)(2,1)S(1)} collective-permute-done((bf16[512,512]{1,0:T(8,128)(2,1)S(1)}, bf16[512,512]{1,0:T(8,128)(2,1)S(1)}, u32[]{:S(2)}, u32[]{:S(2)}) %collective-permute-start.16) | collective-permute-done | bytes 524320 | tf_op jit(solution)/shard_map/ppermute | solution.py:610
  185.2 8.4 %collective-permute-done.15.came_ref.refs_5_ = bf16[512,512]{1,0:T(8,128)(2,1)S(1)} collective-permute-done((bf16[512,512]{1,0:T(8,128)(2,1)S(1)}, bf16[512,512]{1,0:T(8,128)(2,1)S(1)}, u32[]{:S(2)}, u32[]{:S(2)}) %collective-permute-start.15) | collective-permute-done | bytes 524320 | tf_op jit(solution)/shard_map/ppermute | solution.py:610
  195.2 5.4 %collective-permute-start.29 = (f32[4,8,512]{2,1,0:T(8,128)S(1)}, f32[4,8,512]{2,1,0:T(8,128)S(1)}, u32[]{:S(2)}, u32[]{:S(2)}) collective-permute-start(f32[4,8,512]{2,1,0:T(8,128)S(1)} %get-tuple-element.38.refs_17_), channel_id=1, source_target_pairs={{1,9},{3,11},{5,13},{7,15},{9,17},{11,19},{13,21},{15,23},{17,25},... | collective-permute-start | bytes 196616 | tf_op jit(solution)/shard_map/ppermute | solution.py:664
  201.9 11.3 %finish_rows.1 = bf16[16,4,32,512]{3,2,1,0:T(8,128)(2,1)S(1)} custom-call(s32[5]{0:T(128)S(1)} %stack.15.info_ref, f32[1]{0:T(128)} %dynamic_slice.20.rate_ref, bf16[3,512,512]{2,1,0:T(8,128)(2,1)S(1)} %bitcast.22, f32[4,8,512]{2,1,0:T(8,128)S(1)} %broadcast_in_dim.35.refs_5_.place_ref, f32[3,512,512]{2,1,0:T(8,128)} %copy-done, ...), custom_call_target="tpu_custom_call" | custom-call | flops 4294967296 | bytes 11534336 | tf_op jit(solution)/shard_map/finish_rows/pallas_call | solution.py:528
  214.5 24.4 %all-to-all-start = ((bf16[16,4,32,512]{3,2,1,0:T(8,128)(2,1)}), bf16[16,4,32,512]{3,2,1,0:T(8,128)(2,1)S(1)}, u32[]{:S(2)}, u32[]{:S(2)}) async-start(bf16[16,4,32,512]{3,2,1,0:T(8,128)(2,1)} %copy-done.1), calls=%async_computation | async-start | bytes 4194304 | tf_op jit(solution)/shard_map/all_to_all | solution.py:700
  238.9 45.3 %all-to-all-done = bf16[16,4,32,512]{3,2,1,0:T(8,128)(2,1)S(1)} async-done(((bf16[16,4,32,512]{3,2,1,0:T(8,128)(2,1)}), bf16[16,4,32,512]{3,2,1,0:T(8,128)(2,1)S(1)}, u32[]{:S(2)}, u32[]{:S(2)}) %all-to-all-start) | async-done | bytes 2097184 | tf_op jit(solution)/shard_map/all_to_all | solution.py:700
  284.7 6.4 %psum.7 = f32[4,128]{1,0:T(4,128)S(1)} all-reduce(f32[4,128]{1,0:T(4,128)S(1)} %reduce_sum.18), channel_id=1, replica_groups=mesh['seq'=16,'head'=2] {'head'}, use_global_device_ids=true, to_apply=%region_2.3 | all-reduce | flops 512 | bytes 4096 | tf_op jit(solution)/shard_map/psum | solution.py:703
  291.3 2.5 norm_rows.1
  (90 shorter events, 33.3 us)
Async XLA Ops:
  7.0 24.2 %collective-permute-start.8 = (bf16[2,512,512]{2,1,0:T(8,128)(2,1)S(1)}, bf16[2,512,512]{2,1,0:T(8,128)(2,1)}, u32[]{:S(2)}, u32[]{:S(2)}) collective-permute-start(bf16[2,512,512]{2,1,0:T(8,128)(2,1)S(1)} %get-tuple-element.25), channel_id=1, source_target_pairs={{0,2},{2,0},{4,6},{6,4},{8,10},{10,8},{12,14},{14,12},{16,18},{18,... | collective-permute-start | bytes 3145736 | tf_op jit(solution)/shard_map/ppermute | solution.py:80
  8.3 66.9 %collective-permute-start.6 = (bf16[2,512,512]{2,1,0:T(8,128)(2,1)}, bf16[2,512,512]{2,1,0:T(8,128)(2,1)}, u32[]{:S(2)}, u32[]{:S(2)}) collective-permute-start(bf16[2,512,512]{2,1,0:T(8,128)(2,1)} %get-tuple-element.22), channel_id=1, source_target_pairs={{0,4},{2,6},{4,0},{6,2},{8,12},{10,14},{12,8},{14,10},{16,20},{18,... | collective-permute-start | bytes 3145736 | tf_op jit(solution)/shard_map/ppermute | solution.py:80
  8.5 66.7 %collective-permute-start.7 = (bf16[2,512,512]{2,1,0:T(8,128)(2,1)}, bf16[2,512,512]{2,1,0:T(8,128)(2,1)}, u32[]{:S(2)}, u32[]{:S(2)}) collective-permute-start(bf16[2,512,512]{2,1,0:T(8,128)(2,1)} %get-tuple-element.23), channel_id=1, source_target_pairs={{0,6},{2,4},{4,2},{6,0},{8,14},{10,12},{12,10},{14,8},{16,22},{18,... | collective-permute-start | bytes 3145736 | tf_op jit(solution)/shard_map/ppermute | solution.py:80
  9.7 65.5 %collective-permute-start.9 = (bf16[2,512,512]{2,1,0:T(8,128)(2,1)S(1)}, bf16[2,512,512]{2,1,0:T(8,128)(2,1)}, u32[]{:S(2)}, u32[]{:S(2)}) collective-permute-start(bf16[2,512,512]{2,1,0:T(8,128)(2,1)S(1)} %get-tuple-element.24.refs_0_.refs_4_.refs_11_), channel_id=1, source_target_pairs={{0,8},{2,10},{4,12},{6,14},{8,16},{10,18},{12,20},{14,22},{16,24},... | collective-permute-start | bytes 3145736 | tf_op jit(solution)/shard_map/ppermute | solution.py:664
  31.2 44.1 %collective-permute-start.10 = (bf16[2,512,512]{2,1,0:T(8,128)(2,1)}, bf16[2,512,512]{2,1,0:T(8,128)(2,1)}, u32[]{:S(2)}, u32[]{:S(2)}) collective-permute-start(bf16[2,512,512]{2,1,0:T(8,128)(2,1)} %collective-permute-done.8.refs_1_.refs_5_.refs_12_), channel_id=1, source_target_pairs={{0,8},{2,10},{4,12},{6,14},{8,16},{10,18},{12,20},{14,22},{16,24},... | collective-permute-start | bytes 3145736 | tf_op jit(solution)/shard_map/ppermute | solution.py:664
  32.9 2.8 collective-permute-start
  35.8 3.7 %collective-permute-start.1 = (s32[1,4,32]{2,1,0:T(4,128)S(1)}, s32[1,4,32]{2,1,0:T(4,128)S(1)}, u32[]{:S(2)}, u32[]{:S(2)}) collective-permute-start(s32[1,4,32]{2,1,0:T(4,128)S(1)} %get-tuple-element.40), channel_id=1, source_target_pairs={{0,16},{2,18},{4,20},{6,22},{8,24},{10,26},{12,28},{14,30},{16,0},... | collective-permute-start | bytes 1544 | tf_op jit(solution)/shard_map/ppermute | solution.py:633
  39.5 2.8 collective-permute-start.2
  42.4 11.5 %collective-permute-start.3 = (s32[4,4,32]{2,1,0:T(4,128)S(1)}, s32[4,4,32]{2,1,0:T(4,128)S(1)}, u32[]{:S(2)}, u32[]{:S(2)}) collective-permute-start(s32[4,4,32]{2,1,0:T(4,128)S(1)} %constant_dynamic-update-slice_fusion), channel_id=1, source_target_pairs={{0,2},{2,0},{4,6},{6,4},{8,10},{10,8},{12,14},{14,12},{16,18},{18,... | collective-permute-start | bytes 6152 | tf_op jit(solution)/shard_map/ppermute | solution.py:638
  53.9 2.5 collective-permute-start.4
  56.4 11.3 %collective-permute-start.5 = (s32[4,4,32]{2,1,0:T(4,128)S(1)}, s32[4,4,32]{2,1,0:T(4,128)S(1)}, u32[]{:S(2)}, u32[]{:S(2)}) collective-permute-start(s32[4,4,32]{2,1,0:T(4,128)S(1)} %constant_dynamic-update-slice_fusion), channel_id=1, source_target_pairs={{0,6},{2,4},{4,2},{6,0},{8,14},{10,12},{12,10},{14,8},{16,22},{18,... | collective-permute-start | bytes 6152 | tf_op jit(solution)/shard_map/ppermute | solution.py:638
  83.1 110.5 %copy-start = (f32[3,512,512]{2,1,0:T(8,128)}, f32[3,512,512]{2,1,0:T(8,128)S(1)}, u32[]{:S(2)}) copy-start(f32[3,512,512]{2,1,0:T(8,128)S(1)} %get-tuple-element.26.own_any.refs_1_.refs_0_) | copy-start | bytes 9437188
  83.1 55.8 %collective-permute-start.23 = (bf16[2,2,512,512]{3,2,1,0:T(8,128)(2,1)S(1)}, bf16[2,2,512,512]{3,2,1,0:T(8,128)(2,1)S(1)}, u32[]{:S(2)}, u32[]{:S(2)}) collective-permute-start(bf16[2,2,512,512]{3,2,1,0:T(8,128)(2,1)S(1)} %get-tuple-element.36), channel_id=1, source_target_pairs={{0,8},{2,10},{4,12},{6,14},{8,16},{10,18},{12,20},{14,22},{16,24},... | collective-permute-start | bytes 6291464 | tf_op jit(solution)/shard_map/ppermute | solution.py:664
  83.9 9.9 %collective-permute-start.11 = (bf16[512,512]{1,0:T(8,128)(2,1)S(1)}, bf16[512,512]{1,0:T(8,128)(2,1)S(1)}, u32[]{:S(2)}, u32[]{:S(2)}) collective-permute-start(bf16[512,512]{1,0:T(8,128)(2,1)S(1)} %get-tuple-element.27), channel_id=1, source_target_pairs={{0,8},{2,10},{4,12},{6,14},{1,9},{3,11},{5,13},{7,15}} | collective-permute-start | bytes 1572872 | tf_op jit(solution)/shard_map/ppermute | solution.py:610
  86.7 8.7 %collective-permute-start.20 = (bf16[1,512,512]{2,1,0:T(8,128)(2,1)S(1)}, bf16[1,512,512]{2,1,0:T(8,128)(2,1)S(1)}, u32[]{:S(2)}, u32[]{:S(2)}) collective-permute-start(bf16[1,512,512]{2,1,0:T(8,128)(2,1)S(1)} %get-tuple-element.31), channel_id=1, source_target_pairs={{0,2},{2,0},{4,6},{6,4},{8,10},{10,8},{12,14},{14,12},{16,18},{18,... | collective-permute-start | bytes 1572872 | tf_op jit(solution)/shard_map/ppermute | solution.py:80
  87.0 9.7 %collective-permute-start.21 = (bf16[1,512,512]{2,1,0:T(8,128)(2,1)S(1)}, bf16[1,512,512]{2,1,0:T(8,128)(2,1)S(1)}, u32[]{:S(2)}, u32[]{:S(2)}) collective-permute-start(bf16[1,512,512]{2,1,0:T(8,128)(2,1)S(1)} %get-tuple-element.32), channel_id=1, source_target_pairs={{0,4},{2,6},{4,0},{6,2},{8,12},{10,14},{12,8},{14,10},{16,20},{18,... | collective-permute-start | bytes 1572872 | tf_op jit(solution)/shard_map/ppermute | solution.py:80
  88.2 13.1 %collective-permute-start.22 = (bf16[1,512,512]{2,1,0:T(8,128)(2,1)S(1)}, bf16[1,512,512]{2,1,0:T(8,128)(2,1)S(1)}, u32[]{:S(2)}, u32[]{:S(2)}) collective-permute-start(bf16[1,512,512]{2,1,0:T(8,128)(2,1)S(1)} %get-tuple-element.33), channel_id=1, source_target_pairs={{0,6},{2,4},{4,2},{6,0},{8,14},{10,12},{12,10},{14,8},{16,22},{18,... | collective-permute-start | bytes 1572872 | tf_op jit(solution)/shard_map/ppermute | solution.py:80
  93.9 15.8 %collective-permute-start.13 = (bf16[512,512]{1,0:T(8,128)(2,1)S(1)}, bf16[512,512]{1,0:T(8,128)(2,1)S(1)}, u32[]{:S(2)}, u32[]{:S(2)}) collective-permute-start(bf16[512,512]{1,0:T(8,128)(2,1)S(1)} %get-tuple-element.29), channel_id=1, source_target_pairs={{0,8},{2,10},{4,12},{6,14},{1,9},{3,11},{5,13},{7,15}} | collective-permute-start | bytes 1572872 | tf_op jit(solution)/shard_map/ppermute | solution.py:610
  95.4 25.6 %collective-permute-start.12 = (bf16[512,512]{1,0:T(8,128)(2,1)S(1)}, bf16[512,512]{1,0:T(8,128)(2,1)S(1)}, u32[]{:S(2)}, u32[]{:S(2)}) collective-permute-start(bf16[512,512]{1,0:T(8,128)(2,1)S(1)} %get-tuple-element.28), channel_id=1, source_target_pairs={{0,8},{2,10},{4,12},{6,14},{1,9},{3,11},{5,13},{7,15}} | collective-permute-start | bytes 1572872 | tf_op jit(solution)/shard_map/ppermute | solution.py:610
  96.7 26.2 %collective-permute-start.14 = (bf16[512,512]{1,0:T(8,128)(2,1)S(1)}, bf16[512,512]{1,0:T(8,128)(2,1)S(1)}, u32[]{:S(2)}, u32[]{:S(2)}) collective-permute-start(bf16[512,512]{1,0:T(8,128)(2,1)S(1)} %hop_add.6.refs_8_), channel_id=1, source_target_pairs={{8,16},{10,18},{12,20},{14,22},{9,17},{11,19},{13,21},{15,23}} | collective-permute-start | bytes 1572872 | tf_op jit(solution)/shard_map/ppermute | solution.py:610
  101.3 37.6 %collective-permute-start.24 = (bf16[1,512,512]{2,1,0:T(8,128)(2,1)S(1)}, bf16[1,512,512]{2,1,0:T(8,128)(2,1)S(1)}, u32[]{:S(2)}, u32[]{:S(2)}) collective-permute-start(bf16[1,512,512]{2,1,0:T(8,128)(2,1)S(1)} %get-tuple-element.30.refs_0_.refs_10_), channel_id=1, source_target_pairs={{9,1},{11,3},{13,5},{15,7},{17,9},{19,11},{21,13},{23,15},{25,17},... | collective-permute-start | bytes 1572872 | tf_op jit(solution)/shard_map/ppermute | solution.py:669
  109.7 29.2 %collective-permute-start.25 = (bf16[1,512,512]{2,1,0:T(8,128)(2,1)S(1)}, bf16[1,512,512]{2,1,0:T(8,128)(2,1)S(1)}, u32[]{:S(2)}, u32[]{:S(2)}) collective-permute-start(bf16[1,512,512]{2,1,0:T(8,128)(2,1)S(1)} %collective-permute-done.20.refs_1_.refs_11_), channel_id=1, source_target_pairs={{9,1},{11,3},{13,5},{15,7},{17,9},{19,11},{21,13},{23,15},{25,17},... | collective-permute-start | bytes 1572872 | tf_op jit(solution)/shard_map/ppermute | solution.py:669
  120.9 18.0 %collective-permute-start.26 = (bf16[1,512,512]{2,1,0:T(8,128)(2,1)S(1)}, bf16[1,512,512]{2,1,0:T(8,128)(2,1)S(1)}, u32[]{:S(2)}, u32[]{:S(2)}) collective-permute-start(bf16[1,512,512]{2,1,0:T(8,128)(2,1)S(1)} %collective-permute-done.21.refs_2_.refs_12_), channel_id=1, source_target_pairs={{9,1},{11,3},{13,5},{15,7},{17,9},{19,11},{21,13},{23,15},{25,17},... | collective-permute-start | bytes 1572872 | tf_op jit(solution)/shard_map/ppermute | solution.py:669
  122.8 16.1 %collective-permute-start.27 = (bf16[1,512,512]{2,1,0:T(8,128)(2,1)S(1)}, bf16[1,512,512]{2,1,0:T(8,128)(2,1)S(1)}, u32[]{:S(2)}, u32[]{:S(2)}) collective-permute-start(bf16[1,512,512]{2,1,0:T(8,128)(2,1)S(1)} %collective-permute-done.22.refs_3_.refs_13_), channel_id=1, source_target_pairs={{9,1},{11,3},{13,5},{15,7},{17,9},{19,11},{21,13},{23,15},{25,17},... | collective-permute-start | bytes 1572872 | tf_op jit(solution)/shard_map/ppermute | solution.py:669
  152.3 49.5 %collective-permute-start.28 = (bf16[4,512,512]{2,1,0:T(8,128)(2,1)S(1)}, bf16[4,512,512]{2,1,0:T(8,128)(2,1)S(1)}, u32[]{:S(2)}, u32[]{:S(2)}) collective-permute-start(bf16[4,512,512]{2,1,0:T(8,128)(2,1)S(1)} %get-tuple-element.37.refs_16_), channel_id=1, source_target_pairs={{1,9},{3,11},{5,13},{7,15},{9,17},{11,19},{13,21},{15,23},{17,25},... | collective-permute-start | bytes 6291464 | tf_op jit(solution)/shard_map/ppermute | solution.py:664
  155.7 28.6 %collective-permute-start.16 = (bf16[512,512]{1,0:T(8,128)(2,1)S(1)}, bf16[512,512]{1,0:T(8,128)(2,1)S(1)}, u32[]{:S(2)}, u32[]{:S(2)}) collective-permute-start(bf16[512,512]{1,0:T(8,128)(2,1)S(1)} %hop_add.8.refs_17_), channel_id=1, source_target_pairs={{8,16},{10,18},{12,20},{14,22},{9,17},{11,19},{13,21},{15,23}} | collective-permute-start | bytes 1572872 | tf_op jit(solution)/shard_map/ppermute | solution.py:610
  157.7 35.9 %collective-permute-start.15 = (bf16[512,512]{1,0:T(8,128)(2,1)S(1)}, bf16[512,512]{1,0:T(8,128)(2,1)S(1)}, u32[]{:S(2)}, u32[]{:S(2)}) collective-permute-start(bf16[512,512]{1,0:T(8,128)(2,1)S(1)} %hop_add.7.refs_16_), channel_id=1, source_target_pairs={{8,16},{10,18},{12,20},{14,22},{9,17},{11,19},{13,21},{15,23}} | collective-permute-start | bytes 1572872 | tf_op jit(solution)/shard_map/ppermute | solution.py:610
  184.5 16.7 %collective-permute-start.19 = (bf16[512,512]{1,0:T(8,128)(2,1)S(1)}, bf16[512,512]{1,0:T(8,128)(2,1)S(1)}, u32[]{:S(2)}, u32[]{:S(2)}) collective-permute-start(bf16[512,512]{1,0:T(8,128)(2,1)S(1)} %hop_add.11), channel_id=1, source_target_pairs={{16,24},{18,26},{20,28},{22,30},{17,25},{19,27},{21,29},{23,31}} | collective-permute-start | bytes 1572872 | tf_op jit(solution)/shard_map/ppermute | solution.py:610
  193.8 7.4 %collective-permute-start.18 = (bf16[512,512]{1,0:T(8,128)(2,1)S(1)}, bf16[512,512]{1,0:T(8,128)(2,1)S(1)}, u32[]{:S(2)}, u32[]{:S(2)}) collective-permute-start(bf16[512,512]{1,0:T(8,128)(2,1)S(1)} %hop_add.10), channel_id=1, source_target_pairs={{16,24},{18,26},{20,28},{22,30},{17,25},{19,27},{21,29},{23,31}} | collective-permute-start | bytes 1572872 | tf_op jit(solution)/shard_map/ppermute | solution.py:610
  194.5 6.7 %collective-permute-start.17 = (bf16[512,512]{1,0:T(8,128)(2,1)S(1)}, bf16[512,512]{1,0:T(8,128)(2,1)S(1)}, u32[]{:S(2)}, u32[]{:S(2)}) collective-permute-start(bf16[512,512]{1,0:T(8,128)(2,1)S(1)} %hop_add.9.refs_18_), channel_id=1, source_target_pairs={{16,24},{18,26},{20,28},{22,30},{17,25},{19,27},{21,29},{23,31}} | collective-permute-start | bytes 1572872 | tf_op jit(solution)/shard_map/ppermute | solution.py:610
  195.2 6.7 %collective-permute-start.29 = (f32[4,8,512]{2,1,0:T(8,128)S(1)}, f32[4,8,512]{2,1,0:T(8,128)S(1)}, u32[]{:S(2)}, u32[]{:S(2)}) collective-permute-start(f32[4,8,512]{2,1,0:T(8,128)S(1)} %get-tuple-element.38.refs_17_), channel_id=1, source_target_pairs={{1,9},{3,11},{5,13},{7,15},{9,17},{11,19},{13,21},{15,23},{17,25},... | collective-permute-start | bytes 196616 | tf_op jit(solution)/shard_map/ppermute | solution.py:664
  214.5 69.7 %all-to-all-start = ((bf16[16,4,32,512]{3,2,1,0:T(8,128)(2,1)}), bf16[16,4,32,512]{3,2,1,0:T(8,128)(2,1)S(1)}, u32[]{:S(2)}, u32[]{:S(2)}) async-start(bf16[16,4,32,512]{3,2,1,0:T(8,128)(2,1)} %copy-done.1), calls=%async_computation | async-start | bytes 4194304 | tf_op jit(solution)/shard_map/all_to_all | solution.py:700
  (7 other events, 62.5 us)

commit v5 on v3

--- a/solution.py
+++ b/solution.py
@@ -68,9 +68,6 @@
             pltpu.SemaphoreType.DMA((group,)),
         ],
         compiler_params=params(20),
-        cost_estimate=pl.CostEstimate(
-            flops=0, bytes_accessed=4 * total * group * tok * width, transcendentals=0
-        ),
         name="split_heads",
     )(info, *arrays, *after)
 
@@ -141,13 +138,13 @@
     _, tok, width = pairs[0].shape
     rows, hidden, _ = weights.shape
     pieces = last - first
-    sent = rows if last == group else 0
+    whole = last == group
     return pl.pallas_call(
         functools.partial(grad_kernel, group, tok, first, last, len(carried)),
         out_shape=[jax.ShapeDtypeStruct(weights.shape, jnp.float32)]
-        + [jax.ShapeDtypeStruct((hidden, width), jnp.bfloat16)] * sent,
+        + [jax.ShapeDtypeStruct((hidden, width), jnp.bfloat16)] * (rows * whole),
         in_specs=[SMEM, VMEM] + [ANY] * (pieces + len(carried) + len(after)),
-        out_specs=[ANY] + [VMEM] * sent,
+        out_specs=[ANY] + [VMEM] * (rows * whole),
         scratch_shapes=[
             pltpu.VMEM((pieces, 2, tok, width), jnp.bfloat16),
             pltpu.VMEM(weights.shape, jnp.float32),
@@ -155,11 +152,6 @@
             pltpu.SemaphoreType.DMA((2,)),
         ],
         compiler_params=params(28),
-        cost_estimate=pl.CostEstimate(
-            flops=2 * 6 * pieces * tok * hidden * width,
-            bytes_accessed=2 * (2 * pieces * tok * width + 2 * rows * hidden * width),
-            transcendentals=pieces * tok * hidden,
-        ),
         name="weight_sums",
     )(info, weights, *pairs[first:last], *carried, *after)
 
@@ -220,26 +212,31 @@
     return col <= row if lower else col > row
 
 
-def own_kernel(group, tok, part, info_ref, *refs):
-    q_any, kv_any = refs[:group], refs[group : 2 * group]
-    out_ref, level_ref, acc, top, norm, qbuf, kvbuf, sems = refs[-8:]
+def own_kernel(group, tok, part, first, last, info_ref, *refs):
+    count = last - first
+    q_any, kv_any = refs[:count], refs[count : count + group]
+    out_ref, level_ref, onward, acc, top, norm, qbuf, kvbuf, sems, on_sem = refs[-10:]
     member = info_ref[1]
     copies = []
+    for n in range(count):
+        copies.append(pltpu.make_async_copy(q_any[n], qbuf.at[pl.ds(n, 1)], sems.at[0, n]))
     for d in range(group):
-        copies.append(pltpu.make_async_copy(q_any[d], qbuf.at[pl.ds(d, 1)], sems.at[0, d]))
         copies.append(pltpu.make_async_copy(kv_any[d], kvbuf.at[d], sems.at[1, d]))
     for copy in copies:
         copy.start()
     for copy in copies:
         copy.wait()
+    pass_on = pltpu.make_async_copy(kvbuf.at[group - 1], onward, on_sem.at[0])
+    pass_on.start()
     scale = score_scale(qbuf.shape[-1])
 
-    def piece(d, carry):
+    def piece(n, carry):
+        d = first + n
         parts = []
         for r in range(0, tok, part):
             where, keys = pl.ds(r, part), pl.ds(0, r + part)
             mask = triangle(part, r + part, r, 0, True)
-            parts.append((where, qbuf[d, where], kvbuf[d, 0, keys], kvbuf[d, 1, keys], mask))
+            parts.append((where, qbuf[n, where], kvbuf[d, 0, keys], kvbuf[d, 1, keys], mask))
         soft_steps(parts, scale, True, acc, top, norm)
 
         def earlier(other, carry):
@@ -247,15 +244,16 @@
             parts = []
             for r in range(0, tok, part):
                 where = pl.ds(r, part)
-                parts.append((where, qbuf[d, where], kvbuf[e, 0], kvbuf[e, 1], None))
+                parts.append((where, qbuf[n, where], kvbuf[e, 0], kvbuf[e, 1], None))
             soft_steps(parts, scale, False, acc, top, norm)
             return carry
 
         lax.fori_loop(0, member ^ d, earlier, 0)
-        soft_close(scale, acc, top, norm, out_ref.at[d], level_ref.at[d])
+        soft_close(scale, acc, top, norm, out_ref.at[n], level_ref.at[n])
         return carry
 
-    lax.fori_loop(0, group, piece, 0)
+    lax.fori_loop(0, count, piece, 0)
+    pass_on.wait()
 
 
 def soft_shapes(group, tok, width):
@@ -273,33 +271,27 @@
     ]
 
 
-def soft_cost(group, tok, width):
-    return pl.CostEstimate(
-        flops=2 * group * group * tok * tok * width,
-        bytes_accessed=width * group * tok * 8,
-        transcendentals=group * group * tok * tok // 2,
-    )
-
-
-def own_attention(info, queries, pairs, after=()):
+def own_attention(info, queries, pairs, first, last, after=()):
     group = len(queries)
     _, tok, width = pairs[0].shape
     part = min(256, tok)
+    count = last - first
     return pl.pallas_call(
-        functools.partial(own_kernel, group, tok, part),
-        out_shape=soft_shapes(group, tok, width),
-        in_specs=[SMEM] + [ANY] * (2 * group + len(after)),
-        out_specs=[VMEM] * 2,
+        functools.partial(own_kernel, group, tok, part, first, last),
+        out_shape=soft_shapes(count, tok, width)
+        + [jax.ShapeDtypeStruct(pairs[0].shape, jnp.bfloat16)],
+        in_specs=[SMEM] + [ANY] * (count + group + len(after)),
+        out_specs=[VMEM] * 2 + [ANY],
         scratch_shapes=soft_scratch(tok, width)
         + [
-            pltpu.VMEM((group, tok, width), jnp.bfloat16),
+            pltpu.VMEM((count, tok, width), jnp.bfloat16),
             pltpu.VMEM((group, 2, tok, width), jnp.bfloat16),
             pltpu.SemaphoreType.DMA((2, group)),
+            pltpu.SemaphoreType.DMA((1,)),
         ],
         compiler_params=params(28),
-        cost_estimate=soft_cost(group, tok, width),
         name="own_attention",
-    )(info, *queries, *pairs, *after)
+    )(info, *queries[first:last], *pairs, *after)
 
 
 def pick_copy(flag, first, second, into, sem):
@@ -388,23 +380,23 @@
         scratch_shapes=soft_scratch(tok, width)
         + [
             pltpu.VMEM((group, tok, width), jnp.bfloat16),
-            pltpu.VMEM((len(earlier), 2, tok, width), jnp.bfloat16),
+            pltpu.VMEM((behind * group, 2, tok, width), jnp.bfloat16),
             pltpu.SemaphoreType.DMA((group,)),
-            pltpu.SemaphoreType.DMA((len(earlier),)),
+            pltpu.SemaphoreType.DMA((behind * group,)),
         ],
         compiler_params=params(28),
-        cost_estimate=soft_cost(group, tok, width),
         name="cross_attention",
     )(info, *queries, *earlier, *lent, *after)
 
 
-def finish_kernel(group, tok, count, hops, lending, info_ref, rate_ref, w_ref, place_ref, *refs):
+def finish_kernel(group, tok, count, hops, lending, cuts, info_ref, rate_ref, w_ref, place_ref, *refs):
     own_any, refs = refs[0], refs[1:]
     came, refs = refs[: 3 * hops], refs[3 * hops :]
     q_any, refs = refs[:group], refs[group:]
-    own_rows, own_level, cross_any, cross_level = refs[:4]
-    lent_any, lent_level = refs[4:6] if lending else (None, None)
-    out_ref, new_w, sums, cbuf, qbuf, obuf, xbuf, lbuf, sems, q_sems = refs[-10:]
+    own_parts, refs = refs[: 2 * len(cuts)], refs[2 * len(cuts) :]
+    cross_any, cross_level = refs[:2]
+    lent_any, lent_level = refs[2:4] if lending else (None, None)
+    out_ref, new_w, sums, cbuf, qbuf, obuf, xbuf, lbuf, sems, q_sems, own_sems = refs[-11:]
     plane, member, first_len, lends = info_ref[0], info_ref[1], info_ref[2], info_ref[3]
     own_copy = pltpu.make_async_copy(own_any, sums, sems.at[0])
     own_copy.start()
@@ -425,22 +417,20 @@
         def _():
             cbuf[...] = jnp.zeros_like(cbuf)
 
-    level_copies = [
-        pltpu.make_async_copy(own_level, lbuf.at[0], sems.at[4]),
-        pick_copy(lends, cross_level, lent_level, lbuf.at[1], sems.at[5]),
-    ]
-    level_copies[0].start()
+    level_copies = [pick_copy(lends, cross_level, lent_level, lbuf.at[1], sems.at[5])]
+    row_copies = [pick_copy(lends, cross_any, lent_any, xbuf, sems.at[7])]
+    for n, (first, last) in enumerate(cuts):
+        into = pl.ds(first, last - first)
+        rows, level = own_parts[2 * n], own_parts[2 * n + 1]
+        row_copies.append(pltpu.make_async_copy(rows, obuf.at[into], own_sems.at[0, n]))
+        level_copies.append(pltpu.make_async_copy(level, lbuf.at[0, into], own_sems.at[1, n]))
+        row_copies[-1].start()
+        level_copies[-1].start()
     q_copies = [
         pltpu.make_async_copy(q_any[d], qbuf.at[pl.ds(d, 1)], q_sems.at[d]) for d in range(group)
     ]
     for copy in q_copies:
         copy.start()
-    row_copies = [
-        pltpu.make_async_copy(own_rows, obuf, sems.at[6]),
-        pick_copy(lends, cross_any, lent_any, xbuf, sems.at[7]),
-    ]
-    row_copies[0].start()
-
     own_copy.wait()
     if hops:
 
@@ -509,15 +499,19 @@
     lax.fori_loop(0, group, piece, 0)
 
 
-def finish_rows(info, rate, weights, places, own, came, queries, own_part, cross_part, lent, count):
+def finish_rows(
+    info, rate, weights, places, own, came, queries, cuts, own_parts, cross_part, lent, count
+):
     group = len(queries)
     _, tok, width = queries[0].shape
     hidden = weights.shape[1]
     hops = len(came) // 3
     return pl.pallas_call(
-        functools.partial(finish_kernel, group, tok, count, hops, len(lent)),
+        functools.partial(finish_kernel, group, tok, count, hops, len(lent), cuts),
         out_shape=jax.ShapeDtypeStruct((count, group, tok // count, width), jnp.bfloat16),
-        in_specs=[SMEM] * 2 + [VMEM] * 2 + [ANY] * (1 + 3 * hops + group + 4 + len(lent)),
+        in_specs=[SMEM] * 2 + [VMEM] * 2 + [ANY] * (
+            1 + 3 * hops + group + len(own_parts) + 2 + len(lent)
+        ),
         out_specs=VMEM,
         scratch_shapes=[
             pltpu.VMEM(weights.shape, jnp.bfloat16),
@@ -529,15 +523,11 @@
             pltpu.VMEM((2, group, 8, tok), jnp.float32),
             pltpu.SemaphoreType.DMA((8,)),
             pltpu.SemaphoreType.DMA((group,)),
+            pltpu.SemaphoreType.DMA((2, len(cuts))),
         ],
         compiler_params=params(36),
-        cost_estimate=pl.CostEstimate(
-            flops=2 * group * tok * width * (3 * hidden + tok),
-            bytes_accessed=2 * (4 * group * tok * width + 6 * hidden * width),
-            transcendentals=group * tok * hidden,
-        ),
         name="finish_rows",
-    )(info, rate, weights, places, own, *came, *queries, *own_part, *cross_part, *lent)
+    )(info, rate, weights, places, own, *came, *queries, *own_parts, *cross_part, *lent)
 
 
 def norm_kernel(came_ref, scale_ref, gain_ref, out_ref):
@@ -562,21 +552,42 @@
     )(came, scale, gain)
 
 
-def forward_sums(own, sent, group, count):
-    planes = count // group
-    if planes > 8:
-        groups = [[plane * group + m for plane in range(planes)] for m in range(group)]
-        whole = lax.psum(own.astype(jnp.bfloat16), "seq", axis_index_groups=groups)
-        return whole.astype(jnp.float32), []
-    came = []
-    for hop in range(1, planes):
-        pairs = [((hop - 1) * group + m, hop * group + m) for m in range(group)]
-        if hop > 1:
-            sent = [
-                (own[c] + came[-3 + c].astype(jnp.float32)).astype(jnp.bfloat16) for c in range(3)
-            ]
-        came.extend([lax.ppermute(sent[c], "seq", pairs) for c in range(3)])
-    return own, came
+def add_kernel(c, own_any, came_ref, *refs):
+    out_ref, buf, sem = refs[-3:]
+    copy = pltpu.make_async_copy(own_any.at[c], buf, sem.at[0])
+    copy.start()
+    copy.wait()
+    out_ref[...] = (buf[...] + came_ref[...].astype(jnp.float32)).astype(out_ref.dtype)
+
+
+def hop_add(own, came, c, after=()):
+    return pl.pallas_call(
+        functools.partial(add_kernel, c),
+        out_shape=jax.ShapeDtypeStruct(came.shape, came.dtype),
+        in_specs=[ANY, VMEM] + [ANY] * len(after),
+        out_specs=VMEM,
+        scratch_shapes=[pltpu.VMEM(came.shape, jnp.float32), pltpu.SemaphoreType.DMA((1,))],
+        compiler_params=params(8),
+        name="hop_add",
+    )(own, came, *after)
+
+
+def pass_kernel(x_any, *refs):
+    out_any, sem = refs[-2:]
+    copy = pltpu.make_async_copy(x_any, out_any, sem.at[0])
+    copy.start()
+    copy.wait()
+
+
+def pass_after(value, after):
+    return pl.pallas_call(
+        pass_kernel,
+        out_shape=jax.ShapeDtypeStruct(value.shape, value.dtype),
+        in_specs=[ANY] * (1 + len(after)),
+        out_specs=ANY,
+        scratch_shapes=[pltpu.SemaphoreType.DMA((1,))],
+        name="pass_after",
+    )(value, *after)
 
 
 def as_places(asked, group, tok):
@@ -584,28 +595,14 @@
     return jnp.broadcast_to(places, (group, 8, tok))
 
 
-def asked_places(slot_order, plane, member, group, count):
+def asked_places(slot_order, group, count):
     tok = slot_order.shape[0]
     seg, planes = tok // count, count // group
-    wanted = slot_order.reshape(planes, group, seg) % tok
-    if planes > 8:
-        asked = lax.all_gather(wanted.reshape(tok), "seq").reshape(count, count, seg)
-        asked = lax.dynamic_slice_in_dim(asked, plane * group, group, 1)
-        return as_places(asked, group, tok)
-    column = jnp.zeros_like(wanted)
-    for step in range(planes):
-        target = (plane + step) % planes
-        part = lax.dynamic_index_in_dim(wanted, target, 0, keepdims=True)
-        if step:
-            pairs = [(index, (index + step * group) % count) for index in range(count)]
-            part = lax.ppermute(part, "seq", pairs)
-        source = (plane - step) % planes
-        column = lax.dynamic_update_slice_in_dim(column, part, source, 0)
-    whole = jnp.zeros((planes, group, group, seg), jnp.int32)
-    for d in range(group):
-        part = lax.ppermute(column, "seq", swap_pairs(count, d)) if d else column
-        whole = lax.dynamic_update_slice_in_dim(whole, part[:, None], member ^ d, 1)
-    return as_places(whole.reshape(count, group, seg), group, tok)
+    wanted = (slot_order % tok).reshape(planes, 1, group * seg)
+    wanted = jnp.broadcast_to(wanted, (planes, group, group * seg))
+    wanted = wanted.reshape(count, group * seg)
+    asked = lax.all_to_all(wanted, "seq", split_axis=0, concat_axis=0, tiled=True)
+    return as_places(asked.reshape(count, group, seg), group, tok)
 
 
 def per_device(
@@ -637,26 +634,69 @@
         return lax.ppermute(value, ("seq", "head"), both)
 
     mine = split_heads(info, [token_keys, token_values])
-    pairs = trade(mine, count)
-    earlier = []
-    for back in range(behind, 0, -1):
-        earlier.extend([across(pair, back * group, 0) for pair in pairs])
-    asked = trade(split_heads(info, [queries], pairs[1:2]), count)
-    lent = [back_across(piece, 1) for piece in asked] + pairs if lending else []
-
     weights = lax.dynamic_index_in_dim(fast_weights, member, 1, keepdims=False)
     weights = jnp.transpose(weights, (1, 0, 2))
     rate = lax.dynamic_slice_in_dim(learn_rate, member, 1)
-    half = group // 2
-    carried = weight_sums(info, weights, pairs, 0, half) if half else []
-    own, *sent = weight_sums(info, weights, pairs, half, group, carried, earlier[:half])
-    own, came = forward_sums(own, sent, group, count)
-    own_part = own_attention(info, asked, pairs, earlier[half:])
-    cross_part = cross_attention(info, asked, earlier, lent, came[:3])
+    places = asked_places(slot_order, group, count)
+
+    last = group - 1
+    pairs = trade(mine[:last] or mine, count)
+    if last:
+        late = pass_after(mine[last], pairs[1:])
+        pairs = pairs + [lax.ppermute(late, "seq", swap_pairs(count, last))]
+    shifts = [back * group for back in range(behind, 0, -1)]
+    near = [[across(pair, shift, 0) for pair in pairs[:last]] for shift in shifts]
+    carried = weight_sums(info, weights, pairs, 0, last) if last else []
+    waits = [array for arrays in near for array in arrays[:2]] + [places]
+    own, *sent = weight_sums(info, weights, pairs, last, group, carried, waits)
+    asked = trade(split_heads(info, [queries], [own]), count)
+    lent = [back_across(piece, 1) for piece in asked] + pairs if lending else []
+
+    chained = planes <= 8
+    hops = planes - 1 if chained else 0
+    came = {}
+
+    def hop(step, c, value):
+        sources = [(step - 1) * group + m for m in range(group)]
+        came[step, c] = lax.ppermute(value, "seq", [(a, a + group) for a in sources])
+
+    if chained:
+        for c in range(3 if hops else 0):
+            hop(1, c, sent[c])
+    else:
+        groups = [[z * group + m for z in range(planes)] for m in range(group)]
+        own = lax.psum(own.astype(jnp.bfloat16), "seq", axis_index_groups=groups)
+        own = own.astype(jnp.float32)
+    adds = [(step, c) for step in range(2, hops + 1) for c in range(3)]
+    adds.sort(key=lambda add: (sum(add), add))
+    cuts = [cut for cut in ((0, 1), (1, last), (max(1, last), group)) if cut[1] > cut[0]]
+    work = [("own", cuts[0])]
+    for n in range(max(len(adds), len(cuts) - 1)):
+        work.extend([("add", add) for add in adds[n : n + 1]])
+        work.extend([("own", cut) for cut in cuts[n + 1 : n + 2]])
+    work.insert(len(work) - 1 if adds else len(work), ("cross", None))
+    own_parts, cross_part, token, earlier = [], None, [own], []
+    for kind, what in work:
+        if kind == "add":
+            added = hop_add(own, came[what[0] - 1, what[1]], what[1], token)
+            hop(*what, added)
+            token = [added]
+        elif kind == "own":
+            begun = len(own_parts) // 2
+            ready = lent[cuts[begun - 1][0] : cuts[begun - 1][1]] if lending and begun else []
+            rows, level, onward = own_attention(info, asked, pairs, *what, token + ready)
+            if not own_parts:
+                for arrays, shift in zip(near, shifts):
+                    earlier.extend(arrays + [across(onward, shift, 0)])
+            own_parts.extend([rows, level])
+            token = [rows]
+        else:
+            cross_part = cross_attention(info, asked, earlier, lent, token)
+            token = [cross_part[0]]
     lent_part = [across(value, group, 1) for value in cross_part] if lending else []
-    places = asked_places(slot_order, plane, member, group, count)
+    arrived = [came[step, c] for step in range(1, hops + 1) for c in range(3)]
     leaving = finish_rows(
-        info, rate, weights, places, own, came, asked, own_part, cross_part, lent_part, count
+        info, rate, weights, places, own, arrived, asked, cuts, own_parts, cross_part, lent_part, count
     )
 
     came = lax.all_to_all(leaving, "seq", split_axis=0, concat_axis=0, tiled=True)

time: 310 us -> 303 us (0.977)
  waiting for transfers between devices: 166 us -> 120 us
  Pallas kernels: 59.1 us -> 93.6 us
  starting transfers between devices: 51.3 us -> 65.2 us
  local copies, waits for them, and re-layouts: 24.1 us -> 17.9 us
  other arithmetic: 4.98 us -> 0.54 us
    ppermute x15 -> x10, waiting for transfers between devices: 83.1 us -> 42.5 us  [the longest x9 42.5 us: hop(): lax.ppermute(value, 'seq', [(a, a + group) for a in sources])]
    pallas_call x1 -> x10, Pallas kernels: 12.9 us -> 50.9 us  [the longest x1 32.9 us: pass_after(): pl.pallas_call(pass_kernel, out_shape=jax.ShapeDtypeStruct(value.shape, v...]
    ppermute x6 -> x5, waiting for transfers between devices: 46.3 us -> 21.8 us  [trade(): lax.ppermute(piece, 'seq', swap_pairs(count, d))]
    all_to_all x1, starting transfers between devices: 4.89 us -> 18 us  [per_device(): lax.all_to_all(leaving, 'seq', split_axis=0, concat_axis=0, tiled=True)]
    all_to_all x1, waiting for transfers between devices: 36.5 us -> 48.2 us  [per_device(): lax.all_to_all(leaving, 'seq', split_axis=0, concat_axis=0, tiled=True)]
    ppermute x15 -> x10, starting transfers between devices: 21.2 us -> 13.5 us  [the longest x9 12.8 us: hop(): lax.ppermute(value, 'seq', [(a, a + group) for a in sources])]
    unnamed x78 -> x30, local copies, waits for them, and re-layouts: 15.5 us -> 7.88 us
    all_to_all x0 -> x1, waiting for transfers between devices: none -> 7.3 us  [asked_places(): lax.all_to_all(wanted, 'seq', split_axis=0, concat_axis=0, tiled=True)]
  transfers between devices with their start and end apart: 32 -> 27, of which waited for: 11 -> 8; matrix products, arithmetic and copies ran while one was open for 4% -> 3% of each run, Pallas kernels for 9% -> 20%
where the time goes in v5:
time: 303 us; the launch traced here: 302 us
  waiting for transfers between devices  120 us (40%)
  Pallas kernels  93.6 us (31%)
  starting transfers between devices  65.2 us (22%)
  local copies, waits for them, and re-layouts  17.9 us (6%)
  blocking collectives  3.59 us (1%)
    all_to_all x1, waiting for transfers between devices, per_device(): lax.all_to_all(leaving, 'seq', split_axis=0, concat_axis=0, tiled=True)  48.2 us
    ppermute x9, waiting for transfers between devices, hop(): lax.ppermute(value, 'seq', [(a, a + group) for a in sources])  42.5 us
    pallas_call x1, Pallas kernels, pass_after(): pl.pallas_call(pass_kernel, out_shape=jax.ShapeDtypeStruct(value.shape, v...  32.9 us
    ppermute x5, waiting for transfers between devices, trade(): lax.ppermute(piece, 'seq', swap_pairs(count, d))  21.8 us
    all_to_all x1, starting transfers between devices, per_device(): lax.all_to_all(leaving, 'seq', split_axis=0, concat_axis=0, tiled=True)  18 us
    pallas_call x3, Pallas kernels, own_attention(): pl.pallas_call(functools.partial(own_kernel, group, tok, part, first, las...  17 us
    pallas_call x2, Pallas kernels, weight_sums(): pl.pallas_call(functools.partial(grad_kernel, group, tok, first, last, le...  13.2 us
    ppermute x9, starting transfers between devices, hop(): lax.ppermute(value, 'seq', [(a, a + group) for a in sources])  12.8 us
  transfers between devices with their start and end apart: 27, of which 8 were waited for; matrix products, arithmetic and copies ran while one was open for 3% of the time, Pallas kernels for 20%

profile of v5, /device:TPU:13, one launch (start us, length us, event | category | flops | bytes accessed | tf_op | source)
XLA Modules:
  0.0 301.9 jit_solution(18443573096250189542)
XLA Ops:
  0.7 1.6 copy-done.8
  2.3 1.6 copy-done.9
  3.9 1.9 split_heads.2
  8.2 1.7 collective-permute-start.3
  9.8 20.9 %collective-permute-done.refs_0_.refs_1_.refs_2_.refs_3_.refs_13_ = bf16[2,512,512]{2,1,0:T(8,128)(2,1)S(1)} collective-permute-done((bf16[2,512,512]{2,1,0:T(8,128)(2,1)S(1)}, bf16[2,512,512]{2,1,0:T(8,128)(2,1)S(1)}, u32[]{:S(2)}, u32[]{:S(2)}) %collective-permute-start) | collective-permute-done | bytes 1048608 | tf_op jit(solution)/shard_map/ppermute | solution.py:77
  32.7 32.9 %pass_after.1 = bf16[2,512,512]{2,1,0:T(8,128)(2,1)} custom-call(bf16[2,512,512]{2,1,0:T(8,128)(2,1)} %copy-done.11, bf16[2,512,512]{2,1,0:T(8,128)(2,1)} %copy-done.1, bf16[2,512,512]{2,1,0:T(8,128)(2,1)} %copy-done.3), custom_call_target="tpu_custom_call" | custom-call | tf_op jit(solution)/shard_map/pass_after/pallas_call | solution.py:583
  66.3 1.7 collective-permute-start.4
  68.5 6.2 %all-to-all-start = ((s32[16,1,128]{2,1,0:T(1,128)}), s32[16,1,128]{2,1,0:T(1,128)S(1)}, u32[]{:S(2)}, u32[]{:S(2)}) async-start(s32[16,1,128]{2,1,0:T(1,128)} %bitcast.6), calls=%async_computation | async-start | bytes 16384 | tf_op jit(solution)/shard_map/all_to_all | solution.py:604
  74.7 6.0 %constant_dynamic-slice_fusion = bf16[512,1,3,512]{3,1,2,0:T(2,128)(2,1)S(1)} fusion(bf16[512,4,3,512]{3,1,2,0:T(4,128)(2,1)} %param.11, s32[]{:T(128)S(6)} %select_n.29), kind=kLoop, calls=%fused_computation.9 | loop fusion | bytes 3145732 | tf_op jit(solution)/shard_map/jit(dynamic_index_in_dim)/dynamic_slice | solution.py:637
  82.4 7.3 %all-to-all-done = s32[16,1,128]{2,1,0:T(1,128)S(1)} async-done(((s32[16,1,128]{2,1,0:T(1,128)}), s32[16,1,128]{2,1,0:T(1,128)S(1)}, u32[]{:S(2)}, u32[]{:S(2)}) %all-to-all-start) | async-done | bytes 8224 | tf_op jit(solution)/shard_map/all_to_all | solution.py:604
  91.3 8.5 %weight_sums.2.refs_1_ = f32[3,512,512]{2,1,0:T(8,128)S(1)} custom-call(s32[5]{0:T(128)S(1)} %stack.15.info_ref, bf16[3,512,512]{2,1,0:T(8,128)(2,1)S(1)} %bitcast.16, bf16[2,512,512]{2,1,0:T(8,128)(2,1)S(1)} %get-tuple-element.29.refs_0_.refs_1_.refs_2_.refs_12_, bf16[2,512,512]{2,1,0:T(8,128)(2,1)S(1)} %copy-done.2, bf16[2,512,512]{2,1,0:T(8,128)(2,1)S(1)} %copy-done.4), custom_call_target="tpu_custom_call" | custom-call | tf_op jit(solution)/shard_map/weight_sums/pallas_call | solution.py:142
  99.9 4.7 %weight_sums.3 = (f32[3,512,512]{2,1,0:T(8,128)S(1)}, bf16[512,512]{1,0:T(8,128)(2,1)S(1)}, bf16[512,512]{1,0:T(8,128)(2,1)S(1)}, bf16[512,512]{1,0:T(8,128)(2,1)S(1)}) custom-call(s32[5]{0:T(128)S(1)} %stack.15.info_ref, bf16[3,512,512]{2,1,0:T(8,128)(2,1)S(1)} %bitcast.17, bf16[2,512,512]{2,1,0:T(8,128)(2,1)} %collective-permute-done.2.refs_0_.refs_4_.refs_5_.refs_15_, ...), custom_call_target="tpu_custom_call" | custom-call | tf_op jit(solution)/shard_map/weight_sums/pallas_call | solution.py:142
  108.5 4.0 %collective-permute-start.11 = (bf16[1,512,512]{2,1,0:T(8,128)(2,1)S(1)}, bf16[1,512,512]{2,1,0:T(8,128)(2,1)S(1)}, u32[]{:S(2)}, u32[]{:S(2)}) collective-permute-start(bf16[1,512,512]{2,1,0:T(8,128)(2,1)S(1)} %get-tuple-element.34.refs_0_.refs_10_), channel_id=1, source_target_pairs={{9,1},{11,3},{13,5},{15,7},{17,9},{19,11},{21,13},{23,15},{25,17},... | collective-permute-start | bytes 1572872 | tf_op jit(solution)/shard_map/ppermute | solution.py:634
  114.0 3.1 %collective-permute-done.5.came_ref.refs_1_ = bf16[512,512]{1,0:T(8,128)(2,1)S(1)} collective-permute-done((bf16[512,512]{1,0:T(8,128)(2,1)S(1)}, bf16[512,512]{1,0:T(8,128)(2,1)S(1)}, u32[]{:S(2)}, u32[]{:S(2)}) %collective-permute-start.5) | collective-permute-done | bytes 524320 | tf_op jit(solution)/shard_map/ppermute | solution.py:661
  118.5 5.4 %own_attention.3 = (bf16[1,512,512]{2,1,0:T(8,128)(2,1)S(1)}, f32[1,8,512]{2,1,0:T(8,128)S(1)}, bf16[2,512,512]{2,1,0:T(8,128)(2,1)S(1)}) custom-call(s32[5]{0:T(128)S(1)} %stack.15.info_ref, bf16[1,512,512]{2,1,0:T(8,128)(2,1)S(1)} %get-tuple-element.34.refs_0_.refs_10_, bf16[2,512,512]{2,1,0:T(8,128)(2,1)S(1)} %get-tuple-element.29.refs_0_.refs_1_.refs_2_.refs_12_, ...), custom_call_target="tpu_custom_call" | custom-call | tf_op jit(solution)/shard_map/own_attention/pallas_call | solution.py:279
  123.9 1.9 collective-permute-start.14
  126.8 1.9 collective-permute-start.15
  128.7 3.4 %collective-permute-start.8 = (bf16[512,512]{1,0:T(8,128)(2,1)S(1)}, bf16[512,512]{1,0:T(8,128)(2,1)S(1)}, u32[]{:S(2)}, u32[]{:S(2)}) collective-permute-start(bf16[512,512]{1,0:T(8,128)(2,1)S(1)} %hop_add.6.refs_6_), channel_id=1, source_target_pairs={{8,16},{10,18},{12,20},{14,22},{9,17},{11,19},{13,21},{15,23}} | collective-permute-start | bytes 1572872 | tf_op jit(solution)/shard_map/ppermute | solution.py:661
  132.9 7.5 %own_attention.4 = (bf16[2,512,512]{2,1,0:T(8,128)(2,1)S(1)}, f32[2,8,512]{2,1,0:T(8,128)S(1)}, bf16[2,512,512]{2,1,0:T(8,128)(2,1)}) custom-call(s32[5]{0:T(128)S(1)} %stack.15.info_ref, bf16[1,512,512]{2,1,0:T(8,128)(2,1)S(1)} %collective-permute-done.9.refs_0_.refs_1_.refs_11_, bf16[1,512,512]{2,1,0:T(8,128)(2,1)S(1)} %collective-permute-done.10.refs_1_.refs_2_.refs_12_, ...), custom_call_target="tpu_custom_call" | custom-call | tf_op jit(solution)/shard_map/own_attention/pallas_call | solution.py:279
  143.2 3.4 %collective-permute-start.21 = (bf16[1,512,512]{2,1,0:T(8,128)(2,1)S(1)}, bf16[1,512,512]{2,1,0:T(8,128)(2,1)S(1)}, u32[]{:S(2)}, u32[]{:S(2)}) collective-permute-start(bf16[1,512,512]{2,1,0:T(8,128)(2,1)S(1)} %collective-permute-done.13.refs_0_.refs_3_.refs_13_), channel_id=1, source_target_pairs={{9,1},{11,3},{13,5},{15,7},{17,9},{19,11},{21,13},{23,15},{25,17},... | collective-permute-start | bytes 1572872 | tf_op jit(solution)/shard_map/ppermute | solution.py:634
  146.6 4.2 %own_attention.5 = (bf16[1,512,512]{2,1,0:T(8,128)(2,1)S(1)}, f32[1,8,512]{2,1,0:T(8,128)S(1)}, bf16[2,512,512]{2,1,0:T(8,128)(2,1)}) custom-call(s32[5]{0:T(128)S(1)} %stack.15.info_ref, bf16[1,512,512]{2,1,0:T(8,128)(2,1)S(1)} %collective-permute-done.13.refs_0_.refs_3_.refs_13_, ...), custom_call_target="tpu_custom_call" | custom-call | tf_op jit(solution)/shard_map/own_attention/pallas_call | solution.py:279
  150.9 5.5 %collective-permute-done.7.came_ref.refs_3_ = bf16[512,512]{1,0:T(8,128)(2,1)S(1)} collective-permute-done((bf16[512,512]{1,0:T(8,128)(2,1)S(1)}, bf16[512,512]{1,0:T(8,128)(2,1)S(1)}, u32[]{:S(2)}, u32[]{:S(2)}) %collective-permute-start.7) | collective-permute-done | bytes 524320 | tf_op jit(solution)/shard_map/ppermute | solution.py:661
  156.8 12.7 %cross_attention.1 = (bf16[4,512,512]{2,1,0:T(8,128)(2,1)S(1)}, f32[4,8,512]{2,1,0:T(8,128)S(1)}) custom-call(s32[5]{0:T(128)S(1)} %stack.15.info_ref, bf16[1,512,512]{2,1,0:T(8,128)(2,1)S(1)} %get-tuple-element.34.refs_0_.refs_10_, bf16[1,512,512]{2,1,0:T(8,128)(2,1)S(1)} %collective-permute-done.9.refs_0_.refs_1_.refs_11_, ...), custom_call_target="tpu_custom_call" | custom-call | tf_op jit(solution)/shard_map/cross_attention/pallas_call | solution.py:375
  169.5 2.6 collective-permute-start.23
  172.1 1.9 collective-permute-start.16
  175.5 33.9 %collective-permute-done.16.came_ref.refs_6_ = bf16[512,512]{1,0:T(8,128)(2,1)S(1)} collective-permute-done((bf16[512,512]{1,0:T(8,128)(2,1)S(1)}, bf16[512,512]{1,0:T(8,128)(2,1)S(1)}, u32[]{:S(2)}, u32[]{:S(2)}) %collective-permute-start.16) | collective-permute-done | bytes 524320 | tf_op jit(solution)/shard_map/ppermute | solution.py:661
  210.2 4.7 %collective-permute-start.24 = (f32[4,8,512]{2,1,0:T(8,128)S(1)}, f32[4,8,512]{2,1,0:T(8,128)S(1)}, u32[]{:S(2)}, u32[]{:S(2)}) collective-permute-start(f32[4,8,512]{2,1,0:T(8,128)S(1)} %get-tuple-element.46.refs_21_), channel_id=1, source_target_pairs={{1,9},{3,11},{5,13},{7,15},{9,17},{11,19},{13,21},{15,23},{17,25},... | collective-permute-start | bytes 196616 | tf_op jit(solution)/shard_map/ppermute | solution.py:629
  216.3 11.2 %finish_rows.1 = bf16[16,4,32,512]{3,2,1,0:T(8,128)(2,1)S(1)} custom-call(s32[5]{0:T(128)S(1)} %stack.15.info_ref, f32[1]{0:T(128)} %dynamic_slice.7.rate_ref, bf16[3,512,512]{2,1,0:T(8,128)(2,1)S(1)} %bitcast.18, f32[4,8,512]{2,1,0:T(8,128)S(1)} %broadcast_in_dim.20.refs_4_.place_ref, f32[3,512,512]{2,1,0:T(8,128)} %copy-done, ...), custom_call_target="tpu_custom_call" | custom-call | tf_op jit(solution)/shard_map/finish_rows/pallas_call | solution.py:509
  228.8 18.0 %all-to-all-start.1 = ((bf16[16,4,32,512]{3,2,1,0:T(8,128)(2,1)}), bf16[16,4,32,512]{3,2,1,0:T(8,128)(2,1)S(1)}, u32[]{:S(2)}, u32[]{:S(2)}) async-start(bf16[16,4,32,512]{3,2,1,0:T(8,128)(2,1)} %copy-done.7), calls=%async_computation.1 | async-start | bytes 4194304 | tf_op jit(solution)/shard_map/all_to_all | solution.py:702
  246.9 48.2 %all-to-all-done.1 = bf16[16,4,32,512]{3,2,1,0:T(8,128)(2,1)S(1)} async-done(((bf16[16,4,32,512]{3,2,1,0:T(8,128)(2,1)}), bf16[16,4,32,512]{3,2,1,0:T(8,128)(2,1)S(1)}, u32[]{:S(2)}, u32[]{:S(2)}) %all-to-all-start.1) | async-done | bytes 2097184 | tf_op jit(solution)/shard_map/all_to_all | solution.py:702
  295.6 3.6 %psum.7 = f32[4,128]{1,0:T(4,128)S(1)} all-reduce(f32[4,128]{1,0:T(4,128)S(1)} %reduce_sum.18), channel_id=1, replica_groups=mesh['seq'=16,'head'=2] {'head'}, use_global_device_ids=true, to_apply=%region_2.3 | all-reduce | flops 512 | bytes 4096 | tf_op jit(solution)/shard_map/psum | solution.py:705
  299.4 2.5 norm_rows.1
  (87 shorter events, 26.8 us)
Async XLA Ops:
  6.8 24.0 %collective-permute-start = (bf16[2,512,512]{2,1,0:T(8,128)(2,1)S(1)}, bf16[2,512,512]{2,1,0:T(8,128)(2,1)S(1)}, u32[]{:S(2)}, u32[]{:S(2)}) collective-permute-start(bf16[2,512,512]{2,1,0:T(8,128)(2,1)S(1)} %get-tuple-element.27), channel_id=1, source_target_pairs={{0,2},{2,0},{4,6},{6,4},{8,10},{10,8},{12,14},{14,12},{16,18},{18,... | collective-permute-start | bytes 3145736 | tf_op jit(solution)/shard_map/ppermute | solution.py:77
  8.0 23.7 %collective-permute-start.1 = (bf16[2,512,512]{2,1,0:T(8,128)(2,1)S(1)}, bf16[2,512,512]{2,1,0:T(8,128)(2,1)S(1)}, u32[]{:S(2)}, u32[]{:S(2)}) collective-permute-start(bf16[2,512,512]{2,1,0:T(8,128)(2,1)S(1)} %get-tuple-element.28), channel_id=1, source_target_pairs={{0,4},{2,6},{4,0},{6,2},{8,12},{10,14},{12,8},{14,10},{16,20},{18,... | collective-permute-start | bytes 3145736 | tf_op jit(solution)/shard_map/ppermute | solution.py:77
  8.2 91.7 %collective-permute-start.3 = (bf16[2,512,512]{2,1,0:T(8,128)(2,1)S(1)}, bf16[2,512,512]{2,1,0:T(8,128)(2,1)}, u32[]{:S(2)}, u32[]{:S(2)}) collective-permute-start(bf16[2,512,512]{2,1,0:T(8,128)(2,1)S(1)} %get-tuple-element.29.refs_0_.refs_1_.refs_2_.refs_12_), channel_id=1, source_target_pairs={{0,8},{2,10},{4,12},{6,14},{8,16},{10,18},{12,20},{14,22},{16,24},... | collective-permute-start | bytes 3145736 | tf_op jit(solution)/shard_map/ppermute | solution.py:629
  32.7 35.3 %copy-start.13 = (s32[512]{0:T(512)S(1)}, s32[512]{0:T(512)}, u32[]{:S(2)}) copy-start(s32[512]{0:T(512)} %param.15) | copy-start | bytes 6148
  65.5 34.3 %collective-permute-start.2 = (bf16[2,512,512]{2,1,0:T(8,128)(2,1)}, bf16[2,512,512]{2,1,0:T(8,128)(2,1)}, u32[]{:S(2)}, u32[]{:S(2)}) collective-permute-start(bf16[2,512,512]{2,1,0:T(8,128)(2,1)} %pass_after.1), channel_id=1, source_target_pairs={{0,6},{2,4},{4,2},{6,0},{8,14},{10,12},{12,10},{14,8},{16,22},{18,... | collective-permute-start | bytes 3145736 | tf_op jit(solution)/shard_map/ppermute | solution.py:646
  66.3 33.6 %collective-permute-start.4 = (bf16[2,512,512]{2,1,0:T(8,128)(2,1)}, bf16[2,512,512]{2,1,0:T(8,128)(2,1)}, u32[]{:S(2)}, u32[]{:S(2)}) collective-permute-start(bf16[2,512,512]{2,1,0:T(8,128)(2,1)} %copy-done.1), channel_id=1, source_target_pairs={{0,8},{2,10},{4,12},{6,14},{8,16},{10,18},{12,20},{14,22},{16,24},... | collective-permute-start | bytes 3145736 | tf_op jit(solution)/shard_map/ppermute | solution.py:629
  68.5 21.1 %all-to-all-start = ((s32[16,1,128]{2,1,0:T(1,128)}), s32[16,1,128]{2,1,0:T(1,128)S(1)}, u32[]{:S(2)}, u32[]{:S(2)}) async-start(s32[16,1,128]{2,1,0:T(1,128)} %bitcast.6), calls=%async_computation | async-start | bytes 16384 | tf_op jit(solution)/shard_map/all_to_all | solution.py:604
  104.6 104.7 %copy-start = (f32[3,512,512]{2,1,0:T(8,128)}, f32[3,512,512]{2,1,0:T(8,128)S(1)}, u32[]{:S(2)}) copy-start(f32[3,512,512]{2,1,0:T(8,128)S(1)} %get-tuple-element.30.refs_1_.refs_5_.own_any.refs_0_) | copy-start | bytes 9437188
  104.6 12.5 %collective-permute-start.5 = (bf16[512,512]{1,0:T(8,128)(2,1)S(1)}, bf16[512,512]{1,0:T(8,128)(2,1)S(1)}, u32[]{:S(2)}, u32[]{:S(2)}) collective-permute-start(bf16[512,512]{1,0:T(8,128)(2,1)S(1)} %get-tuple-element.31), channel_id=1, source_target_pairs={{0,8},{2,10},{4,12},{6,14},{1,9},{3,11},{5,13},{7,15}} | collective-permute-start | bytes 1572872 | tf_op jit(solution)/shard_map/ppermute | solution.py:661
  107.2 16.7 %collective-permute-start.9 = (bf16[1,512,512]{2,1,0:T(8,128)(2,1)S(1)}, bf16[1,512,512]{2,1,0:T(8,128)(2,1)S(1)}, u32[]{:S(2)}, u32[]{:S(2)}) collective-permute-start(bf16[1,512,512]{2,1,0:T(8,128)(2,1)S(1)} %get-tuple-element.36), channel_id=1, source_target_pairs={{0,2},{2,0},{4,6},{6,4},{8,10},{10,8},{12,14},{14,12},{16,18},{18,... | collective-permute-start | bytes 1572872 | tf_op jit(solution)/shard_map/ppermute | solution.py:77
  108.2 17.8 %collective-permute-start.10 = (bf16[1,512,512]{2,1,0:T(8,128)(2,1)S(1)}, bf16[1,512,512]{2,1,0:T(8,128)(2,1)S(1)}, u32[]{:S(2)}, u32[]{:S(2)}) collective-permute-start(bf16[1,512,512]{2,1,0:T(8,128)(2,1)S(1)} %get-tuple-element.37), channel_id=1, source_target_pairs={{0,4},{2,6},{4,0},{6,2},{8,12},{10,14},{12,8},{14,10},{16,20},{18,... | collective-permute-start | bytes 1572872 | tf_op jit(solution)/shard_map/ppermute | solution.py:77
  108.5 18.2 %collective-permute-start.11 = (bf16[1,512,512]{2,1,0:T(8,128)(2,1)S(1)}, bf16[1,512,512]{2,1,0:T(8,128)(2,1)S(1)}, u32[]{:S(2)}, u32[]{:S(2)}) collective-permute-start(bf16[1,512,512]{2,1,0:T(8,128)(2,1)S(1)} %get-tuple-element.34.refs_0_.refs_10_), channel_id=1, source_target_pairs={{9,1},{11,3},{13,5},{15,7},{17,9},{19,11},{21,13},{23,15},{25,17},... | collective-permute-start | bytes 1572872 | tf_op jit(solution)/shard_map/ppermute | solution.py:634
  112.5 16.2 %collective-permute-start.6 = (bf16[512,512]{1,0:T(8,128)(2,1)S(1)}, bf16[512,512]{1,0:T(8,128)(2,1)S(1)}, u32[]{:S(2)}, u32[]{:S(2)}) collective-permute-start(bf16[512,512]{1,0:T(8,128)(2,1)S(1)} %get-tuple-element.32), channel_id=1, source_target_pairs={{0,8},{2,10},{4,12},{6,14},{1,9},{3,11},{5,13},{7,15}} | collective-permute-start | bytes 1572872 | tf_op jit(solution)/shard_map/ppermute | solution.py:661
  117.1 15.0 %collective-permute-start.13 = (bf16[1,512,512]{2,1,0:T(8,128)(2,1)S(1)}, bf16[1,512,512]{2,1,0:T(8,128)(2,1)S(1)}, u32[]{:S(2)}, u32[]{:S(2)}) collective-permute-start(bf16[1,512,512]{2,1,0:T(8,128)(2,1)S(1)} %get-tuple-element.39), channel_id=1, source_target_pairs={{0,6},{2,4},{4,2},{6,0},{8,14},{10,12},{12,10},{14,8},{16,22},{18,... | collective-permute-start | bytes 1572872 | tf_op jit(solution)/shard_map/ppermute | solution.py:77
  123.9 16.6 %collective-permute-start.14 = (bf16[1,512,512]{2,1,0:T(8,128)(2,1)S(1)}, bf16[1,512,512]{2,1,0:T(8,128)(2,1)S(1)}, u32[]{:S(2)}, u32[]{:S(2)}) collective-permute-start(bf16[1,512,512]{2,1,0:T(8,128)(2,1)S(1)} %collective-permute-done.9.refs_0_.refs_1_.refs_11_), channel_id=1, source_target_pairs={{9,1},{11,3},{13,5},{15,7},{17,9},{19,11},{21,13},{23,15},{25,17},... | collective-permute-start | bytes 1572872 | tf_op jit(solution)/shard_map/ppermute | solution.py:634
  126.0 30.7 %collective-permute-start.19 = (bf16[2,512,512]{2,1,0:T(8,128)(2,1)S(1)}, bf16[2,512,512]{2,1,0:T(8,128)(2,1)S(1)}, u32[]{:S(2)}, u32[]{:S(2)}) collective-permute-start(bf16[2,512,512]{2,1,0:T(8,128)(2,1)S(1)} %copy-done.4), channel_id=1, source_target_pairs={{0,8},{2,10},{4,12},{6,14},{8,16},{10,18},{12,20},{14,22},{16,24},... | collective-permute-start | bytes 3145736 | tf_op jit(solution)/shard_map/ppermute | solution.py:629
  126.8 15.0 %collective-permute-start.15 = (bf16[1,512,512]{2,1,0:T(8,128)(2,1)S(1)}, bf16[1,512,512]{2,1,0:T(8,128)(2,1)S(1)}, u32[]{:S(2)}, u32[]{:S(2)}) collective-permute-start(bf16[1,512,512]{2,1,0:T(8,128)(2,1)S(1)} %collective-permute-done.10.refs_1_.refs_2_.refs_12_), channel_id=1, source_target_pairs={{9,1},{11,3},{13,5},{15,7},{17,9},{19,11},{21,13},{23,15},{25,17},... | collective-permute-start | bytes 1572872 | tf_op jit(solution)/shard_map/ppermute | solution.py:634
  128.7 14.4 %collective-permute-start.8 = (bf16[512,512]{1,0:T(8,128)(2,1)S(1)}, bf16[512,512]{1,0:T(8,128)(2,1)S(1)}, u32[]{:S(2)}, u32[]{:S(2)}) collective-permute-start(bf16[512,512]{1,0:T(8,128)(2,1)S(1)} %hop_add.6.refs_6_), channel_id=1, source_target_pairs={{8,16},{10,18},{12,20},{14,22},{9,17},{11,19},{13,21},{15,23}} | collective-permute-start | bytes 1572872 | tf_op jit(solution)/shard_map/ppermute | solution.py:661
  132.1 24.7 %collective-permute-start.20 = (bf16[2,512,512]{2,1,0:T(8,128)(2,1)S(1)}, bf16[2,512,512]{2,1,0:T(8,128)(2,1)S(1)}, u32[]{:S(2)}, u32[]{:S(2)}) collective-permute-start(bf16[2,512,512]{2,1,0:T(8,128)(2,1)S(1)} %get-tuple-element.41), channel_id=1, source_target_pairs={{0,8},{2,10},{4,12},{6,14},{8,16},{10,18},{12,20},{14,22},{16,24},... | collective-permute-start | bytes 3145736 | tf_op jit(solution)/shard_map/ppermute | solution.py:629
  140.5 15.9 %collective-permute-start.7 = (bf16[512,512]{1,0:T(8,128)(2,1)S(1)}, bf16[512,512]{1,0:T(8,128)(2,1)S(1)}, u32[]{:S(2)}, u32[]{:S(2)}) collective-permute-start(bf16[512,512]{1,0:T(8,128)(2,1)S(1)} %get-tuple-element.33), channel_id=1, source_target_pairs={{0,8},{2,10},{4,12},{6,14},{1,9},{3,11},{5,13},{7,15}} | collective-permute-start | bytes 1572872 | tf_op jit(solution)/shard_map/ppermute | solution.py:661
  141.8 14.8 %collective-permute-start.12 = (bf16[512,512]{1,0:T(8,128)(2,1)S(1)}, bf16[512,512]{1,0:T(8,128)(2,1)S(1)}, u32[]{:S(2)}, u32[]{:S(2)}) collective-permute-start(bf16[512,512]{1,0:T(8,128)(2,1)S(1)} %hop_add.7.refs_5_), channel_id=1, source_target_pairs={{8,16},{10,18},{12,20},{14,22},{9,17},{11,19},{13,21},{15,23}} | collective-permute-start | bytes 1572872 | tf_op jit(solution)/shard_map/ppermute | solution.py:661
  143.2 13.6 %collective-permute-start.21 = (bf16[1,512,512]{2,1,0:T(8,128)(2,1)S(1)}, bf16[1,512,512]{2,1,0:T(8,128)(2,1)S(1)}, u32[]{:S(2)}, u32[]{:S(2)}) collective-permute-start(bf16[1,512,512]{2,1,0:T(8,128)(2,1)S(1)} %collective-permute-done.13.refs_0_.refs_3_.refs_13_), channel_id=1, source_target_pairs={{9,1},{11,3},{13,5},{15,7},{17,9},{19,11},{21,13},{23,15},{25,17},... | collective-permute-start | bytes 1572872 | tf_op jit(solution)/shard_map/ppermute | solution.py:634
  169.5 45.4 %copy-start.14 = (f32[4]{0:T(128)S(1)}, f32[4]{0:T(128)}, u32[]{:S(2)}) copy-start(f32[4]{0:T(128)} %param.12) | copy-start | bytes 52
  169.5 46.8 %copy-start.6 = (bf16[512,1,3,512]{3,0,2,1:T(8,128)(2,1)S(1)}, bf16[512,1,3,512]{3,0,2,1:T(8,128)(2,1)}, u32[]{:S(2)}) copy-start(bf16[512,1,3,512]{3,0,2,1:T(8,128)(2,1)} %copy.22) | copy-start | bytes 4718596
  169.5 46.7 %collective-permute-start.23 = (bf16[4,512,512]{2,1,0:T(8,128)(2,1)S(1)}, bf16[4,512,512]{2,1,0:T(8,128)(2,1)S(1)}, u32[]{:S(2)}, u32[]{:S(2)}) collective-permute-start(bf16[4,512,512]{2,1,0:T(8,128)(2,1)S(1)} %get-tuple-element.42.refs_0_.refs_20_), channel_id=1, source_target_pairs={{1,9},{3,11},{5,13},{7,15},{9,17},{11,19},{13,21},{15,23},{17,25},... | collective-permute-start | bytes 6291464 | tf_op jit(solution)/shard_map/ppermute | solution.py:629
  172.1 37.2 %collective-permute-start.16 = (bf16[512,512]{1,0:T(8,128)(2,1)S(1)}, bf16[512,512]{1,0:T(8,128)(2,1)S(1)}, u32[]{:S(2)}, u32[]{:S(2)}) collective-permute-start(bf16[512,512]{1,0:T(8,128)(2,1)S(1)} %hop_add.9.refs_0_), channel_id=1, source_target_pairs={{8,16},{10,18},{12,20},{14,22},{9,17},{11,19},{13,21},{15,23}} | collective-permute-start | bytes 1572872 | tf_op jit(solution)/shard_map/ppermute | solution.py:661
  174.1 42.2 %collective-permute-start.18 = (bf16[512,512]{1,0:T(8,128)(2,1)S(1)}, bf16[512,512]{1,0:T(8,128)(2,1)S(1)}, u32[]{:S(2)}, u32[]{:S(2)}) collective-permute-start(bf16[512,512]{1,0:T(8,128)(2,1)S(1)} %hop_add.10.refs_16_), channel_id=1, source_target_pairs={{16,24},{18,26},{20,28},{22,30},{17,25},{19,27},{21,29},{23,31}} | collective-permute-start | bytes 1572872 | tf_op jit(solution)/shard_map/ppermute | solution.py:661
  174.8 41.5 %collective-permute-start.17 = (bf16[512,512]{1,0:T(8,128)(2,1)S(1)}, bf16[512,512]{1,0:T(8,128)(2,1)S(1)}, u32[]{:S(2)}, u32[]{:S(2)}) collective-permute-start(bf16[512,512]{1,0:T(8,128)(2,1)S(1)} %hop_add.8.refs_0_), channel_id=1, source_target_pairs={{16,24},{18,26},{20,28},{22,30},{17,25},{19,27},{21,29},{23,31}} | collective-permute-start | bytes 1572872 | tf_op jit(solution)/shard_map/ppermute | solution.py:661
  209.5 6.8 %collective-permute-start.22 = (bf16[512,512]{1,0:T(8,128)(2,1)S(1)}, bf16[512,512]{1,0:T(8,128)(2,1)S(1)}, u32[]{:S(2)}, u32[]{:S(2)}) collective-permute-start(bf16[512,512]{1,0:T(8,128)(2,1)S(1)} %hop_add.11), channel_id=1, source_target_pairs={{16,24},{18,26},{20,28},{22,30},{17,25},{19,27},{21,29},{23,31}} | collective-permute-start | bytes 1572872 | tf_op jit(solution)/shard_map/ppermute | solution.py:661
  210.2 6.1 %collective-permute-start.24 = (f32[4,8,512]{2,1,0:T(8,128)S(1)}, f32[4,8,512]{2,1,0:T(8,128)S(1)}, u32[]{:S(2)}, u32[]{:S(2)}) collective-permute-start(f32[4,8,512]{2,1,0:T(8,128)S(1)} %get-tuple-element.46.refs_21_), channel_id=1, source_target_pairs={{1,9},{3,11},{5,13},{7,15},{9,17},{11,19},{13,21},{15,23},{17,25},... | collective-permute-start | bytes 196616 | tf_op jit(solution)/shard_map/ppermute | solution.py:629
  228.8 18.0 %copy-start.12 = (f32[4,512]{1,0:T(4,128)S(1)}, f32[4,512]{1,0:T(4,128)}, u32[]{:S(2)}) copy-start(f32[4,512]{1,0:T(4,128)} %param.13) | copy-start | bytes 24580
  228.8 66.2 %all-to-all-start.1 = ((bf16[16,4,32,512]{3,2,1,0:T(8,128)(2,1)}), bf16[16,4,32,512]{3,2,1,0:T(8,128)(2,1)S(1)}, u32[]{:S(2)}, u32[]{:S(2)}) async-start(bf16[16,4,32,512]{3,2,1,0:T(8,128)(2,1)} %copy-done.7), calls=%async_computation.1 | async-start | bytes 4194304 | tf_op jit(solution)/shard_map/all_to_all | solution.py:702
  (10 other events, 33.1 us)

commit v6 on v5

--- a/solution.py
+++ b/solution.py
@@ -125,26 +125,25 @@
 
     lax.fori_loop(0, pieces, piece, 0)
     whole = last == group
-    outs = refs[len(refs) - 4 - (4 if whole else 1) : len(refs) - 4]
-    keep = pltpu.make_async_copy(acc, outs[0], acc_sem.at[1])
-    keep.start()
-    for c, sent in enumerate(outs[1:]):
-        sent[...] = acc[c].astype(sent.dtype)
-    keep.wait()
+    out = refs[len(refs) - 5]
+    if whole:
+        out[...] = acc[...].astype(out.dtype)
+    else:
+        keep = pltpu.make_async_copy(acc, out, acc_sem.at[1])
+        keep.start()
+        keep.wait()
 
 
 def weight_sums(info, weights, pairs, first, last, carried=(), after=()):
     group = len(pairs)
     _, tok, width = pairs[0].shape
-    rows, hidden, _ = weights.shape
     pieces = last - first
     whole = last == group
     return pl.pallas_call(
         functools.partial(grad_kernel, group, tok, first, last, len(carried)),
-        out_shape=[jax.ShapeDtypeStruct(weights.shape, jnp.float32)]
-        + [jax.ShapeDtypeStruct((hidden, width), jnp.bfloat16)] * (rows * whole),
+        out_shape=jax.ShapeDtypeStruct(weights.shape, jnp.bfloat16 if whole else jnp.float32),
         in_specs=[SMEM, VMEM] + [ANY] * (pieces + len(carried) + len(after)),
-        out_specs=[ANY] + [VMEM] * (rows * whole),
+        out_specs=VMEM if whole else ANY,
         scratch_shapes=[
             pltpu.VMEM((pieces, 2, tok, width), jnp.bfloat16),
             pltpu.VMEM(weights.shape, jnp.float32),
@@ -215,7 +214,7 @@
 def own_kernel(group, tok, part, first, last, info_ref, *refs):
     count = last - first
     q_any, kv_any = refs[:count], refs[count : count + group]
-    out_ref, level_ref, onward, acc, top, norm, qbuf, kvbuf, sems, on_sem = refs[-10:]
+    out_ref, level_ref, acc, top, norm, qbuf, kvbuf, sems = refs[-8:]
     member = info_ref[1]
     copies = []
     for n in range(count):
@@ -226,8 +225,6 @@
         copy.start()
     for copy in copies:
         copy.wait()
-    pass_on = pltpu.make_async_copy(kvbuf.at[group - 1], onward, on_sem.at[0])
-    pass_on.start()
     scale = score_scale(qbuf.shape[-1])
 
     def piece(n, carry):
@@ -253,7 +250,6 @@
         return carry
 
     lax.fori_loop(0, count, piece, 0)
-    pass_on.wait()
 
 
 def soft_shapes(group, tok, width):
@@ -278,16 +274,14 @@
     count = last - first
     return pl.pallas_call(
         functools.partial(own_kernel, group, tok, part, first, last),
-        out_shape=soft_shapes(count, tok, width)
-        + [jax.ShapeDtypeStruct(pairs[0].shape, jnp.bfloat16)],
+        out_shape=soft_shapes(count, tok, width),
         in_specs=[SMEM] + [ANY] * (count + group + len(after)),
-        out_specs=[VMEM] * 2 + [ANY],
+        out_specs=[VMEM] * 2,
         scratch_shapes=soft_scratch(tok, width)
         + [
             pltpu.VMEM((count, tok, width), jnp.bfloat16),
             pltpu.VMEM((group, 2, tok, width), jnp.bfloat16),
             pltpu.SemaphoreType.DMA((2, group)),
-            pltpu.SemaphoreType.DMA((1,)),
         ],
         compiler_params=params(28),
         name="own_attention",
@@ -311,21 +305,21 @@
     return pltpu.make_async_copy(first, into, sem)
 
 
-def cross_kernel(group, tok, behind, part, lending, info_ref, *refs):
-    pieces = behind * group
-    q_any, refs = refs[:group], refs[group:]
+def cross_kernel(group, tok, behind, part, lending, first, last, info_ref, *refs):
+    pieces, count = behind * group, last - first
+    q_any, refs = refs[:count], refs[count:]
     kv_any, refs = refs[:pieces], refs[pieces:]
-    lent_q, lent_kv = [None] * group, [None] * pieces
+    lent_q, lent_kv = [None] * count, [None] * pieces
     if lending:
-        lent_q, lent_kv, refs = refs[:group], refs[group : 2 * group], refs[2 * group :]
+        lent_q, lent_kv, refs = refs[:count], refs[count : count + group], refs[count + group :]
     out_ref, level_ref, acc, top, norm, qbuf, kvbuf, sems, kv_sems = refs[-9:]
     plane, member, lends, planes = info_ref[0], info_ref[1], info_ref[3], info_ref[4]
     copies = [
         pick_copy(lends, kv_any[at], lent_kv[at], kvbuf.at[at], kv_sems.at[at])
         for at in range(pieces)
     ]
-    for d in range(group):
-        copies.append(pick_copy(lends, q_any[d], lent_q[d], qbuf.at[pl.ds(d, 1)], sems.at[d]))
+    for n in range(count):
+        copies.append(pick_copy(lends, q_any[n], lent_q[n], qbuf.at[pl.ds(n, 1)], sems.at[n]))
     for copy in copies:
         copy.wait()
     scale = score_scale(qbuf.shape[-1])
@@ -333,7 +327,8 @@
     if lending:
         valid = jnp.where(lends == 0, valid, jnp.where(plane + 1 < planes, 0, pieces))
 
-    def piece(d, carry):
+    def piece(n, carry):
+        d = first + n
         at = member ^ d
 
         @pl.when(at >= valid)
@@ -342,7 +337,7 @@
             for r in range(0, tok, part):
                 where, keys = pl.ds(r, part), pl.ds(r, tok - r)
                 mask = triangle(part, tok - r, r, r, False)
-                parts.append((where, qbuf[d, where], kvbuf[d, 0, keys], kvbuf[d, 1, keys], mask))
+                parts.append((where, qbuf[n, where], kvbuf[d, 0, keys], kvbuf[d, 1, keys], mask))
             soft_steps(parts, scale, True, acc, top, norm)
 
         @pl.when(at < valid)
@@ -356,88 +351,70 @@
             parts = []
             for r in range(0, tok, part):
                 where = pl.ds(r, part)
-                parts.append((where, qbuf[d, where], kvbuf[e, 0], kvbuf[e, 1], None))
+                parts.append((where, qbuf[n, where], kvbuf[e, 0], kvbuf[e, 1], None))
             soft_steps(parts, scale, False, acc, top, norm)
             return carry
 
         lax.fori_loop(jnp.maximum(at + 1, valid), pieces, later, 0)
-        soft_close(scale, acc, top, norm, out_ref.at[d], level_ref.at[d])
+        soft_close(scale, acc, top, norm, out_ref.at[n], level_ref.at[n])
         return carry
 
-    lax.fori_loop(0, group, piece, 0)
-
-
-def cross_attention(info, queries, earlier, lent, after=()):
+    lax.fori_loop(0, count, piece, 0)
+
+
+def cross_attention(info, queries, earlier, lent, pairs, first, last, after=()):
     group = len(queries)
     _, tok, width = queries[0].shape
     behind = len(earlier) // group
     part = min(256, tok)
+    count = last - first
+    others = lent[first:last] + pairs if lent else []
     return pl.pallas_call(
-        functools.partial(cross_kernel, group, tok, behind, part, len(lent)),
-        out_shape=soft_shapes(group, tok, width),
-        in_specs=[SMEM] + [ANY] * (group + len(earlier) + len(lent) + len(after)),
+        functools.partial(cross_kernel, group, tok, behind, part, len(lent), first, last),
+        out_shape=soft_shapes(count, tok, width),
+        in_specs=[SMEM] + [ANY] * (count + len(earlier) + len(others) + len(after)),
         out_specs=[VMEM] * 2,
         scratch_shapes=soft_scratch(tok, width)
         + [
-            pltpu.VMEM((group, tok, width), jnp.bfloat16),
+            pltpu.VMEM((count, tok, width), jnp.bfloat16),
             pltpu.VMEM((behind * group, 2, tok, width), jnp.bfloat16),
-            pltpu.SemaphoreType.DMA((group,)),
+            pltpu.SemaphoreType.DMA((count,)),
             pltpu.SemaphoreType.DMA((behind * group,)),
         ],
         compiler_params=params(28),
         name="cross_attention",
-    )(info, *queries, *earlier, *lent, *after)
-
-
-def finish_kernel(group, tok, count, hops, lending, cuts, info_ref, rate_ref, w_ref, place_ref, *refs):
-    own_any, refs = refs[0], refs[1:]
-    came, refs = refs[: 3 * hops], refs[3 * hops :]
+    )(info, *queries[first:last], *earlier, *others, *after)
+
+
+def finish_kernel(
+    group, tok, count, lending, cuts, cross_cuts, info_ref, rate_ref, w_ref, place_ref, sum_ref, *refs
+):
     q_any, refs = refs[:group], refs[group:]
     own_parts, refs = refs[: 2 * len(cuts)], refs[2 * len(cuts) :]
-    cross_any, cross_level = refs[:2]
-    lent_any, lent_level = refs[2:4] if lending else (None, None)
-    out_ref, new_w, sums, cbuf, qbuf, obuf, xbuf, lbuf, sems, q_sems, own_sems = refs[-11:]
+    cross_parts, refs = refs[: 2 * len(cross_cuts)], refs[2 * len(cross_cuts) :]
+    lent_parts = refs[: 2 * len(cross_cuts)] if lending else [None] * 2 * len(cross_cuts)
+    out_ref, new_w, qbuf, obuf, xbuf, lbuf, q_sems, own_sems, cross_sems = refs[-9:]
     plane, member, first_len, lends = info_ref[0], info_ref[1], info_ref[2], info_ref[3]
-    own_copy = pltpu.make_async_copy(own_any, sums, sems.at[0])
-    own_copy.start()
-
-    def came_copy(hop, c):
-        return pltpu.make_async_copy(came[3 * hop + c], cbuf.at[c], sems.at[1 + c])
-
-    for hop in range(hops):
-
-        @pl.when(plane == hop + 1)
-        def _():
-            for c in range(3):
-                came_copy(hop, c).start()
-
-    if hops:
-
-        @pl.when((plane == 0) | (plane > hops))
-        def _():
-            cbuf[...] = jnp.zeros_like(cbuf)
-
-    level_copies = [pick_copy(lends, cross_level, lent_level, lbuf.at[1], sems.at[5])]
-    row_copies = [pick_copy(lends, cross_any, lent_any, xbuf, sems.at[7])]
+    copies = []
+    for d in range(group):
+        copies.append(pltpu.make_async_copy(q_any[d], qbuf.at[pl.ds(d, 1)], q_sems.at[d]))
     for n, (first, last) in enumerate(cuts):
         into = pl.ds(first, last - first)
         rows, level = own_parts[2 * n], own_parts[2 * n + 1]
-        row_copies.append(pltpu.make_async_copy(rows, obuf.at[into], own_sems.at[0, n]))
-        level_copies.append(pltpu.make_async_copy(level, lbuf.at[0, into], own_sems.at[1, n]))
-        row_copies[-1].start()
-        level_copies[-1].start()
-    q_copies = [
-        pltpu.make_async_copy(q_any[d], qbuf.at[pl.ds(d, 1)], q_sems.at[d]) for d in range(group)
-    ]
-    for copy in q_copies:
+        copies.append(pltpu.make_async_copy(level, lbuf.at[0, into], own_sems.at[1, n]))
+        copies.append(pltpu.make_async_copy(rows, obuf.at[into], own_sems.at[0, n]))
+    for copy in copies:
         copy.start()
-    own_copy.wait()
-    if hops:
-
-        @pl.when((plane > 0) & (plane <= hops))
-        def _():
-            for c in range(3):
-                came_copy(0, c).wait()
+    for n, (first, last) in enumerate(cross_cuts):
+        into, rows, level = pl.ds(first, last - first), 2 * n, 2 * n + 1
+        copies.append(
+            pick_copy(
+                lends, cross_parts[level], lent_parts[level], lbuf.at[1, into], cross_sems.at[1, n]
+            )
+        )
+        copies.append(
+            pick_copy(lends, cross_parts[rows], lent_parts[rows], xbuf.at[into], cross_sems.at[0, n])
+        )
 
     step = rate_ref[0] / first_len.astype(jnp.float32)
 
@@ -445,15 +422,12 @@
     def _():
         for c in range(3):
             previous = w_ref[c].astype(jnp.float32)
-            summed = sums[c]
-            if hops:
-                summed = summed + cbuf[c].astype(jnp.float32)
-            updated = previous + step * summed
+            updated = previous + step * sum_ref[c].astype(jnp.float32)
             old_norm = jnp.sqrt(jnp.sum(previous * previous, axis=1, keepdims=True) + eps)
             new_norm = jnp.sqrt(jnp.sum(updated * updated, axis=1, keepdims=True) + eps)
             new_w[c] = (updated * (old_norm / new_norm)).astype(new_w.dtype)
 
-    for copy in q_copies + level_copies + row_copies:
+    for copy in copies:
         copy.wait()
 
     def apply(rows, weights):
@@ -500,34 +474,30 @@
 
 
 def finish_rows(
-    info, rate, weights, places, own, came, queries, cuts, own_parts, cross_part, lent, count
+    info, rate, weights, places, sums, queries, cuts, own_parts, cross_cuts, cross_parts, lent, count
 ):
     group = len(queries)
     _, tok, width = queries[0].shape
-    hidden = weights.shape[1]
-    hops = len(came) // 3
     return pl.pallas_call(
-        functools.partial(finish_kernel, group, tok, count, hops, len(lent), cuts),
+        functools.partial(finish_kernel, group, tok, count, len(lent), cuts, cross_cuts),
         out_shape=jax.ShapeDtypeStruct((count, group, tok // count, width), jnp.bfloat16),
-        in_specs=[SMEM] * 2 + [VMEM] * 2 + [ANY] * (
-            1 + 3 * hops + group + len(own_parts) + 2 + len(lent)
-        ),
+        in_specs=[SMEM] * 2
+        + [VMEM] * 3
+        + [ANY] * (group + len(own_parts) + len(cross_parts) + len(lent)),
         out_specs=VMEM,
         scratch_shapes=[
-            pltpu.VMEM(weights.shape, jnp.bfloat16),
-            pltpu.VMEM(weights.shape, jnp.float32),
             pltpu.VMEM(weights.shape, jnp.bfloat16),
             pltpu.VMEM((group, tok, width), jnp.bfloat16),
             pltpu.VMEM((group, tok, width), jnp.bfloat16),
             pltpu.VMEM((group, tok, width), jnp.bfloat16),
             pltpu.VMEM((2, group, 8, tok), jnp.float32),
-            pltpu.SemaphoreType.DMA((8,)),
             pltpu.SemaphoreType.DMA((group,)),
             pltpu.SemaphoreType.DMA((2, len(cuts))),
+            pltpu.SemaphoreType.DMA((2, len(cross_cuts))),
         ],
-        compiler_params=params(36),
+        compiler_params=params(30),
         name="finish_rows",
-    )(info, rate, weights, places, own, *came, *queries, *own_parts, *cross_part, *lent)
+    )(info, rate, weights, places, sums, *queries, *own_parts, *cross_parts, *lent)
 
 
 def norm_kernel(came_ref, scale_ref, gain_ref, out_ref):
@@ -552,31 +522,12 @@
     )(came, scale, gain)
 
 
-def add_kernel(c, own_any, came_ref, *refs):
-    out_ref, buf, sem = refs[-3:]
-    copy = pltpu.make_async_copy(own_any.at[c], buf, sem.at[0])
-    copy.start()
-    copy.wait()
-    out_ref[...] = (buf[...] + came_ref[...].astype(jnp.float32)).astype(out_ref.dtype)
-
-
-def hop_add(own, came, c, after=()):
-    return pl.pallas_call(
-        functools.partial(add_kernel, c),
-        out_shape=jax.ShapeDtypeStruct(came.shape, came.dtype),
-        in_specs=[ANY, VMEM] + [ANY] * len(after),
-        out_specs=VMEM,
-        scratch_shapes=[pltpu.VMEM(came.shape, jnp.float32), pltpu.SemaphoreType.DMA((1,))],
-        compiler_params=params(8),
-        name="hop_add",
-    )(own, came, *after)
-
-
 def pass_kernel(x_any, *refs):
-    out_any, sem = refs[-2:]
-    copy = pltpu.make_async_copy(x_any, out_any, sem.at[0])
-    copy.start()
-    copy.wait()
+    out_any, buf, sem = refs[-3:]
+    for source, target in ((x_any, buf), (buf, out_any)):
+        copy = pltpu.make_async_copy(source, target, sem.at[0])
+        copy.start()
+        copy.wait()
 
 
 def pass_after(value, after):
@@ -585,7 +536,8 @@
         out_shape=jax.ShapeDtypeStruct(value.shape, value.dtype),
         in_specs=[ANY] * (1 + len(after)),
         out_specs=ANY,
-        scratch_shapes=[pltpu.SemaphoreType.DMA((1,))],
+        scratch_shapes=[pltpu.VMEM(value.shape, value.dtype), pltpu.SemaphoreType.DMA((1,))],
+        compiler_params=params(8),
         name="pass_after",
     )(value, *after)
 
@@ -642,61 +594,37 @@
     last = group - 1
     pairs = trade(mine[:last] or mine, count)
     if last:
-        late = pass_after(mine[last], pairs[1:])
+        late = pass_after(mine[last], pairs[1:] + [weights, places])
         pairs = pairs + [lax.ppermute(late, "seq", swap_pairs(count, last))]
     shifts = [back * group for back in range(behind, 0, -1)]
-    near = [[across(pair, shift, 0) for pair in pairs[:last]] for shift in shifts]
-    carried = weight_sums(info, weights, pairs, 0, last) if last else []
-    waits = [array for arrays in near for array in arrays[:2]] + [places]
-    own, *sent = weight_sums(info, weights, pairs, last, group, carried, waits)
-    asked = trade(split_heads(info, [queries], [own]), count)
-    lent = [back_across(piece, 1) for piece in asked] + pairs if lending else []
-
-    chained = planes <= 8
-    hops = planes - 1 if chained else 0
-    came = {}
-
-    def hop(step, c, value):
-        sources = [(step - 1) * group + m for m in range(group)]
-        came[step, c] = lax.ppermute(value, "seq", [(a, a + group) for a in sources])
-
-    if chained:
-        for c in range(3 if hops else 0):
-            hop(1, c, sent[c])
-    else:
-        groups = [[z * group + m for z in range(planes)] for m in range(group)]
-        own = lax.psum(own.astype(jnp.bfloat16), "seq", axis_index_groups=groups)
-        own = own.astype(jnp.float32)
-    adds = [(step, c) for step in range(2, hops + 1) for c in range(3)]
-    adds.sort(key=lambda add: (sum(add), add))
+    earlier = [across(pair, shift, 0) for shift in shifts for pair in pairs]
+    carried = weight_sums(info, weights, pairs, 0, last) if last else None
+    waits = earlier[:2] if last else []
+    carried = [carried] if last else []
+    sums = weight_sums(info, weights, pairs, last, group, carried, waits)
+    asked = split_heads(info, [queries], [sums])
+    groups = [[z * group + m for z in range(planes)] for m in range(group)]
+    sums = lax.psum(sums, "seq", axis_index_groups=groups)
+    asked = trade(asked, count)
+    lent = [back_across(piece, 1) for piece in asked] if lending else []
+
     cuts = [cut for cut in ((0, 1), (1, last), (max(1, last), group)) if cut[1] > cut[0]]
-    work = [("own", cuts[0])]
-    for n in range(max(len(adds), len(cuts) - 1)):
-        work.extend([("add", add) for add in adds[n : n + 1]])
-        work.extend([("own", cut) for cut in cuts[n + 1 : n + 2]])
-    work.insert(len(work) - 1 if adds else len(work), ("cross", None))
-    own_parts, cross_part, token, earlier = [], None, [own], []
-    for kind, what in work:
-        if kind == "add":
-            added = hop_add(own, came[what[0] - 1, what[1]], what[1], token)
-            hop(*what, added)
-            token = [added]
-        elif kind == "own":
-            begun = len(own_parts) // 2
-            ready = lent[cuts[begun - 1][0] : cuts[begun - 1][1]] if lending and begun else []
-            rows, level, onward = own_attention(info, asked, pairs, *what, token + ready)
-            if not own_parts:
-                for arrays, shift in zip(near, shifts):
-                    earlier.extend(arrays + [across(onward, shift, 0)])
-            own_parts.extend([rows, level])
-            token = [rows]
-        else:
-            cross_part = cross_attention(info, asked, earlier, lent, token)
-            token = [cross_part[0]]
-    lent_part = [across(value, group, 1) for value in cross_part] if lending else []
-    arrived = [came[step, c] for step in range(1, hops + 1) for c in range(3)]
+    cross_cuts = [(0, group)]
+    own_parts, cross_parts, lent_parts, token = [], [], [], []
+    for n, (first, end) in enumerate(cuts):
+        if n and lending:
+            token = token + lent[cuts[n - 1][0] : cuts[n - 1][1]]
+        rows, level = own_attention(info, asked, pairs, first, end, token)
+        own_parts.extend([rows, level])
+        token = [rows] + (earlier[2:3] if n == 0 else [])
+    for first, end in cross_cuts:
+        rows, level = cross_attention(info, asked, earlier, lent, pairs, first, end, token)
+        cross_parts.extend([rows, level])
+        token = [rows]
+        if lending:
+            lent_parts.extend([across(rows, group, 1), across(level, group, 1)])
     leaving = finish_rows(
-        info, rate, weights, places, own, arrived, asked, cuts, own_parts, cross_part, lent_part, count
+        info, rate, weights, places, sums, asked, cuts, own_parts, cross_cuts, cross_parts, lent_parts, count
     )
 
     came = lax.all_to_all(leaving, "seq", split_axis=0, concat_axis=0, tiled=True)

time: 303 us -> 307 us (1.013)
  waiting for transfers between devices: 120 us -> 159 us
  Pallas kernels: 93.6 us -> 62.8 us
  starting transfers between devices: 65.2 us -> 35.8 us
  local copies, waits for them, and re-layouts: 17.9 us -> 32 us
  between operations: 0.56 us -> 13.9 us
    ppermute x6, waiting for transfers between devices: 0.67 us -> 47.2 us  [across(): return lax.ppermute(value, ('seq', 'head'), both)]
    ppermute x9 -> x0, waiting for transfers between devices: 42.5 us -> none  [hop(): lax.ppermute(value, 'seq', [(a, a + group) for a in sources])]
    pallas_call x1, Pallas kernels: 32.9 us -> 0.15 us  [pass_after(): pl.pallas_call(pass_kernel, out_shape=jax.ShapeDtypeStruct(value.shape, v...]
    psum x0 -> x1, waiting for transfers between devices: none -> 30.8 us  [per_device(): sums = lax.psum(sums, 'seq', axis_index_groups=groups)]
    unnamed x30 -> x64, local copies, waits for them, and re-layouts: 7.88 us -> 23.2 us
    ppermute x9 -> x0, starting transfers between devices: 12.8 us -> none  [hop(): lax.ppermute(value, 'seq', [(a, a + group) for a in sources])]
    all_to_all x1, starting transfers between devices: 18 us -> 6.87 us  [per_device(): lax.all_to_all(leaving, 'seq', split_axis=0, concat_axis=0, tiled=True)]
    ppermute x1, waiting for transfers between devices: 0.01 us -> 10.7 us  [per_device(): pairs = pairs + [lax.ppermute(late, 'seq', swap_pairs(count, last))]]
  transfers between devices with their start and end apart: 27 -> 19, of which waited for: 8 -> 7; matrix products, arithmetic and copies ran while one was open for 3% -> 3% of each run, Pallas kernels for 20% -> 10%
where the time goes in v6:
time: 307 us
  waiting for transfers between devices  159 us (52%)
  Pallas kernels  62.8 us (20%)
  starting transfers between devices  35.8 us (12%)
  local copies, waits for them, and re-layouts  32 us (10%)
  between operations  13.9 us (5%)
  blocking collectives  3.57 us (1%)
    all_to_all x1, waiting for transfers between devices, per_device(): lax.all_to_all(leaving, 'seq', split_axis=0, concat_axis=0, tiled=True)  47.9 us
    ppermute x6, waiting for transfers between devices, across(): return lax.ppermute(value, ('seq', 'head'), both)  47.2 us
    psum x1, waiting for transfers between devices, per_device(): sums = lax.psum(sums, 'seq', axis_index_groups=groups)  30.8 us
    unnamed x64, local copies, waits for them, and re-layouts  23.2 us
    pallas_call x3, Pallas kernels, own_attention(): pl.pallas_call(functools.partial(own_kernel, group, tok, part, first, las...  17.4 us
    pallas_call x1, Pallas kernels, cross_attention(): pl.pallas_call(functools.partial(cross_kernel, group, tok, behind, part,...  14.1 us
    pallas_call x2, Pallas kernels, weight_sums(): pl.pallas_call(functools.partial(grad_kernel, group, tok, first, last, le...  13.2 us
    ppermute x5, waiting for transfers between devices, trade(): lax.ppermute(piece, 'seq', swap_pairs(count, d))  12.5 us
  transfers between devices with their start and end apart: 19, of which 7 were waited for; matrix products, arithmetic and copies ran while one was open for 3% of the time, Pallas kernels for 10%

profile of v6, /device:TPU:13, one launch (start us, length us, event | category | flops | bytes accessed | tf_op | source)
XLA Modules:
  0.0 307.1 jit_solution(16077642975428997163)
XLA Ops:
  7.3 1.6 copy-done.18
  8.9 1.6 copy-done.19
  10.4 3.2 %split_heads.2 = (bf16[2,512,512]{2,1,0:T(8,128)(2,1)}, bf16[2,512,512]{2,1,0:T(8,128)(2,1)}, bf16[2,512,512]{2,1,0:T(8,128)(2,1)}, bf16[2,512,512]{2,1,0:T(8,128)(2,1)S(1)}) custom-call(s32[5]{0:T(128)S(1)} %stack.15.info_ref, bf16[512,4,512]{2,1,0:T(4,128)(2,1)S(1)} %copy-done.18, bf16[512,4,512]{2,1,0:T(4,128)(2,1)S(1)} %copy-done.19), custom_call_target="tpu_custom_call" | custom-call | tf_op jit(solution)/shard_map/split_heads/pallas_call | solution.py:61
  16.7 5.7 %all-to-all-start = ((s32[16,1,128]{2,1,0:T(1,128)}), s32[16,1,128]{2,1,0:T(1,128)S(1)}, u32[]{:S(2)}, u32[]{:S(2)}) async-start(s32[16,1,128]{2,1,0:T(1,128)} %bitcast.6), calls=%async_computation | async-start | bytes 16384 | tf_op jit(solution)/shard_map/all_to_all | solution.py:556
  22.5 1.6 collective-permute-start.3
  24.1 6.0 %constant_dynamic-slice_fusion = bf16[512,1,3,512]{3,1,2,0:T(2,128)(2,1)S(1)} fusion(bf16[512,4,3,512]{3,1,2,0:T(4,128)(2,1)} %param.11, s32[]{:T(128)S(6)} %select_n.29), kind=kLoop, calls=%fused_computation.9 | loop fusion | bytes 3145732 | tf_op jit(solution)/shard_map/jit(dynamic_index_in_dim)/dynamic_slice | solution.py:589
  30.6 9.4 %all-to-all-done = s32[16,1,128]{2,1,0:T(1,128)S(1)} async-done(((s32[16,1,128]{2,1,0:T(1,128)}), s32[16,1,128]{2,1,0:T(1,128)S(1)}, u32[]{:S(2)}, u32[]{:S(2)}) %all-to-all-start) | async-done | bytes 8224 | tf_op jit(solution)/shard_map/all_to_all | solution.py:556
  43.2 1.7 collective-permute-start.8
  44.9 9.8 %weight_sums.2.refs_1_ = f32[3,512,512]{2,1,0:T(8,128)S(1)} custom-call(s32[5]{0:T(128)S(1)} %stack.15.info_ref, bf16[3,512,512]{2,1,0:T(8,128)(2,1)S(1)} %bitcast.17, bf16[2,512,512]{2,1,0:T(8,128)(2,1)} %get-tuple-element.24.refs_0_.refs_1_.refs_2_.refs_12_, bf16[2,512,512]{2,1,0:T(8,128)(2,1)S(1)} %collective-permute-done.refs_0_.refs_1_.refs_2_.refs_3_.refs_13_, ...), custom_call_target="tpu_custom_call" | custom-call | tf_op jit(solution)/shard_map/weight_sums/pallas_call | solution.py:142
  54.7 10.7 %collective-permute-done.2.refs_0_.refs_4_.refs_5_.refs_15_ = bf16[2,512,512]{2,1,0:T(8,128)(2,1)S(1)} collective-permute-done((bf16[2,512,512]{2,1,0:T(8,128)(2,1)S(1)}, bf16[2,512,512]{2,1,0:T(8,128)(2,1)S(1)}, u32[]{:S(2)}, u32[]{:S(2)}) %collective-permute-start.2) | collective-permute-done | bytes 1048608 | tf_op jit(solution)/shard_map/ppermute | solution.py:598
  65.4 3.5 %weight_sums.3.refs_1_ = bf16[3,512,512]{2,1,0:T(8,128)(2,1)S(1)} custom-call(s32[5]{0:T(128)S(1)} %stack.15.info_ref, bf16[3,512,512]{2,1,0:T(8,128)(2,1)S(1)} %bitcast.18, bf16[2,512,512]{2,1,0:T(8,128)(2,1)S(1)} %collective-permute-done.2.refs_0_.refs_4_.refs_5_.refs_15_, f32[3,512,512]{2,1,0:T(8,128)S(1)} %weight_sums.2.refs_1_, ...), custom_call_target="tpu_custom_call" | custom-call | tf_op jit(solution)/shard_map/weight_sums/pallas_call | solution.py:142
  73.4 1.6 copy-done.20
  79.8 1.5 collective-permute-start.7
  82.0 2.1 collective-permute-start.9
  84.2 5.3 %collective-permute-done.5.refs_0_.refs_1_ = bf16[1,512,512]{2,1,0:T(8,128)(2,1)S(1)} collective-permute-done((bf16[1,512,512]{2,1,0:T(8,128)(2,1)}, bf16[1,512,512]{2,1,0:T(8,128)(2,1)S(1)}, u32[]{:S(2)}, u32[]{:S(2)}) %collective-permute-start.5) | collective-permute-done | bytes 524320 | tf_op jit(solution)/shard_map/ppermute | solution.py:77
  89.5 2.1 collective-permute-start.10
  91.6 1.9 collective-permute-start.11
  93.6 7.1 %collective-permute-done.7.refs_0_.refs_3_ = bf16[1,512,512]{2,1,0:T(8,128)(2,1)S(1)} collective-permute-done((bf16[1,512,512]{2,1,0:T(8,128)(2,1)}, bf16[1,512,512]{2,1,0:T(8,128)(2,1)S(1)}, u32[]{:S(2)}, u32[]{:S(2)}) %collective-permute-start.7) | collective-permute-done | bytes 524320 | tf_op jit(solution)/shard_map/ppermute | solution.py:77
  100.7 2.1 collective-permute-start.13
  104.0 5.4 %own_attention.3 = (bf16[1,512,512]{2,1,0:T(8,128)(2,1)S(1)}, f32[1,8,512]{2,1,0:T(8,128)S(1)}) custom-call(s32[5]{0:T(128)S(1)} %stack.15.info_ref, bf16[1,512,512]{2,1,0:T(8,128)(2,1)S(1)} %get-tuple-element.25.refs_0_, bf16[2,512,512]{2,1,0:T(8,128)(2,1)} %get-tuple-element.24.refs_0_.refs_1_.refs_2_.refs_12_, ...), custom_call_target="tpu_custom_call" | custom-call | tf_op jit(solution)/shard_map/own_attention/pallas_call | solution.py:275
  109.5 7.6 %own_attention.4 = (bf16[2,512,512]{2,1,0:T(8,128)(2,1)S(1)}, f32[2,8,512]{2,1,0:T(8,128)S(1)}) custom-call(s32[5]{0:T(128)S(1)} %stack.15.info_ref, bf16[1,512,512]{2,1,0:T(8,128)(2,1)S(1)} %collective-permute-done.5.refs_0_.refs_1_, bf16[1,512,512]{2,1,0:T(8,128)(2,1)S(1)} %collective-permute-done.6.refs_1_.refs_2_, ...), custom_call_target="tpu_custom_call" | custom-call | tf_op jit(solution)/shard_map/own_attention/pallas_call | solution.py:275
  117.1 4.4 %own_attention.5 = (bf16[1,512,512]{2,1,0:T(8,128)(2,1)S(1)}, f32[1,8,512]{2,1,0:T(8,128)S(1)}) custom-call(s32[5]{0:T(128)S(1)} %stack.15.info_ref, bf16[1,512,512]{2,1,0:T(8,128)(2,1)S(1)} %collective-permute-done.7.refs_0_.refs_3_, bf16[2,512,512]{2,1,0:T(8,128)(2,1)} %get-tuple-element.24.refs_0_.refs_1_.refs_2_.refs_12_, ...), custom_call_target="tpu_custom_call" | custom-call | tf_op jit(solution)/shard_map/own_attention/pallas_call | solution.py:275
  121.6 14.1 %cross_attention.1 = (bf16[4,512,512]{2,1,0:T(8,128)(2,1)}, f32[4,8,512]{2,1,0:T(8,128)S(1)}) custom-call(s32[5]{0:T(128)S(1)} %stack.15.info_ref, bf16[1,512,512]{2,1,0:T(8,128)(2,1)S(1)} %get-tuple-element.25.refs_0_, bf16[1,512,512]{2,1,0:T(8,128)(2,1)S(1)} %collective-permute-done.5.refs_0_.refs_1_, ...), custom_call_target="tpu_custom_call" | custom-call | tf_op jit(solution)/shard_map/cross_attention/pallas_call | solution.py:372
  135.7 3.3 %collective-permute-start.14 = (bf16[4,512,512]{2,1,0:T(8,128)(2,1)}, bf16[4,512,512]{2,1,0:T(8,128)(2,1)}, u32[]{:S(2)}, u32[]{:S(2)}) collective-permute-start(bf16[4,512,512]{2,1,0:T(8,128)(2,1)} %get-tuple-element.35.refs_10_), channel_id=1, source_target_pairs={{1,9},{3,11},{5,13},{7,15},{9,17},{11,19},{13,21},{15,23},{17,25},... | collective-permute-start | bytes 6291464 | tf_op jit(solution)/shard_map/ppermute | solution.py:581
  139.1 1.9 collective-permute-start.15
  141.6 47.2 %collective-permute-done.15.refs_13_ = f32[4,8,512]{2,1,0:T(8,128)S(1)} collective-permute-done((f32[4,8,512]{2,1,0:T(8,128)S(1)}, f32[4,8,512]{2,1,0:T(8,128)S(1)}, u32[]{:S(2)}, u32[]{:S(2)}) %collective-permute-start.15) | collective-permute-done | bytes 65568 | tf_op jit(solution)/shard_map/ppermute | solution.py:581
  188.8 30.8 %all-reduce.2.cloned.1.call-done.sum_ref = bf16[3,512,512]{2,1,0:T(8,128)(2,1)} async-done(((bf16[3,512,512]{2,1,0:T(8,128)(2,1)}), bf16[3,512,512]{2,1,0:T(8,128)(2,1)}) %all-reduce.2.cloned.1.call-update) | async-done | bytes 1572880 | tf_op jit(solution)/shard_map/psum | solution.py:607
  226.3 11.1 %finish_rows.1 = bf16[16,4,32,512]{3,2,1,0:T(8,128)(2,1)S(1)} custom-call(s32[5]{0:T(128)S(1)} %stack.15.info_ref, f32[1]{0:T(128)} %dynamic_slice.7.rate_ref, bf16[3,512,512]{2,1,0:T(8,128)(2,1)S(1)} %bitcast.19, f32[4,8,512]{2,1,0:T(8,128)S(1)} %broadcast_in_dim.20.refs_3_.place_ref, bf16[3,512,512]{2,1,0:T(8,128)(2,1)S(1)} %copy-done.23, ...), custom_call_target="tpu_custom_call" | custom-call | tf_op jit(solution)/shard_map/finish_rows/pallas_call | solution.py:481
  238.7 6.9 %all-to-all-start.1 = ((bf16[16,4,32,512]{3,2,1,0:T(8,128)(2,1)}), bf16[16,4,32,512]{3,2,1,0:T(8,128)(2,1)S(1)}, u32[]{:S(2)}, u32[]{:S(2)}) async-start(bf16[16,4,32,512]{3,2,1,0:T(8,128)(2,1)} %copy-done.5), calls=%async_computation.1 | async-start | bytes 4194304 | tf_op jit(solution)/shard_map/all_to_all | solution.py:630
  245.6 47.9 %all-to-all-done.1 = bf16[16,4,32,512]{3,2,1,0:T(8,128)(2,1)S(1)} async-done(((bf16[16,4,32,512]{3,2,1,0:T(8,128)(2,1)}), bf16[16,4,32,512]{3,2,1,0:T(8,128)(2,1)S(1)}, u32[]{:S(2)}, u32[]{:S(2)}) %all-to-all-start.1) | async-done | bytes 2097184 | tf_op jit(solution)/shard_map/all_to_all | solution.py:630
  294.1 3.6 %psum.15 = f32[4,128]{1,0:T(4,128)S(1)} all-reduce(f32[4,128]{1,0:T(4,128)S(1)} %reduce_sum.18), channel_id=1, replica_groups=mesh['seq'=16,'head'=2] {'head'}, use_global_device_ids=true, to_apply=%region_3.4 | all-reduce | flops 512 | bytes 4096 | tf_op jit(solution)/shard_map/psum | solution.py:633
  297.8 2.5 norm_rows.1
  (100 shorter events, 28.0 us)
Async XLA Ops:
  7.3 1.6 copy-start.18
  10.4 5.7 %copy-start.30 = (s32[512]{0:T(512)S(1)}, s32[512]{0:T(512)}, u32[]{:S(2)}) copy-start(s32[512]{0:T(512)} %param.15) | copy-start | bytes 6148
  14.7 25.5 %collective-permute-start = (bf16[2,512,512]{2,1,0:T(8,128)(2,1)}, bf16[2,512,512]{2,1,0:T(8,128)(2,1)S(1)}, u32[]{:S(2)}, u32[]{:S(2)}) collective-permute-start(bf16[2,512,512]{2,1,0:T(8,128)(2,1)} %get-tuple-element.22), channel_id=1, source_target_pairs={{0,2},{2,0},{4,6},{6,4},{8,10},{10,8},{12,14},{14,12},{16,18},{18,... | collective-permute-start | bytes 3145736 | tf_op jit(solution)/shard_map/ppermute | solution.py:77
  15.9 24.3 %collective-permute-start.1 = (bf16[2,512,512]{2,1,0:T(8,128)(2,1)}, bf16[2,512,512]{2,1,0:T(8,128)(2,1)}, u32[]{:S(2)}, u32[]{:S(2)}) collective-permute-start(bf16[2,512,512]{2,1,0:T(8,128)(2,1)} %get-tuple-element.23), channel_id=1, source_target_pairs={{0,4},{2,6},{4,0},{6,2},{8,12},{10,14},{12,8},{14,10},{16,20},{18,... | collective-permute-start | bytes 3145736 | tf_op jit(solution)/shard_map/ppermute | solution.py:77
  16.7 23.3 %all-to-all-start = ((s32[16,1,128]{2,1,0:T(1,128)}), s32[16,1,128]{2,1,0:T(1,128)S(1)}, u32[]{:S(2)}, u32[]{:S(2)}) async-start(s32[16,1,128]{2,1,0:T(1,128)} %bitcast.6), calls=%async_computation | async-start | bytes 16384 | tf_op jit(solution)/shard_map/all_to_all | solution.py:556
  22.5 32.2 %collective-permute-start.3 = (bf16[2,512,512]{2,1,0:T(8,128)(2,1)}, bf16[2,512,512]{2,1,0:T(8,128)(2,1)}, u32[]{:S(2)}, u32[]{:S(2)}) collective-permute-start(bf16[2,512,512]{2,1,0:T(8,128)(2,1)} %get-tuple-element.24.refs_0_.refs_1_.refs_2_.refs_12_), channel_id=1, source_target_pairs={{0,8},{2,10},{4,12},{6,14},{8,16},{10,18},{12,20},{14,22},{16,24},... | collective-permute-start | bytes 3145736 | tf_op jit(solution)/shard_map/ppermute | solution.py:581
  41.6 23.7 %collective-permute-start.2 = (bf16[2,512,512]{2,1,0:T(8,128)(2,1)S(1)}, bf16[2,512,512]{2,1,0:T(8,128)(2,1)S(1)}, u32[]{:S(2)}, u32[]{:S(2)}) collective-permute-start(bf16[2,512,512]{2,1,0:T(8,128)(2,1)S(1)} %pass_after.1), channel_id=1, source_target_pairs={{0,6},{2,4},{4,2},{6,0},{8,14},{10,12},{12,10},{14,8},{16,22},{18,... | collective-permute-start | bytes 3145736 | tf_op jit(solution)/shard_map/ppermute | solution.py:598
  42.5 22.9 %collective-permute-start.4 = (bf16[2,512,512]{2,1,0:T(8,128)(2,1)S(1)}, bf16[2,512,512]{2,1,0:T(8,128)(2,1)S(1)}, u32[]{:S(2)}, u32[]{:S(2)}) collective-permute-start(bf16[2,512,512]{2,1,0:T(8,128)(2,1)S(1)} %collective-permute-done.refs_0_.refs_1_.refs_2_.refs_3_.refs_13_), channel_id=1, source_target_pairs={{0,8},{2,10},{4,12},{6,14},{8,16},{10,18},{12,20},{14,22},{16,24},... | collective-permute-start | bytes 3145736 | tf_op jit(solution)/shard_map/ppermute | solution.py:581
  43.2 38.8 %collective-permute-start.8 = (bf16[2,512,512]{2,1,0:T(8,128)(2,1)}, bf16[2,512,512]{2,1,0:T(8,128)(2,1)}, u32[]{:S(2)}, u32[]{:S(2)}) collective-permute-start(bf16[2,512,512]{2,1,0:T(8,128)(2,1)} %collective-permute-done.1.refs_1_.refs_2_.refs_3_.refs_4_.refs_14_), channel_id=1, source_target_pairs={{0,8},{2,10},{4,12},{6,14},{8,16},{10,18},{12,20},{14,22},{16,24},... | collective-permute-start | bytes 3145736 | tf_op jit(solution)/shard_map/ppermute | solution.py:581
  78.7 141.0 %all-reduce.2.cloned.1.call-start = ((), (), s32[]{:S(2)}) async-start(), calls=%async_computation.2 | async-start | bytes 3145728 | tf_op jit(solution)/shard_map/psum | solution.py:607
  78.7 10.8 %collective-permute-start.5 = (bf16[1,512,512]{2,1,0:T(8,128)(2,1)}, bf16[1,512,512]{2,1,0:T(8,128)(2,1)S(1)}, u32[]{:S(2)}, u32[]{:S(2)}) collective-permute-start(bf16[1,512,512]{2,1,0:T(8,128)(2,1)} %copy-done.28), channel_id=1, source_target_pairs={{0,2},{2,0},{4,6},{6,4},{8,10},{10,8},{12,14},{14,12},{16,18},{18,... | collective-permute-start | bytes 1572872 | tf_op jit(solution)/shard_map/ppermute | solution.py:77
  79.0 12.6 %collective-permute-start.6 = (bf16[1,512,512]{2,1,0:T(8,128)(2,1)}, bf16[1,512,512]{2,1,0:T(8,128)(2,1)S(1)}, u32[]{:S(2)}, u32[]{:S(2)}) collective-permute-start(bf16[1,512,512]{2,1,0:T(8,128)(2,1)} %copy-done.27), channel_id=1, source_target_pairs={{0,4},{2,6},{4,0},{6,2},{8,12},{10,14},{12,8},{14,10},{16,20},{18,... | collective-permute-start | bytes 1572872 | tf_op jit(solution)/shard_map/ppermute | solution.py:77
  79.8 20.9 %collective-permute-start.7 = (bf16[1,512,512]{2,1,0:T(8,128)(2,1)}, bf16[1,512,512]{2,1,0:T(8,128)(2,1)S(1)}, u32[]{:S(2)}, u32[]{:S(2)}) collective-permute-start(bf16[1,512,512]{2,1,0:T(8,128)(2,1)} %copy-done.26), channel_id=1, source_target_pairs={{0,6},{2,4},{4,2},{6,0},{8,14},{10,12},{12,10},{14,8},{16,22},{18,... | collective-permute-start | bytes 1572872 | tf_op jit(solution)/shard_map/ppermute | solution.py:77
  81.3 40.2 %collective-permute-start.12 = (bf16[2,512,512]{2,1,0:T(8,128)(2,1)}, bf16[2,512,512]{2,1,0:T(8,128)(2,1)S(1)}, u32[]{:S(2)}, u32[]{:S(2)}) collective-permute-start(bf16[2,512,512]{2,1,0:T(8,128)(2,1)} %copy-done), channel_id=1, source_target_pairs={{0,8},{2,10},{4,12},{6,14},{8,16},{10,18},{12,20},{14,22},{16,24},... | collective-permute-start | bytes 3145736 | tf_op jit(solution)/shard_map/ppermute | solution.py:581
  82.0 27.4 %collective-permute-start.9 = (bf16[1,512,512]{2,1,0:T(8,128)(2,1)S(1)}, bf16[1,512,512]{2,1,0:T(8,128)(2,1)S(1)}, u32[]{:S(2)}, u32[]{:S(2)}) collective-permute-start(bf16[1,512,512]{2,1,0:T(8,128)(2,1)S(1)} %get-tuple-element.25.refs_0_), channel_id=1, source_target_pairs={{9,1},{11,3},{13,5},{15,7},{17,9},{19,11},{21,13},{23,15},{25,17},... | collective-permute-start | bytes 1572872 | tf_op jit(solution)/shard_map/ppermute | solution.py:586
  89.5 32.1 %copy-start.6 = (bf16[1,512,512]{2,1,0:T(8,128)(2,1)}, bf16[1,512,512]{2,1,0:T(8,128)(2,1)S(1)}, u32[]{:S(2)}) copy-start(bf16[1,512,512]{2,1,0:T(8,128)(2,1)S(1)} %collective-permute-done.5.refs_0_.refs_1_) | copy-start | bytes 1572868
  89.5 27.6 %collective-permute-start.10 = (bf16[1,512,512]{2,1,0:T(8,128)(2,1)S(1)}, bf16[1,512,512]{2,1,0:T(8,128)(2,1)S(1)}, u32[]{:S(2)}, u32[]{:S(2)}) collective-permute-start(bf16[1,512,512]{2,1,0:T(8,128)(2,1)S(1)} %collective-permute-done.5.refs_0_.refs_1_), channel_id=1, source_target_pairs={{9,1},{11,3},{13,5},{15,7},{17,9},{19,11},{21,13},{23,15},{25,17},... | collective-permute-start | bytes 1572872 | tf_op jit(solution)/shard_map/ppermute | solution.py:586
  91.6 30.0 %copy-start.8 = (bf16[1,512,512]{2,1,0:T(8,128)(2,1)}, bf16[1,512,512]{2,1,0:T(8,128)(2,1)S(1)}, u32[]{:S(2)}) copy-start(bf16[1,512,512]{2,1,0:T(8,128)(2,1)S(1)} %collective-permute-done.6.refs_1_.refs_2_) | copy-start | bytes 1572868
  91.6 25.5 %collective-permute-start.11 = (bf16[1,512,512]{2,1,0:T(8,128)(2,1)S(1)}, bf16[1,512,512]{2,1,0:T(8,128)(2,1)S(1)}, u32[]{:S(2)}, u32[]{:S(2)}) collective-permute-start(bf16[1,512,512]{2,1,0:T(8,128)(2,1)S(1)} %collective-permute-done.6.refs_1_.refs_2_), channel_id=1, source_target_pairs={{9,1},{11,3},{13,5},{15,7},{17,9},{19,11},{21,13},{23,15},{25,17},... | collective-permute-start | bytes 1572872 | tf_op jit(solution)/shard_map/ppermute | solution.py:586
  100.7 20.9 %copy-start.10 = (bf16[1,512,512]{2,1,0:T(8,128)(2,1)}, bf16[1,512,512]{2,1,0:T(8,128)(2,1)S(1)}, u32[]{:S(2)}) copy-start(bf16[1,512,512]{2,1,0:T(8,128)(2,1)S(1)} %collective-permute-done.7.refs_0_.refs_3_) | copy-start | bytes 1572868
  100.7 20.9 %collective-permute-start.13 = (bf16[1,512,512]{2,1,0:T(8,128)(2,1)S(1)}, bf16[1,512,512]{2,1,0:T(8,128)(2,1)S(1)}, u32[]{:S(2)}, u32[]{:S(2)}) collective-permute-start(bf16[1,512,512]{2,1,0:T(8,128)(2,1)S(1)} %collective-permute-done.7.refs_0_.refs_3_), channel_id=1, source_target_pairs={{9,1},{11,3},{13,5},{15,7},{17,9},{19,11},{21,13},{23,15},{25,17},... | collective-permute-start | bytes 1572872 | tf_op jit(solution)/shard_map/ppermute | solution.py:586
  104.0 5.5 %copy-start.2 = (bf16[2,512,512]{2,1,0:T(8,128)(2,1)S(1)}, bf16[2,512,512]{2,1,0:T(8,128)(2,1)}, u32[]{:S(2)}) copy-start(bf16[2,512,512]{2,1,0:T(8,128)(2,1)} %copy-done) | copy-start | bytes 3145732
  109.5 7.6 %copy-start.21 = (bf16[1,512,512]{2,1,0:T(8,128)(2,1)}, bf16[1,512,512]{2,1,0:T(8,128)(2,1)S(1)}, u32[]{:S(2)}) copy-start(bf16[1,512,512]{2,1,0:T(8,128)(2,1)S(1)} %get-tuple-element.29.refs_6_.refs_4_) | copy-start | bytes 1572868
  117.1 4.4 %copy-start.14 = (bf16[2,512,512]{2,1,0:T(8,128)(2,1)}, bf16[2,512,512]{2,1,0:T(8,128)(2,1)S(1)}, u32[]{:S(2)}) copy-start(bf16[2,512,512]{2,1,0:T(8,128)(2,1)S(1)} %get-tuple-element.31.refs_5_.refs_6_) | copy-start | bytes 3145732
  117.1 4.5 %copy-start.13 = (bf16[2,512,512]{2,1,0:T(8,128)(2,1)S(1)}, bf16[2,512,512]{2,1,0:T(8,128)(2,1)}, u32[]{:S(2)}) copy-start(bf16[2,512,512]{2,1,0:T(8,128)(2,1)} %copy-done.12) | copy-start | bytes 3145732
  121.5 14.2 %copy-start.16 = (bf16[1,512,512]{2,1,0:T(8,128)(2,1)}, bf16[1,512,512]{2,1,0:T(8,128)(2,1)S(1)}, u32[]{:S(2)}) copy-start(bf16[1,512,512]{2,1,0:T(8,128)(2,1)S(1)} %get-tuple-element.33.refs_16_.refs_8_) | copy-start | bytes 1572868
  121.6 19.4 %copy-start.31 = (f32[4]{0:T(128)S(1)}, f32[4]{0:T(128)}, u32[]{:S(2)}) copy-start(f32[4]{0:T(128)} %param.12) | copy-start | bytes 52
  135.7 84.0 %copy-start.15 = (bf16[2,512,512]{2,1,0:T(8,128)(2,1)S(1)}, bf16[2,512,512]{2,1,0:T(8,128)(2,1)}, u32[]{:S(2)}) copy-start(bf16[2,512,512]{2,1,0:T(8,128)(2,1)} %copy-done.14) | copy-start | bytes 3145732
  135.7 84.0 %collective-permute-start.14 = (bf16[4,512,512]{2,1,0:T(8,128)(2,1)}, bf16[4,512,512]{2,1,0:T(8,128)(2,1)}, u32[]{:S(2)}, u32[]{:S(2)}) collective-permute-start(bf16[4,512,512]{2,1,0:T(8,128)(2,1)} %get-tuple-element.35.refs_10_), channel_id=1, source_target_pairs={{1,9},{3,11},{5,13},{7,15},{9,17},{11,19},{13,21},{15,23},{17,25},... | collective-permute-start | bytes 6291464 | tf_op jit(solution)/shard_map/ppermute | solution.py:581
  139.1 49.8 %collective-permute-start.15 = (f32[4,8,512]{2,1,0:T(8,128)S(1)}, f32[4,8,512]{2,1,0:T(8,128)S(1)}, u32[]{:S(2)}, u32[]{:S(2)}) collective-permute-start(f32[4,8,512]{2,1,0:T(8,128)S(1)} %get-tuple-element.36.refs_11_), channel_id=1, source_target_pairs={{1,9},{3,11},{5,13},{7,15},{9,17},{11,19},{13,21},{15,23},{17,25},... | collective-permute-start | bytes 196616 | tf_op jit(solution)/shard_map/ppermute | solution.py:581
  238.7 6.9 %copy-start.29 = (f32[4,512]{1,0:T(4,128)S(1)}, f32[4,512]{1,0:T(4,128)}, u32[]{:S(2)}) copy-start(f32[4,512]{1,0:T(4,128)} %param.13) | copy-start | bytes 24580
  238.7 54.8 %all-to-all-start.1 = ((bf16[16,4,32,512]{3,2,1,0:T(8,128)(2,1)}), bf16[16,4,32,512]{3,2,1,0:T(8,128)(2,1)S(1)}, u32[]{:S(2)}, u32[]{:S(2)}) async-start(bf16[16,4,32,512]{3,2,1,0:T(8,128)(2,1)} %copy-done.5), calls=%async_computation.1 | async-start | bytes 4194304 | tf_op jit(solution)/shard_map/all_to_all | solution.py:630
  (19 other events, 21.6 us)
Sparse Core Ops, SparseCore 0:
  139.2 80.4 all-reduce.1

commit v7 on v6

v7 whole, which is shorter than its diff:
```python
import functools
import math

import jax
import jax.numpy as jnp
from jax import lax
from jax.experimental import pallas as pl
from jax.experimental.pallas import tpu as pltpu
from jax.sharding import PartitionSpec as P

WINDOW = 2048
NEG = -1e30
MIB = 1024 * 1024

eps = 1e-06

NT = (((1,), (1,)), ((), ()))
TN = (((0,), (0,)), ((), ()))
NN = (((1,), (0,)), ((), ()))

ANY = pl.BlockSpec(memory_space=pl.ANY)
SMEM = pl.BlockSpec(memory_space=pltpu.SMEM)
VMEM = pl.BlockSpec(memory_space=pltpu.VMEM)


def dot(left, right, dims):
    return lax.dot_general(left, right, dims, preferred_element_type=jnp.float32)


def params(mib):
    return pltpu.CompilerParams(vmem_limit_bytes=mib * MIB)


def swap_pairs(count, distance):
    return [(index, index ^ distance) for index in range(count)]


def plane_pairs(count, steps):
    return [(index, index + steps) for index in range(count - steps)]


def run(copies):
    for copy in copies:
        copy.start()
    for copy in copies:
        copy.wait()


def split_kernel(group, total, info_ref, *refs):
    x_any, outs = refs[:total], refs[-4 - group : -4]
    held, buf, in_sems, sems = refs[-4:]
    member = info_ref[1]
    loads = [pltpu.make_async_copy(x_any[t], held.at[t], in_sems.at[t]) for t in range(total)]
    for load in loads:
        load.start()
    copies = []
    for t in range(total):
        loads[t].wait()
        buf[:, t] = jnp.swapaxes(held[t], 0, 1)
        for d in range(group):
            source = buf.at[member ^ d, t]
            copies.append(pltpu.make_async_copy(source, outs[d].at[t], sems.at[t, d]))
            copies[-1].start()
    for copy in copies:
        copy.wait()


def split_heads(info, arrays, after=()):
    tok, group, width = arrays[0].shape
    total = len(arrays)
    return pl.pallas_call(
        functools.partial(split_kernel, group, total),
        out_shape=[jax.ShapeDtypeStruct((total, tok, width), jnp.bfloat16)] * group,
        in_specs=[SMEM] + [ANY] * (total + len(after)),
        out_specs=[ANY] * group,
        scratch_shapes=[
            pltpu.VMEM((total, tok, group, width), jnp.bfloat16),
            pltpu.VMEM((group, total, tok, width), jnp.bfloat16),
            pltpu.SemaphoreType.DMA((total,)),
            pltpu.SemaphoreType.DMA((total, group)),
        ],
        compiler_params=params(60),
        name="split_heads",
    )(info, *arrays, *after)


def trade(pieces, count):
    return [
        lax.ppermute(piece, "seq", swap_pairs(count, d)) if d else piece
        for d, piece in enumerate(pieces)
    ]


def grad_kernel(group, tok, first, last, carried, chunks, info_ref, w_ref, *refs):
    pieces = last - first
    piece_any, refs = refs[:pieces], refs[pieces:]
    kvbuf, acc, sems = refs[-3:]
    *outs, last_piece = refs[-4 - chunks : -3] if last == group else (refs[-4], None)
    onward = [last_piece] if last == group else []
    plane, member, first_len = info_ref[0], info_ref[1], info_ref[2]
    copies = [
        pltpu.make_async_copy(piece_any[n], kvbuf.at[n], sems.at[n]) for n in range(pieces)
    ]
    if carried:
        copies.append(pltpu.make_async_copy(refs[0], acc, sems.at[pieces]))
    run(copies)
    leaving = [pltpu.make_async_copy(kvbuf.at[pieces - 1], to, sems.at[0]) for to in onward]
    for copy in leaving:
        copy.start()
    if not carried:
        acc[...] = jnp.zeros_like(acc)
    hidden = w_ref.shape[1]
    part = min(256, hidden)

    def piece(n, carry):
        first_tok = (plane * group + (member ^ (first + n))) * tok

        @pl.when(first_tok < first_len)
        def _():
            keys = kvbuf[n, 0]
            token = first_tok + lax.broadcasted_iota(jnp.int32, (tok, 1), 0)
            values = jnp.where(token < first_len, kvbuf[n, 1].astype(jnp.float32), 0.0)
            values = values.astype(jnp.bfloat16)
            for f in range(0, hidden, part):
                rows = pl.ds(f, part)
                gate = dot(keys, w_ref[0, rows, :], NT)
                up = dot(keys, w_ref[1, rows, :], NT)
                back = dot(values, w_ref[2, rows, :], NT)
                sig = jax.nn.sigmoid(gate)
                silu = gate * sig
                act = (silu * up).astype(jnp.bfloat16)
                grad_up = (back * silu).astype(jnp.bfloat16)
                grad_gate = (back * up * sig * (1.0 + gate * (1.0 - sig))).astype(jnp.bfloat16)
                acc[0, rows, :] += dot(grad_gate, keys, TN)
                acc[1, rows, :] += dot(grad_up, keys, TN)
                acc[2, rows, :] += dot(act, values, TN)

        return carry

    lax.fori_loop(0, pieces, piece, 0)
    rows = hidden // chunks
    for n, out in enumerate(outs):
        at = pl.multiple_of((plane + n) % chunks * rows, rows)
        out[...] = acc[:, pl.ds(at, rows), :].astype(out.dtype)
    for copy in leaving:
        copy.wait()


def weight_sums(info, weights, pairs, first, last, carried=(), after=(), chunks=1):
    group = len(pairs)
    pieces = last - first
    kind = jnp.bfloat16 if last == group else jnp.float32
    return pl.pallas_call(
        functools.partial(grad_kernel, group, pairs[0].shape[1], first, last, len(carried), chunks),
        out_shape=[jax.ShapeDtypeStruct((3, weights.shape[1] // chunks, weights.shape[2]), kind)] * chunks
        + [jax.ShapeDtypeStruct(pairs[0].shape, jnp.bfloat16)] * (last == group),
        in_specs=[SMEM, VMEM] + [ANY] * (pieces + len(carried) + len(after)),
        out_specs=[VMEM] * chunks + [ANY] * (last == group),
        scratch_shapes=[
            pltpu.VMEM((pieces,) + pairs[0].shape, jnp.bfloat16),
            pltpu.VMEM(weights.shape, jnp.float32),
            pltpu.SemaphoreType.DMA((pieces + 1,)),
        ],
        compiler_params=params(60),
        name="weight_sums",
    )(info, weights, *pairs[first:last], *carried, *after)


def lanes_sum(expo):
    total = expo[:, :128]
    for lane in range(128, expo.shape[1], 128):
        total = total + expo[:, lane : lane + 128]
    return total


def soft_steps(parts, scale, fresh, acc, top, norm):
    scores = [
        dot(rows, keys, NT) if mask is None else jnp.where(mask, dot(rows, keys, NT), NEG)
        for _, rows, keys, _, mask in parts
    ]
    done = []
    for (where, _, _, _, _), score in zip(parts, scores):
        peak = jnp.max(score, axis=1, keepdims=True)
        if fresh:
            decay = None
        else:
            before = top[where, :1]
            peak = jnp.maximum(peak, before)
            decay = jnp.exp2((before - peak) * scale)
        expo = jnp.exp2((score - peak) * scale)
        done.append((peak, decay, lanes_sum(expo), expo.astype(jnp.bfloat16)))
    for (where, _, _, values, _), (peak, decay, total, expo) in zip(parts, done):
        mixed = dot(expo, values, NN)
        wide = (peak.shape[0], 128)
        top[where, :] = jnp.broadcast_to(peak, wide)
        if fresh:
            norm[where, :] = total
            acc[where, :] = mixed
        else:
            norm[where, :] = norm[where, :] * decay + total
            acc[where, :] = acc[where, :] * decay + mixed


def soft_close(scale, acc, top, norm, out_ref, level_ref):
    total = jnp.sum(norm[...], axis=1, keepdims=True)
    out_ref[...] = (acc[...] / jnp.maximum(total, 1e-30)).astype(out_ref.dtype)
    level = top[...] * scale + jnp.log2(jnp.maximum(total, 1e-30))
    level_ref[...] = jnp.transpose(level)[:8]


def as_column(rows):
    return jnp.transpose(jnp.concatenate([rows] * 16, axis=0))[:, :1]


def score_scale(width):
    return math.log2(math.e) / math.sqrt(width)


def triangle(rows, cols, first_row, first_col, lower):
    row = first_row + lax.broadcasted_iota(jnp.int32, (rows, cols), 0)
    col = first_col + lax.broadcasted_iota(jnp.int32, (rows, cols), 1)
    return col <= row if lower else col > row


def own_kernel(group, tok, part, first, last, info_ref, *refs):
    count = last - first
    out_ref, level_ref, acc, top, norm, qbuf, kvbuf, sems = refs[-8:]
    member = info_ref[1]
    copies = [
        pltpu.make_async_copy(refs[n], qbuf.at[pl.ds(n, 1)], sems.at[n]) for n in range(count)
    ]
    for d in range(group):
        copies.append(pltpu.make_async_copy(refs[count + d], kvbuf.at[d], sems.at[count + d]))
    run(copies)
    scale = score_scale(qbuf.shape[-1])

    def piece(n, carry):
        d = first + n
        parts = []
        for r in range(0, tok, part):
            where, keys = pl.ds(r, part), pl.ds(0, r + part)
            mask = triangle(part, r + part, r, 0, True)
            parts.append((where, qbuf[n, where], kvbuf[d, 0, keys], kvbuf[d, 1, keys], mask))
        soft_steps(parts, scale, True, acc, top, norm)

        def earlier(other, carry):
            e = member ^ other
            parts = []
            for r in range(0, tok, part):
                where = pl.ds(r, part)
                parts.append((where, qbuf[n, where], kvbuf[e, 0], kvbuf[e, 1], None))
            soft_steps(parts, scale, False, acc, top, norm)
            return carry

        lax.fori_loop(0, member ^ d, earlier, 0)
        soft_close(scale, acc, top, norm, out_ref.at[n], level_ref.at[n])
        return carry

    lax.fori_loop(0, count, piece, 0)


def soft_shapes(group, tok, width):
    return [
        jax.ShapeDtypeStruct((group, tok, width), jnp.bfloat16),
        jax.ShapeDtypeStruct((group, 8, tok), jnp.float32),
    ]


def soft_scratch(tok, width):
    return [
        pltpu.VMEM((tok, width), jnp.float32),
        pltpu.VMEM((tok, 128), jnp.float32),
        pltpu.VMEM((tok, 128), jnp.float32),
    ]


def own_attention(info, asked, pairs, first, last, after=()):
    group = len(asked)
    _, tok, width = asked[0].shape
    count = last - first
    return pl.pallas_call(
        functools.partial(own_kernel, group, tok, min(256, tok), first, last),
        out_shape=soft_shapes(count, tok, width),
        in_specs=[SMEM] + [ANY] * (count + group + len(after)),
        out_specs=[VMEM] * 2,
        scratch_shapes=soft_scratch(tok, width)
        + [
            pltpu.VMEM((count, tok, width), jnp.bfloat16),
            pltpu.VMEM((group, 2, tok, width), jnp.bfloat16),
            pltpu.SemaphoreType.DMA((count + group,)),
        ],
        compiler_params=params(60),
        name="own_attention",
    )(info, *asked[first:last], *pairs, *after)


def renorm_kernel(terms, info_ref, rate_ref, w_ref, *refs):
    out_ref = refs[-1]
    rows = out_ref.shape[1]
    mine = pl.ds(pl.multiple_of(info_ref[0] * rows, rows), rows)
    step = rate_ref[0] / info_ref[2].astype(jnp.float32)
    for c in range(w_ref.shape[0]):
        previous = w_ref[c, mine, :].astype(jnp.float32)
        summed = refs[0][c].astype(jnp.float32)
        for term in refs[1:terms]:
            summed = summed + term[c].astype(jnp.float32)
        updated = previous + step * summed
        old_norm = jnp.sqrt(jnp.sum(previous * previous, axis=1, keepdims=True) + eps)
        new_norm = jnp.sqrt(jnp.sum(updated * updated, axis=1, keepdims=True) + eps)
        out_ref[c] = (updated * (old_norm / new_norm)).astype(out_ref.dtype)


def renorm(info, rate, weights, sums, after=()):
    return pl.pallas_call(
        functools.partial(renorm_kernel, len(sums)),
        out_shape=jax.ShapeDtypeStruct(sums[0].shape, jnp.bfloat16),
        in_specs=[SMEM] * 2 + [VMEM] * (1 + len(sums)) + [ANY] * len(after),
        out_specs=VMEM,
        compiler_params=params(60),
        name="renorm",
    )(info, rate, weights, *sums, *after)


def cross_kernel(group, tok, behind, part, info_ref, *refs):
    pieces = behind * group
    out_ref, level_ref, acc, top, norm, qbuf, kvbuf, sems = refs[-8:]
    plane, member = info_ref[0], info_ref[1]
    moves = [(refs[d], qbuf.at[pl.ds(d, 1)]) for d in range(group)]
    moves += [(refs[group + at], kvbuf.at[at]) for at in range(pieces)]
    run([pltpu.make_async_copy(*move, sems.at[n]) for n, move in enumerate(moves)])
    scale = score_scale(qbuf.shape[-1])
    valid = jnp.maximum(behind - plane, 0) * group

    def piece(d, carry):
        at = member ^ d

        @pl.when(at >= valid)
        def _():
            parts = []
            for r in range(0, tok, part):
                where, keys = pl.ds(r, part), pl.ds(r, tok - r)
                mask = triangle(part, tok - r, r, r, False)
                parts.append((where, qbuf[d, where], kvbuf[d, 0, keys], kvbuf[d, 1, keys], mask))
            soft_steps(parts, scale, True, acc, top, norm)

        @pl.when(at < valid)
        def _():
            acc[...] = jnp.zeros_like(acc)
            norm[...] = jnp.zeros_like(norm)
            top[...] = jnp.full_like(top, NEG)

        def later(other, carry):
            e = other // group * group + (member ^ (other % group))
            parts = []
            for r in range(0, tok, part):
                where = pl.ds(r, part)
                parts.append((where, qbuf[d, where], kvbuf[e, 0], kvbuf[e, 1], None))
            soft_steps(parts, scale, False, acc, top, norm)
            return carry

        lax.fori_loop(jnp.maximum(at + 1, valid), pieces, later, 0)
        soft_close(scale, acc, top, norm, out_ref.at[d], level_ref.at[d])
        return carry

    lax.fori_loop(0, group, piece, 0)


def cross_attention(info, asked, earlier, after=()):
    group = len(asked)
    _, tok, width = asked[0].shape
    behind = len(earlier) // group
    operands = [*asked, *earlier, *after]
    return pl.pallas_call(
        functools.partial(cross_kernel, group, tok, behind, min(256, tok)),
        out_shape=soft_shapes(group, tok, width),
        in_specs=[SMEM] + [ANY] * len(operands),
        out_specs=[VMEM] * 2,
        scratch_shapes=soft_scratch(tok, width)
        + [
            pltpu.VMEM((group, tok, width), jnp.bfloat16),
            pltpu.VMEM((behind * group, 2, tok, width), jnp.bfloat16),
            pltpu.SemaphoreType.DMA((group + behind * group,)),
        ],
        compiler_params=params(60),
        name="cross_attention",
    )(info, *operands)


def fast_apply(rows, weights):
    gate = dot(rows, weights[0], NT)
    up = dot(rows, weights[1], NT)
    act = (gate * jax.nn.sigmoid(gate) * up).astype(jnp.bfloat16)
    return dot(act, weights[2], NN)


def first_kernel(group, tok, cuts, info_ref, w_any, *refs):
    out_ref, wbuf, qbuf, obuf, xbuf, lbuf, sems = refs[-7:]
    plane, member, first_len = info_ref[0], info_ref[1], info_ref[2]
    moves = [(w_any, wbuf)] + [(refs[d], qbuf.at[pl.ds(d, 1)]) for d in range(group)]
    for n, (first, last) in enumerate(cuts):
        into = pl.ds(first, last - first)
        rows, level = refs[group + 2 * n], refs[group + 2 * n + 1]
        moves += [(rows, obuf.at[into]), (level, lbuf.at[0, into])]
    rows, level = refs[group + 2 * len(cuts)], refs[group + 2 * len(cuts) + 1]
    moves += [(rows, xbuf), (level, lbuf.at[1])]
    run([pltpu.make_async_copy(*move, sems.at[n]) for n, move in enumerate(moves)])

    def piece(d, carry):
        first_tok = (plane * group + (member ^ d)) * tok
        own_log, cross_log = as_column(lbuf[0, d]), as_column(lbuf[1, d])
        own_part = 1.0 / (1.0 + jnp.exp2(cross_log - own_log))
        cross_part = 1.0 / (1.0 + jnp.exp2(own_log - cross_log))
        mixed = obuf[d].astype(jnp.float32) * own_part + xbuf[d].astype(jnp.float32) * cross_part
        out_ref[d] = mixed.astype(out_ref.dtype)

        @pl.when(first_tok < first_len)
        def _():
            token = first_tok + lax.broadcasted_iota(jnp.int32, (tok, 1), 0)
            fast = jnp.where(token < first_len, fast_apply(qbuf[d], wbuf), 0.0)
            out_ref[d] = (out_ref[d].astype(jnp.float32) + fast).astype(out_ref.dtype)

        return carry

    lax.fori_loop(0, group, piece, 0)


def first_rows(info, weights, asked, cuts, parts):
    group = len(asked)
    _, tok, width = asked[0].shape
    operands = [*asked, *parts]
    whole = pltpu.VMEM((group, tok, width), jnp.bfloat16)
    return pl.pallas_call(
        functools.partial(first_kernel, group, tok, cuts),
        out_shape=jax.ShapeDtypeStruct((group, tok, width), jnp.bfloat16),
        in_specs=[SMEM, ANY] + [ANY] * len(operands),
        out_specs=VMEM,
        scratch_shapes=[
            pltpu.VMEM(weights.shape, jnp.bfloat16),
            whole,
            whole,
            whole,
            pltpu.VMEM((2, group, 8, tok), jnp.float32),
            pltpu.SemaphoreType.DMA((len(operands) + 1,)),
        ],
        compiler_params=params(60),
        name="first_rows",
    )(info, weights, *operands)


def finish_kernel(group, tok, count, chunks, info_ref, place_ref, base_any, *refs):
    out_ref, wbuf, qbuf, bbuf, sems = refs[-5:]
    plane, member, first_len = info_ref[0], info_ref[1], info_ref[2]

    def base_copy(d):
        return pltpu.make_async_copy(base_any.at[d], bbuf.at[d], sems.at[group + chunks + d])

    moves = [(refs[d], qbuf.at[pl.ds(d, 1)]) for d in range(group)]
    rows = wbuf.shape[1] // chunks
    for n in range(chunks):
        at = pl.multiple_of((plane + chunks - n) % chunks * rows, rows)
        moves.append((refs[group + n], wbuf.at[:, pl.ds(at, rows), :]))
    copies = [pltpu.make_async_copy(*move, sems.at[n]) for n, move in enumerate(moves)]
    for copy in copies:
        copy.start()
    for d in range(group):
        base_copy(d).start()
    for copy in copies:
        copy.wait()
    seg = tok // count

    def piece(d, carry):
        at = member ^ d
        first_tok = (plane * group + at) * tok
        base_copy(d).wait()

        @pl.when(first_tok + tok > first_len)
        def _():
            token = first_tok + lax.broadcasted_iota(jnp.int32, (tok, 1), 0)
            fast = jnp.where(token < first_len, 0.0, fast_apply(qbuf[d], wbuf))
            bbuf[d] = (bbuf[d].astype(jnp.float32) + fast).astype(bbuf.dtype)

        pick = as_column(place_ref[at]).astype(jnp.int32)
        pick = (pick == lax.broadcasted_iota(jnp.int32, (tok, tok), 1)).astype(jnp.bfloat16)
        sorted_rows = dot(pick, bbuf[d], NN)
        sorted_rows = sorted_rows.reshape(count, seg, sorted_rows.shape[-1])
        out_ref[:, at] = sorted_rows.astype(out_ref.dtype)
        return carry

    lax.fori_loop(0, group, piece, 0)


def finish_rows(info, places, new, base, asked, count):
    group = len(asked)
    _, tok, width = asked[0].shape
    whole = pltpu.VMEM((group, tok, width), jnp.bfloat16)
    return pl.pallas_call(
        functools.partial(finish_kernel, group, tok, count, len(new)),
        out_shape=jax.ShapeDtypeStruct((count, group, tok // count, width), jnp.bfloat16),
        in_specs=[SMEM, VMEM, ANY] + [ANY] * (group + len(new)),
        out_specs=VMEM,
        scratch_shapes=[
            pltpu.VMEM((3, new[0].shape[1] * len(new), width), jnp.bfloat16),
            whole,
            whole,
            pltpu.SemaphoreType.DMA((2 * group + len(new),)),
        ],
        compiler_params=params(60),
        name="finish_rows",
    )(info, places, base, *asked, *new)


def norm_kernel(came_ref, scale_ref, gain_ref, out_ref):
    scaled = came_ref[0].astype(jnp.float32) * scale_ref[...] * gain_ref[...]
    out_ref[...] = jnp.swapaxes(scaled.astype(out_ref.dtype), 0, 1)


def norm_rows(came, scale, gain):
    planes, group, rows, width = came.shape
    return pl.pallas_call(
        norm_kernel,
        grid=(planes,),
        out_shape=jax.ShapeDtypeStruct((planes * rows, group, width), jnp.bfloat16),
        in_specs=[
            pl.BlockSpec((1, group, rows, width), lambda z: (z, 0, 0, 0)),
            pl.BlockSpec((1, rows, 1), lambda z: (z, 0, 0)),
            pl.BlockSpec((group, 1, width), lambda z: (0, 0, 0)),
        ],
        out_specs=pl.BlockSpec((rows, group, width), lambda z: (z, 0, 0)),
        compiler_params=params(20),
        name="norm_rows",
    )(came, scale, gain)


def pass_kernel(count, *refs):
    for n in range(count):
        refs[len(refs) - count + n][...] = refs[n][...]


def pass_after(values, after):
    return pl.pallas_call(
        functools.partial(pass_kernel, len(values)),
        out_shape=[jax.ShapeDtypeStruct(value.shape, value.dtype) for value in values],
        in_specs=[VMEM] * len(values) + [ANY] * len(after),
        out_specs=[VMEM] * len(values),
        compiler_params=params(20),
        name="pass_after",
    )(*values, *after)


def as_places(asked, group, tok):
    places = jnp.transpose(asked, (1, 0, 2)).reshape(group, 1, tok).astype(jnp.float32)
    return jnp.broadcast_to(places, (group, 8, tok))


def asked_places(slot_order, group, count):
    tok = slot_order.shape[0]
    seg, planes = tok // count, count // group
    wanted = (slot_order % tok).reshape(planes, 1, group * seg)
    wanted = jnp.broadcast_to(wanted, (planes, group, group * seg))
    wanted = wanted.reshape(count, group * seg)
    asked = lax.all_to_all(wanted, "seq", split_axis=0, concat_axis=0, tiled=True)
    return as_places(asked.reshape(count, group, seg), group, tok)


def per_device(
    queries, token_keys, token_values, fast_weights, learn_rate, out_gain, group_lengths, slot_order
):
    tok, group, width = queries.shape
    count = lax.axis_size("seq")
    seg = tok // count
    planes = count // group
    behind = WINDOW // (group * tok)
    position = lax.axis_index("seq")
    plane, member = position // group, position % group
    info = jnp.stack([plane, member, group_lengths[0]]).astype(jnp.int32)

    weights = lax.dynamic_index_in_dim(fast_weights, member, 1, keepdims=False)
    weights = jnp.transpose(weights, (1, 0, 2))
    rate = lax.dynamic_slice_in_dim(learn_rate, member, 1)
    places = asked_places(slot_order, group, count)

    last = group - 1
    mine = split_heads(info, [token_keys, token_values])
    pairs = list(mine)
    if last:
        pairs = trade(pairs[:last], count)
        (late,) = pass_after(mine[last:], [*pairs[1:], weights, places])
        pairs = pairs + [lax.ppermute(late, "seq", swap_pairs(count, last))]
    carried = [weight_sums(info, weights, pairs, 0, last)[0]] if last else []
    asked = trade(split_heads(info, [queries], carried), count)
    shifts = [back * group for back in range(behind, 0, -1)]
    sources = [plane_pairs(count, shift) for shift in shifts]
    near = [[lax.ppermute(pair, "seq", source) for pair in pairs[:last]] for source in sources]
    waits = [asked[0], *near[-1][:2]]
    direct = planes <= 8
    chunks = planes if direct else 1
    *sums, onward = weight_sums(info, weights, pairs, last, group, carried, waits, chunks)
    earlier = []
    for source, arrays in zip(sources, near):
        earlier.extend(arrays + [lax.ppermute(onward, "seq", source)])

    groups = [[z * group + m for z in range(planes)] for m in range(group)]
    cuts = [(0, group)]
    parts = list(own_attention(info, asked, pairs, 0, group))

    def turned(value, steps):
        pairs_of_turn = [(index, (index + steps * group) % count) for index in range(count)]
        return lax.ppermute(value, "seq", pairs_of_turn)

    if direct:
        sums = sums[:1] + [turned(sums[step], step) for step in range(1, planes)]
    else:
        sums = [
            lax.psum_scatter(
                sums[0], "seq", scatter_dimension=1, axis_index_groups=groups, tiled=True
            )
        ]
    part = renorm(info, rate, weights, sums, parts[1:] + earlier[min(2, last) :])
    if direct:
        new = [part] + [turned(part, step) for step in range(1, planes)]
    else:
        new = [lax.all_gather(part, "seq", axis_index_groups=groups, axis=1, tiled=True)]
    parts.extend(cross_attention(info, asked, earlier, [part]))
    base = first_rows(info, weights, asked, cuts, parts)
    leaving = finish_rows(info, places, new, base, asked, count)

    came = lax.all_to_all(leaving, "seq", split_axis=0, concat_axis=0, tiled=True)
    came = came.reshape(planes, group, group * seg, width)
    wide = came.astype(jnp.float32)
    power = lax.psum(jnp.sum(wide * wide, axis=(1, 3)), "head")
    scale = lax.rsqrt(power / (group * lax.axis_size("head") * width) + eps)
    return norm_rows(came, scale[:, :, None], out_gain[:, None, :])


def solution(mesh):
    return jax.shard_map(
        per_device,
        mesh=mesh,
        in_specs=(
            P("seq", "head", None),
            P("seq", "head", None),
            P("seq", "head", None),
            P(None, "head", None, None),
            P("head"),
            P("head", None),
            P(),
            P("seq"),
        ),
        out_specs=P("seq", "head", None),
        check_vma=False,
    )
```

time: 307 us -> 253 us (0.82)
  waiting for transfers between devices: 159 us -> 112 us
  Pallas kernels: 62.8 us -> 86.4 us
  local copies, waits for them, and re-layouts: 32 us -> 12.5 us
  between operations: 13.9 us -> 0.28 us
    psum x1 -> x0, waiting for transfers between devices: 30.8 us -> none  [per_device(): sums = lax.psum(sums, 'seq', axis_index_groups=groups)]
    pallas_call x10, Pallas kernels: 60.4 us -> 83.9 us  [the longest x2 20.1 us: weight_sums(): pl.pallas_call(functools.partial(grad_kernel, group, pairs[0].shape[1], f...]
    unnamed x64 -> x34, local copies, waits for them, and re-layouts: 23.2 us -> 4.35 us
    ppermute x1, waiting for transfers between devices: 10.7 us -> 1.23 us  [per_device(): pairs = pairs + [lax.ppermute(late, 'seq', swap_pairs(count, last))]]
    ppermute x10, waiting for transfers between devices: 47.2 us -> 39 us  [the longest x6 35.1 us: turned(): return lax.ppermute(value, 'seq', pairs_of_turn)]
    ppermute x5, waiting for transfers between devices: 12.5 us -> 15.7 us  [trade(): lax.ppermute(piece, 'seq', swap_pairs(count, d))]
  transfers between devices with their start and end apart: 19 -> 18, of which waited for: 7 -> 10; matrix products, arithmetic and copies ran while one was open for 3% -> 3% of each run, Pallas kernels for 10% -> 27%
where the time goes in v7:
time: 253 us; the launch traced here: 252 us
  waiting for transfers between devices  112 us (44%)
  Pallas kernels  86.4 us (34%)
  starting transfers between devices  35.4 us (14%)
  local copies, waits for them, and re-layouts  12.5 us (5%)
  blocking collectives  3.59 us (1%)
    all_to_all x1, waiting for transfers between devices, per_device(): lax.all_to_all(leaving, 'seq', split_axis=0, concat_axis=0, tiled=True)  48.1 us
    ppermute x6, waiting for transfers between devices, turned(): return lax.ppermute(value, 'seq', pairs_of_turn)  35.1 us
    pallas_call x2, Pallas kernels, weight_sums(): pl.pallas_call(functools.partial(grad_kernel, group, pairs[0].shape[1], f...  20.1 us
    ppermute x5, waiting for transfers between devices, trade(): lax.ppermute(piece, 'seq', swap_pairs(count, d))  15.7 us
    pallas_call x1, Pallas kernels, cross_attention(): pl.pallas_call(functools.partial(cross_kernel, group, tok, behind, min(25...  15.5 us
    pallas_call x1, Pallas kernels, own_attention(): pl.pallas_call(functools.partial(own_kernel, group, tok, min(256, tok), f...  15.5 us
    pallas_call x1, Pallas kernels, first_rows(): pl.pallas_call(functools.partial(first_kernel, group, tok, cuts), out_sha...  11.6 us
    pallas_call x2, Pallas kernels, split_heads(): pl.pallas_call(functools.partial(split_kernel, group, total), out_shape=[...  9.11 us
  transfers between devices with their start and end apart: 18, of which 10 were waited for; matrix products, arithmetic and copies ran while one was open for 3% of the time, Pallas kernels for 27%

profile of v7, /device:TPU:13, one launch (start us, length us, event | category | flops | bytes accessed | tf_op | source)
XLA Modules:
  0.0 251.9 jit_solution(10884194009187302758)
XLA Ops:
  1.3 5.0 %split_heads.2 = (bf16[2,512,512]{2,1,0:T(8,128)(2,1)}, bf16[2,512,512]{2,1,0:T(8,128)(2,1)}, bf16[2,512,512]{2,1,0:T(8,128)(2,1)}, bf16[2,512,512]{2,1,0:T(8,128)(2,1)}) custom-call(s32[3]{0:T(128)} %pad_add_fusion.info_ref, bf16[512,4,512]{2,1,0:T(4,128)(2,1)} %refs_0_.2, bf16[512,4,512]{2,1,0:T(4,128)(2,1)} %refs_1_.1), custom_call_target="tpu_custom_call" | custom-call | tf_op jit(solution)/shard_map/split_heads/pallas_call | solution.py:71
  6.3 1.3 collective-permute-start
  8.4 5.7 %all-to-all-start = ((s32[16,1,128]{2,1,0:T(1,128)}), s32[16,1,128]{2,1,0:T(1,128)S(1)}, u32[]{:S(2)}, u32[]{:S(2)}) async-start(s32[16,1,128]{2,1,0:T(1,128)} %bitcast.3), calls=%async_computation | async-start | bytes 16384 | tf_op jit(solution)/shard_map/all_to_all | solution.py:561
  14.1 3.1 %collective-permute-start.6 = (bf16[2,512,512]{2,1,0:T(8,128)(2,1)}, bf16[2,512,512]{2,1,0:T(8,128)(2,1)}, u32[]{:S(2)}, u32[]{:S(2)}) collective-permute-start(bf16[2,512,512]{2,1,0:T(8,128)(2,1)} %get-tuple-element.22.refs_0_.refs_4_), channel_id=1, source_target_pairs={{0,8},{2,10},{4,12},{6,14},{8,16},{10,18},{12,20},{14,22},{16,24},... | collective-permute-start | bytes 3145736 | tf_op jit(solution)/shard_map/ppermute | solution.py:593
  17.2 6.0 %constant_dynamic-slice_fusion = bf16[512,1,3,512]{3,1,2,0:T(2,128)(2,1)S(1)} fusion(bf16[512,4,3,512]{3,1,2,0:T(4,128)(2,1)} %param.11, s32[]{:T(128)S(6)} %select_n.25), kind=kLoop, calls=%fused_computation.10 | loop fusion | bytes 3145732 | tf_op jit(solution)/shard_map/jit(dynamic_index_in_dim)/dynamic_slice | solution.py:577
  23.7 7.9 %all-to-all-done = s32[16,1,128]{2,1,0:T(1,128)S(1)} async-done(((s32[16,1,128]{2,1,0:T(1,128)}), s32[16,1,128]{2,1,0:T(1,128)S(1)}, u32[]{:S(2)}, u32[]{:S(2)}) %all-to-all-start) | async-done | bytes 8224 | tf_op jit(solution)/shard_map/all_to_all | solution.py:561
  31.9 1.6 copy-done.2
  35.3 3.2 %collective-permute-start.7 = (bf16[2,512,512]{2,1,0:T(8,128)(2,1)S(1)}, bf16[2,512,512]{2,1,0:T(8,128)(2,1)S(1)}, u32[]{:S(2)}, u32[]{:S(2)}) collective-permute-start(bf16[2,512,512]{2,1,0:T(8,128)(2,1)S(1)} %collective-permute-done.refs_1_.refs_5_), channel_id=1, source_target_pairs={{0,8},{2,10},{4,12},{6,14},{8,16},{10,18},{12,20},{14,22},{16,24},... | collective-permute-start | bytes 3145736 | tf_op jit(solution)/shard_map/ppermute | solution.py:593
  38.5 12.7 %weight_sums.2.refs_1_ = f32[3,512,512]{2,1,0:T(8,128)} custom-call(s32[3]{0:T(128)} %pad_add_fusion.info_ref, bf16[3,512,512]{2,1,0:T(8,128)(2,1)} %bitcast.16, bf16[2,512,512]{2,1,0:T(8,128)(2,1)} %get-tuple-element.22.refs_0_.refs_4_, bf16[2,512,512]{2,1,0:T(8,128)(2,1)} %copy-done.1, bf16[2,512,512]{2,1,0:T(8,128)(2,1)} %collective-permute-done.1.refs_2_.refs_6_), custom_call_target="tpu_custom_call" | custom-call | tf_op jit(solution)/shard_map/weight_sums/pallas_call | solution.py:153
  51.2 4.1 %split_heads.3 = (bf16[1,512,512]{2,1,0:T(8,128)(2,1)}, bf16[1,512,512]{2,1,0:T(8,128)(2,1)}, bf16[1,512,512]{2,1,0:T(8,128)(2,1)}, bf16[1,512,512]{2,1,0:T(8,128)(2,1)}) custom-call(s32[3]{0:T(128)} %pad_add_fusion.info_ref, bf16[512,4,512]{2,1,0:T(4,128)(2,1)} %refs_0_.3, f32[3,512,512]{2,1,0:T(8,128)} %weight_sums.2.refs_1_), custom_call_target="tpu_custom_call" | custom-call | tf_op jit(solution)/shard_map/split_heads/pallas_call | solution.py:71
  55.3 1.9 collective-permute-start.8
  58.5 3.9 %collective-permute-done.7.refs_4_.refs_5_ = bf16[2,512,512]{2,1,0:T(8,128)(2,1)S(1)} collective-permute-done((bf16[2,512,512]{2,1,0:T(8,128)(2,1)S(1)}, bf16[2,512,512]{2,1,0:T(8,128)(2,1)S(1)}, u32[]{:S(2)}, u32[]{:S(2)}) %collective-permute-start.7) | collective-permute-done | bytes 1048608 | tf_op jit(solution)/shard_map/ppermute | solution.py:593
  63.4 7.4 %weight_sums.3 = (bf16[3,128,512]{2,1,0:T(8,128)(2,1)}, bf16[3,128,512]{2,1,0:T(8,128)(2,1)}, bf16[3,128,512]{2,1,0:T(8,128)(2,1)}, bf16[3,128,512]{2,1,0:T(8,128)(2,1)}, bf16[2,512,512]{2,1,0:T(8,128)(2,1)}) custom-call(s32[3]{0:T(128)} %pad_add_fusion.info_ref, bf16[3,512,512]{2,1,0:T(8,128)(2,1)} %bitcast.17, ...), custom_call_target="tpu_custom_call" | custom-call | tf_op jit(solution)/shard_map/weight_sums/pallas_call | solution.py:153
  70.9 3.4 %collective-permute-start.9 = (bf16[2,512,512]{2,1,0:T(8,128)(2,1)}, bf16[2,512,512]{2,1,0:T(8,128)(2,1)S(1)}, u32[]{:S(2)}, u32[]{:S(2)}) collective-permute-start(bf16[2,512,512]{2,1,0:T(8,128)(2,1)} %get-tuple-element.32), channel_id=1, source_target_pairs={{0,8},{2,10},{4,12},{6,14},{8,16},{10,18},{12,20},{14,22},{16,24},... | collective-permute-start | bytes 3145736 | tf_op jit(solution)/shard_map/ppermute | solution.py:600
  75.4 1.6 collective-permute-start.4
  77.0 7.7 %collective-permute-done.2.refs_1_ = bf16[1,512,512]{2,1,0:T(8,128)(2,1)S(1)} collective-permute-done((bf16[1,512,512]{2,1,0:T(8,128)(2,1)}, bf16[1,512,512]{2,1,0:T(8,128)(2,1)S(1)}, u32[]{:S(2)}, u32[]{:S(2)}) %collective-permute-start.2) | collective-permute-done | bytes 524320 | tf_op jit(solution)/shard_map/ppermute | solution.py:89
  85.0 1.8 collective-permute-start.11
  86.8 8.0 %collective-permute-done.4.refs_3_ = bf16[1,512,512]{2,1,0:T(8,128)(2,1)S(1)} collective-permute-done((bf16[1,512,512]{2,1,0:T(8,128)(2,1)}, bf16[1,512,512]{2,1,0:T(8,128)(2,1)S(1)}, u32[]{:S(2)}, u32[]{:S(2)}) %collective-permute-start.4) | collective-permute-done | bytes 524320 | tf_op jit(solution)/shard_map/ppermute | solution.py:89
  96.2 15.5 %own_attention.1 = (bf16[4,512,512]{2,1,0:T(8,128)(2,1)}, f32[4,8,512]{2,1,0:T(8,128)}) custom-call(s32[3]{0:T(128)} %pad_add_fusion.info_ref, bf16[1,512,512]{2,1,0:T(8,128)(2,1)} %get-tuple-element.25.refs_0_.refs_2_, bf16[1,512,512]{2,1,0:T(8,128)(2,1)} %copy-done.4, bf16[1,512,512]{2,1,0:T(8,128)(2,1)} %copy-done.5, bf16[1,512,512]{2,1,0:T(8,128)(2,1)} %copy-done.6, ...), custom_call_target="tpu_custom_call" | custom-call | tf_op jit(solution)/shard_map/own_attention/pallas_call | solution.py:281
  111.7 4.1 %collective-permute-done.10.refs_1_ = bf16[3,128,512]{2,1,0:T(8,128)(2,1)S(1)} collective-permute-done((bf16[3,128,512]{2,1,0:T(8,128)(2,1)}, bf16[3,128,512]{2,1,0:T(8,128)(2,1)S(1)}, u32[]{:S(2)}, u32[]{:S(2)}) %collective-permute-start.10) | collective-permute-done | bytes 393248 | tf_op jit(solution)/shard_map/ppermute | solution.py:608
  115.8 24.5 %collective-permute-done.11.refs_2_ = bf16[3,128,512]{2,1,0:T(8,128)(2,1)} collective-permute-done((bf16[3,128,512]{2,1,0:T(8,128)(2,1)}, bf16[3,128,512]{2,1,0:T(8,128)(2,1)}, u32[]{:S(2)}, u32[]{:S(2)}) %collective-permute-start.11) | collective-permute-done | bytes 393248 | tf_op jit(solution)/shard_map/ppermute | solution.py:608
  141.3 3.7 %renorm.1.refs_8_.refs_4_ = bf16[3,128,512]{2,1,0:T(8,128)(2,1)} custom-call(s32[3]{0:T(128)} %pad_add_fusion.info_ref, f32[1]{0:T(128)} %dynamic_slice.8.rate_ref, bf16[3,512,512]{2,1,0:T(8,128)(2,1)} %bitcast.18, bf16[3,128,512]{2,1,0:T(8,128)(2,1)} %get-tuple-element.33.refs_0_, bf16[3,128,512]{2,1,0:T(8,128)(2,1)} %copy-done.13, ...), custom_call_target="tpu_custom_call" | custom-call | tf_op jit(solution)/shard_map/renorm/pallas_call | solution.py:314
  145.0 3.1 %collective-permute-start.14 = (bf16[3,128,512]{2,1,0:T(8,128)(2,1)}, bf16[3,128,512]{2,1,0:T(8,128)(2,1)S(1)}, u32[]{:S(2)}, u32[]{:S(2)}) collective-permute-start(bf16[3,128,512]{2,1,0:T(8,128)(2,1)} %renorm.1.refs_8_.refs_4_), channel_id=1, source_target_pairs={{0,16},{2,18},{4,20},{6,22},{8,24},{10,26},{12,28},{14,30},{16,0},... | collective-permute-start | bytes 1179656 | tf_op jit(solution)/shard_map/ppermute | solution.py:608
  148.1 1.5 collective-permute-start.15
  149.6 15.5 %cross_attention.1 = (bf16[4,512,512]{2,1,0:T(8,128)(2,1)}, f32[4,8,512]{2,1,0:T(8,128)}) custom-call(s32[3]{0:T(128)} %pad_add_fusion.info_ref, bf16[1,512,512]{2,1,0:T(8,128)(2,1)} %get-tuple-element.25.refs_0_.refs_2_, bf16[1,512,512]{2,1,0:T(8,128)(2,1)} %copy-done.4, bf16[1,512,512]{2,1,0:T(8,128)(2,1)} %copy-done.5, bf16[1,512,512]{2,1,0:T(8,128)(2,1)} %copy-done.6, ...), custom_call_target="tpu_custom_call" | custom-call | tf_op jit(solution)/shard_map/cross_attention/pallas_call | solution.py:373
  165.1 11.6 %first_rows.1.base_any = bf16[4,512,512]{2,1,0:T(8,128)(2,1)} custom-call(s32[3]{0:T(128)} %pad_add_fusion.info_ref, bf16[3,512,512]{2,1,0:T(8,128)(2,1)} %bitcast.19, bf16[1,512,512]{2,1,0:T(8,128)(2,1)} %get-tuple-element.25.refs_0_.refs_2_, bf16[1,512,512]{2,1,0:T(8,128)(2,1)} %copy-done.4, bf16[1,512,512]{2,1,0:T(8,128)(2,1)} %copy-done.5, ...), custom_call_target="tpu_custom_call" | custom-call | tf_op jit(solution)/shard_map/first_rows/pallas_call | solution.py:432
  177.6 5.6 %collective-permute-done.15.refs_7_ = bf16[3,128,512]{2,1,0:T(8,128)(2,1)S(1)} collective-permute-done((bf16[3,128,512]{2,1,0:T(8,128)(2,1)}, bf16[3,128,512]{2,1,0:T(8,128)(2,1)S(1)}, u32[]{:S(2)}, u32[]{:S(2)}) %collective-permute-start.15) | collective-permute-done | bytes 393248 | tf_op jit(solution)/shard_map/ppermute | solution.py:608
  184.0 7.3 %finish_rows.1 = bf16[16,4,32,512]{3,2,1,0:T(8,128)(2,1)} custom-call(s32[3]{0:T(128)} %pad_add_fusion.info_ref, f32[4,8,512]{2,1,0:T(8,128)} %copy-done.3, bf16[4,512,512]{2,1,0:T(8,128)(2,1)} %first_rows.1.base_any, bf16[1,512,512]{2,1,0:T(8,128)(2,1)} %get-tuple-element.25.refs_0_.refs_2_, bf16[1,512,512]{2,1,0:T(8,128)(2,1)} %copy-done.4, ...), custom_call_target="tpu_custom_call" | custom-call | tf_op jit(solution)/shard_map/finish_rows/pallas_call | solution.py:496
  191.3 5.6 %all-to-all-start.1 = ((bf16[16,4,32,512]{3,2,1,0:T(8,128)(2,1)}), bf16[16,4,32,512]{3,2,1,0:T(8,128)(2,1)S(1)}, u32[]{:S(2)}, u32[]{:S(2)}) async-start(bf16[16,4,32,512]{3,2,1,0:T(8,128)(2,1)} %finish_rows.1), calls=%async_computation.1 | async-start | bytes 4194304 | tf_op jit(solution)/shard_map/all_to_all | solution.py:627
  196.9 48.1 %all-to-all-done.1 = bf16[16,4,32,512]{3,2,1,0:T(8,128)(2,1)S(1)} async-done(((bf16[16,4,32,512]{3,2,1,0:T(8,128)(2,1)}), bf16[16,4,32,512]{3,2,1,0:T(8,128)(2,1)S(1)}, u32[]{:S(2)}, u32[]{:S(2)}) %all-to-all-start.1) | async-done | bytes 2097184 | tf_op jit(solution)/shard_map/all_to_all | solution.py:627
  245.6 3.6 %psum.7 = f32[4,128]{1,0:T(4,128)S(1)} all-reduce(f32[4,128]{1,0:T(4,128)S(1)} %reduce_sum.18), channel_id=1, replica_groups=mesh['seq'=16,'head'=2] {'head'}, use_global_device_ids=true, to_apply=%region_2.3 | all-reduce | flops 512 | bytes 4096 | tf_op jit(solution)/shard_map/psum | solution.py:630
  249.4 2.5 norm_rows.1
  (67 shorter events, 13.0 us)
Async XLA Ops:
  1.3 6.5 %copy-start.15 = (s32[512]{0:T(512)S(1)}, s32[512]{0:T(512)}, u32[]{:S(2)}) copy-start(s32[512]{0:T(512)} %param.15) | copy-start | bytes 6148
  6.3 25.6 %collective-permute-start = (bf16[2,512,512]{2,1,0:T(8,128)(2,1)}, bf16[2,512,512]{2,1,0:T(8,128)(2,1)S(1)}, u32[]{:S(2)}, u32[]{:S(2)}) collective-permute-start(bf16[2,512,512]{2,1,0:T(8,128)(2,1)} %get-tuple-element.23), channel_id=1, source_target_pairs={{0,2},{2,0},{4,6},{6,4},{8,10},{10,8},{12,14},{14,12},{16,18},{18,... | collective-permute-start | bytes 3145736 | tf_op jit(solution)/shard_map/ppermute | solution.py:89
  7.5 24.3 %collective-permute-start.1 = (bf16[2,512,512]{2,1,0:T(8,128)(2,1)}, bf16[2,512,512]{2,1,0:T(8,128)(2,1)}, u32[]{:S(2)}, u32[]{:S(2)}) collective-permute-start(bf16[2,512,512]{2,1,0:T(8,128)(2,1)} %get-tuple-element.24), channel_id=1, source_target_pairs={{0,4},{2,6},{4,0},{6,2},{8,12},{10,14},{12,8},{14,10},{16,20},{18,... | collective-permute-start | bytes 3145736 | tf_op jit(solution)/shard_map/ppermute | solution.py:89
  8.4 23.3 %all-to-all-start = ((s32[16,1,128]{2,1,0:T(1,128)}), s32[16,1,128]{2,1,0:T(1,128)S(1)}, u32[]{:S(2)}, u32[]{:S(2)}) async-start(s32[16,1,128]{2,1,0:T(1,128)} %bitcast.3), calls=%async_computation | async-start | bytes 16384 | tf_op jit(solution)/shard_map/all_to_all | solution.py:561
  14.1 43.2 %collective-permute-start.6 = (bf16[2,512,512]{2,1,0:T(8,128)(2,1)}, bf16[2,512,512]{2,1,0:T(8,128)(2,1)}, u32[]{:S(2)}, u32[]{:S(2)}) collective-permute-start(bf16[2,512,512]{2,1,0:T(8,128)(2,1)} %get-tuple-element.22.refs_0_.refs_4_), channel_id=1, source_target_pairs={{0,8},{2,10},{4,12},{6,14},{8,16},{10,18},{12,20},{14,22},{16,24},... | collective-permute-start | bytes 3145736 | tf_op jit(solution)/shard_map/ppermute | solution.py:593
  23.7 10.8 %copy-start = (bf16[512,1,3,512]{3,0,2,1:T(8,128)(2,1)}, bf16[512,1,3,512]{3,0,2,1:T(8,128)(2,1)S(1)}, u32[]{:S(2)}) copy-start(bf16[512,1,3,512]{3,0,2,1:T(8,128)(2,1)S(1)} %copy.22) | copy-start | bytes 4718596
  31.8 3.5 %copy-start.1 = (bf16[2,512,512]{2,1,0:T(8,128)(2,1)}, bf16[2,512,512]{2,1,0:T(8,128)(2,1)S(1)}, u32[]{:S(2)}) copy-start(bf16[2,512,512]{2,1,0:T(8,128)(2,1)S(1)} %collective-permute-done.refs_1_.refs_5_) | copy-start | bytes 3145732
  31.9 1.6 copy-start.2
  33.5 1.0 copy-start.3
  34.5 24.0 %collective-permute-start.5 = (bf16[2,512,512]{2,1,0:T(8,128)(2,1)}, bf16[2,512,512]{2,1,0:T(8,128)(2,1)}, u32[]{:S(2)}, u32[]{:S(2)}) collective-permute-start(bf16[2,512,512]{2,1,0:T(8,128)(2,1)} %pass_after.1), channel_id=1, source_target_pairs={{0,6},{2,4},{4,2},{6,0},{8,14},{10,12},{12,10},{14,8},{16,22},{18,... | collective-permute-start | bytes 3145736 | tf_op jit(solution)/shard_map/ppermute | solution.py:588
  35.3 27.1 %collective-permute-start.7 = (bf16[2,512,512]{2,1,0:T(8,128)(2,1)S(1)}, bf16[2,512,512]{2,1,0:T(8,128)(2,1)S(1)}, u32[]{:S(2)}, u32[]{:S(2)}) collective-permute-start(bf16[2,512,512]{2,1,0:T(8,128)(2,1)S(1)} %collective-permute-done.refs_1_.refs_5_), channel_id=1, source_target_pairs={{0,8},{2,10},{4,12},{6,14},{8,16},{10,18},{12,20},{14,22},{16,24},... | collective-permute-start | bytes 3145736 | tf_op jit(solution)/shard_map/ppermute | solution.py:593
  55.3 56.3 %collective-permute-start.8 = (bf16[2,512,512]{2,1,0:T(8,128)(2,1)}, bf16[2,512,512]{2,1,0:T(8,128)(2,1)S(1)}, u32[]{:S(2)}, u32[]{:S(2)}) collective-permute-start(bf16[2,512,512]{2,1,0:T(8,128)(2,1)} %collective-permute-done.1.refs_2_.refs_6_), channel_id=1, source_target_pairs={{0,8},{2,10},{4,12},{6,14},{8,16},{10,18},{12,20},{14,22},{16,24},... | collective-permute-start | bytes 3145736 | tf_op jit(solution)/shard_map/ppermute | solution.py:593
  63.4 32.1 %copy-start.16 = (f32[4]{0:T(128)S(1)}, f32[4]{0:T(128)}, u32[]{:S(2)}) copy-start(f32[4]{0:T(128)} %param.12) | copy-start | bytes 52
  70.9 69.4 %collective-permute-start.9 = (bf16[2,512,512]{2,1,0:T(8,128)(2,1)}, bf16[2,512,512]{2,1,0:T(8,128)(2,1)S(1)}, u32[]{:S(2)}, u32[]{:S(2)}) collective-permute-start(bf16[2,512,512]{2,1,0:T(8,128)(2,1)} %get-tuple-element.32), channel_id=1, source_target_pairs={{0,8},{2,10},{4,12},{6,14},{8,16},{10,18},{12,20},{14,22},{16,24},... | collective-permute-start | bytes 3145736 | tf_op jit(solution)/shard_map/ppermute | solution.py:600
  74.3 10.4 %collective-permute-start.2 = (bf16[1,512,512]{2,1,0:T(8,128)(2,1)}, bf16[1,512,512]{2,1,0:T(8,128)(2,1)S(1)}, u32[]{:S(2)}, u32[]{:S(2)}) collective-permute-start(bf16[1,512,512]{2,1,0:T(8,128)(2,1)} %get-tuple-element.26), channel_id=1, source_target_pairs={{0,2},{2,0},{4,6},{6,4},{8,10},{10,8},{12,14},{14,12},{16,18},{18,... | collective-permute-start | bytes 1572872 | tf_op jit(solution)/shard_map/ppermute | solution.py:89
  74.9 10.1 %collective-permute-start.3 = (bf16[1,512,512]{2,1,0:T(8,128)(2,1)}, bf16[1,512,512]{2,1,0:T(8,128)(2,1)S(1)}, u32[]{:S(2)}, u32[]{:S(2)}) collective-permute-start(bf16[1,512,512]{2,1,0:T(8,128)(2,1)} %get-tuple-element.27), channel_id=1, source_target_pairs={{0,4},{2,6},{4,0},{6,2},{8,12},{10,14},{12,8},{14,10},{16,20},{18,... | collective-permute-start | bytes 1572872 | tf_op jit(solution)/shard_map/ppermute | solution.py:89
  75.4 19.4 %collective-permute-start.4 = (bf16[1,512,512]{2,1,0:T(8,128)(2,1)}, bf16[1,512,512]{2,1,0:T(8,128)(2,1)S(1)}, u32[]{:S(2)}, u32[]{:S(2)}) collective-permute-start(bf16[1,512,512]{2,1,0:T(8,128)(2,1)} %get-tuple-element.28), channel_id=1, source_target_pairs={{0,6},{2,4},{4,2},{6,0},{8,14},{10,12},{12,10},{14,8},{16,22},{18,... | collective-permute-start | bytes 1572872 | tf_op jit(solution)/shard_map/ppermute | solution.py:89
  84.7 11.5 %copy-start.4 = (bf16[1,512,512]{2,1,0:T(8,128)(2,1)}, bf16[1,512,512]{2,1,0:T(8,128)(2,1)S(1)}, u32[]{:S(2)}) copy-start(bf16[1,512,512]{2,1,0:T(8,128)(2,1)S(1)} %collective-permute-done.2.refs_1_) | copy-start | bytes 1572868
  84.7 31.1 %collective-permute-start.10 = (bf16[3,128,512]{2,1,0:T(8,128)(2,1)}, bf16[3,128,512]{2,1,0:T(8,128)(2,1)S(1)}, u32[]{:S(2)}, u32[]{:S(2)}) collective-permute-start(bf16[3,128,512]{2,1,0:T(8,128)(2,1)} %get-tuple-element.34), channel_id=1, source_target_pairs={{0,8},{2,10},{4,12},{6,14},{8,16},{10,18},{12,20},{14,22},{16,24},... | collective-permute-start | bytes 1179656 | tf_op jit(solution)/shard_map/ppermute | solution.py:608
  85.0 11.2 %copy-start.5 = (bf16[1,512,512]{2,1,0:T(8,128)(2,1)}, bf16[1,512,512]{2,1,0:T(8,128)(2,1)S(1)}, u32[]{:S(2)}) copy-start(bf16[1,512,512]{2,1,0:T(8,128)(2,1)S(1)} %collective-permute-done.3.refs_2_) | copy-start | bytes 1572868
  85.0 55.3 %collective-permute-start.11 = (bf16[3,128,512]{2,1,0:T(8,128)(2,1)}, bf16[3,128,512]{2,1,0:T(8,128)(2,1)}, u32[]{:S(2)}, u32[]{:S(2)}) collective-permute-start(bf16[3,128,512]{2,1,0:T(8,128)(2,1)} %get-tuple-element.35), channel_id=1, source_target_pairs={{0,16},{2,18},{4,20},{6,22},{8,24},{10,26},{12,28},{14,30},{16,0},... | collective-permute-start | bytes 1179656 | tf_op jit(solution)/shard_map/ppermute | solution.py:608
  94.8 1.4 copy-start.6
  94.8 45.5 %collective-permute-start.12 = (bf16[3,128,512]{2,1,0:T(8,128)(2,1)}, bf16[3,128,512]{2,1,0:T(8,128)(2,1)}, u32[]{:S(2)}, u32[]{:S(2)}) collective-permute-start(bf16[3,128,512]{2,1,0:T(8,128)(2,1)} %get-tuple-element.36), channel_id=1, source_target_pairs={{0,24},{2,26},{4,28},{6,30},{8,0},{10,2},{12,4},{14,6},{16,8},{18,... | collective-permute-start | bytes 1179656 | tf_op jit(solution)/shard_map/ppermute | solution.py:608
  111.7 28.6 %copy-start.8 = (bf16[2,512,512]{2,1,0:T(8,128)(2,1)}, bf16[2,512,512]{2,1,0:T(8,128)(2,1)S(1)}, u32[]{:S(2)}) copy-start(bf16[2,512,512]{2,1,0:T(8,128)(2,1)S(1)} %collective-permute-done.8.refs_5_.refs_6_) | copy-start | bytes 3145732
  115.8 24.5 %copy-start.13 = (bf16[3,128,512]{2,1,0:T(8,128)(2,1)}, bf16[3,128,512]{2,1,0:T(8,128)(2,1)S(1)}, u32[]{:S(2)}) copy-start(bf16[3,128,512]{2,1,0:T(8,128)(2,1)S(1)} %collective-permute-done.10.refs_1_) | copy-start | bytes 1179652
  145.0 31.7 %collective-permute-start.13 = (bf16[3,128,512]{2,1,0:T(8,128)(2,1)}, bf16[3,128,512]{2,1,0:T(8,128)(2,1)S(1)}, u32[]{:S(2)}, u32[]{:S(2)}) collective-permute-start(bf16[3,128,512]{2,1,0:T(8,128)(2,1)} %renorm.1.refs_8_.refs_4_), channel_id=1, source_target_pairs={{0,8},{2,10},{4,12},{6,14},{8,16},{10,18},{12,20},{14,22},{16,24},... | collective-permute-start | bytes 1179656 | tf_op jit(solution)/shard_map/ppermute | solution.py:608
  145.0 32.6 %collective-permute-start.14 = (bf16[3,128,512]{2,1,0:T(8,128)(2,1)}, bf16[3,128,512]{2,1,0:T(8,128)(2,1)S(1)}, u32[]{:S(2)}, u32[]{:S(2)}) collective-permute-start(bf16[3,128,512]{2,1,0:T(8,128)(2,1)} %renorm.1.refs_8_.refs_4_), channel_id=1, source_target_pairs={{0,16},{2,18},{4,20},{6,22},{8,24},{10,26},{12,28},{14,30},{16,0},... | collective-permute-start | bytes 1179656 | tf_op jit(solution)/shard_map/ppermute | solution.py:608
  148.1 35.1 %collective-permute-start.15 = (bf16[3,128,512]{2,1,0:T(8,128)(2,1)}, bf16[3,128,512]{2,1,0:T(8,128)(2,1)S(1)}, u32[]{:S(2)}, u32[]{:S(2)}) collective-permute-start(bf16[3,128,512]{2,1,0:T(8,128)(2,1)} %renorm.1.refs_8_.refs_4_), channel_id=1, source_target_pairs={{0,24},{2,26},{4,28},{6,30},{8,0},{10,2},{12,4},{14,6},{16,8},{18,... | collective-permute-start | bytes 1179656 | tf_op jit(solution)/shard_map/ppermute | solution.py:608
  176.8 6.5 %copy-start.10 = (bf16[3,128,512]{2,1,0:T(8,128)(2,1)}, bf16[3,128,512]{2,1,0:T(8,128)(2,1)S(1)}, u32[]{:S(2)}) copy-start(bf16[3,128,512]{2,1,0:T(8,128)(2,1)S(1)} %collective-permute-done.13.refs_5_) | copy-start | bytes 1179652
  177.6 5.6 %copy-start.11 = (bf16[3,128,512]{2,1,0:T(8,128)(2,1)}, bf16[3,128,512]{2,1,0:T(8,128)(2,1)S(1)}, u32[]{:S(2)}) copy-start(bf16[3,128,512]{2,1,0:T(8,128)(2,1)S(1)} %collective-permute-done.14.refs_6_) | copy-start | bytes 1179652
  191.3 5.6 %copy-start.14 = (f32[4,512]{1,0:T(4,128)S(1)}, f32[4,512]{1,0:T(4,128)}, u32[]{:S(2)}) copy-start(f32[4,512]{1,0:T(4,128)} %param.13) | copy-start | bytes 24580
  191.3 53.8 %all-to-all-start.1 = ((bf16[16,4,32,512]{3,2,1,0:T(8,128)(2,1)}), bf16[16,4,32,512]{3,2,1,0:T(8,128)(2,1)S(1)}, u32[]{:S(2)}, u32[]{:S(2)}) async-start(bf16[16,4,32,512]{3,2,1,0:T(8,128)(2,1)} %finish_rows.1), calls=%async_computation.1 | async-start | bytes 4194304 | tf_op jit(solution)/shard_map/all_to_all | solution.py:627
  (3 other events, 2.7 us)

commit v8 on v7

--- a/solution.py
+++ b/solution.py
@@ -591,7 +591,7 @@
     shifts = [back * group for back in range(behind, 0, -1)]
     sources = [plane_pairs(count, shift) for shift in shifts]
     near = [[lax.ppermute(pair, "seq", source) for pair in pairs[:last]] for source in sources]
-    waits = [asked[0], *near[-1][:2]]
+    waits = [*asked[:3], *near[-1][:2]]
     direct = planes <= 8
     chunks = planes if direct else 1
     *sums, onward = weight_sums(info, weights, pairs, last, group, carried, waits, chunks)

time: 253 us -> 254 us (level)
    ppermute x5, waiting for transfers between devices: 15.7 us -> 21.8 us  [trade(): lax.ppermute(piece, 'seq', swap_pairs(count, d))]
    ppermute x3, waiting for transfers between devices: 3.95 us -> 0.01 us  [per_device(): lax.ppermute(pair, 'seq', source)]
  transfers between devices with their start and end apart: 18 -> 18, of which waited for: 10 -> 9; matrix products, arithmetic and copies ran while one was open for 3% -> 3% of each run, Pallas kernels for 27% -> 27%
where the time goes in v8:
time: 254 us
  waiting for transfers between devices  112 us (44%)
  Pallas kernels  86.2 us (34%)
  starting transfers between devices  36.8 us (14%)
  local copies, waits for them, and re-layouts  13.1 us (5%)
  blocking collectives  3.59 us (1%)
    all_to_all x1, waiting for transfers between devices, per_device(): lax.all_to_all(leaving, 'seq', split_axis=0, concat_axis=0, tiled=True)  48.1 us
    ppermute x6, waiting for transfers between devices, turned(): return lax.ppermute(value, 'seq', pairs_of_turn)  34.3 us
    ppermute x5, waiting for transfers between devices, trade(): lax.ppermute(piece, 'seq', swap_pairs(count, d))  21.8 us
    pallas_call x2, Pallas kernels, weight_sums(): pl.pallas_call(functools.partial(grad_kernel, group, pairs[0].shape[1], f...  20.1 us
    pallas_call x1, Pallas kernels, cross_attention(): pl.pallas_call(functools.partial(cross_kernel, group, tok, behind, min(25...  15.5 us
    pallas_call x1, Pallas kernels, own_attention(): pl.pallas_call(functools.partial(own_kernel, group, tok, min(256, tok), f...  15.5 us
    pallas_call x1, Pallas kernels, first_rows(): pl.pallas_call(functools.partial(first_kernel, group, tok, cuts), out_sha...  11.6 us
    pallas_call x2, Pallas kernels, split_heads(): pl.pallas_call(functools.partial(split_kernel, group, total), out_shape=[...  9.04 us
  transfers between devices with their start and end apart: 18, of which 9 were waited for; matrix products, arithmetic and copies ran while one was open for 3% of the time, Pallas kernels for 27%

profile of v8, /device:TPU:13, one launch (start us, length us, event | category | flops | bytes accessed | tf_op | source)
XLA Modules:
  0.0 253.9 jit_solution(12365073175745862585)
XLA Ops:
  0.0 1.3 pad_add_fusion.info_ref
  1.3 4.9 %split_heads.2 = (bf16[2,512,512]{2,1,0:T(8,128)(2,1)}, bf16[2,512,512]{2,1,0:T(8,128)(2,1)}, bf16[2,512,512]{2,1,0:T(8,128)(2,1)}, bf16[2,512,512]{2,1,0:T(8,128)(2,1)}) custom-call(s32[3]{0:T(128)} %pad_add_fusion.info_ref, bf16[512,4,512]{2,1,0:T(4,128)(2,1)} %refs_0_.2, bf16[512,4,512]{2,1,0:T(4,128)(2,1)} %refs_1_.1), custom_call_target="tpu_custom_call" | custom-call | tf_op jit(solution)/shard_map/split_heads/pallas_call | solution.py:71
  6.2 1.3 collective-permute-start
  8.3 5.7 %all-to-all-start = ((s32[16,1,128]{2,1,0:T(1,128)}), s32[16,1,128]{2,1,0:T(1,128)S(1)}, u32[]{:S(2)}, u32[]{:S(2)}) async-start(s32[16,1,128]{2,1,0:T(1,128)} %bitcast.3), calls=%async_computation | async-start | bytes 16384 | tf_op jit(solution)/shard_map/all_to_all | solution.py:561
  14.1 3.1 %collective-permute-start.6 = (bf16[2,512,512]{2,1,0:T(8,128)(2,1)}, bf16[2,512,512]{2,1,0:T(8,128)(2,1)}, u32[]{:S(2)}, u32[]{:S(2)}) collective-permute-start(bf16[2,512,512]{2,1,0:T(8,128)(2,1)} %get-tuple-element.22.refs_0_.refs_4_), channel_id=1, source_target_pairs={{0,8},{2,10},{4,12},{6,14},{8,16},{10,18},{12,20},{14,22},{16,24},... | collective-permute-start | bytes 3145736 | tf_op jit(solution)/shard_map/ppermute | solution.py:593
  17.2 6.0 %constant_dynamic-slice_fusion = bf16[512,1,3,512]{3,1,2,0:T(2,128)(2,1)S(1)} fusion(bf16[512,4,3,512]{3,1,2,0:T(4,128)(2,1)} %param.11, s32[]{:T(128)S(6)} %select_n.25), kind=kLoop, calls=%fused_computation.10 | loop fusion | bytes 3145732 | tf_op jit(solution)/shard_map/jit(dynamic_index_in_dim)/dynamic_slice | solution.py:577
  23.7 7.9 %all-to-all-done = s32[16,1,128]{2,1,0:T(1,128)S(1)} async-done(((s32[16,1,128]{2,1,0:T(1,128)}), s32[16,1,128]{2,1,0:T(1,128)S(1)}, u32[]{:S(2)}, u32[]{:S(2)}) %all-to-all-start) | async-done | bytes 8224 | tf_op jit(solution)/shard_map/all_to_all | solution.py:561
  31.8 1.6 copy-done.2
  35.3 3.2 %collective-permute-start.7 = (bf16[2,512,512]{2,1,0:T(8,128)(2,1)S(1)}, bf16[2,512,512]{2,1,0:T(8,128)(2,1)S(1)}, u32[]{:S(2)}, u32[]{:S(2)}) collective-permute-start(bf16[2,512,512]{2,1,0:T(8,128)(2,1)S(1)} %collective-permute-done.refs_1_.refs_5_), channel_id=1, source_target_pairs={{0,8},{2,10},{4,12},{6,14},{8,16},{10,18},{12,20},{14,22},{16,24},... | collective-permute-start | bytes 3145736 | tf_op jit(solution)/shard_map/ppermute | solution.py:593
  38.5 12.7 %weight_sums.2.refs_1_ = f32[3,512,512]{2,1,0:T(8,128)} custom-call(s32[3]{0:T(128)} %pad_add_fusion.info_ref, bf16[3,512,512]{2,1,0:T(8,128)(2,1)} %bitcast.16, bf16[2,512,512]{2,1,0:T(8,128)(2,1)} %get-tuple-element.22.refs_0_.refs_4_, bf16[2,512,512]{2,1,0:T(8,128)(2,1)} %copy-done.1, bf16[2,512,512]{2,1,0:T(8,128)(2,1)} %collective-permute-done.1.refs_2_.refs_6_), custom_call_target="tpu_custom_call" | custom-call | tf_op jit(solution)/shard_map/weight_sums/pallas_call | solution.py:153
  51.2 4.1 %split_heads.3 = (bf16[1,512,512]{2,1,0:T(8,128)(2,1)}, bf16[1,512,512]{2,1,0:T(8,128)(2,1)}, bf16[1,512,512]{2,1,0:T(8,128)(2,1)}, bf16[1,512,512]{2,1,0:T(8,128)(2,1)}) custom-call(s32[3]{0:T(128)} %pad_add_fusion.info_ref, bf16[512,4,512]{2,1,0:T(4,128)(2,1)} %refs_0_.3, f32[3,512,512]{2,1,0:T(8,128)} %weight_sums.2.refs_1_), custom_call_target="tpu_custom_call" | custom-call | tf_op jit(solution)/shard_map/split_heads/pallas_call | solution.py:71
  55.9 1.2 collective-permute-start.3
  57.2 1.9 collective-permute-start.8
  59.1 10.6 %collective-permute-done.2.refs_1_.refs_3_ = bf16[1,512,512]{2,1,0:T(8,128)(2,1)S(1)} collective-permute-done((bf16[1,512,512]{2,1,0:T(8,128)(2,1)}, bf16[1,512,512]{2,1,0:T(8,128)(2,1)S(1)}, u32[]{:S(2)}, u32[]{:S(2)}) %collective-permute-start.2) | collective-permute-done | bytes 524320 | tf_op jit(solution)/shard_map/ppermute | solution.py:89
  71.7 7.4 %weight_sums.3 = (bf16[3,128,512]{2,1,0:T(8,128)(2,1)}, bf16[3,128,512]{2,1,0:T(8,128)(2,1)}, bf16[3,128,512]{2,1,0:T(8,128)(2,1)}, bf16[3,128,512]{2,1,0:T(8,128)(2,1)}, bf16[2,512,512]{2,1,0:T(8,128)(2,1)}) custom-call(s32[3]{0:T(128)} %pad_add_fusion.info_ref, bf16[3,512,512]{2,1,0:T(8,128)(2,1)} %bitcast.17, ...), custom_call_target="tpu_custom_call" | custom-call | tf_op jit(solution)/shard_map/weight_sums/pallas_call | solution.py:153
  79.1 3.3 %collective-permute-start.9 = (bf16[2,512,512]{2,1,0:T(8,128)(2,1)}, bf16[2,512,512]{2,1,0:T(8,128)(2,1)S(1)}, u32[]{:S(2)}, u32[]{:S(2)}) collective-permute-start(bf16[2,512,512]{2,1,0:T(8,128)(2,1)} %get-tuple-element.32), channel_id=1, source_target_pairs={{0,8},{2,10},{4,12},{6,14},{8,16},{10,18},{12,20},{14,22},{16,24},... | collective-permute-start | bytes 3145736 | tf_op jit(solution)/shard_map/ppermute | solution.py:600
  83.3 1.3 collective-permute-start.10
  85.8 10.4 %collective-permute-done.4.refs_3_ = bf16[1,512,512]{2,1,0:T(8,128)(2,1)S(1)} collective-permute-done((bf16[1,512,512]{2,1,0:T(8,128)(2,1)S(1)}, bf16[1,512,512]{2,1,0:T(8,128)(2,1)S(1)}, u32[]{:S(2)}, u32[]{:S(2)}) %collective-permute-start.4) | collective-permute-done | bytes 524320 | tf_op jit(solution)/shard_map/ppermute | solution.py:89
  97.0 15.5 %own_attention.1 = (bf16[4,512,512]{2,1,0:T(8,128)(2,1)}, f32[4,8,512]{2,1,0:T(8,128)}) custom-call(s32[3]{0:T(128)} %pad_add_fusion.info_ref, bf16[1,512,512]{2,1,0:T(8,128)(2,1)} %get-tuple-element.25.refs_0_.refs_2_, bf16[1,512,512]{2,1,0:T(8,128)(2,1)} %copy-done.4, bf16[1,512,512]{2,1,0:T(8,128)(2,1)} %copy-done.5, bf16[1,512,512]{2,1,0:T(8,128)(2,1)} %copy-done.6, ...), custom_call_target="tpu_custom_call" | custom-call | tf_op jit(solution)/shard_map/own_attention/pallas_call | solution.py:281
  112.5 3.0 %collective-permute-done.10.refs_1_ = bf16[3,128,512]{2,1,0:T(8,128)(2,1)S(1)} collective-permute-done((bf16[3,128,512]{2,1,0:T(8,128)(2,1)}, bf16[3,128,512]{2,1,0:T(8,128)(2,1)S(1)}, u32[]{:S(2)}, u32[]{:S(2)}) %collective-permute-start.10) | collective-permute-done | bytes 393248 | tf_op jit(solution)/shard_map/ppermute | solution.py:608
  115.5 24.8 %collective-permute-done.11.refs_2_ = bf16[3,128,512]{2,1,0:T(8,128)(2,1)S(1)} collective-permute-done((bf16[3,128,512]{2,1,0:T(8,128)(2,1)}, bf16[3,128,512]{2,1,0:T(8,128)(2,1)S(1)}, u32[]{:S(2)}, u32[]{:S(2)}) %collective-permute-start.11) | collective-permute-done | bytes 393248 | tf_op jit(solution)/shard_map/ppermute | solution.py:608
  141.6 3.7 %renorm.1.refs_8_.refs_4_ = bf16[3,128,512]{2,1,0:T(8,128)(2,1)} custom-call(s32[3]{0:T(128)} %pad_add_fusion.info_ref, f32[1]{0:T(128)} %dynamic_slice.8.rate_ref, bf16[3,512,512]{2,1,0:T(8,128)(2,1)} %bitcast.18, bf16[3,128,512]{2,1,0:T(8,128)(2,1)} %get-tuple-element.33.refs_0_, bf16[3,128,512]{2,1,0:T(8,128)(2,1)} %copy-done.12, ...), custom_call_target="tpu_custom_call" | custom-call | tf_op jit(solution)/shard_map/renorm/pallas_call | solution.py:314
  145.3 3.0 %collective-permute-start.14 = (bf16[3,128,512]{2,1,0:T(8,128)(2,1)}, bf16[3,128,512]{2,1,0:T(8,128)(2,1)S(1)}, u32[]{:S(2)}, u32[]{:S(2)}) collective-permute-start(bf16[3,128,512]{2,1,0:T(8,128)(2,1)} %renorm.1.refs_8_.refs_4_), channel_id=1, source_target_pairs={{0,16},{2,18},{4,20},{6,22},{8,24},{10,26},{12,28},{14,30},{16,0},... | collective-permute-start | bytes 1179656 | tf_op jit(solution)/shard_map/ppermute | solution.py:608
  148.3 1.5 collective-permute-start.15
  149.7 15.5 %cross_attention.1 = (bf16[4,512,512]{2,1,0:T(8,128)(2,1)}, f32[4,8,512]{2,1,0:T(8,128)}) custom-call(s32[3]{0:T(128)} %pad_add_fusion.info_ref, bf16[1,512,512]{2,1,0:T(8,128)(2,1)} %get-tuple-element.25.refs_0_.refs_2_, bf16[1,512,512]{2,1,0:T(8,128)(2,1)} %copy-done.4, bf16[1,512,512]{2,1,0:T(8,128)(2,1)} %copy-done.5, bf16[1,512,512]{2,1,0:T(8,128)(2,1)} %copy-done.6, ...), custom_call_target="tpu_custom_call" | custom-call | tf_op jit(solution)/shard_map/cross_attention/pallas_call | solution.py:373
  165.2 11.6 %first_rows.1.base_any = bf16[4,512,512]{2,1,0:T(8,128)(2,1)} custom-call(s32[3]{0:T(128)} %pad_add_fusion.info_ref, bf16[3,512,512]{2,1,0:T(8,128)(2,1)} %bitcast.19, bf16[1,512,512]{2,1,0:T(8,128)(2,1)} %get-tuple-element.25.refs_0_.refs_2_, bf16[1,512,512]{2,1,0:T(8,128)(2,1)} %copy-done.4, bf16[1,512,512]{2,1,0:T(8,128)(2,1)} %copy-done.5, ...), custom_call_target="tpu_custom_call" | custom-call | tf_op jit(solution)/shard_map/first_rows/pallas_call | solution.py:432
  177.9 5.5 %collective-permute-done.15.refs_7_ = bf16[3,128,512]{2,1,0:T(8,128)(2,1)S(1)} collective-permute-done((bf16[3,128,512]{2,1,0:T(8,128)(2,1)}, bf16[3,128,512]{2,1,0:T(8,128)(2,1)S(1)}, u32[]{:S(2)}, u32[]{:S(2)}) %collective-permute-start.15) | collective-permute-done | bytes 393248 | tf_op jit(solution)/shard_map/ppermute | solution.py:608
  184.1 7.3 %finish_rows.1 = bf16[16,4,32,512]{3,2,1,0:T(8,128)(2,1)} custom-call(s32[3]{0:T(128)} %pad_add_fusion.info_ref, f32[4,8,512]{2,1,0:T(8,128)} %copy-done.3, bf16[4,512,512]{2,1,0:T(8,128)(2,1)} %first_rows.1.base_any, bf16[1,512,512]{2,1,0:T(8,128)(2,1)} %get-tuple-element.25.refs_0_.refs_2_, bf16[1,512,512]{2,1,0:T(8,128)(2,1)} %copy-done.4, ...), custom_call_target="tpu_custom_call" | custom-call | tf_op jit(solution)/shard_map/finish_rows/pallas_call | solution.py:496
  191.4 7.5 %all-to-all-start.1 = ((bf16[16,4,32,512]{3,2,1,0:T(8,128)(2,1)}), bf16[16,4,32,512]{3,2,1,0:T(8,128)(2,1)S(1)}, u32[]{:S(2)}, u32[]{:S(2)}) async-start(bf16[16,4,32,512]{3,2,1,0:T(8,128)(2,1)} %finish_rows.1), calls=%async_computation.1 | async-start | bytes 4194304 | tf_op jit(solution)/shard_map/all_to_all | solution.py:627
  198.9 48.1 %all-to-all-done.1 = bf16[16,4,32,512]{3,2,1,0:T(8,128)(2,1)S(1)} async-done(((bf16[16,4,32,512]{3,2,1,0:T(8,128)(2,1)}), bf16[16,4,32,512]{3,2,1,0:T(8,128)(2,1)S(1)}, u32[]{:S(2)}, u32[]{:S(2)}) %all-to-all-start.1) | async-done | bytes 2097184 | tf_op jit(solution)/shard_map/all_to_all | solution.py:627
  247.7 3.6 %psum.7 = f32[4,128]{1,0:T(4,128)S(1)} all-reduce(f32[4,128]{1,0:T(4,128)S(1)} %reduce_sum.18), channel_id=1, replica_groups=mesh['seq'=16,'head'=2] {'head'}, use_global_device_ids=true, to_apply=%region_2.3 | all-reduce | flops 512 | bytes 4096 | tf_op jit(solution)/shard_map/psum | solution.py:630
  251.4 2.5 norm_rows.1
  (71 shorter events, 12.7 us)
Async XLA Ops:
  1.3 6.5 %copy-start.16 = (s32[512]{0:T(512)S(1)}, s32[512]{0:T(512)}, u32[]{:S(2)}) copy-start(s32[512]{0:T(512)} %param.15) | copy-start | bytes 6148
  6.2 25.6 %collective-permute-start = (bf16[2,512,512]{2,1,0:T(8,128)(2,1)}, bf16[2,512,512]{2,1,0:T(8,128)(2,1)S(1)}, u32[]{:S(2)}, u32[]{:S(2)}) collective-permute-start(bf16[2,512,512]{2,1,0:T(8,128)(2,1)} %get-tuple-element.23), channel_id=1, source_target_pairs={{0,2},{2,0},{4,6},{6,4},{8,10},{10,8},{12,14},{14,12},{16,18},{18,... | collective-permute-start | bytes 3145736 | tf_op jit(solution)/shard_map/ppermute | solution.py:89
  7.5 24.3 %collective-permute-start.1 = (bf16[2,512,512]{2,1,0:T(8,128)(2,1)}, bf16[2,512,512]{2,1,0:T(8,128)(2,1)}, u32[]{:S(2)}, u32[]{:S(2)}) collective-permute-start(bf16[2,512,512]{2,1,0:T(8,128)(2,1)} %get-tuple-element.24), channel_id=1, source_target_pairs={{0,4},{2,6},{4,0},{6,2},{8,12},{10,14},{12,8},{14,10},{16,20},{18,... | collective-permute-start | bytes 3145736 | tf_op jit(solution)/shard_map/ppermute | solution.py:89
  8.3 23.3 %all-to-all-start = ((s32[16,1,128]{2,1,0:T(1,128)}), s32[16,1,128]{2,1,0:T(1,128)S(1)}, u32[]{:S(2)}, u32[]{:S(2)}) async-start(s32[16,1,128]{2,1,0:T(1,128)} %bitcast.3), calls=%async_computation | async-start | bytes 16384 | tf_op jit(solution)/shard_map/all_to_all | solution.py:561
  14.1 43.1 %collective-permute-start.6 = (bf16[2,512,512]{2,1,0:T(8,128)(2,1)}, bf16[2,512,512]{2,1,0:T(8,128)(2,1)}, u32[]{:S(2)}, u32[]{:S(2)}) collective-permute-start(bf16[2,512,512]{2,1,0:T(8,128)(2,1)} %get-tuple-element.22.refs_0_.refs_4_), channel_id=1, source_target_pairs={{0,8},{2,10},{4,12},{6,14},{8,16},{10,18},{12,20},{14,22},{16,24},... | collective-permute-start | bytes 3145736 | tf_op jit(solution)/shard_map/ppermute | solution.py:593
  23.6 10.8 %copy-start = (bf16[512,1,3,512]{3,0,2,1:T(8,128)(2,1)}, bf16[512,1,3,512]{3,0,2,1:T(8,128)(2,1)S(1)}, u32[]{:S(2)}) copy-start(bf16[512,1,3,512]{3,0,2,1:T(8,128)(2,1)S(1)} %copy.22) | copy-start | bytes 4718596
  31.8 3.5 %copy-start.1 = (bf16[2,512,512]{2,1,0:T(8,128)(2,1)}, bf16[2,512,512]{2,1,0:T(8,128)(2,1)S(1)}, u32[]{:S(2)}) copy-start(bf16[2,512,512]{2,1,0:T(8,128)(2,1)S(1)} %collective-permute-done.refs_1_.refs_5_) | copy-start | bytes 3145732
  31.8 1.6 copy-start.2
  33.4 1.0 copy-start.3
  34.5 36.0 %collective-permute-start.5 = (bf16[2,512,512]{2,1,0:T(8,128)(2,1)}, bf16[2,512,512]{2,1,0:T(8,128)(2,1)}, u32[]{:S(2)}, u32[]{:S(2)}) collective-permute-start(bf16[2,512,512]{2,1,0:T(8,128)(2,1)} %pass_after.1), channel_id=1, source_target_pairs={{0,6},{2,4},{4,2},{6,0},{8,14},{10,12},{12,10},{14,8},{16,22},{18,... | collective-permute-start | bytes 3145736 | tf_op jit(solution)/shard_map/ppermute | solution.py:588
  35.3 35.2 %collective-permute-start.7 = (bf16[2,512,512]{2,1,0:T(8,128)(2,1)S(1)}, bf16[2,512,512]{2,1,0:T(8,128)(2,1)S(1)}, u32[]{:S(2)}, u32[]{:S(2)}) collective-permute-start(bf16[2,512,512]{2,1,0:T(8,128)(2,1)S(1)} %collective-permute-done.refs_1_.refs_5_), channel_id=1, source_target_pairs={{0,8},{2,10},{4,12},{6,14},{8,16},{10,18},{12,20},{14,22},{16,24},... | collective-permute-start | bytes 3145736 | tf_op jit(solution)/shard_map/ppermute | solution.py:593
  55.3 14.4 %collective-permute-start.2 = (bf16[1,512,512]{2,1,0:T(8,128)(2,1)}, bf16[1,512,512]{2,1,0:T(8,128)(2,1)S(1)}, u32[]{:S(2)}, u32[]{:S(2)}) collective-permute-start(bf16[1,512,512]{2,1,0:T(8,128)(2,1)} %get-tuple-element.26), channel_id=1, source_target_pairs={{0,2},{2,0},{4,6},{6,4},{8,10},{10,8},{12,14},{14,12},{16,18},{18,... | collective-permute-start | bytes 1572872 | tf_op jit(solution)/shard_map/ppermute | solution.py:89
  55.9 14.6 %collective-permute-start.3 = (bf16[1,512,512]{2,1,0:T(8,128)(2,1)}, bf16[1,512,512]{2,1,0:T(8,128)(2,1)S(1)}, u32[]{:S(2)}, u32[]{:S(2)}) collective-permute-start(bf16[1,512,512]{2,1,0:T(8,128)(2,1)} %get-tuple-element.27), channel_id=1, source_target_pairs={{0,4},{2,6},{4,0},{6,2},{8,12},{10,14},{12,8},{14,10},{16,20},{18,... | collective-permute-start | bytes 1572872 | tf_op jit(solution)/shard_map/ppermute | solution.py:89
  57.2 55.3 %collective-permute-start.8 = (bf16[2,512,512]{2,1,0:T(8,128)(2,1)}, bf16[2,512,512]{2,1,0:T(8,128)(2,1)}, u32[]{:S(2)}, u32[]{:S(2)}) collective-permute-start(bf16[2,512,512]{2,1,0:T(8,128)(2,1)} %collective-permute-done.1.refs_2_.refs_6_), channel_id=1, source_target_pairs={{0,8},{2,10},{4,12},{6,14},{8,16},{10,18},{12,20},{14,22},{16,24},... | collective-permute-start | bytes 3145736 | tf_op jit(solution)/shard_map/ppermute | solution.py:593
  69.6 0.9 copy-start.4
  70.5 1.1 copy-start.7
  71.7 10.8 %copy-start.17 = (bf16[1,512,512]{2,1,0:T(8,128)(2,1)S(1)}, bf16[1,512,512]{2,1,0:T(8,128)(2,1)}, u32[]{:S(2)}) copy-start(bf16[1,512,512]{2,1,0:T(8,128)(2,1)} %get-tuple-element.28) | copy-start | bytes 1572868
  71.7 24.5 %copy-start.18 = (f32[4]{0:T(128)S(1)}, f32[4]{0:T(128)}, u32[]{:S(2)}) copy-start(f32[4]{0:T(128)} %param.12) | copy-start | bytes 52
  79.1 61.2 %collective-permute-start.9 = (bf16[2,512,512]{2,1,0:T(8,128)(2,1)}, bf16[2,512,512]{2,1,0:T(8,128)(2,1)S(1)}, u32[]{:S(2)}, u32[]{:S(2)}) collective-permute-start(bf16[2,512,512]{2,1,0:T(8,128)(2,1)} %get-tuple-element.32), channel_id=1, source_target_pairs={{0,8},{2,10},{4,12},{6,14},{8,16},{10,18},{12,20},{14,22},{16,24},... | collective-permute-start | bytes 3145736 | tf_op jit(solution)/shard_map/ppermute | solution.py:600
  82.5 13.7 %collective-permute-start.4 = (bf16[1,512,512]{2,1,0:T(8,128)(2,1)S(1)}, bf16[1,512,512]{2,1,0:T(8,128)(2,1)S(1)}, u32[]{:S(2)}, u32[]{:S(2)}) collective-permute-start(bf16[1,512,512]{2,1,0:T(8,128)(2,1)S(1)} %copy-done.17), channel_id=1, source_target_pairs={{0,6},{2,4},{4,2},{6,0},{8,14},{10,12},{12,10},{14,8},{16,22},{18,... | collective-permute-start | bytes 1572872 | tf_op jit(solution)/shard_map/ppermute | solution.py:89
  83.3 32.2 %collective-permute-start.10 = (bf16[3,128,512]{2,1,0:T(8,128)(2,1)}, bf16[3,128,512]{2,1,0:T(8,128)(2,1)S(1)}, u32[]{:S(2)}, u32[]{:S(2)}) collective-permute-start(bf16[3,128,512]{2,1,0:T(8,128)(2,1)} %get-tuple-element.34), channel_id=1, source_target_pairs={{0,8},{2,10},{4,12},{6,14},{8,16},{10,18},{12,20},{14,22},{16,24},... | collective-permute-start | bytes 1179656 | tf_op jit(solution)/shard_map/ppermute | solution.py:608
  84.6 55.6 %collective-permute-start.11 = (bf16[3,128,512]{2,1,0:T(8,128)(2,1)}, bf16[3,128,512]{2,1,0:T(8,128)(2,1)S(1)}, u32[]{:S(2)}, u32[]{:S(2)}) collective-permute-start(bf16[3,128,512]{2,1,0:T(8,128)(2,1)} %get-tuple-element.35), channel_id=1, source_target_pairs={{0,16},{2,18},{4,20},{6,22},{8,24},{10,26},{12,28},{14,30},{16,0},... | collective-permute-start | bytes 1179656 | tf_op jit(solution)/shard_map/ppermute | solution.py:608
  96.2 44.1 %collective-permute-start.12 = (bf16[3,128,512]{2,1,0:T(8,128)(2,1)}, bf16[3,128,512]{2,1,0:T(8,128)(2,1)S(1)}, u32[]{:S(2)}, u32[]{:S(2)}) collective-permute-start(bf16[3,128,512]{2,1,0:T(8,128)(2,1)} %get-tuple-element.36), channel_id=1, source_target_pairs={{0,24},{2,26},{4,28},{6,30},{8,0},{10,2},{12,4},{14,6},{16,8},{18,... | collective-permute-start | bytes 1179656 | tf_op jit(solution)/shard_map/ppermute | solution.py:608
  115.5 24.8 %copy-start.12 = (bf16[3,128,512]{2,1,0:T(8,128)(2,1)}, bf16[3,128,512]{2,1,0:T(8,128)(2,1)S(1)}, u32[]{:S(2)}) copy-start(bf16[3,128,512]{2,1,0:T(8,128)(2,1)S(1)} %collective-permute-done.10.refs_1_) | copy-start | bytes 1179652
  140.3 1.3 copy-start.8
  145.3 31.5 %collective-permute-start.13 = (bf16[3,128,512]{2,1,0:T(8,128)(2,1)}, bf16[3,128,512]{2,1,0:T(8,128)(2,1)S(1)}, u32[]{:S(2)}, u32[]{:S(2)}) collective-permute-start(bf16[3,128,512]{2,1,0:T(8,128)(2,1)} %renorm.1.refs_8_.refs_4_), channel_id=1, source_target_pairs={{0,8},{2,10},{4,12},{6,14},{8,16},{10,18},{12,20},{14,22},{16,24},... | collective-permute-start | bytes 1179656 | tf_op jit(solution)/shard_map/ppermute | solution.py:608
  145.3 32.6 %collective-permute-start.14 = (bf16[3,128,512]{2,1,0:T(8,128)(2,1)}, bf16[3,128,512]{2,1,0:T(8,128)(2,1)S(1)}, u32[]{:S(2)}, u32[]{:S(2)}) collective-permute-start(bf16[3,128,512]{2,1,0:T(8,128)(2,1)} %renorm.1.refs_8_.refs_4_), channel_id=1, source_target_pairs={{0,16},{2,18},{4,20},{6,22},{8,24},{10,26},{12,28},{14,30},{16,0},... | collective-permute-start | bytes 1179656 | tf_op jit(solution)/shard_map/ppermute | solution.py:608
  148.3 35.1 %collective-permute-start.15 = (bf16[3,128,512]{2,1,0:T(8,128)(2,1)}, bf16[3,128,512]{2,1,0:T(8,128)(2,1)S(1)}, u32[]{:S(2)}, u32[]{:S(2)}) collective-permute-start(bf16[3,128,512]{2,1,0:T(8,128)(2,1)} %renorm.1.refs_8_.refs_4_), channel_id=1, source_target_pairs={{0,24},{2,26},{4,28},{6,30},{8,0},{10,2},{12,4},{14,6},{16,8},{18,... | collective-permute-start | bytes 1179656 | tf_op jit(solution)/shard_map/ppermute | solution.py:608
  176.8 6.6 %copy-start.9 = (bf16[3,128,512]{2,1,0:T(8,128)(2,1)}, bf16[3,128,512]{2,1,0:T(8,128)(2,1)S(1)}, u32[]{:S(2)}) copy-start(bf16[3,128,512]{2,1,0:T(8,128)(2,1)S(1)} %collective-permute-done.13.refs_5_) | copy-start | bytes 1179652
  177.9 5.5 %copy-start.10 = (bf16[3,128,512]{2,1,0:T(8,128)(2,1)}, bf16[3,128,512]{2,1,0:T(8,128)(2,1)S(1)}, u32[]{:S(2)}) copy-start(bf16[3,128,512]{2,1,0:T(8,128)(2,1)S(1)} %collective-permute-done.14.refs_6_) | copy-start | bytes 1179652
  191.4 7.5 %copy-start.15 = (f32[4,512]{1,0:T(4,128)S(1)}, f32[4,512]{1,0:T(4,128)}, u32[]{:S(2)}) copy-start(f32[4,512]{1,0:T(4,128)} %param.13) | copy-start | bytes 24580
  191.4 55.6 %all-to-all-start.1 = ((bf16[16,4,32,512]{3,2,1,0:T(8,128)(2,1)}), bf16[16,4,32,512]{3,2,1,0:T(8,128)(2,1)S(1)}, u32[]{:S(2)}, u32[]{:S(2)}) async-start(bf16[16,4,32,512]{3,2,1,0:T(8,128)(2,1)} %finish_rows.1), calls=%async_computation.1 | async-start | bytes 4194304 | tf_op jit(solution)/shard_map/all_to_all | solution.py:627
  (5 other events, 4.0 us)

commit v9 on v8

--- a/solution.py
+++ b/solution.py
@@ -297,7 +297,7 @@
 def renorm_kernel(terms, info_ref, rate_ref, w_ref, *refs):
     out_ref = refs[-1]
     rows = out_ref.shape[1]
-    mine = pl.ds(pl.multiple_of(info_ref[0] * rows, rows), rows)
+    mine = pl.ds(pl.multiple_of(info_ref[0] % (w_ref.shape[1] // rows) * rows, rows), rows)
     step = rate_ref[0] / info_ref[2].astype(jnp.float32)
     for c in range(w_ref.shape[0]):
         previous = w_ref[c, mine, :].astype(jnp.float32)
@@ -424,7 +424,7 @@
     lax.fori_loop(0, group, piece, 0)
 
 
-def first_rows(info, weights, asked, cuts, parts):
+def first_rows(info, weights, asked, cuts, parts, after=()):
     group = len(asked)
     _, tok, width = asked[0].shape
     operands = [*asked, *parts]
@@ -432,7 +432,7 @@
     return pl.pallas_call(
         functools.partial(first_kernel, group, tok, cuts),
         out_shape=jax.ShapeDtypeStruct((group, tok, width), jnp.bfloat16),
-        in_specs=[SMEM, ANY] + [ANY] * len(operands),
+        in_specs=[SMEM, ANY] + [ANY] * (len(operands) + len(after)),
         out_specs=VMEM,
         scratch_shapes=[
             pltpu.VMEM(weights.shape, jnp.bfloat16),
@@ -444,7 +444,7 @@
         ],
         compiler_params=params(60),
         name="first_rows",
-    )(info, weights, *operands)
+    )(info, weights, *operands, *after)
 
 
 def finish_kernel(group, tok, count, chunks, info_ref, place_ref, base_any, *refs):
@@ -455,15 +455,28 @@
         return pltpu.make_async_copy(base_any.at[d], bbuf.at[d], sems.at[group + chunks + d])
 
     moves = [(refs[d], qbuf.at[pl.ds(d, 1)]) for d in range(group)]
-    rows = wbuf.shape[1] // chunks
-    for n in range(chunks):
-        at = pl.multiple_of((plane + chunks - n) % chunks * rows, rows)
-        moves.append((refs[group + n], wbuf.at[:, pl.ds(at, rows), :]))
+    if chunks == 1:
+        moves.append((refs[group], wbuf))
     copies = [pltpu.make_async_copy(*move, sems.at[n]) for n, move in enumerate(moves)]
     for copy in copies:
         copy.start()
     for d in range(group):
         base_copy(d).start()
+    if chunks > 1:
+        own, near, far, near_on, far_on = refs[group : group + chunks]
+        rows = own.shape[1]
+        halves = [wbuf.at[:, pl.ds(half * rows, rows), :] for half in range(2)]
+        for at_plane, pair in ((1, (near, own)), (2, (far, near)), (3, (far_on, near_on))):
+
+            @pl.when(plane == at_plane)
+            def _():
+                run(
+                    [
+                        pltpu.make_async_copy(pair[half], halves[half], sems.at[group + half])
+                        for half in range(2)
+                    ]
+                )
+
     for copy in copies:
         copy.wait()
     seg = tok // count
@@ -499,7 +512,7 @@
         in_specs=[SMEM, VMEM, ANY] + [ANY] * (group + len(new)),
         out_specs=VMEM,
         scratch_shapes=[
-            pltpu.VMEM((3, new[0].shape[1] * len(new), width), jnp.bfloat16),
+            pltpu.VMEM((3, new[0].shape[1] * min(2, len(new)), width), jnp.bfloat16),
             whole,
             whole,
             pltpu.SemaphoreType.DMA((2 * group + len(new),)),
@@ -592,8 +605,8 @@
     sources = [plane_pairs(count, shift) for shift in shifts]
     near = [[lax.ppermute(pair, "seq", source) for pair in pairs[:last]] for source in sources]
     waits = [*asked[:3], *near[-1][:2]]
-    direct = planes <= 8
-    chunks = planes if direct else 1
+    direct = planes == 4
+    chunks = 2 if direct else 1
     *sums, onward = weight_sums(info, weights, pairs, last, group, carried, waits, chunks)
     earlier = []
     for source, arrays in zip(sources, near):
@@ -603,12 +616,14 @@
     cuts = [(0, group)]
     parts = list(own_attention(info, asked, pairs, 0, group))
 
-    def turned(value, steps):
-        pairs_of_turn = [(index, (index + steps * group) % count) for index in range(count)]
-        return lax.ppermute(value, "seq", pairs_of_turn)
+    def between(value, hops):
+        return lax.ppermute(
+            value, "seq", [(a * group + m, b * group + m) for a, b in hops for m in range(group)]
+        )
 
     if direct:
-        sums = sums[:1] + [turned(sums[step], step) for step in range(1, planes)]
+        own, other = sums
+        sums = [own, between(other, [(0, 1), (1, 0)]), between(own, [(2, 0)]), between(other, [(2, 1)])]
     else:
         sums = [
             lax.psum_scatter(
@@ -617,11 +632,15 @@
         ]
     part = renorm(info, rate, weights, sums, parts[1:] + earlier[min(2, last) :])
     if direct:
-        new = [part] + [turned(part, step) for step in range(1, planes)]
+        near, far = between(part, [(0, 1), (1, 2)]), between(part, [(0, 2)])
     else:
         new = [lax.all_gather(part, "seq", axis_index_groups=groups, axis=1, tiled=True)]
     parts.extend(cross_attention(info, asked, earlier, [part]))
     base = first_rows(info, weights, asked, cuts, parts)
+    if direct:
+        (near_on,) = pass_after([near], parts[-1:])
+        (far_on,) = pass_after([far], [base])
+        new = [part, near, far, between(near_on, [(2, 3)]), between(far_on, [(2, 3)])]
     leaving = finish_rows(info, places, new, base, asked, count)
 
     came = lax.all_to_all(leaving, "seq", split_axis=0, concat_axis=0, tiled=True)

time: 254 us -> 261 us (1.028)
  starting transfers between devices: 36.8 us -> 57.4 us
  waiting for transfers between devices: 112 us -> 94.3 us
  local copies, waits for them, and re-layouts: 13.1 us -> 15.9 us
    all_to_all x1, starting transfers between devices: 7.48 us -> 24.1 us  [per_device(): lax.all_to_all(leaving, 'seq', split_axis=0, concat_axis=0, tiled=True)]
    ppermute x6 -> x7, waiting for transfers between devices: 34.3 us -> 24 us  [between(): lax.ppermute(value, 'seq', [(a * group + m, b * group + m) for a, b in ho...]
    ppermute x5, waiting for transfers between devices: 21.8 us -> 15.4 us  [trade(): lax.ppermute(piece, 'seq', swap_pairs(count, d))]
    pallas_call x2, Pallas kernels: 20.1 us -> 15.2 us  [weight_sums(): pl.pallas_call(functools.partial(grad_kernel, group, pairs[0].shape[1], f...]
    pallas_call x1, Pallas kernels: 7.28 us -> 10.9 us  [finish_rows(): pl.pallas_call(functools.partial(finish_kernel, group, tok, count, len(ne...]
    unnamed x38 -> x42, local copies, waits for them, and re-layouts: 4.91 us -> 7.81 us
    ppermute x6 -> x7, starting transfers between devices: 6.94 us -> 9.02 us  [between(): lax.ppermute(value, 'seq', [(a * group + m, b * group + m) for a, b in ho...]
  transfers between devices with their start and end apart: 18 -> 19, of which waited for: 9 -> 5; matrix products, arithmetic and copies ran while one was open for 3% -> 3% of each run, Pallas kernels for 27% -> 24%
where the time goes in v9:
time: 261 us; the launch traced here: 259 us
  waiting for transfers between devices  94.3 us (36%)
  Pallas kernels  84.2 us (32%)
  starting transfers between devices  57.4 us (22%)
  local copies, waits for them, and re-layouts  15.9 us (6%)
  blocking collectives  4.81 us (2%)
    all_to_all x1, waiting for transfers between devices, per_device(): lax.all_to_all(leaving, 'seq', split_axis=0, concat_axis=0, tiled=True)  46.8 us
    all_to_all x1, starting transfers between devices, per_device(): lax.all_to_all(leaving, 'seq', split_axis=0, concat_axis=0, tiled=True)  24.1 us
    ppermute x7, waiting for transfers between devices, between(): lax.ppermute(value, 'seq', [(a * group + m, b * group + m) for a, b in ho...  24 us
    pallas_call x1, Pallas kernels, cross_attention(): pl.pallas_call(functools.partial(cross_kernel, group, tok, behind, min(25...  15.5 us
    ppermute x5, waiting for transfers between devices, trade(): lax.ppermute(piece, 'seq', swap_pairs(count, d))  15.4 us
    pallas_call x1, Pallas kernels, own_attention(): pl.pallas_call(functools.partial(own_kernel, group, tok, min(256, tok), f...  15.4 us
    pallas_call x2, Pallas kernels, weight_sums(): pl.pallas_call(functools.partial(grad_kernel, group, pairs[0].shape[1], f...  15.2 us
    pallas_call x1, Pallas kernels, finish_rows(): pl.pallas_call(functools.partial(finish_kernel, group, tok, count, len(ne...  10.9 us
  transfers between devices with their start and end apart: 19, of which 5 were waited for; matrix products, arithmetic and copies ran while one was open for 3% of the time, Pallas kernels for 24%

profile of v9, /device:TPU:13, one launch (start us, length us, event | category | flops | bytes accessed | tf_op | source)
XLA Modules:
  0.0 258.9 jit_solution(17711571581848217525)
XLA Ops:
  0.0 1.2 pad_add_fusion.info_ref
  1.2 5.0 %split_heads.2 = (bf16[2,512,512]{2,1,0:T(8,128)(2,1)}, bf16[2,512,512]{2,1,0:T(8,128)(2,1)}, bf16[2,512,512]{2,1,0:T(8,128)(2,1)}, bf16[2,512,512]{2,1,0:T(8,128)(2,1)}) custom-call(s32[3]{0:T(128)} %pad_add_fusion.info_ref, bf16[512,4,512]{2,1,0:T(4,128)(2,1)} %refs_0_.2, bf16[512,4,512]{2,1,0:T(4,128)(2,1)} %refs_1_.1), custom_call_target="tpu_custom_call" | custom-call | tf_op jit(solution)/shard_map/split_heads/pallas_call | solution.py:71
  6.3 1.3 collective-permute-start
  8.4 5.7 %all-to-all-start = ((s32[16,1,128]{2,1,0:T(1,128)}), s32[16,1,128]{2,1,0:T(1,128)S(1)}, u32[]{:S(2)}, u32[]{:S(2)}) async-start(s32[16,1,128]{2,1,0:T(1,128)} %bitcast.3), calls=%async_computation | async-start | bytes 16384 | tf_op jit(solution)/shard_map/all_to_all | solution.py:574
  14.1 3.1 %collective-permute-start.6 = (bf16[2,512,512]{2,1,0:T(8,128)(2,1)}, bf16[2,512,512]{2,1,0:T(8,128)(2,1)}, u32[]{:S(2)}, u32[]{:S(2)}) collective-permute-start(bf16[2,512,512]{2,1,0:T(8,128)(2,1)} %get-tuple-element.20.refs_0_.refs_4_), channel_id=1, source_target_pairs={{0,8},{2,10},{4,12},{6,14},{8,16},{10,18},{12,20},{14,22},{16,24},... | collective-permute-start | bytes 3145736 | tf_op jit(solution)/shard_map/ppermute | solution.py:606
  17.2 6.0 %constant_dynamic-slice_fusion = bf16[512,1,3,512]{3,1,2,0:T(2,128)(2,1)S(1)} fusion(bf16[512,4,3,512]{3,1,2,0:T(4,128)(2,1)} %param.11, s32[]{:T(128)S(6)} %select_n.25), kind=kLoop, calls=%fused_computation.10 | loop fusion | bytes 3145732 | tf_op jit(solution)/shard_map/jit(dynamic_index_in_dim)/dynamic_slice | solution.py:590
  23.7 7.9 %all-to-all-done = s32[16,1,128]{2,1,0:T(1,128)S(1)} async-done(((s32[16,1,128]{2,1,0:T(1,128)}), s32[16,1,128]{2,1,0:T(1,128)S(1)}, u32[]{:S(2)}, u32[]{:S(2)}) %all-to-all-start) | async-done | bytes 8224 | tf_op jit(solution)/shard_map/all_to_all | solution.py:574
  31.9 1.6 copy-done.5
  33.5 1.0 pass_after.3
  35.3 3.2 %collective-permute-start.7 = (bf16[2,512,512]{2,1,0:T(8,128)(2,1)S(1)}, bf16[2,512,512]{2,1,0:T(8,128)(2,1)S(1)}, u32[]{:S(2)}, u32[]{:S(2)}) collective-permute-start(bf16[2,512,512]{2,1,0:T(8,128)(2,1)S(1)} %collective-permute-done.refs_1_.refs_5_), channel_id=1, source_target_pairs={{0,8},{2,10},{4,12},{6,14},{8,16},{10,18},{12,20},{14,22},{16,24},... | collective-permute-start | bytes 3145736 | tf_op jit(solution)/shard_map/ppermute | solution.py:606
  38.5 7.8 %weight_sums.2.refs_1_ = f32[3,512,512]{2,1,0:T(8,128)} custom-call(s32[3]{0:T(128)} %pad_add_fusion.info_ref, bf16[3,512,512]{2,1,0:T(8,128)(2,1)} %bitcast.16, bf16[2,512,512]{2,1,0:T(8,128)(2,1)} %get-tuple-element.20.refs_0_.refs_4_, bf16[2,512,512]{2,1,0:T(8,128)(2,1)} %copy-done.2, bf16[2,512,512]{2,1,0:T(8,128)(2,1)} %collective-permute-done.1.refs_2_.refs_6_), custom_call_target="tpu_custom_call" | custom-call | tf_op jit(solution)/shard_map/weight_sums/pallas_call | solution.py:153
  46.4 4.1 %split_heads.3 = (bf16[1,512,512]{2,1,0:T(8,128)(2,1)}, bf16[1,512,512]{2,1,0:T(8,128)(2,1)}, bf16[1,512,512]{2,1,0:T(8,128)(2,1)}, bf16[1,512,512]{2,1,0:T(8,128)(2,1)}) custom-call(s32[3]{0:T(128)} %pad_add_fusion.info_ref, bf16[512,4,512]{2,1,0:T(4,128)(2,1)} %refs_0_.3, f32[3,512,512]{2,1,0:T(8,128)} %weight_sums.2.refs_1_), custom_call_target="tpu_custom_call" | custom-call | tf_op jit(solution)/shard_map/split_heads/pallas_call | solution.py:71
  51.1 3.7 %collective-permute-start.3 = (bf16[1,512,512]{2,1,0:T(8,128)(2,1)}, bf16[1,512,512]{2,1,0:T(8,128)(2,1)S(1)}, u32[]{:S(2)}, u32[]{:S(2)}) collective-permute-start(bf16[1,512,512]{2,1,0:T(8,128)(2,1)} %get-tuple-element.25), channel_id=1, source_target_pairs={{0,4},{2,6},{4,0},{6,2},{8,12},{10,14},{12,8},{14,10},{16,20},{18,... | collective-permute-start | bytes 1572872 | tf_op jit(solution)/shard_map/ppermute | solution.py:89
  54.8 13.9 %collective-permute-done.2.refs_1_.refs_3_ = bf16[1,512,512]{2,1,0:T(8,128)(2,1)S(1)} collective-permute-done((bf16[1,512,512]{2,1,0:T(8,128)(2,1)}, bf16[1,512,512]{2,1,0:T(8,128)(2,1)S(1)}, u32[]{:S(2)}, u32[]{:S(2)}) %collective-permute-start.2) | collective-permute-done | bytes 524320 | tf_op jit(solution)/shard_map/ppermute | solution.py:89
  68.7 3.2 %collective-permute-start.8 = (bf16[2,512,512]{2,1,0:T(8,128)(2,1)}, bf16[2,512,512]{2,1,0:T(8,128)(2,1)}, u32[]{:S(2)}, u32[]{:S(2)}) collective-permute-start(bf16[2,512,512]{2,1,0:T(8,128)(2,1)} %collective-permute-done.1.refs_2_.refs_6_), channel_id=1, source_target_pairs={{0,8},{2,10},{4,12},{6,14},{8,16},{10,18},{12,20},{14,22},{16,24},... | collective-permute-start | bytes 3145736 | tf_op jit(solution)/shard_map/ppermute | solution.py:606
  71.9 1.6 collective-permute-done.3.refs_2_.refs_4_
  74.7 7.4 %weight_sums.3 = (bf16[3,256,512]{2,1,0:T(8,128)(2,1)}, bf16[3,256,512]{2,1,0:T(8,128)(2,1)}, bf16[2,512,512]{2,1,0:T(8,128)(2,1)}) custom-call(s32[3]{0:T(128)} %pad_add_fusion.info_ref, bf16[3,512,512]{2,1,0:T(8,128)(2,1)} %bitcast.17, bf16[2,512,512]{2,1,0:T(8,128)(2,1)} %collective-permute-done.5.refs_7_.refs_0_, f32[3,512,512]{2,1,0:T(8,128)} %weight_sums.2.refs_1_, ...), custom_call_target="tpu_custom_call" | custom-call | tf_op jit(solution)/shard_map/weight_sums/pallas_call | solution.py:153
  82.0 2.4 collective-permute-start.9
  84.4 3.0 %collective-permute-start.10 = (bf16[3,256,512]{2,1,0:T(8,128)(2,1)}, bf16[3,256,512]{2,1,0:T(8,128)(2,1)S(1)}, u32[]{:S(2)}, u32[]{:S(2)}) collective-permute-start(bf16[3,256,512]{2,1,0:T(8,128)(2,1)} %get-tuple-element.32), channel_id=1, source_target_pairs={{0,8},{2,10},{4,12},{6,14},{8,0},{10,2},{12,4},{14,6},{1,9},{3,11}... | collective-permute-start | bytes 2359304 | tf_op jit(solution)/shard_map/ppermute | solution.py:620
  88.1 1.3 collective-permute-start.12
  90.1 15.4 %own_attention.1 = (bf16[4,512,512]{2,1,0:T(8,128)(2,1)}, f32[4,8,512]{2,1,0:T(8,128)}) custom-call(s32[3]{0:T(128)} %pad_add_fusion.info_ref, bf16[1,512,512]{2,1,0:T(8,128)(2,1)} %get-tuple-element.23.refs_0_.refs_2_, bf16[1,512,512]{2,1,0:T(8,128)(2,1)} %copy-done.8, bf16[1,512,512]{2,1,0:T(8,128)(2,1)} %copy-done.9, bf16[1,512,512]{2,1,0:T(8,128)(2,1)} %copy-done.10, ...), custom_call_target="tpu_custom_call" | custom-call | tf_op jit(solution)/shard_map/own_attention/pallas_call | solution.py:281
  105.6 24.0 %collective-permute-done.10.refs_1_ = bf16[3,256,512]{2,1,0:T(8,128)(2,1)S(1)} collective-permute-done((bf16[3,256,512]{2,1,0:T(8,128)(2,1)}, bf16[3,256,512]{2,1,0:T(8,128)(2,1)S(1)}, u32[]{:S(2)}, u32[]{:S(2)}) %collective-permute-start.10) | collective-permute-done | bytes 786464 | tf_op jit(solution)/shard_map/ppermute | solution.py:620
  131.3 4.9 %renorm.1.refs_8_.refs_4_ = bf16[3,256,512]{2,1,0:T(8,128)(2,1)} custom-call(s32[3]{0:T(128)} %pad_add_fusion.info_ref, f32[1]{0:T(128)} %dynamic_slice.8.rate_ref, bf16[3,512,512]{2,1,0:T(8,128)(2,1)} %bitcast.18, bf16[3,256,512]{2,1,0:T(8,128)(2,1)} %get-tuple-element.31.refs_0_, bf16[3,256,512]{2,1,0:T(8,128)(2,1)} %copy-done.13, ...), custom_call_target="tpu_custom_call" | custom-call | tf_op jit(solution)/shard_map/renorm/pallas_call | solution.py:314
  136.2 1.9 collective-permute-start.13
  138.9 15.5 %cross_attention.1 = (bf16[4,512,512]{2,1,0:T(8,128)(2,1)}, f32[4,8,512]{2,1,0:T(8,128)}) custom-call(s32[3]{0:T(128)} %pad_add_fusion.info_ref, bf16[1,512,512]{2,1,0:T(8,128)(2,1)} %get-tuple-element.23.refs_0_.refs_2_, bf16[1,512,512]{2,1,0:T(8,128)(2,1)} %copy-done.8, bf16[1,512,512]{2,1,0:T(8,128)(2,1)} %copy-done.9, bf16[1,512,512]{2,1,0:T(8,128)(2,1)} %copy-done.10, ...), custom_call_target="tpu_custom_call" | custom-call | tf_op jit(solution)/shard_map/cross_attention/pallas_call | solution.py:373
  154.3 9.7 %first_rows.1.refs_1_.base_any = bf16[4,512,512]{2,1,0:T(8,128)(2,1)} custom-call(s32[3]{0:T(128)} %pad_add_fusion.info_ref, bf16[3,512,512]{2,1,0:T(8,128)(2,1)} %bitcast.19, bf16[1,512,512]{2,1,0:T(8,128)(2,1)} %get-tuple-element.23.refs_0_.refs_2_, bf16[1,512,512]{2,1,0:T(8,128)(2,1)} %copy-done.8, bf16[1,512,512]{2,1,0:T(8,128)(2,1)} %copy-done.9, ...), custom_call_target="tpu_custom_call" | custom-call | tf_op jit(solution)/shard_map/first_rows/pallas_call | solution.py:432
  164.8 1.6 copy-done.1
  169.0 10.9 %finish_rows.1 = bf16[16,4,32,512]{3,2,1,0:T(8,128)(2,1)} custom-call(s32[3]{0:T(128)} %pad_add_fusion.info_ref, f32[4,8,512]{2,1,0:T(8,128)} %copy-done.6, bf16[4,512,512]{2,1,0:T(8,128)(2,1)} %first_rows.1.refs_1_.base_any, bf16[1,512,512]{2,1,0:T(8,128)(2,1)} %get-tuple-element.23.refs_0_.refs_2_, bf16[1,512,512]{2,1,0:T(8,128)(2,1)} %copy-done.8, ...), custom_call_target="tpu_custom_call" | custom-call | tf_op jit(solution)/shard_map/finish_rows/pallas_call | solution.py:509
  179.9 24.1 %all-to-all-start.1 = ((bf16[16,4,32,512]{3,2,1,0:T(8,128)(2,1)}), bf16[16,4,32,512]{3,2,1,0:T(8,128)(2,1)S(1)}, u32[]{:S(2)}, u32[]{:S(2)}) async-start(bf16[16,4,32,512]{3,2,1,0:T(8,128)(2,1)} %finish_rows.1), calls=%async_computation.1 | async-start | bytes 4194304 | tf_op jit(solution)/shard_map/all_to_all | solution.py:646
  204.0 46.8 %all-to-all-done.1 = bf16[16,4,32,512]{3,2,1,0:T(8,128)(2,1)S(1)} async-done(((bf16[16,4,32,512]{3,2,1,0:T(8,128)(2,1)}), bf16[16,4,32,512]{3,2,1,0:T(8,128)(2,1)S(1)}, u32[]{:S(2)}, u32[]{:S(2)}) %all-to-all-start.1) | async-done | bytes 2097184 | tf_op jit(solution)/shard_map/all_to_all | solution.py:646
  251.4 4.8 %psum.7 = f32[4,128]{1,0:T(4,128)S(1)} all-reduce(f32[4,128]{1,0:T(4,128)S(1)} %reduce_sum.18), channel_id=1, replica_groups=mesh['seq'=16,'head'=2] {'head'}, use_global_device_ids=true, to_apply=%region_2.3 | all-reduce | flops 512 | bytes 4096 | tf_op jit(solution)/shard_map/psum | solution.py:649
  256.4 2.5 norm_rows.1
  (79 shorter events, 12.0 us)
Async XLA Ops:
  1.2 6.5 %copy-start.19 = (s32[512]{0:T(512)S(1)}, s32[512]{0:T(512)}, u32[]{:S(2)}) copy-start(s32[512]{0:T(512)} %param.15) | copy-start | bytes 6148
  6.3 25.6 %collective-permute-start = (bf16[2,512,512]{2,1,0:T(8,128)(2,1)}, bf16[2,512,512]{2,1,0:T(8,128)(2,1)S(1)}, u32[]{:S(2)}, u32[]{:S(2)}) collective-permute-start(bf16[2,512,512]{2,1,0:T(8,128)(2,1)} %get-tuple-element.21), channel_id=1, source_target_pairs={{0,2},{2,0},{4,6},{6,4},{8,10},{10,8},{12,14},{14,12},{16,18},{18,... | collective-permute-start | bytes 3145736 | tf_op jit(solution)/shard_map/ppermute | solution.py:89
  7.5 24.3 %collective-permute-start.1 = (bf16[2,512,512]{2,1,0:T(8,128)(2,1)}, bf16[2,512,512]{2,1,0:T(8,128)(2,1)}, u32[]{:S(2)}, u32[]{:S(2)}) collective-permute-start(bf16[2,512,512]{2,1,0:T(8,128)(2,1)} %get-tuple-element.22), channel_id=1, source_target_pairs={{0,4},{2,6},{4,0},{6,2},{8,12},{10,14},{12,8},{14,10},{16,20},{18,... | collective-permute-start | bytes 3145736 | tf_op jit(solution)/shard_map/ppermute | solution.py:89
  8.4 23.3 %all-to-all-start = ((s32[16,1,128]{2,1,0:T(1,128)}), s32[16,1,128]{2,1,0:T(1,128)S(1)}, u32[]{:S(2)}, u32[]{:S(2)}) async-start(s32[16,1,128]{2,1,0:T(1,128)} %bitcast.3), calls=%async_computation | async-start | bytes 16384 | tf_op jit(solution)/shard_map/all_to_all | solution.py:574
  14.1 40.7 %collective-permute-start.6 = (bf16[2,512,512]{2,1,0:T(8,128)(2,1)}, bf16[2,512,512]{2,1,0:T(8,128)(2,1)}, u32[]{:S(2)}, u32[]{:S(2)}) collective-permute-start(bf16[2,512,512]{2,1,0:T(8,128)(2,1)} %get-tuple-element.20.refs_0_.refs_4_), channel_id=1, source_target_pairs={{0,8},{2,10},{4,12},{6,14},{8,16},{10,18},{12,20},{14,22},{16,24},... | collective-permute-start | bytes 3145736 | tf_op jit(solution)/shard_map/ppermute | solution.py:606
  23.7 10.8 %copy-start = (bf16[512,1,3,512]{3,0,2,1:T(8,128)(2,1)}, bf16[512,1,3,512]{3,0,2,1:T(8,128)(2,1)S(1)}, u32[]{:S(2)}) copy-start(bf16[512,1,3,512]{3,0,2,1:T(8,128)(2,1)S(1)} %copy.22) | copy-start | bytes 4718596
  31.8 3.5 %copy-start.2 = (bf16[2,512,512]{2,1,0:T(8,128)(2,1)}, bf16[2,512,512]{2,1,0:T(8,128)(2,1)S(1)}, u32[]{:S(2)}) copy-start(bf16[2,512,512]{2,1,0:T(8,128)(2,1)S(1)} %collective-permute-done.refs_1_.refs_5_) | copy-start | bytes 3145732
  31.9 2.7 %copy-start.6 = (f32[4,8,512]{2,1,0:T(8,128)}, f32[4,8,512]{2,1,0:T(8,128)S(1)}, u32[]{:S(2)}) copy-start(f32[4,8,512]{2,1,0:T(8,128)S(1)} %broadcast_in_dim.20.refs_4_.place_ref) | copy-start | bytes 196612
  31.9 1.6 copy-start.5
  34.5 39.0 %collective-permute-start.5 = (bf16[2,512,512]{2,1,0:T(8,128)(2,1)}, bf16[2,512,512]{2,1,0:T(8,128)(2,1)}, u32[]{:S(2)}, u32[]{:S(2)}) collective-permute-start(bf16[2,512,512]{2,1,0:T(8,128)(2,1)} %pass_after.3), channel_id=1, source_target_pairs={{0,6},{2,4},{4,2},{6,0},{8,14},{10,12},{12,10},{14,8},{16,22},{18,... | collective-permute-start | bytes 3145736 | tf_op jit(solution)/shard_map/ppermute | solution.py:601
  35.3 38.2 %collective-permute-start.7 = (bf16[2,512,512]{2,1,0:T(8,128)(2,1)S(1)}, bf16[2,512,512]{2,1,0:T(8,128)(2,1)S(1)}, u32[]{:S(2)}, u32[]{:S(2)}) collective-permute-start(bf16[2,512,512]{2,1,0:T(8,128)(2,1)S(1)} %collective-permute-done.refs_1_.refs_5_), channel_id=1, source_target_pairs={{0,8},{2,10},{4,12},{6,14},{8,16},{10,18},{12,20},{14,22},{16,24},... | collective-permute-start | bytes 3145736 | tf_op jit(solution)/shard_map/ppermute | solution.py:606
  50.5 18.2 %collective-permute-start.2 = (bf16[1,512,512]{2,1,0:T(8,128)(2,1)}, bf16[1,512,512]{2,1,0:T(8,128)(2,1)S(1)}, u32[]{:S(2)}, u32[]{:S(2)}) collective-permute-start(bf16[1,512,512]{2,1,0:T(8,128)(2,1)} %get-tuple-element.24), channel_id=1, source_target_pairs={{0,2},{2,0},{4,6},{6,4},{8,10},{10,8},{12,14},{14,12},{16,18},{18,... | collective-permute-start | bytes 1572872 | tf_op jit(solution)/shard_map/ppermute | solution.py:89
  51.1 22.4 %collective-permute-start.3 = (bf16[1,512,512]{2,1,0:T(8,128)(2,1)}, bf16[1,512,512]{2,1,0:T(8,128)(2,1)S(1)}, u32[]{:S(2)}, u32[]{:S(2)}) collective-permute-start(bf16[1,512,512]{2,1,0:T(8,128)(2,1)} %get-tuple-element.25), channel_id=1, source_target_pairs={{0,4},{2,6},{4,0},{6,2},{8,12},{10,14},{12,8},{14,10},{16,20},{18,... | collective-permute-start | bytes 1572872 | tf_op jit(solution)/shard_map/ppermute | solution.py:89
  54.8 33.3 %collective-permute-start.4 = (bf16[1,512,512]{2,1,0:T(8,128)(2,1)}, bf16[1,512,512]{2,1,0:T(8,128)(2,1)S(1)}, u32[]{:S(2)}, u32[]{:S(2)}) collective-permute-start(bf16[1,512,512]{2,1,0:T(8,128)(2,1)} %get-tuple-element.26), channel_id=1, source_target_pairs={{0,6},{2,4},{4,2},{6,0},{8,14},{10,12},{12,10},{14,8},{16,22},{18,... | collective-permute-start | bytes 1572872 | tf_op jit(solution)/shard_map/ppermute | solution.py:89
  68.7 4.8 %copy-start.8 = (bf16[1,512,512]{2,1,0:T(8,128)(2,1)}, bf16[1,512,512]{2,1,0:T(8,128)(2,1)S(1)}, u32[]{:S(2)}) copy-start(bf16[1,512,512]{2,1,0:T(8,128)(2,1)S(1)} %collective-permute-done.2.refs_1_.refs_3_) | copy-start | bytes 1572868
  68.7 36.8 %collective-permute-start.8 = (bf16[2,512,512]{2,1,0:T(8,128)(2,1)}, bf16[2,512,512]{2,1,0:T(8,128)(2,1)}, u32[]{:S(2)}, u32[]{:S(2)}) collective-permute-start(bf16[2,512,512]{2,1,0:T(8,128)(2,1)} %collective-permute-done.1.refs_2_.refs_6_), channel_id=1, source_target_pairs={{0,8},{2,10},{4,12},{6,14},{8,16},{10,18},{12,20},{14,22},{16,24},... | collective-permute-start | bytes 3145736 | tf_op jit(solution)/shard_map/ppermute | solution.py:606
  74.7 14.8 %copy-start.20 = (f32[4]{0:T(128)S(1)}, f32[4]{0:T(128)}, u32[]{:S(2)}) copy-start(f32[4]{0:T(128)} %param.12) | copy-start | bytes 52
  82.0 47.6 %collective-permute-start.9 = (bf16[2,512,512]{2,1,0:T(8,128)(2,1)}, bf16[2,512,512]{2,1,0:T(8,128)(2,1)S(1)}, u32[]{:S(2)}, u32[]{:S(2)}) collective-permute-start(bf16[2,512,512]{2,1,0:T(8,128)(2,1)} %get-tuple-element.30), channel_id=1, source_target_pairs={{0,8},{2,10},{4,12},{6,14},{8,16},{10,18},{12,20},{14,22},{16,24},... | collective-permute-start | bytes 3145736 | tf_op jit(solution)/shard_map/ppermute | solution.py:613
  84.4 45.1 %collective-permute-start.10 = (bf16[3,256,512]{2,1,0:T(8,128)(2,1)}, bf16[3,256,512]{2,1,0:T(8,128)(2,1)S(1)}, u32[]{:S(2)}, u32[]{:S(2)}) collective-permute-start(bf16[3,256,512]{2,1,0:T(8,128)(2,1)} %get-tuple-element.32), channel_id=1, source_target_pairs={{0,8},{2,10},{4,12},{6,14},{8,0},{10,2},{12,4},{14,6},{1,9},{3,11}... | collective-permute-start | bytes 2359304 | tf_op jit(solution)/shard_map/ppermute | solution.py:620
  87.4 42.2 %collective-permute-start.11 = (bf16[3,256,512]{2,1,0:T(8,128)(2,1)}, bf16[3,256,512]{2,1,0:T(8,128)(2,1)S(1)}, u32[]{:S(2)}, u32[]{:S(2)}) collective-permute-start(bf16[3,256,512]{2,1,0:T(8,128)(2,1)} %get-tuple-element.31.refs_0_), channel_id=1, source_target_pairs={{16,0},{18,2},{20,4},{22,6},{17,1},{19,3},{21,5},{23,7}} | collective-permute-start | bytes 2359304 | tf_op jit(solution)/shard_map/ppermute | solution.py:620
  88.1 2.0 copy-start.10
  88.1 41.4 %collective-permute-start.12 = (bf16[3,256,512]{2,1,0:T(8,128)(2,1)}, bf16[3,256,512]{2,1,0:T(8,128)(2,1)S(1)}, u32[]{:S(2)}, u32[]{:S(2)}) collective-permute-start(bf16[3,256,512]{2,1,0:T(8,128)(2,1)} %get-tuple-element.32), channel_id=1, source_target_pairs={{16,8},{18,10},{20,12},{22,14},{17,9},{19,11},{21,13},{23,15}} | collective-permute-start | bytes 2359304 | tf_op jit(solution)/shard_map/ppermute | solution.py:620
  129.6 1.7 copy-start.12
  136.2 27.8 %collective-permute-start.13 = (bf16[3,256,512]{2,1,0:T(8,128)(2,1)}, bf16[3,256,512]{2,1,0:T(8,128)(2,1)S(1)}, u32[]{:S(2)}, u32[]{:S(2)}) collective-permute-start(bf16[3,256,512]{2,1,0:T(8,128)(2,1)} %renorm.1.refs_8_.refs_4_), channel_id=1, source_target_pairs={{0,8},{2,10},{4,12},{6,14},{8,16},{10,18},{12,20},{14,22},{1,9},{3... | collective-permute-start | bytes 2359304 | tf_op jit(solution)/shard_map/ppermute | solution.py:620
  138.1 26.7 %collective-permute-start.14 = (bf16[3,256,512]{2,1,0:T(8,128)(2,1)}, bf16[3,256,512]{2,1,0:T(8,128)(2,1)S(1)}, u32[]{:S(2)}, u32[]{:S(2)}) collective-permute-start(bf16[3,256,512]{2,1,0:T(8,128)(2,1)} %renorm.1.refs_8_.refs_4_), channel_id=1, source_target_pairs={{0,16},{2,18},{4,20},{6,22},{1,17},{3,19},{5,21},{7,23}} | collective-permute-start | bytes 2359304 | tf_op jit(solution)/shard_map/ppermute | solution.py:620
  154.3 9.7 %copy-start.7 = (f32[4,8,512]{2,1,0:T(8,128)S(1)}, f32[4,8,512]{2,1,0:T(8,128)}, u32[]{:S(2)}) copy-start(f32[4,8,512]{2,1,0:T(8,128)} %get-tuple-element.34.refs_7_.refs_1_) | copy-start | bytes 196612
  164.0 2.5 copy-start.4
  164.1 3.1 %collective-permute-start.15 = (bf16[3,256,512]{2,1,0:T(8,128)(2,1)S(1)}, bf16[3,256,512]{2,1,0:T(8,128)(2,1)S(1)}, u32[]{:S(2)}, u32[]{:S(2)}) collective-permute-start(bf16[3,256,512]{2,1,0:T(8,128)(2,1)S(1)} %pass_after.4), channel_id=1, source_target_pairs={{16,24},{18,26},{20,28},{22,30},{17,25},{19,27},{21,29},{23,31}} | collective-permute-start | bytes 2359304 | tf_op jit(solution)/shard_map/ppermute | solution.py:620
  164.8 1.6 copy-start.1
  166.5 0.7 collective-permute-start.16
  179.9 24.1 %copy-start.18 = (f32[4,512]{1,0:T(4,128)S(1)}, f32[4,512]{1,0:T(4,128)}, u32[]{:S(2)}) copy-start(f32[4,512]{1,0:T(4,128)} %param.13) | copy-start | bytes 24580
  179.9 70.9 %all-to-all-start.1 = ((bf16[16,4,32,512]{3,2,1,0:T(8,128)(2,1)}), bf16[16,4,32,512]{3,2,1,0:T(8,128)(2,1)S(1)}, u32[]{:S(2)}, u32[]{:S(2)}) async-start(bf16[16,4,32,512]{3,2,1,0:T(8,128)(2,1)} %finish_rows.1), calls=%async_computation.1 | async-start | bytes 4194304 | tf_op jit(solution)/shard_map/all_to_all | solution.py:646
  (8 other events, 8.0 us)
